TPU v7x, 32 devices: a whole 2x2x4 slice. The times are simulated.
32 devices in a mesh: sec: 4 (over x, core), seq: 4 (over z), tp: 2 (over y).
Axes of the slice: x: 2, y: 2, z: 4, core: 2. Of those that a mesh axis runs over, the one named last changes fastest.
Arguments:
- vis_rows: bfloat16 [512, 3200], P('seq'), may hold values from -6 to 6
- vis_gain: float32 [3200], replicated, may hold values from 0.1 to 1.9
- key_value_proj: bfloat16 [3200, 2048], P(None, ('sec', 'tp')), may hold values from -0.109375 to 0.109375
- pieces: int32 [8], replicated, may hold values from 1 to 127, as said below
- text_kv: bfloat16 [512, 2048], P('seq', ('sec', 'tp')), may hold values from -6 to 6
- queries: bfloat16 [512, 4096], P('seq', ('sec', 'tp')), may hold values from -256 to 256
- grad_out: bfloat16 [512, 4096], P('seq', ('sec', 'tp')), may hold values from -6 to 6
Outputs:
- attended: bfloat16 [512, 4096], P('seq', ('sec', 'tp'))
- vis_grad: bfloat16 [512, 3200], P('seq')
Inputs may be any that keep to these rules, and one draw needn't show every extreme that they name: `pieces`: entries alternate: the text positions before image j, then the tokens of image j, for j = 0 to 3; entries 2 j and 2 j + 1 sum to 128; image j's tokens are the leading rows of block b_j of vis_rows.
All inputs are finite; a program needn't handle non-finite values.
Results may differ from a plain program's by a relative error of at most 0.033.
Values may be sent and summed in bfloat16 or wider, within the bound.
No kernel may reach another device: no remote copies, remote signals or barrier semaphores. Data moves between devices by JAX's collectives and lax.ppermute only.
A program may use at most 64 MiB of HBM per device.

v0:
```python
import math

import jax
import jax.numpy as jnp
from jax import lax
from jax.sharding import PartitionSpec as P

HD = 128


EPS = 1e-06
NEG = -1e30


def image_layout(pieces):
    totals = jnp.cumsum(pieces)
    lens_img = pieces[1::2]
    starts_img = totals[1::2] - lens_img
    return (starts_img, lens_img)


def owner_block(image_ids, image_count):
    half_count = image_count // 2
    return jnp.where(
        image_ids >= half_count, image_ids - half_count, half_count + (image_ids + 1) % half_count
    )


def image_held(block_ids, image_count):
    half_count = image_count // 2
    return jnp.where(
        block_ids < half_count, block_ids + half_count, (block_ids - half_count - 1) % half_count
    )


def compose_keys(image_all, text_all, starts_img, lens_img, rows_each):
    total_rows = text_all.shape[0]
    image_count = starts_img.shape[0]
    positions = jnp.arange(total_rows, dtype=jnp.int32)
    offset_rows = positions[:, None] - starts_img[None, :]
    inside = (offset_rows >= 0) & (offset_rows < lens_img[None, :])
    owners = owner_block(jnp.arange(image_count, dtype=jnp.int32), image_count)
    source = jnp.sum(jnp.where(inside, owners[None, :] * rows_each + offset_rows, 0), axis=1)
    marked = jnp.any(inside, axis=1)
    return jnp.where(marked[:, None], image_all[source], text_all)


def head_group(query_part, grad_part, key_blocks, value_blocks, query_pos, score_scale):
    block_count, key_block, head_size = key_blocks.shape
    group_size = query_part.shape[1]
    row_count = query_part.shape[0]
    last_pos = query_pos[row_count - 1]
    block_starts = jnp.arange(block_count, dtype=jnp.int32) * key_block

    def scores_at(key_blk, start):
        scores = (
            jnp.einsum("rhe,ke->hrk", query_part, key_blk, preferred_element_type=jnp.float32)
            * score_scale
        )
        key_pos = start + jnp.arange(key_block, dtype=jnp.int32)
        allowed = key_pos[None, None, :] <= query_pos[None, :, None]
        return jnp.where(allowed, scores, NEG)

    def stat_step(carry, inputs):
        key_blk, start = inputs

        def stat_live(state):
            run_max, run_sum = state
            scores = scores_at(key_blk, start)
            new_max = jnp.maximum(run_max, jnp.max(scores, axis=-1))
            new_sum = run_sum * jnp.exp(run_max - new_max) + jnp.sum(
                jnp.exp(scores - new_max[:, :, None]), axis=-1
            )
            return (new_max, new_sum)

        return (lax.cond(start <= last_pos, stat_live, lambda state: state, carry), None)

    start_state = (
        jnp.full((group_size, row_count), NEG, jnp.float32),
        jnp.zeros((group_size, row_count), jnp.float32),
    )
    (row_max, row_sum), _ = lax.scan(stat_step, start_state, (key_blocks, block_starts))

    def probs_at(key_blk, start):
        scores = scores_at(key_blk, start)
        return jnp.exp(scores - row_max[:, :, None]) / row_sum[:, :, None]

    def mix_step(carry, inputs):
        key_blk, value_blk, start = inputs

        def mix_live(total):
            weights_low = probs_at(key_blk, start).astype(jnp.bfloat16)
            return total + jnp.einsum(
                "hrk,ke->rhe", weights_low, value_blk, preferred_element_type=jnp.float32
            )

        return (lax.cond(start <= last_pos, mix_live, lambda total: total, carry), None)

    mixed_rows, _ = lax.scan(
        mix_step,
        jnp.zeros((row_count, group_size, head_size), jnp.float32),
        (key_blocks, value_blocks, block_starts),
    )
    row_drift = jnp.transpose(jnp.sum(grad_part.astype(jnp.float32) * mixed_rows, axis=-1))

    def grad_step(carry, inputs):
        key_blk, value_blk, start = inputs

        def grad_live(operands):
            weights = probs_at(key_blk, start)
            weights_low = weights.astype(jnp.bfloat16)
            weight_grads = jnp.einsum(
                "rhe,ke->hrk", grad_part, value_blk, preferred_element_type=jnp.float32
            )
            score_grads = (weights * (weight_grads - row_drift[:, :, None]) * score_scale).astype(
                jnp.bfloat16
            )
            key_part = jnp.einsum(
                "hrk,rhe->ke", score_grads, query_part, preferred_element_type=jnp.float32
            )
            value_part = jnp.einsum(
                "hrk,rhe->ke", weights_low, grad_part, preferred_element_type=jnp.float32
            )
            return (key_part, value_part)

        def dead(operands):
            empty = jnp.zeros((key_block, head_size), jnp.float32)
            return (empty, empty)

        return (carry, lax.cond(start <= last_pos, grad_live, dead, 0))

    _, (key_parts, value_parts) = lax.scan(grad_step, 0, (key_blocks, value_blocks, block_starts))
    total_rows = block_count * key_block
    return (
        mixed_rows,
        key_parts.reshape(total_rows, head_size),
        value_parts.reshape(total_rows, head_size),
    )


def on_device(vis_rows, vis_gain, key_value_proj, pieces, text_kv, queries, grad_out):
    row_count = vis_rows.shape[0]
    kv_local = key_value_proj.shape[1] // (2 * HD)
    group_size = queries.shape[1] // HD // kv_local
    score_scale = 1.0 / math.sqrt(HD)
    seq_rank = lax.axis_index("seq")
    seq_count = lax.axis_size("seq")
    starts_img, lens_img = image_layout(pieces)
    wide_rows = vis_rows.astype(jnp.float32)
    inverse = lax.rsqrt(jnp.mean(wide_rows * wide_rows, axis=-1, keepdims=True) + EPS)
    normed_rows = (wide_rows * inverse * vis_gain).astype(jnp.bfloat16)
    text_all = lax.all_gather(text_kv, "seq", axis=0, tiled=True)
    image_kv = jnp.dot(normed_rows, key_value_proj, preferred_element_type=jnp.float32).astype(
        jnp.bfloat16
    )
    image_all = lax.all_gather(image_kv, "seq", axis=0, tiled=True)
    seq_kv = compose_keys(image_all, text_all, starts_img, lens_img, row_count)
    total_rows = seq_kv.shape[0]
    key_block = math.gcd(total_rows, 512)
    block_count = total_rows // key_block
    query_pos = seq_rank * row_count + jnp.arange(row_count, dtype=jnp.int32)
    grad_blocks = []
    key_blocks = seq_kv[:, 0:HD].reshape(block_count, key_block, HD)
    value_blocks = seq_kv[:, HD : 2 * HD].reshape(block_count, key_block, HD)
    query_part = queries.reshape(row_count, group_size, HD)
    grad_part = grad_out.reshape(row_count, group_size, HD)
    mixed_rows, key_total, value_total = head_group(
        query_part, grad_part, key_blocks, value_blocks, query_pos, score_scale
    )
    out_blocks = mixed_rows.reshape(row_count, group_size * HD).astype(jnp.bfloat16)
    grad_blocks.append(key_total)
    grad_blocks.append(value_total)
    key_terms = jnp.concatenate(grad_blocks, axis=1)
    row_ids = jnp.arange(row_count, dtype=jnp.int32)
    own_sum = lax.psum_scatter(
        key_terms.astype(jnp.bfloat16), "seq", scatter_dimension=0, tiled=True
    )
    gathered = lax.all_gather(own_sum, "seq", axis=0, tiled=True)
    image_index = image_held(seq_rank, seq_count)
    image_start = lax.dynamic_index_in_dim(starts_img, image_index, keepdims=False)
    row_total = lax.dynamic_index_in_dim(lens_img, image_index, keepdims=False)
    targets = jnp.clip(image_start + row_ids, 0, total_rows - 1)
    image_grad = jnp.where(
        (row_ids < row_total)[:, None], gathered[targets], jnp.zeros((), jnp.bfloat16)
    )
    partial_grad = lax.dot_general(
        image_grad, key_value_proj, (((1,), (1,)), ((), ())), preferred_element_type=jnp.float32
    )
    feature_grad = lax.psum(partial_grad.astype(jnp.bfloat16), ("sec", "tp")).astype(jnp.float32)
    scaled_grad = feature_grad * vis_gain
    row_stat = jnp.mean(wide_rows * scaled_grad, axis=-1, keepdims=True)
    vis_grad = (scaled_grad * inverse - wide_rows * inverse * inverse * inverse * row_stat).astype(
        jnp.bfloat16
    )
    return (out_blocks, vis_grad)


def solution(mesh):
    in_specs = (
        P("seq", None),
        P(),
        P(None, ("sec", "tp")),
        P(),
        P("seq", ("sec", "tp")),
        P("seq", ("sec", "tp")),
        P("seq", ("sec", "tp")),
    )
    out_specs = (P("seq", ("sec", "tp")), P("seq", None))
    return jax.shard_map(
        on_device, mesh=mesh, in_specs=in_specs, out_specs=out_specs, check_vma=False
    )
```

profile of v0, /device:TPU:0, one launch (start us, length us, event | category | flops | bytes accessed | tf_op | source)
XLA Modules:
  0.0 154.4 jit_solution(65366707792703910)
XLA Ops:
  7.2 0.0 copy-start
  7.2 0.0 reduce-scatter.2.cloned.1.call-start
  7.3 0.6 slice.15
  8.5 1.4 fusion.49
  9.9 0.0 copy-start.6
  9.9 1.6 %convolution_convert_fusion.1 = bf16[128,256]{1,0:T(8,128)(2,1)S(1)} fusion(bf16[3200,256]{1,0:T(8,128)(2,1)S(1)} %copy-done, bf16[128,3200]{1,0:T(8,128)(2,1)} %param.13, f32[3200]{0:T(1024)} %param.14, f32[128]{0:T(128)S(1)} %add_rsqrt_fusion), kind=kOutput, calls=%fused_computation.66 | convolution fusion | flops 211386368 | bytes 2536448 | tf_op jit(solution)/shard_map/dot_general | solution.py:153
  11.5 15.6 %all_gather.9 = bf16[512,256]{1,0:T(8,128)(2,1)S(1)} all-gather(bf16[128,256]{1,0:T(8,128)(2,1)S(1)} %convolution_convert_fusion.1), channel_id=1, replica_groups=mesh['sec'=4,'seq'=4,'tp'=2] {'seq'}, dimensions={0}, use_global_device_ids=true | all-gather | bytes 327680 | tf_op jit(solution)/shard_map/all_gather | solution.py:156
  27.2 0.1 slice.17
  27.3 0.2 reduce-window.9
  27.5 0.1 slice.16
  27.6 0.1 fusion.65
  27.7 0.1 select_reduce_fusion
  27.8 14.4 %all_gather.10 = bf16[512,256]{1,0:T(8,128)(2,1)S(1)} all-gather(bf16[128,256]{1,0:T(8,128)(2,1)S(1)} %copy-done.6), channel_id=1, replica_groups=mesh['sec'=4,'seq'=4,'tp'=2] {'seq'}, dimensions={0}, use_global_device_ids=true | all-gather | bytes 327680 | tf_op jit(solution)/shard_map/all_gather | solution.py:152
  42.2 1.9 %gather_fusion = bf16[512,256]{1,0:T(8,128)(2,1)S(1)} fusion(bf16[512,256]{1,0:T(8,128)(2,1)S(1)} %all_gather.9, s32[1024]{0:T(1024)S(1)} %pad_clamp_fusion.1), kind=kCustom, calls=%fused_computation | custom fusion | bytes 526336 | tf_op jit(solution)/shard_map/gather | solution.py:45
  44.2 0.1 broadcast_select_fusion
  44.3 0.7 fusion.67
  45.0 0.0 copy-done.3
  45.0 0.1 copy.20
  45.1 1.5 conditional.3
  45.2 1.2 fusion.66
  46.4 0.2 exponential_reduce_fusion
  46.6 0.0 copy-start.4
  46.7 1.6 %conditional.4 = (f32[128,4,128]{2,0,1:T(8,128)S(1)}) conditional(s32[]{:T(128)} %bitcast.12, f32[128,4,128]{2,0,1:T(8,128)S(1)} %broadcast_in_dim.89, (s32[128]{0:T(128)S(1)}, bf16[512,128]{1,0:T(8,128)(2,1)}, bf16[128,4,128]{0,2,1:T(8,128)(2,1)S(1)}, f32[4,128]{1,0:T(4,128)S(1)}, f32[4,128]{1,0:T(4,128)S(1)}, ...), branch_computations={%region_8.9_spmd, %region_9.10_spmd} | conditional | flops 135659520 | bytes 1053192 | solution.py:97
  46.7 1.6 %fusion.11 = f32[128,4,128]{2,0,1:T(8,128)S(1)} fusion(f32[128,4,128]{2,0,1:T(8,128)S(1)} %get-tuple-element.114, bf16[128,4,128]{0,2,1:T(8,128)(2,1)S(1)} %get-tuple-element.208, f32[4,128]{1,0:T(4,128)S(1)} %get-tuple-element.140, f32[4,128]{1,0:T(4,128)S(1)} %get-tuple-element.139, pred[128,512]{0,1:T(8,128)(4,1)S(1)} %iota_compare_fusion.1, ...), kind=kOutput, calls=%fused_computation.18 | convolution fusion | flops 135593984 | bytes 987136 | tf_op jit(solution)/shard_map/while/body/eval_jaxpr/cond/branch_1_fun/hrk,ke->rhe/dot_general | solution.py:93
  48.3 0.1 copy.24
  48.4 0.1 copy.25
  48.6 2.7 %conditional.5 = (bf16[512,128]{1,0:T(8,128)(2,1)S(1)}, bf16[512,128]{1,0:T(8,128)(2,1)}) conditional(s32[]{:T(128)} %bitcast.12, () %tuple.49, (s32[128]{0:T(128)S(1)}, bf16[512,128]{1,0:T(8,128)(2,1)}, bf16[128,4,128]{0,2,1:T(8,128)(2,1)S(1)}, f32[4,128]{1,0:T(4,128)S(1)}, f32[4,128]{1,0:T(4,128)S(1)}, ...), branch_computations={%region_11.12_spmd, %region_12.13_spmd} | conditional | flops 270991360 | bytes 4332048 | solution.py:130
  48.7 1.3 fusion.29
  50.0 0.4 fusion.33
  50.4 0.9 fusion.34
  51.4 1.6 %pad_maximum_fusion = bf16[512,256]{1,0:T(8,128)(2,1)} fusion(bf16[512,128]{1,0:T(8,128)(2,1)} %get-tuple-element.173, bf16[512,128]{1,0:T(8,128)(2,1)S(1)} %get-tuple-element.172), kind=kLoop, calls=%fused_computation.69 | loop fusion | flops 524288 | bytes 524288 | tf_op jit(solution)/shard_map/concatenate | solution.py:173
  53.0 0.0 reduce-scatter.2.cloned.1.call-update
  53.0 0.0 all-reduce.2.cloned.1.call-start
  53.1 0.6 dynamic_slice.26
  53.7 0.6 dynamic_slice.25
  54.3 0.7 fusion.63
  55.0 0.6 iota_compare_fusion.3
  55.6 18.3 %reduce-scatter.2.cloned.1.call-done = bf16[128,256]{1,0:T(8,128)(2,1)} async-done(((bf16[512,256]{1,0:T(8,128)(2,1)}), bf16[128,256]{1,0:T(8,128)(2,1)}) %reduce-scatter.2.cloned.1.call-update) | async-done | bytes 65552 | tf_op jit(solution)/shard_map/reduce_scatter | solution.py:175
  73.9 14.1 %all_gather.11 = bf16[512,256]{1,0:T(8,128)(2,1)S(1)} all-gather(bf16[128,256]{1,0:T(8,128)(2,1)} %reduce-scatter.2.cloned.1.call-done), channel_id=1, replica_groups=mesh['sec'=4,'seq'=4,'tp'=2] {'seq'}, dimensions={0}, use_global_device_ids=true | all-gather | bytes 327680 | tf_op jit(solution)/shard_map/all_gather | solution.py:178
  88.0 0.8 gather_fusion.1
  88.8 0.0 copy-start.1
  88.8 0.0 copy-start.5
  88.8 1.6 %convolution_convert_fusion = bf16[128,3200]{1,0:T(8,128)(2,1)} fusion(bf16[3200,256]{1,0:T(8,128)(2,1)S(1)} %copy-done, bf16[128,256]{1,0:T(8,128)(2,1)S(1)} %gather_fusion.1, pred[128]{0:T(512)(128)(4,1)S(1)} %iota_compare_fusion.3), kind=kOutput, calls=%fused_computation.52 | convolution fusion | flops 210157568 | bytes 2523264 | tf_op jit(solution)/shard_map/dot_general | solution.py:186
  90.4 0.0 all-reduce.2.cloned.1.call-update
  90.4 0.7 copy_bitcast_fusion
  91.1 53.4 %all-reduce.2.cloned.1.call-done = bf16[128,3200]{1,0:T(8,128)(2,1)} async-done(((bf16[128,3200]{1,0:T(8,128)(2,1)}), bf16[128,3200]{1,0:T(8,128)(2,1)}) %all-reduce.2.cloned.1.call-update) | async-done | bytes 819216 | tf_op jit(solution)/shard_map/psum | solution.py:189
  144.5 1.6 %fusion.50 = f32[128]{0:T(128)S(1)} fusion(bf16[128,3200]{1,0:T(8,128)(2,1)S(1)} %copy-done.1, bf16[128,3200]{1,0:T(8,128)(2,1)} %all-reduce.2.cloned.1.call-done, f32[3200]{0:T(1024)S(1)} %copy-done.5), kind=kLoop, calls=%fused_computation.64 | loop fusion | flops 2047872 | bytes 1651712 | tf_op jit(solution)/shard_map/reduce_sum | solution.py:191
  146.1 1.5 fusion.48
  (28 shorter events, 0.3 us)
Async XLA Ops:
  7.2 2.8 %copy-start = (bf16[3200,256]{1,0:T(8,128)(2,1)S(1)}, bf16[3200,256]{1,0:T(8,128)(2,1)}, u32[]{:S(2)}) copy-start(bf16[3200,256]{1,0:T(8,128)(2,1)} %param.15) | copy-start | bytes 4915204
  7.2 66.7 %reduce-scatter.2.cloned.1.call-start = ((), (), s32[]{:S(2)}) async-start(), calls=%async_computation.1 | async-start | bytes 327680 | tf_op jit(solution)/shard_map/reduce_scatter | solution.py:175
  9.9 17.3 %copy-start.7 = (s32[8]{0:T(128)S(1)}, s32[8]{0:T(128)}, u32[]{:S(2)}) copy-start(s32[8]{0:T(128)} %param.16) | copy-start | bytes 100
  9.9 17.9 %copy-start.6 = (bf16[128,256]{1,0:T(8,128)(2,1)S(1)}, bf16[128,256]{1,0:T(8,128)(2,1)}, u32[]{:S(2)}) copy-start(bf16[128,256]{1,0:T(8,128)(2,1)} %param.17) | copy-start | bytes 196612
  42.2 2.8 %copy-start.3 = (bf16[128,512]{1,0:T(8,128)(2,1)S(1)}, bf16[128,512]{1,0:T(8,128)(2,1)}, u32[]{:S(2)}) copy-start(bf16[128,512]{1,0:T(8,128)(2,1)} %param.18) | copy-start | bytes 393220
  46.6 1.7 %copy-start.4 = (bf16[128,512]{1,0:T(8,128)(2,1)S(1)}, bf16[128,512]{1,0:T(8,128)(2,1)}, u32[]{:S(2)}) copy-start(bf16[128,512]{1,0:T(8,128)(2,1)} %param.19) | copy-start | bytes 393220
  53.0 91.5 %all-reduce.2.cloned.1.call-start = ((), (), s32[]{:S(2)}) async-start(), calls=%async_computation.2 | async-start | bytes 1638400 | tf_op jit(solution)/shard_map/psum | solution.py:189
  88.8 55.7 %copy-start.1 = (bf16[128,3200]{1,0:T(8,128)(2,1)S(1)}, bf16[128,3200]{1,0:T(8,128)(2,1)}, u32[]{:S(2)}) copy-start(bf16[128,3200]{1,0:T(8,128)(2,1)} %param.13) | copy-start | bytes 2457604
  88.8 55.7 %copy-start.5 = (f32[3200]{0:T(1024)S(1)}, f32[3200]{0:T(1024)}, u32[]{:S(2)}) copy-start(f32[3200]{0:T(1024)} %param.14) | copy-start | bytes 38404
  144.5 1.6 %copy-start.2 = (bf16[128,3200]{1,0:T(8,128)(2,1)S(1)}, bf16[128,3200]{1,0:T(8,128)(2,1)}, u32[]{:S(2)}) copy-start(bf16[128,3200]{1,0:T(8,128)(2,1)} %all-reduce.2.cloned.1.call-done) | copy-start | bytes 2457604
Sparse Core Ops, SparseCore 0:
  53.1 20.6 reduce-scatter.1
  90.5 53.9 all-reduce.1
where the time goes:
time: 155 us; the launch traced here: 154 us
  waiting for transfers between devices  71.7 us (46%)
  blocking collectives  44.2 us (29%)
  between operations  14.9 us (10%)
  other arithmetic  8.92 us (6%)
  matrix products  8.61 us (6%)
  local copies, waits for them, and re-layouts  5.89 us (4%)
    psum x1, waiting for transfers between devices, on_device(): lax.psum(partial_grad.astype(jnp.bfloat16), ('sec', 'tp'))  53.4 us
    reduce_scatter x1, waiting for transfers between devices, on_device(): lax.psum_scatter(key_terms.astype(jnp.bfloat16), 'seq', scatter_dimension...  18.3 us
    all_gather x1, blocking collectives, on_device(): image_all = lax.all_gather(image_kv, 'seq', axis=0, tiled=True)  15.6 us
    all_gather x1, blocking collectives, on_device(): text_all = lax.all_gather(text_kv, 'seq', axis=0, tiled=True)  14.4 us
    all_gather x1, blocking collectives, on_device(): gathered = lax.all_gather(own_sum, 'seq', axis=0, tiled=True)  14.1 us
  transfers between devices with their start and end apart: 2, of which 2 were waited for; matrix products, arithmetic and copies ran while one was open for 2% of the time, Pallas kernels for 0%

commit v1 on v0

v1 whole, which is shorter than its diff:
```python
import math

import jax
import jax.numpy as jnp
from jax import lax
from jax.sharding import PartitionSpec as P

HD = 128
EPS = 1e-06
NEG = -1e30


def owner_block(image, count):
    half = count // 2
    return image - half if image >= half else half + (image + 1) % half


def shift_rows(rows, shift, length, offset):
    count = rows.shape[0]
    r = lax.broadcasted_iota(jnp.int32, (count, count), 0)
    c = lax.broadcasted_iota(jnp.int32, (count, count), 1)
    pick = (c == r + offset) & (r + shift >= 0) & (r + shift < length)
    return jnp.dot(pick.astype(jnp.bfloat16), rows, preferred_element_type=jnp.float32)


def on_device(vis_rows, vis_gain, key_value_proj, pieces, text_kv, queries, grad_out):
    rows, width = vis_rows.shape
    group = queries.shape[1] // HD
    scale = 1.0 / math.sqrt(HD)
    seq_n = lax.axis_size("seq")
    me = lax.axis_index("seq")
    owners = [owner_block(j, seq_n) for j in range(seq_n)]
    held = [owners.index(b) for b in range(seq_n)]
    my_image = jnp.array(held, jnp.int32)[me]
    texts_len = pieces[0::2]

    text_in = [text_kv]
    for k in range(1, seq_n):
        text_in.append(lax.ppermute(text_kv, "seq", [(j, j + k) for j in range(seq_n - k)]))

    wide = vis_rows.astype(jnp.float32)
    inverse = lax.rsqrt(jnp.mean(wide * wide, axis=-1, keepdims=True) + EPS)
    normed = (wide * inverse * vis_gain).astype(jnp.bfloat16)
    image_kv = jnp.dot(normed, key_value_proj, preferred_element_type=jnp.float32).astype(jnp.bfloat16)

    rounds = []
    for k in range(seq_n):
        pairs = [(owners[j], j + k) for j in range(seq_n - k)]
        rounds.append([p for p in pairs if p[0] != p[1]])
    blocks = []
    for k in range(seq_n):
        got = jnp.zeros_like(image_kv)
        if rounds[k]:
            got = lax.ppermute(image_kv, "seq", rounds[k])
        if any(owners[j] == j + k for j in range(seq_n - k)):
            got = jnp.where(my_image == me - k, image_kv, got)
        before = texts_len[jnp.maximum(me - k, 0)]
        placed = shift_rows(got, -before, rows, -before).astype(jnp.bfloat16)
        row_ids = jnp.arange(rows, dtype=jnp.int32)
        blocks.append(jnp.where((row_ids < before)[:, None], text_in[k], placed))
    keys = jnp.concatenate([b[:, :HD] for b in blocks], axis=0)
    values = jnp.concatenate([b[:, HD:] for b in blocks], axis=0)

    q = queries.reshape(rows, group, HD)
    g = grad_out.reshape(rows, group, HD)
    scores = jnp.einsum("rhe,ke->hrk", q, keys, preferred_element_type=jnp.float32) * scale
    key_ids = jnp.arange(seq_n * rows, dtype=jnp.int32)
    row_ids = jnp.arange(rows, dtype=jnp.int32)
    block_ids = key_ids // rows
    allowed = jnp.where(block_ids == 0, key_ids[None, :] <= row_ids[:, None], (block_ids <= me)[None, :])
    scores = jnp.where(allowed[None], scores, NEG)
    top = jnp.max(scores, axis=-1, keepdims=True)
    weights = jnp.exp(scores - top)
    weights = weights / jnp.sum(weights, axis=-1, keepdims=True)
    low = weights.astype(jnp.bfloat16)
    mixed = jnp.einsum("hrk,ke->rhe", low, values, preferred_element_type=jnp.float32)
    drift = jnp.transpose(jnp.sum(g.astype(jnp.float32) * mixed, axis=-1))
    dprob = jnp.einsum("rhe,ke->hrk", g, values, preferred_element_type=jnp.float32)
    dscore = (weights * (dprob - drift[:, :, None]) * scale).astype(jnp.bfloat16)
    dkeys = jnp.einsum("hrk,rhe->ke", dscore, q, preferred_element_type=jnp.float32)
    dvalues = jnp.einsum("hrk,rhe->ke", low, g, preferred_element_type=jnp.float32)
    dkv = jnp.concatenate([dkeys, dvalues], axis=1).astype(jnp.bfloat16)
    attended = mixed.reshape(rows, group * HD).astype(jnp.bfloat16)

    total = jnp.zeros((rows, 2 * HD), jnp.float32)
    for k in range(seq_n):
        part = dkv[k * rows : (k + 1) * rows]
        if rounds[k]:
            total += lax.ppermute(part, "seq", [(d, s) for s, d in rounds[k]]).astype(jnp.float32)
        if any(owners[j] == j + k for j in range(seq_n - k)):
            total += jnp.where(my_image == me - k, part, 0).astype(jnp.float32)

    names = ("sec", "tp")
    tp_n = lax.axis_size("tp")
    n = lax.axis_size("sec") * tp_n
    piece = rows // n
    mine = lax.axis_index("sec") * tp_n + lax.axis_index("tp")
    odd = (mine // 2) % 2
    slot = lax.broadcasted_iota(jnp.int32, (rows, rows), 0)
    source = lax.broadcasted_iota(jnp.int32, (rows, rows), 1)
    q_id = slot // piece
    y_first = (q_id // 4) ^ odd == 1
    first = jnp.where(y_first, 1, 4)
    second = jnp.where(y_first, 4, 1)
    rel = (q_id // 4) * 2 + ((q_id // 2) % 2) * first + (q_id % 2) * second
    row = (rel ^ mine) * piece + slot % piece
    text_mine = texts_len[my_image]
    pick = (source == row + text_mine) & (row < rows - text_mine)
    image_grad = jnp.dot(pick.astype(jnp.bfloat16), total.astype(jnp.bfloat16), preferred_element_type=jnp.float32)
    image_grad = image_grad.astype(jnp.bfloat16)
    part = lax.dot_general(
        image_grad, key_value_proj, (((1,), (1,)), ((), ())), preferred_element_type=jnp.float32
    ).astype(jnp.bfloat16)

    core_pairs = [(i, i ^ 2) for i in range(n)]
    one = [(i, i ^ (1 if (i // 2) % 2 else 4)) for i in range(n)]
    two = [(i, i ^ (4 if (i // 2) % 2 else 1)) for i in range(n)]
    for pairs in (core_pairs, one, two):
        half = part.shape[0] // 2
        got = lax.ppermute(part[half:], names, pairs)
        part = (part[:half].astype(jnp.float32) + got.astype(jnp.float32)).astype(jnp.bfloat16)

    own = lax.dynamic_slice_in_dim(vis_rows, mine * piece, piece, 0).astype(jnp.float32)
    own_inverse = lax.rsqrt(jnp.mean(own * own, axis=-1, keepdims=True) + EPS)
    scaled = part.astype(jnp.float32) * vis_gain
    stat = jnp.mean(own * scaled, axis=-1, keepdims=True)
    out = (scaled * own_inverse - own * own_inverse * own_inverse * own_inverse * stat).astype(jnp.bfloat16)

    for pairs in (two, one, core_pairs):
        out = jnp.concatenate([out, lax.ppermute(out, names, pairs)], axis=0)
    dest = jnp.arange(n, dtype=jnp.int32) ^ mine
    bit_core, bit_x, bit_y = (dest // 2) % 2, dest // 4, dest % 2
    where_from = bit_core * 4 + jnp.where(odd ^ bit_core == 1, bit_y * 2 + bit_x, bit_x * 2 + bit_y)
    vis_grad = out.reshape(n, piece, width)[where_from].reshape(rows, width)
    return (attended, vis_grad)


def solution(mesh):
    in_specs = (
        P("seq", None),
        P(),
        P(None, ("sec", "tp")),
        P(),
        P("seq", ("sec", "tp")),
        P("seq", ("sec", "tp")),
        P("seq", ("sec", "tp")),
    )
    out_specs = (P("seq", ("sec", "tp")), P("seq", None))
    return jax.shard_map(
        on_device, mesh=mesh, in_specs=in_specs, out_specs=out_specs, check_vma=False
    )
```

time: 155 us -> 77 us (0.50)
  blocking collectives: 44.2 us -> 0 us
  waiting for transfers between devices: 71.7 us -> 29.1 us
  starting transfers between devices: 0.08 us -> 23.4 us
  between operations: 14.9 us -> 7.6 us
  matrix products: 8.61 us -> 5.52 us
  other arithmetic: 8.92 us -> 6.86 us
  local copies, waits for them, and re-layouts: 5.89 us -> 4.09 us
    psum x1 -> x0, waiting for transfers between devices: 53.4 us -> none  [on_device(): lax.psum(partial_grad.astype(jnp.bfloat16), ('sec', 'tp'))]
    all_gather x3 -> x0, blocking collectives: 44.2 us -> none  [the longest x1 15.6 us: on_device(): image_all = lax.all_gather(image_kv, 'seq', axis=0, tiled=True)]
    ppermute x0 -> x15, waiting for transfers between devices: none -> 29.1 us  [the longest x3 9.14 us: on_device(): got = lax.ppermute(part[half:], names, pairs)]
    ppermute x0 -> x15, starting transfers between devices: none -> 23.4 us  [the longest x3 7.68 us: on_device(): got = lax.ppermute(image_kv, 'seq', rounds[k])]
    reduce_scatter x1 -> x0, waiting for transfers between devices: 18.3 us -> none  [on_device(): lax.psum_scatter(key_terms.astype(jnp.bfloat16), 'seq', scatter_dimension...]
    dot_general x6 -> x8, matrix products: 7.04 us -> 3.52 us  [the longest x1 1.61 us: on_device(): jnp.dot(normed, key_value_proj, preferred_element_type=jnp.float32)]
    lt x1 -> x8, other arithmetic: 0.61 us -> 2.55 us  [the longest x4 2.52 us: on_device(): blocks.append(jnp.where((row_ids < before)[:, None], text_in[k], placed))]
    reduce_sum x5 -> x2, other arithmetic: 3.25 us -> 2.59 us  [the longest x1 1.51 us: on_device(): inverse = lax.rsqrt(jnp.mean(wide * wide, axis=-1, keepdims=True) + EPS)]
  transfers between devices with their start and end apart: 2 -> 15, of which waited for: 2 -> 9; matrix products, arithmetic and copies ran while one was open for 2% -> 8% of each run, Pallas kernels for 0% -> 0%
where the time goes in v1:
time: 77 us; the launch traced here: 76.5 us
  waiting for transfers between devices  29.1 us (38%)
  starting transfers between devices  23.4 us (30%)
  between operations  7.6 us (10%)
  other arithmetic  6.86 us (9%)
  matrix products  5.52 us (7%)
  local copies, waits for them, and re-layouts  4.09 us (5%)
    ppermute x3, waiting for transfers between devices, on_device(): got = lax.ppermute(part[half:], names, pairs)  9.14 us
    ppermute x3, waiting for transfers between devices, on_device(): out = jnp.concatenate([out, lax.ppermute(out, names, pairs)], axis=0)  8.7 us
    ppermute x3, starting transfers between devices, on_device(): got = lax.ppermute(image_kv, 'seq', rounds[k])  7.68 us
    ppermute x3, starting transfers between devices, on_device(): lax.ppermute(text_kv, 'seq', [(j, j + k) for j in range(seq_n - k)])  7.27 us
    ppermute x3, waiting for transfers between devices, on_device(): lax.ppermute(part, 'seq', [(d, s) for s, d in rounds[k]])  5.98 us
    ppermute x3, waiting for transfers between devices, on_device(): got = lax.ppermute(image_kv, 'seq', rounds[k])  5.25 us
    ppermute x3, starting transfers between devices, on_device(): got = lax.ppermute(part[half:], names, pairs)  3.22 us
    ppermute x3, starting transfers between devices, on_device(): out = jnp.concatenate([out, lax.ppermute(out, names, pairs)], axis=0)  3.22 us
  transfers between devices with their start and end apart: 15, of which 9 were waited for; matrix products, arithmetic and copies ran while one was open for 8% of the time, Pallas kernels for 0%

profile of v1, /device:TPU:0, one launch (start us, length us, event | category | flops | bytes accessed | tf_op | source)
XLA Modules:
  0.0 76.5 jit_solution(17222470640537153925)
XLA Ops:
  0.6 1.5 %fusion.1 = f32[128]{0:T(128)S(1)} fusion(bf16[128,3200]{1,0:T(8,128)(2,1)} %param.8), kind=kLoop, calls=%fused_computation.5 | loop fusion | flops 1228672 | bytes 819712 | tf_op jit(solution)/shard_map/reduce_sum | solution.py:42
  2.2 0.1 copy-done
  2.3 1.6 %convolution_convert_fusion.6 = bf16[128,256]{1,0:T(8,128)(2,1)S(1)} fusion(bf16[3200,256]{1,0:T(8,128)(2,1)S(1)} %copy-done, bf16[128,3200]{1,0:T(8,128)(2,1)} %param.8, f32[3200]{0:T(1024)} %param.9, f32[128]{0:T(128)S(1)} %add_rsqrt_fusion.1), kind=kOutput, calls=%fused_computation.29 | convolution fusion | flops 211386368 | bytes 2536448 | tf_op jit(solution)/shard_map/dot_general | solution.py:44
  3.9 7.0 %collective-permute-start.2 = (bf16[128,256]{1,0:T(8,128)(2,1)S(1)}, bf16[128,256]{1,0:T(8,128)(2,1)S(1)}, u32[]{:S(2)}, u32[]{:S(2)}) collective-permute-start(bf16[128,256]{1,0:T(8,128)(2,1)S(1)} %convolution_convert_fusion.6), channel_id=1, source_target_pairs={{6,2},{0,6},{7,3},{1,7},{14,10},{8,14},{15,11},{9,15},{22,18},{16,... | collective-permute-start | bytes 196616 | tf_op jit(solution)/shard_map/ppermute | solution.py:54
  10.9 0.7 collective-permute-start.4
  11.6 1.3 %collective-permute-start.1 = (bf16[128,256]{1,0:T(8,128)(2,1)S(1)}, bf16[128,256]{1,0:T(8,128)(2,1)S(1)}, u32[]{:S(2)}, u32[]{:S(2)}) collective-permute-start(bf16[128,256]{1,0:T(8,128)(2,1)S(1)} %copy-done.4), channel_id=1, source_target_pairs={{0,2},{2,4},{4,6},{1,3},{3,5},{5,7},{8,10},{10,12},{12,14},{9,11},... | collective-permute-start | bytes 196616 | tf_op jit(solution)/shard_map/ppermute | solution.py:39
  12.9 4.7 %collective-permute-start.3 = (bf16[128,256]{1,0:T(8,128)(2,1)S(1)}, bf16[128,256]{1,0:T(8,128)(2,1)S(1)}, u32[]{:S(2)}, u32[]{:S(2)}) collective-permute-start(bf16[128,256]{1,0:T(8,128)(2,1)S(1)} %copy-done.4), channel_id=1, source_target_pairs={{0,4},{2,6},{1,5},{3,7},{8,12},{10,14},{9,13},{11,15},{16,20},{18,... | collective-permute-start | bytes 196616 | tf_op jit(solution)/shard_map/ppermute | solution.py:39
  17.6 1.3 %collective-permute-start.5 = (bf16[128,256]{1,0:T(8,128)(2,1)S(1)}, bf16[128,256]{1,0:T(8,128)(2,1)S(1)}, u32[]{:S(2)}, u32[]{:S(2)}) collective-permute-start(bf16[128,256]{1,0:T(8,128)(2,1)S(1)} %copy-done.4), channel_id=1, source_target_pairs={{0,6},{1,7},{8,14},{9,15},{16,22},{17,23},{24,30},{25,31}} | collective-permute-start | bytes 196616 | tf_op jit(solution)/shard_map/ppermute | solution.py:39
  18.9 0.6 dynamic_slice.23
  20.8 0.1 slice.57
  21.5 0.7 fusion.198
  22.9 0.6 iota_compare_fusion.7
  24.8 0.6 iota_compare_fusion.6
  26.1 0.6 iota_compare_fusion.5
  28.1 0.1 copy.29
  28.2 0.1 copy.13
  28.4 0.2 fusion.26
  29.2 0.6 iota_compare_fusion.8
  30.0 0.2 fusion.17
  30.2 0.2 fusion.18
  30.5 0.2 fusion.19
  30.7 5.2 %collective-permute-done = bf16[128,256]{1,0:T(8,128)(2,1)S(1)} collective-permute-done((bf16[128,256]{1,0:T(8,128)(2,1)S(1)}, bf16[128,256]{1,0:T(8,128)(2,1)S(1)}, u32[]{:S(2)}, u32[]{:S(2)}) %collective-permute-start) | collective-permute-done | bytes 65568 | tf_op jit(solution)/shard_map/ppermute | solution.py:54
  36.0 0.2 fusion.16
  36.2 0.5 fusion.199
  36.7 0.1 fusion.25
  36.8 0.3 fusion.15
  37.1 0.3 multiply_reduce_fusion
  37.4 0.4 fusion.14
  37.9 1.3 %collective-permute-start.7 = (bf16[128,256]{1,0:T(8,128)(2,1)S(1)}, bf16[128,256]{1,0:T(8,128)(2,1)S(1)}, u32[]{:S(2)}, u32[]{:S(2)}) collective-permute-start(bf16[128,256]{1,0:T(8,128)(2,1)S(1)} %get-tuple-element.7), channel_id=1, source_target_pairs={{2,6},{6,0},{3,7},{7,1},{10,14},{14,8},{11,15},{15,9},{18,22},{22,... | collective-permute-start | bytes 196616 | tf_op jit(solution)/shard_map/ppermute | solution.py:89
  39.2 0.7 collective-permute-start.8
  39.9 3.6 %collective-permute-done.6 = bf16[128,256]{1,0:T(8,128)(2,1)S(1)} collective-permute-done((bf16[128,256]{1,0:T(8,128)(2,1)S(1)}, bf16[128,256]{1,0:T(8,128)(2,1)S(1)}, u32[]{:S(2)}, u32[]{:S(2)}) %collective-permute-start.6) | collective-permute-done | bytes 65568 | tf_op jit(solution)/shard_map/ppermute | solution.py:89
  43.5 2.4 %collective-permute-done.7 = bf16[128,256]{1,0:T(8,128)(2,1)S(1)} collective-permute-done((bf16[128,256]{1,0:T(8,128)(2,1)S(1)}, bf16[128,256]{1,0:T(8,128)(2,1)S(1)}, u32[]{:S(2)}, u32[]{:S(2)}) %collective-permute-start.7) | collective-permute-done | bytes 65568 | tf_op jit(solution)/shard_map/ppermute | solution.py:89
  45.9 1.5 %convolution_convert_fusion = bf16[128,3200]{1,0:T(8,128)(2,1)S(1)} fusion(bf16[3200,256]{1,0:T(8,128)(2,1)S(1)} %copy-done, bf16[128,256]{1,0:T(8,128)(2,1)S(1)} %collective-permute-done.8, bf16[128,256]{1,0:T(8,128)(2,1)S(1)} %collective-permute-done.7, bf16[128,256]{1,0:T(8,128)(2,1)S(1)} %collective-permute-done.6, bf16[512,128]{1,0:T(8,128)(2,1)S(1)} %fusion.15, ...), kind=kOutput, calls=%fused_computation.2 | convolution fusion | flops 220020736 | bytes 2984210 | tf_op jit(solution)/shard_map/dot_general | solution.py:111
  47.5 1.7 %collective-permute-done.9 = bf16[64,3200]{1,0:T(8,128)(2,1)S(1)} collective-permute-done((bf16[64,3200]{1,0:T(8,128)(2,1)S(1)}, bf16[64,3200]{1,0:T(8,128)(2,1)S(1)}, u32[]{:S(2)}, u32[]{:S(2)}) %collective-permute-start.9) | collective-permute-done | bytes 409632 | tf_op jit(solution)/shard_map/ppermute | solution.py:120
  49.3 0.1 add_convert_fusion
  49.4 1.6 %collective-permute-start.10 = (bf16[32,3200]{1,0:T(8,128)(2,1)S(1)}, bf16[32,3200]{1,0:T(8,128)(2,1)S(1)}, u32[]{:S(2)}, u32[]{:S(2)}) collective-permute-start(bf16[32,3200]{1,0:T(8,128)(2,1)S(1)} %slice.95), channel_id=1, source_target_pairs={{0,16},{1,17},{8,9},{9,8},{16,0},{17,1},{24,25},{25,24},{2,18},{3,... | collective-permute-start | bytes 614408 | tf_op jit(solution)/shard_map/ppermute | solution.py:120
  51.0 4.3 %collective-permute-done.10 = bf16[32,3200]{1,0:T(8,128)(2,1)S(1)} collective-permute-done((bf16[32,3200]{1,0:T(8,128)(2,1)S(1)}, bf16[32,3200]{1,0:T(8,128)(2,1)S(1)}, u32[]{:S(2)}, u32[]{:S(2)}) %collective-permute-start.10) | collective-permute-done | bytes 204832 | tf_op jit(solution)/shard_map/ppermute | solution.py:120
  55.3 1.6 %collective-permute-start.11 = (bf16[16,3200]{1,0:T(8,128)(2,1)S(1)}, bf16[16,3200]{1,0:T(8,128)(2,1)S(1)}, u32[]{:S(2)}, u32[]{:S(2)}) collective-permute-start(bf16[16,3200]{1,0:T(8,128)(2,1)S(1)} %slice.97), channel_id=1, source_target_pairs={{0,1},{1,0},{8,24},{9,25},{16,17},{17,16},{24,8},{25,9},{2,3},{3,2... | collective-permute-start | bytes 307208 | tf_op jit(solution)/shard_map/ppermute | solution.py:120
  56.9 3.1 %collective-permute-done.11 = bf16[16,3200]{1,0:T(8,128)(2,1)S(1)} collective-permute-done((bf16[16,3200]{1,0:T(8,128)(2,1)S(1)}, bf16[16,3200]{1,0:T(8,128)(2,1)S(1)}, u32[]{:S(2)}, u32[]{:S(2)}) %collective-permute-start.11) | collective-permute-done | bytes 102432 | tf_op jit(solution)/shard_map/ppermute | solution.py:120
  60.0 1.1 %fusion.27 = (f32[16]{0:T(128)S(1)}, f32[16]{0:T(128)S(1)}) fusion(bf16[128,3200]{1,0:T(8,128)(2,1)} %param.8, s32[]{:T(128)S(6)} %select_n.216, f32[3200]{0:T(1024)S(1)} %copy-done.3, bf16[16,3200]{1,0:T(8,128)(2,1)S(1)} %collective-permute-done.11, bf16[32,3200]{1,0:T(8,128)(2,1)S(1)} %add_convert_fusion.1), kind=kLoop, calls=%fused_computation.56 | loop fusion | flops 563168 | bytes 320132 | tf_op jit(solution)/shard_map/reduce_sum | solution.py:124
  61.1 1.0 %fusion.32 = bf16[16,3200]{1,0:T(8,128)(2,1)S(1)} fusion(f32[16]{0:T(128)S(1)} %broadcast_multiply_fusion, f32[16]{0:T(128)S(1)} %add_rsqrt_fusion, f32[3200]{0:T(1024)S(1)} %copy-done.3, bf16[128,3200]{1,0:T(8,128)(2,1)} %param.8, s32[]{:T(128)S(6)} %select_n.216, bf16[16,3200]{1,0:T(8,128)(2,1)S(1)} %collective-permute-done.11, ...), kind=kLoop, calls=%fused_computation.61 | loop fusion | flops 716800 | bytes 422532 | tf_op jit(solution)/shard_map/convert_element_type | solution.py:127
  62.1 1.6 %collective-permute-start.12 = (bf16[16,3200]{1,0:T(8,128)(2,1)S(1)}, bf16[16,3200]{1,0:T(8,128)(2,1)S(1)}, u32[]{:S(2)}, u32[]{:S(2)}) collective-permute-start(bf16[16,3200]{1,0:T(8,128)(2,1)S(1)} %fusion.32), channel_id=1, source_target_pairs={{0,1},{1,0},{8,24},{9,25},{16,17},{17,16},{24,8},{25,9},{2,3},{3,2... | collective-permute-start | bytes 307208 | tf_op jit(solution)/shard_map/ppermute | solution.py:130
  63.7 3.5 %collective-permute-done.12 = bf16[16,3200]{1,0:T(8,128)(2,1)S(1)} collective-permute-done((bf16[16,3200]{1,0:T(8,128)(2,1)S(1)}, bf16[16,3200]{1,0:T(8,128)(2,1)S(1)}, u32[]{:S(2)}, u32[]{:S(2)}) %collective-permute-start.12) | collective-permute-done | bytes 102432 | tf_op jit(solution)/shard_map/ppermute | solution.py:130
  67.3 1.6 %collective-permute-start.13 = (bf16[32,3200]{1,0:T(8,128)(2,1)S(1)}, bf16[32,3200]{1,0:T(8,128)(2,1)S(1)}, u32[]{:S(2)}, u32[]{:S(2)}) collective-permute-start(bf16[32,3200]{1,0:T(8,128)(2,1)S(1)} %pad_maximum_fusion.2), channel_id=1, source_target_pairs={{0,16},{1,17},{8,9},{9,8},{16,0},{17,1},{24,25},{25,24},{2,18},{3,... | collective-permute-start | bytes 614408 | tf_op jit(solution)/shard_map/ppermute | solution.py:130
  68.8 4.3 %collective-permute-done.13 = bf16[32,3200]{1,0:T(8,128)(2,1)S(1)} collective-permute-done((bf16[32,3200]{1,0:T(8,128)(2,1)S(1)}, bf16[32,3200]{1,0:T(8,128)(2,1)S(1)}, u32[]{:S(2)}, u32[]{:S(2)}) %collective-permute-start.13) | collective-permute-done | bytes 204832 | tf_op jit(solution)/shard_map/ppermute | solution.py:130
  73.2 0.8 %copy.19 = bf16[128,512]{1,0:T(8,128)(2,1)} copy(bf16[128,512]{0,1:T(8,128)(2,1)S(1)} %bitcast.82) | data formatting | bytes 262144
  74.0 0.9 %collective-permute-done.14 = bf16[64,3200]{1,0:T(8,128)(2,1)S(1)} collective-permute-done((bf16[64,3200]{1,0:T(8,128)(2,1)S(1)}, bf16[64,3200]{1,0:T(8,128)(2,1)S(1)}, u32[]{:S(2)}, u32[]{:S(2)}) %collective-permute-start.14) | collective-permute-done | bytes 409632 | tf_op jit(solution)/shard_map/ppermute | solution.py:130
  75.0 1.5 %gather_fusion = bf16[8,16,3200]{2,1,0:T(8,128)(2,1)} fusion(bf16[8,16,3200]{2,1,0:T(8,128)(2,1)S(1)} %bitcast.78, s32[1024]{0:T(1024)S(1)} %pad_clamp_fusion), kind=kCustom, calls=%fused_computation | custom fusion | bytes 1638432 | tf_op jit(solution)/shard_map/gather | solution.py:134
  (52 shorter events, 0.7 us)
Async XLA Ops:
  0.6 1.7 %copy-start = (bf16[3200,256]{1,0:T(8,128)(2,1)S(1)}, bf16[3200,256]{1,0:T(8,128)(2,1)}, u32[]{:S(2)}) copy-start(bf16[3200,256]{1,0:T(8,128)(2,1)} %param.10) | copy-start | bytes 4915204
  2.2 9.4 %copy-start.4 = (bf16[128,256]{1,0:T(8,128)(2,1)S(1)}, bf16[128,256]{1,0:T(8,128)(2,1)}, u32[]{:S(2)}) copy-start(bf16[128,256]{1,0:T(8,128)(2,1)} %param.12) | copy-start | bytes 196612
  2.2 16.7 %copy-start.6 = (s32[4]{0:T(128)S(1)}, s32[4]{0:T(128)}, u32[]{:S(2)}) copy-start(s32[4]{0:T(128)} %constant.185.clone) | copy-start | bytes 52
  2.2 18.6 %copy-start.5 = (s32[8]{0:T(128)S(1)}, s32[8]{0:T(128)}, u32[]{:S(2)}) copy-start(s32[8]{0:T(128)} %param.11) | copy-start | bytes 100
  2.2 25.9 %copy-start.1 = (bf16[128,512]{1,0:T(8,128)(2,1)S(1)}, bf16[128,512]{1,0:T(8,128)(2,1)}, u32[]{:S(2)}) copy-start(bf16[128,512]{1,0:T(8,128)(2,1)} %param.13) | copy-start | bytes 393220
  2.3 25.9 %copy-start.2 = (bf16[128,512]{1,0:T(8,128)(2,1)S(1)}, bf16[128,512]{1,0:T(8,128)(2,1)}, u32[]{:S(2)}) copy-start(bf16[128,512]{1,0:T(8,128)(2,1)} %param.14) | copy-start | bytes 393220
  3.9 25.9 %collective-permute-start.2 = (bf16[128,256]{1,0:T(8,128)(2,1)S(1)}, bf16[128,256]{1,0:T(8,128)(2,1)S(1)}, u32[]{:S(2)}, u32[]{:S(2)}) collective-permute-start(bf16[128,256]{1,0:T(8,128)(2,1)S(1)} %convolution_convert_fusion.6), channel_id=1, source_target_pairs={{6,2},{0,6},{7,3},{1,7},{14,10},{8,14},{15,11},{9,15},{22,18},{16,... | collective-permute-start | bytes 196616 | tf_op jit(solution)/shard_map/ppermute | solution.py:54
  10.9 19.3 %collective-permute-start.4 = (bf16[128,256]{1,0:T(8,128)(2,1)S(1)}, bf16[128,256]{1,0:T(8,128)(2,1)S(1)}, u32[]{:S(2)}, u32[]{:S(2)}) collective-permute-start(bf16[128,256]{1,0:T(8,128)(2,1)S(1)} %convolution_convert_fusion.6), channel_id=1, source_target_pairs={{6,4},{4,6},{7,5},{5,7},{14,12},{12,14},{15,13},{13,15},{22,20},{2... | collective-permute-start | bytes 196616 | tf_op jit(solution)/shard_map/ppermute | solution.py:54
  11.6 18.4 %collective-permute-start.1 = (bf16[128,256]{1,0:T(8,128)(2,1)S(1)}, bf16[128,256]{1,0:T(8,128)(2,1)S(1)}, u32[]{:S(2)}, u32[]{:S(2)}) collective-permute-start(bf16[128,256]{1,0:T(8,128)(2,1)S(1)} %copy-done.4), channel_id=1, source_target_pairs={{0,2},{2,4},{4,6},{1,3},{3,5},{5,7},{8,10},{10,12},{12,14},{9,11},... | collective-permute-start | bytes 196616 | tf_op jit(solution)/shard_map/ppermute | solution.py:39
  12.9 17.3 %collective-permute-start.3 = (bf16[128,256]{1,0:T(8,128)(2,1)S(1)}, bf16[128,256]{1,0:T(8,128)(2,1)S(1)}, u32[]{:S(2)}, u32[]{:S(2)}) collective-permute-start(bf16[128,256]{1,0:T(8,128)(2,1)S(1)} %copy-done.4), channel_id=1, source_target_pairs={{0,4},{2,6},{1,5},{3,7},{8,12},{10,14},{9,13},{11,15},{16,20},{18,... | collective-permute-start | bytes 196616 | tf_op jit(solution)/shard_map/ppermute | solution.py:39
  17.6 12.9 %collective-permute-start.5 = (bf16[128,256]{1,0:T(8,128)(2,1)S(1)}, bf16[128,256]{1,0:T(8,128)(2,1)S(1)}, u32[]{:S(2)}, u32[]{:S(2)}) collective-permute-start(bf16[128,256]{1,0:T(8,128)(2,1)S(1)} %copy-done.4), channel_id=1, source_target_pairs={{0,6},{1,7},{8,14},{9,15},{16,22},{17,23},{24,30},{25,31}} | collective-permute-start | bytes 196616 | tf_op jit(solution)/shard_map/ppermute | solution.py:39
  29.9 6.1 %collective-permute-start = (bf16[128,256]{1,0:T(8,128)(2,1)S(1)}, bf16[128,256]{1,0:T(8,128)(2,1)S(1)}, u32[]{:S(2)}, u32[]{:S(2)}) collective-permute-start(bf16[128,256]{1,0:T(8,128)(2,1)S(1)} %convolution_convert_fusion.6), channel_id=1, source_target_pairs={{6,0},{4,2},{0,4},{2,6},{7,1},{5,3},{1,5},{3,7},{14,8},{12,10},{8,... | collective-permute-start | bytes 196616 | tf_op jit(solution)/shard_map/ppermute | solution.py:54
  37.9 5.6 %collective-permute-start.6 = (bf16[128,256]{1,0:T(8,128)(2,1)S(1)}, bf16[128,256]{1,0:T(8,128)(2,1)S(1)}, u32[]{:S(2)}, u32[]{:S(2)}) collective-permute-start(bf16[128,256]{1,0:T(8,128)(2,1)S(1)} %get-tuple-element.6), channel_id=1, source_target_pairs={{0,6},{2,4},{4,0},{6,2},{1,7},{3,5},{5,1},{7,3},{8,14},{10,12},{12... | collective-permute-start | bytes 196616 | tf_op jit(solution)/shard_map/ppermute | solution.py:89
  37.9 8.0 %collective-permute-start.7 = (bf16[128,256]{1,0:T(8,128)(2,1)S(1)}, bf16[128,256]{1,0:T(8,128)(2,1)S(1)}, u32[]{:S(2)}, u32[]{:S(2)}) collective-permute-start(bf16[128,256]{1,0:T(8,128)(2,1)S(1)} %get-tuple-element.7), channel_id=1, source_target_pairs={{2,6},{6,0},{3,7},{7,1},{10,14},{14,8},{11,15},{15,9},{18,22},{22,... | collective-permute-start | bytes 196616 | tf_op jit(solution)/shard_map/ppermute | solution.py:89
  39.2 6.7 %collective-permute-start.8 = (bf16[128,256]{1,0:T(8,128)(2,1)S(1)}, bf16[128,256]{1,0:T(8,128)(2,1)S(1)}, u32[]{:S(2)}, u32[]{:S(2)}) collective-permute-start(bf16[128,256]{1,0:T(8,128)(2,1)S(1)} %get-tuple-element.8), channel_id=1, source_target_pairs={{4,6},{6,4},{5,7},{7,5},{12,14},{14,12},{13,15},{15,13},{20,22},{2... | collective-permute-start | bytes 196616 | tf_op jit(solution)/shard_map/ppermute | solution.py:89
  47.4 12.6 %copy-start.3 = (f32[3200]{0:T(1024)S(1)}, f32[3200]{0:T(1024)}, u32[]{:S(2)}) copy-start(f32[3200]{0:T(1024)} %param.9) | copy-start | bytes 38404
  47.5 1.8 %collective-permute-start.9 = (bf16[64,3200]{1,0:T(8,128)(2,1)S(1)}, bf16[64,3200]{1,0:T(8,128)(2,1)S(1)}, u32[]{:S(2)}, u32[]{:S(2)}) collective-permute-start(bf16[64,3200]{1,0:T(8,128)(2,1)S(1)} %slice.93), channel_id=1, source_target_pairs={{0,8},{1,9},{8,0},{9,1},{16,24},{17,25},{24,16},{25,17},{2,10},{3,... | collective-permute-start | bytes 1228808 | tf_op jit(solution)/shard_map/ppermute | solution.py:120
  49.4 5.8 %collective-permute-start.10 = (bf16[32,3200]{1,0:T(8,128)(2,1)S(1)}, bf16[32,3200]{1,0:T(8,128)(2,1)S(1)}, u32[]{:S(2)}, u32[]{:S(2)}) collective-permute-start(bf16[32,3200]{1,0:T(8,128)(2,1)S(1)} %slice.95), channel_id=1, source_target_pairs={{0,16},{1,17},{8,9},{9,8},{16,0},{17,1},{24,25},{25,24},{2,18},{3,... | collective-permute-start | bytes 614408 | tf_op jit(solution)/shard_map/ppermute | solution.py:120
  55.3 4.7 %collective-permute-start.11 = (bf16[16,3200]{1,0:T(8,128)(2,1)S(1)}, bf16[16,3200]{1,0:T(8,128)(2,1)S(1)}, u32[]{:S(2)}, u32[]{:S(2)}) collective-permute-start(bf16[16,3200]{1,0:T(8,128)(2,1)S(1)} %slice.97), channel_id=1, source_target_pairs={{0,1},{1,0},{8,24},{9,25},{16,17},{17,16},{24,8},{25,9},{2,3},{3,2... | collective-permute-start | bytes 307208 | tf_op jit(solution)/shard_map/ppermute | solution.py:120
  62.1 5.1 %collective-permute-start.12 = (bf16[16,3200]{1,0:T(8,128)(2,1)S(1)}, bf16[16,3200]{1,0:T(8,128)(2,1)S(1)}, u32[]{:S(2)}, u32[]{:S(2)}) collective-permute-start(bf16[16,3200]{1,0:T(8,128)(2,1)S(1)} %fusion.32), channel_id=1, source_target_pairs={{0,1},{1,0},{8,24},{9,25},{16,17},{17,16},{24,8},{25,9},{2,3},{3,2... | collective-permute-start | bytes 307208 | tf_op jit(solution)/shard_map/ppermute | solution.py:130
  67.3 5.8 %collective-permute-start.13 = (bf16[32,3200]{1,0:T(8,128)(2,1)S(1)}, bf16[32,3200]{1,0:T(8,128)(2,1)S(1)}, u32[]{:S(2)}, u32[]{:S(2)}) collective-permute-start(bf16[32,3200]{1,0:T(8,128)(2,1)S(1)} %pad_maximum_fusion.2), channel_id=1, source_target_pairs={{0,16},{1,17},{8,9},{9,8},{16,0},{17,1},{24,25},{25,24},{2,18},{3,... | collective-permute-start | bytes 614408 | tf_op jit(solution)/shard_map/ppermute | solution.py:130
  73.1 1.8 %collective-permute-start.14 = (bf16[64,3200]{1,0:T(8,128)(2,1)S(1)}, bf16[64,3200]{1,0:T(8,128)(2,1)S(1)}, u32[]{:S(2)}, u32[]{:S(2)}) collective-permute-start(bf16[64,3200]{1,0:T(8,128)(2,1)S(1)} %pad_maximum_fusion.1), channel_id=1, source_target_pairs={{0,8},{1,9},{8,0},{9,1},{16,24},{17,25},{24,16},{25,17},{2,10},{3,... | collective-permute-start | bytes 1228808 | tf_op jit(solution)/shard_map/ppermute | solution.py:130

commit v2 on v1

v2 whole, which is shorter than its diff:
```python
import functools
import math

import jax
import jax.numpy as jnp
from jax import lax
from jax.experimental import pallas as pl
from jax.experimental.pallas import tpu as pltpu
from jax.sharding import PartitionSpec as P

HD = 128
EPS = 1e-06
NEG = -1e30
VMEM_LIMIT = 48 * 1024 * 1024
WIDE_LIMIT = 60 * 1024 * 1024
WHOLE = pl.BlockSpec(memory_space=pltpu.VMEM)
SCALARS = pl.BlockSpec(memory_space=pltpu.SMEM)


def owner_block(image, count):
    half = count // 2
    return image - half if image >= half else half + (image + 1) % half


def held_image(block, count):
    half = count // 2
    return jnp.where(block < half, block + half, lax.rem(block + half - 1, half))


def group_place():
    sec, tp = lax.axis_index("sec"), lax.axis_index("tp")
    return lax.rem(sec, 2), lax.div(sec, 2) * lax.axis_size("tp") + tp


def dot(a, b, dims):
    return lax.dot_general(a, b, (dims, ((), ())), preferred_element_type=jnp.float32)


def call(body, out_shape, in_specs, out_specs, flops, moved, limit=VMEM_LIMIT, **more):
    return pl.pallas_call(
        body,
        out_shape=out_shape,
        in_specs=in_specs,
        out_specs=out_specs,
        compiler_params=pltpu.CompilerParams(vmem_limit_bytes=limit),
        cost_estimate=pl.CostEstimate(flops=flops, bytes_accessed=moved, transcendentals=0),
        **more,
    )


def cuts(width):
    size = max(width // (4 * 256), 1) * 256
    edges = [i * size for i in range(4)] + [width]
    return list(zip(edges[:-1], edges[1:]))


def project_body(piece, vis_hbm, gain_hbm, proj_hbm, kv_ref, own_ref, vis, gain_ref, proj, vis_sems, proj_sems, gain_sem):
    rows, width = vis.shape
    gain_copy = pltpu.make_async_copy(gain_hbm, gain_ref, gain_sem)
    gain_copy.start()
    copies = []
    for n, (low, high) in enumerate(cuts(width)):
        vis_copy = pltpu.make_async_copy(vis_hbm.at[:, low:high], vis.at[:, low:high], vis_sems.at[n])
        proj_copy = pltpu.make_async_copy(proj_hbm.at[low:high, :], proj.at[low:high, :], proj_sems.at[n])
        vis_copy.start()
        proj_copy.start()
        copies.append((vis_copy, proj_copy))
    gain_copy.wait()
    squares = jnp.zeros((rows, HD), jnp.float32)
    total = jnp.zeros(kv_ref.shape, jnp.float32)
    for (low, high), (vis_copy, proj_copy) in zip(cuts(width), copies):
        vis_copy.wait()
        scaled = []
        for c in range(low, high, HD):
            wide = vis[:, c : c + HD].astype(jnp.float32)
            squares += wide * wide
            scaled.append((wide * gain_ref[c // HD : c // HD + 1, :]).astype(jnp.bfloat16))
        proj_copy.wait()
        total += jnp.dot(jnp.concatenate(scaled, axis=1), proj[low:high, :], preferred_element_type=jnp.float32)
    inverse = lax.rsqrt(jnp.sum(squares, axis=1, keepdims=True) / width + EPS)
    kv_ref[...] = (total * inverse).astype(jnp.bfloat16)
    parity, place = group_place()
    start = pl.multiple_of(parity * (rows // 2) + place * piece, piece)
    own_ref[...] = vis[pl.ds(start, piece), :]


def place_body(seq_n, pieces_ref, image_ref, text_ref, out_ref):
    rows = image_ref.shape[0]
    before = pieces_ref[2 * held_image(lax.axis_index("seq"), seq_n)]
    to = lax.broadcasted_iota(jnp.int32, (rows, rows), 0)
    source = lax.broadcasted_iota(jnp.int32, (rows, rows), 1)
    pick = jnp.where(source == to - before, 1.0, 0.0).astype(jnp.bfloat16)
    moved = jnp.dot(pick, image_ref[...], preferred_element_type=jnp.float32)
    row = lax.broadcasted_iota(jnp.int32, moved.shape, 0)
    out_ref[...] = jnp.where(row < before, text_ref[...].astype(jnp.float32), moved).astype(jnp.bfloat16)


def pick_static(table, index):
    value = jnp.int32(table[0])
    for n in range(1, len(table)):
        value = jnp.where(index == n, table[n], value)
    return value


def attend_body(seq_n, tables, q_ref, g_ref, own_ref, *refs):
    got_refs, out_ref, grad_refs = refs[: len(tables)], refs[len(tables)], refs[len(tables) + 1 :]
    rows = q_ref.shape[0]
    group = q_ref.shape[1] // HD
    scale = 1.0 / math.sqrt(HD)
    me = lax.axis_index("seq")
    images = [held_image(me, seq_n)] + [pick_static(table, me) for table in tables]
    kv = jnp.concatenate([own_ref[...]] + [ref[...] for ref in got_refs], axis=0)
    keys, values = kv[:, :HD], kv[:, HD:]
    together = group if kv.shape[0] <= 1024 else 1
    span = together * rows
    offset = lax.broadcasted_iota(jnp.int32, (rows, span), 0)
    offset = offset - lax.rem(lax.broadcasted_iota(jnp.int32, (rows, span), 1), rows)
    masks = [offset <= (me - image) * rows for image in images]
    key_total = value_total = None
    for first in range(0, group, together):
        heads = range(first, first + together)
        q = jnp.concatenate([q_ref[:, h * HD : (h + 1) * HD] for h in heads], axis=0)
        g = jnp.concatenate([g_ref[:, h * HD : (h + 1) * HD] for h in heads], axis=0)
        scores = dot(keys, q, ((1,), (1,)))
        scores = jnp.concatenate(
            [jnp.where(mask, scores[n * rows : (n + 1) * rows], NEG) for n, mask in enumerate(masks)], axis=0
        )
        top = jnp.max(scores, axis=0, keepdims=True)
        weights = jnp.exp((scores - top) * scale)
        weights = weights * (1.0 / jnp.sum(weights, axis=0, keepdims=True))
        low = weights.astype(jnp.bfloat16)
        mixed = dot(values, low, ((0,), (0,)))
        dprob = dot(values, g, ((1,), (1,)))
        drift = jnp.sum(low.astype(jnp.float32) * dprob, axis=0, keepdims=True)
        dscore = (weights * (dprob - drift) * scale).astype(jnp.bfloat16)
        dkeys = jnp.dot(dscore, q, preferred_element_type=jnp.float32)
        dvalues = jnp.dot(low, g, preferred_element_type=jnp.float32)
        key_total = dkeys if key_total is None else key_total + dkeys
        value_total = dvalues if value_total is None else value_total + dvalues
        for n, h in enumerate(heads):
            part = jnp.transpose(mixed[:, n * rows : (n + 1) * rows])
            out_ref[:, h * HD : (h + 1) * HD] = part.astype(jnp.bfloat16)
    for n, ref in enumerate(grad_refs):
        ref[:, :HD] = key_total[n * rows : (n + 1) * rows].astype(jnp.bfloat16)
        ref[:, HD:] = value_total[n * rows : (n + 1) * rows].astype(jnp.bfloat16)


def back_body(seq_n, piece, pieces_ref, proj_ref, *refs):
    part_refs, (keep_ref, send_ref) = refs[:-2], refs[-2:]
    rows = part_refs[0].shape[0]
    half = rows // 2
    before = pieces_ref[2 * held_image(lax.axis_index("seq"), seq_n)]
    parity, place = group_place()
    total = part_refs[0][...].astype(jnp.float32)
    for ref in part_refs[1:]:
        total += ref[...].astype(jnp.float32)
    slot = lax.broadcasted_iota(jnp.int32, (rows, rows), 0)
    to = (lax.div(slot, half) ^ parity) * half
    to += (lax.div(lax.rem(slot, half), piece) ^ place) * piece + lax.rem(slot, piece)
    source = lax.broadcasted_iota(jnp.int32, (rows, rows), 1)
    pick = jnp.where(source == to + before, 1.0, 0.0).astype(jnp.bfloat16)
    image_grad = jnp.dot(pick, total.astype(jnp.bfloat16), preferred_element_type=jnp.float32)
    product = dot(image_grad.astype(jnp.bfloat16), proj_ref[...], ((1,), (1,)))
    keep_ref[...] = product[:half]
    send_ref[...] = product[half:].astype(jnp.bfloat16)


def pair_body(piece, keep_ref, other_ref, own_ref, *send_refs):
    own_ref[...] = keep_ref[:piece] + other_ref[:piece].astype(jnp.float32)
    for n, ref in enumerate(send_refs):
        part = slice((n + 1) * piece, (n + 2) * piece)
        ref[...] = (keep_ref[part] + other_ref[part].astype(jnp.float32)).astype(jnp.bfloat16)


def final_body(total_ref, own_ref, gain_ref, *refs):
    out_ref = refs[-1]
    width = own_ref.shape[1]
    square = stat = None
    scaled = []
    for c in range(0, width, HD):
        cols = slice(c, c + HD)
        total = total_ref[:, cols]
        for ref in refs[:-1]:
            total += ref[:, cols].astype(jnp.float32)
        own = own_ref[:, cols].astype(jnp.float32)
        grad = total * gain_ref[c // HD : c // HD + 1, :]
        scaled.append(grad)
        square = own * own if square is None else square + own * own
        stat = own * grad if stat is None else stat + own * grad
    inverse = lax.rsqrt(jnp.sum(square, axis=1, keepdims=True) / width + EPS)
    lead = inverse * inverse * inverse * (jnp.sum(stat, axis=1, keepdims=True) / width)
    for n, c in enumerate(range(0, width, HD)):
        own = own_ref[:, c : c + HD].astype(jnp.float32)
        out_ref[:, c : c + HD] = (scaled[n] * inverse - own * lead).astype(jnp.bfloat16)


def gather_body(count, *refs):
    part_refs, out_hbm, sems = refs[: 2 * count], refs[2 * count], refs[2 * count + 1]
    piece = part_refs[0].shape[0]
    parity, place = group_place()
    copies = []
    for n, ref in enumerate(part_refs):
        core, step = divmod(n, count)
        row = ((parity ^ core) * count + (place ^ step)) * piece
        copy = pltpu.make_async_copy(ref, out_hbm.at[pl.ds(pl.multiple_of(row, piece), piece), :], sems.at[n])
        copy.start()
        copies.append(copy)
    for copy in copies:
        copy.wait()


def rounds_of(edges):
    rounds = []
    for source, target in sorted(edges, key=lambda e: (-abs(e[0] - e[1]), e)):
        for pairs in rounds:
            if all(source != s and target != t for s, t in pairs):
                pairs.append((source, target))
                break
        else:
            rounds.append([(source, target)])
    return rounds


def on_device(vis_rows, vis_gain, key_value_proj, pieces, text_kv, queries, grad_out):
    rows, width = vis_rows.shape
    columns = key_value_proj.shape[1]
    seq_n = lax.axis_size("seq")
    tp_n = lax.axis_size("tp")
    n = lax.axis_size("sec") * tp_n
    count = n // 2
    piece = rows // n
    bf16, f32 = jnp.bfloat16, jnp.float32
    owners = [owner_block(j, seq_n) for j in range(seq_n)]
    names = ("sec", "tp")
    core_pairs = [(i, (i // tp_n ^ 1) * tp_n + i % tp_n) for i in range(n)]

    def far_pairs(step):
        pairs = []
        for i in range(n):
            sec, tp = divmod(i, tp_n)
            place = (sec // 2 * tp_n + tp) ^ step
            pairs.append((i, (place // tp_n * 2 + sec % 2) * tp_n + place % tp_n))
        return pairs

    gain = vis_gain.reshape(width // HD, HD)
    text = lax.ppermute(text_kv, "seq", [(j, owners[j]) for j in range(seq_n)])
    chunks = len(cuts(width))
    hbm = pl.BlockSpec(memory_space=pltpu.HBM)
    image_kv, own_rows = call(
        functools.partial(project_body, piece),
        [jax.ShapeDtypeStruct((rows, columns), bf16), jax.ShapeDtypeStruct((piece, width), bf16)],
        [hbm, hbm, hbm],
        [WHOLE, WHOLE],
        2 * rows * width * columns,
        2 * width * (rows + columns),
        limit=WIDE_LIMIT,
        scratch_shapes=[
            pltpu.VMEM((rows, width), bf16),
            pltpu.VMEM(gain.shape, f32),
            pltpu.VMEM((width, columns), bf16),
            pltpu.SemaphoreType.DMA((chunks,)),
            pltpu.SemaphoreType.DMA((chunks,)),
            pltpu.SemaphoreType.DMA,
        ],
    )(vis_rows, gain, key_value_proj)
    block = call(
        functools.partial(place_body, seq_n),
        jax.ShapeDtypeStruct((rows, columns), bf16),
        [SCALARS, WHOLE, WHOLE],
        WHOLE,
        2 * rows * rows * columns,
        6 * rows * columns,
    )(pieces, image_kv, text)

    rounds = rounds_of([(owners[j], s) for j in range(seq_n) for s in range(j, seq_n) if owners[j] != s])
    held = [owners.index(b) for b in range(seq_n)]
    tables = []
    for pairs in rounds:
        table = [seq_n] * seq_n
        for source, target in pairs:
            table[target] = held[source]
        tables.append(table)
    got = [lax.ppermute(block, "seq", pairs) for pairs in rounds]
    attended, own_grad, *grads = call(
        functools.partial(attend_body, seq_n, tables),
        [jax.ShapeDtypeStruct(queries.shape, bf16)] + [jax.ShapeDtypeStruct((rows, columns), bf16)] * (1 + len(got)),
        [WHOLE] * (3 + len(got)),
        [WHOLE] * (2 + len(got)),
        10 * seq_n * rows * rows * queries.shape[1],
        6 * rows * queries.shape[1] + 4 * seq_n * rows * columns,
    )(queries, grad_out, block, *got)
    parts = [lax.ppermute(g, "seq", [(t, s) for s, t in pairs]) for g, pairs in zip(grads, rounds)]

    keep, send = call(
        functools.partial(back_body, seq_n, piece),
        [jax.ShapeDtypeStruct((rows // 2, width), f32), jax.ShapeDtypeStruct((rows // 2, width), bf16)],
        [SCALARS] + [WHOLE] * (2 + len(parts)),
        [WHOLE, WHOLE],
        2 * rows * width * columns,
        2 * width * columns + 3 * rows * width,
    )(pieces, key_value_proj, own_grad, *parts)
    other = lax.ppermute(send, names, core_pairs)
    steps = list(range(1, count))
    own_sum, *sends = call(
        functools.partial(pair_body, piece),
        [jax.ShapeDtypeStruct((piece, width), f32)] + [jax.ShapeDtypeStruct((piece, width), bf16)] * len(steps),
        [WHOLE, WHOLE],
        [WHOLE] * count,
        0,
        6 * rows // 2 * width,
    )(keep, other)
    far_first = steps[::-1]
    shares = [lax.ppermute(sends[d - 1], names, far_pairs(d)) for d in far_first]
    mine = call(
        final_body,
        jax.ShapeDtypeStruct((piece, width), bf16),
        [WHOLE] * (3 + len(shares)),
        WHOLE,
        0,
        12 * piece * width,
    )(own_sum, own_rows, gain, *shares)
    mines = {0: mine}
    for d in far_first:
        mines[d] = lax.ppermute(mine, names, far_pairs(d))
    theirs = {d: lax.ppermute(mines[d], names, core_pairs) for d in [0] + far_first}
    vis_grad = call(
        functools.partial(gather_body, count),
        jax.ShapeDtypeStruct((rows, width), bf16),
        [WHOLE] * n,
        hbm,
        0,
        4 * rows * width,
        scratch_shapes=[pltpu.SemaphoreType.DMA((n,))],
    )(*[mines[d] for d in range(count)], *[theirs[d] for d in range(count)])
    return (attended, vis_grad)


def solution(mesh):
    in_specs = (
        P("seq", None),
        P(),
        P(None, ("sec", "tp")),
        P(),
        P("seq", ("sec", "tp")),
        P("seq", ("sec", "tp")),
        P("seq", ("sec", "tp")),
    )
    out_specs = (P("seq", ("sec", "tp")), P("seq", None))
    return jax.shard_map(
        on_device, mesh=mesh, in_specs=in_specs, out_specs=out_specs, check_vma=False
    )
```

time: 77 us -> 59.6 us (0.77)
  Pallas kernels: 0 us -> 8.4 us
  other arithmetic: 6.86 us -> 0 us
  between operations: 7.6 us -> 0.79 us
  waiting for transfers between devices: 29.1 us -> 22.9 us
  matrix products: 5.52 us -> 0 us
  local copies, waits for them, and re-layouts: 4.09 us -> 0.86 us
  starting transfers between devices: 23.4 us -> 26 us
    pallas_call x0 -> x7, Pallas kernels: none -> 8.4 us  [the longest x1 3.12 us: on_device(): call(functools.partial(project_body, piece), [jax.ShapeDtypeStruct((rows,...]
    ppermute x15 -> x18, waiting for transfers between devices: 29.1 us -> 22.9 us  [the longest x3 6.01 us: on_device(): got = [lax.ppermute(block, 'seq', pairs) for pairs in rounds]]
    dot_general x9 -> x0, matrix products: 5.04 us -> none  [the longest x1 1.61 us: on_device(): jnp.dot(normed, key_value_proj, preferred_element_type=jnp.float32)]
    ppermute x15 -> x18, starting transfers between devices: 23.4 us -> 26 us  [the longest x3 9.42 us: on_device(): got = [lax.ppermute(block, 'seq', pairs) for pairs in rounds]]
    reduce_sum x2 -> x0, other arithmetic: 2.59 us -> none  [the longest x1 1.51 us: on_device(): inverse = lax.rsqrt(jnp.mean(wide * wide, axis=-1, keepdims=True) + EPS)]
    lt x8 -> x0, other arithmetic: 2.55 us -> none  [the longest x4 2.52 us: on_device(): blocks.append(jnp.where((row_ids < before)[:, None], text_in[k], placed))]
    gather x1 -> x0, local copies, waits for them, and re-layouts: 1.52 us -> none  [on_device(): vis_grad = out.reshape(n, piece, width)[where_from].reshape(rows, width)]
    convert_element_type x4 -> x0, other arithmetic: 1.26 us -> none  [the longest x1 1.03 us: on_device(): (scaled * own_inverse - own * own_inverse * own_inverse * own_inverse * s...]
  transfers between devices with their start and end apart: 15 -> 18, of which waited for: 9 -> 11; matrix products, arithmetic and copies ran while one was open for 8% -> 0% of each run, Pallas kernels for 0% -> 5%
where the time goes in v2:
time: 59.6 us; the launch traced here: 59 us
  starting transfers between devices  26 us (44%)
  waiting for transfers between devices  22.9 us (38%)
  Pallas kernels  8.4 us (14%)
  local copies, waits for them, and re-layouts  0.86 us (1%)
  between operations  0.79 us (1%)
    ppermute x3, starting transfers between devices, on_device(): got = [lax.ppermute(block, 'seq', pairs) for pairs in rounds]  9.42 us
    ppermute x3, waiting for transfers between devices, on_device(): got = [lax.ppermute(block, 'seq', pairs) for pairs in rounds]  6.01 us
    ppermute x3, waiting for transfers between devices, on_device(): lax.ppermute(g, 'seq', [(t, s) for s, t in pairs])  5.15 us
    ppermute x1, starting transfers between devices, on_device(): text = lax.ppermute(text_kv, 'seq', [(j, owners[j]) for j in range(seq_n)])  5.1 us
    ppermute x3, waiting for transfers between devices, on_device(): lax.ppermute(sends[d - 1], names, far_pairs(d))  4.59 us
    ppermute x3, waiting for transfers between devices, on_device(): mines[d] = lax.ppermute(mine, names, far_pairs(d))  4.45 us
    ppermute x3, starting transfers between devices, on_device(): lax.ppermute(g, 'seq', [(t, s) for s, t in pairs])  4 us
    ppermute x3, starting transfers between devices, on_device(): lax.ppermute(sends[d - 1], names, far_pairs(d))  3.55 us
  transfers between devices with their start and end apart: 18, of which 11 were waited for; matrix products, arithmetic and copies ran while one was open for 0% of the time, Pallas kernels for 5%

profile of v2, /device:TPU:0, one launch (start us, length us, event | category | flops | bytes accessed | tf_op | source)
XLA Modules:
  0.0 59.0 jit_solution(15581630928592024125)
XLA Ops:
  0.6 0.0 copy-start.4
  0.6 0.0 copy-start.6
  0.7 5.1 %collective-permute-start = (bf16[128,256]{1,0:T(8,128)(2,1)}, bf16[128,256]{1,0:T(8,128)(2,1)S(1)}, u32[]{:S(2)}, u32[]{:S(2)}) collective-permute-start(bf16[128,256]{1,0:T(8,128)(2,1)} %param.11), channel_id=1, source_target_pairs={{0,6},{2,4},{4,0},{6,2},{1,7},{3,5},{5,1},{7,3},{8,14},{10,12},{12... | collective-permute-start | bytes 196616 | tf_op jit(solution)/shard_map/ppermute | solution.py:246
  5.8 3.1 %shard_map.86 = (bf16[128,256]{1,0:T(8,128)(2,1)}, bf16[16,3200]{1,0:T(8,128)(2,1)}) custom-call(bf16[128,3200]{1,0:T(8,128)(2,1)} %vis_hbm.1, f32[25,128]{1,0:T(8,128)} %bitcast.1, bf16[3200,256]{1,0:T(8,128)(2,1)} %proj_ref.1), custom_call_target="tpu_custom_call" | custom-call | flops 209715200 | bytes 2457600 | tf_op jit(solution)/shard_map/pallas_call | solution.py:249
  8.9 0.0 collective-permute-done.text_ref
  8.9 0.0 copy-start.3
  8.9 0.8 %copy-done.3 = bf16[128,256]{1,0:T(8,128)(2,1)S(1)} copy-done((bf16[128,256]{1,0:T(8,128)(2,1)S(1)}, bf16[128,256]{1,0:T(8,128)(2,1)}, u32[]{:S(2)}) %copy-start.3) | copy-done | bytes 65560
  9.8 0.7 %shard_map.87.own_ref = bf16[128,256]{1,0:T(8,128)(2,1)S(1)} custom-call(s32[8]{0:T(128)S(1)} %copy-done.4, bf16[128,256]{1,0:T(8,128)(2,1)S(1)} %copy-done.3, bf16[128,256]{1,0:T(8,128)(2,1)S(1)} %collective-permute-done.text_ref), custom_call_target="tpu_custom_call" | custom-call | flops 8388608 | bytes 196608 | tf_op jit(solution)/shard_map/pallas_call | solution.py:266
  10.5 0.7 %collective-permute-start.3 = (bf16[128,256]{1,0:T(8,128)(2,1)S(1)}, bf16[128,256]{1,0:T(8,128)(2,1)S(1)}, u32[]{:S(2)}, u32[]{:S(2)}) collective-permute-start(bf16[128,256]{1,0:T(8,128)(2,1)S(1)} %shard_map.87.own_ref), channel_id=1, source_target_pairs={{4,6},{6,4},{5,7},{7,5},{12,14},{14,12},{13,15},{15,13},{20,22},{2... | collective-permute-start | bytes 196616 | tf_op jit(solution)/shard_map/ppermute | solution.py:283
  11.1 6.8 %collective-permute-start.2 = (bf16[128,256]{1,0:T(8,128)(2,1)S(1)}, bf16[128,256]{1,0:T(8,128)(2,1)S(1)}, u32[]{:S(2)}, u32[]{:S(2)}) collective-permute-start(bf16[128,256]{1,0:T(8,128)(2,1)S(1)} %shard_map.87.own_ref), channel_id=1, source_target_pairs={{0,4},{2,6},{6,2},{1,5},{3,7},{7,3},{8,12},{10,14},{14,10},{9,13},... | collective-permute-start | bytes 196616 | tf_op jit(solution)/shard_map/ppermute | solution.py:283
  18.0 1.9 %collective-permute-start.1 = (bf16[128,256]{1,0:T(8,128)(2,1)S(1)}, bf16[128,256]{1,0:T(8,128)(2,1)S(1)}, u32[]{:S(2)}, u32[]{:S(2)}) collective-permute-start(bf16[128,256]{1,0:T(8,128)(2,1)S(1)} %shard_map.87.own_ref), channel_id=1, source_target_pairs={{0,6},{6,0},{4,2},{1,7},{7,1},{5,3},{8,14},{14,8},{12,10},{9,15},{... | collective-permute-start | bytes 196616 | tf_op jit(solution)/shard_map/ppermute | solution.py:283
  19.9 0.0 collective-permute-done.3.refs_2_
  19.9 0.0 collective-permute-done.2.refs_1_
  19.9 6.0 %collective-permute-done.1.refs_0_ = bf16[128,256]{1,0:T(8,128)(2,1)S(1)} collective-permute-done((bf16[128,256]{1,0:T(8,128)(2,1)S(1)}, bf16[128,256]{1,0:T(8,128)(2,1)S(1)}, u32[]{:S(2)}, u32[]{:S(2)}) %collective-permute-start.1) | collective-permute-done | bytes 65568 | tf_op jit(solution)/shard_map/ppermute | solution.py:283
  25.9 0.0 copy-done.5
  25.9 2.1 %shard_map.88 = (bf16[128,512]{1,0:T(8,128)(2,1)}, bf16[128,256]{1,0:T(8,128)(2,1)S(1)}, bf16[128,256]{1,0:T(8,128)(2,1)S(1)}, bf16[128,256]{1,0:T(8,128)(2,1)S(1)}, bf16[128,256]{1,0:T(8,128)(2,1)S(1)}) custom-call(bf16[128,512]{1,0:T(8,128)(2,1)S(1)} %copy-done.5, bf16[128,512]{1,0:T(8,128)(2,1)S(1)} %copy-done.6, bf16[128,256]{1,0:T(8,128)(2,1)S(1)} %shard_map.87.own_ref, ...), custom_call_target="tpu_custom_call" | custom-call | flops 335544320 | bytes 917504 | tf_op jit(solution)/shard_map/pallas_call | solution.py:284
  28.0 2.0 %collective-permute-start.4 = (bf16[128,256]{1,0:T(8,128)(2,1)S(1)}, bf16[128,256]{1,0:T(8,128)(2,1)S(1)}, u32[]{:S(2)}, u32[]{:S(2)}) collective-permute-start(bf16[128,256]{1,0:T(8,128)(2,1)S(1)} %get-tuple-element.18), channel_id=1, source_target_pairs={{6,0},{0,6},{2,4},{7,1},{1,7},{3,5},{14,8},{8,14},{10,12},{15,9},{... | collective-permute-start | bytes 196616 | tf_op jit(solution)/shard_map/ppermute | solution.py:292
  30.1 1.3 %collective-permute-start.5 = (bf16[128,256]{1,0:T(8,128)(2,1)S(1)}, bf16[128,256]{1,0:T(8,128)(2,1)S(1)}, u32[]{:S(2)}, u32[]{:S(2)}) collective-permute-start(bf16[128,256]{1,0:T(8,128)(2,1)S(1)} %get-tuple-element.19), channel_id=1, source_target_pairs={{4,0},{6,2},{2,6},{5,1},{7,3},{3,7},{12,8},{14,10},{10,14},{13,9},... | collective-permute-start | bytes 196616 | tf_op jit(solution)/shard_map/ppermute | solution.py:292
  31.4 0.7 %collective-permute-start.6 = (bf16[128,256]{1,0:T(8,128)(2,1)S(1)}, bf16[128,256]{1,0:T(8,128)(2,1)S(1)}, u32[]{:S(2)}, u32[]{:S(2)}) collective-permute-start(bf16[128,256]{1,0:T(8,128)(2,1)S(1)} %get-tuple-element.20), channel_id=1, source_target_pairs={{6,4},{4,6},{7,5},{5,7},{14,12},{12,14},{15,13},{13,15},{22,20},{2... | collective-permute-start | bytes 196616 | tf_op jit(solution)/shard_map/ppermute | solution.py:292
  32.0 4.5 %collective-permute-done.4.refs_1_ = bf16[128,256]{1,0:T(8,128)(2,1)S(1)} collective-permute-done((bf16[128,256]{1,0:T(8,128)(2,1)S(1)}, bf16[128,256]{1,0:T(8,128)(2,1)S(1)}, u32[]{:S(2)}, u32[]{:S(2)}) %collective-permute-start.4) | collective-permute-done | bytes 65568 | tf_op jit(solution)/shard_map/ppermute | solution.py:292
  36.5 0.6 %collective-permute-done.5.refs_2_ = bf16[128,256]{1,0:T(8,128)(2,1)S(1)} collective-permute-done((bf16[128,256]{1,0:T(8,128)(2,1)S(1)}, bf16[128,256]{1,0:T(8,128)(2,1)S(1)}, u32[]{:S(2)}, u32[]{:S(2)}) %collective-permute-start.5) | collective-permute-done | bytes 65568 | tf_op jit(solution)/shard_map/ppermute | solution.py:292
  37.2 0.0 collective-permute-done.6.refs_3_
  37.2 1.3 %shard_map.89 = (f32[64,3200]{1,0:T(8,128)S(1)}, bf16[64,3200]{1,0:T(8,128)(2,1)S(1)}) custom-call(s32[8]{0:T(128)S(1)} %copy-done.4, bf16[3200,256]{1,0:T(8,128)(2,1)S(1)} %copy-done, bf16[128,256]{1,0:T(8,128)(2,1)S(1)} %get-tuple-element.17.refs_0_, bf16[128,256]{1,0:T(8,128)(2,1)S(1)} %collective-permute-done.4.refs_1_, ...), custom_call_target="tpu_custom_call" | custom-call | flops 209715200 | bytes 2867200 | tf_op jit(solution)/shard_map/pallas_call | solution.py:294
  38.5 0.1 collective-permute-start.7
  38.6 1.7 %collective-permute-done.7.other_ref = bf16[64,3200]{1,0:T(8,128)(2,1)S(1)} collective-permute-done((bf16[64,3200]{1,0:T(8,128)(2,1)S(1)}, bf16[64,3200]{1,0:T(8,128)(2,1)S(1)}, u32[]{:S(2)}, u32[]{:S(2)}) %collective-permute-start.7) | collective-permute-done | bytes 409632 | tf_op jit(solution)/shard_map/ppermute | solution.py:302
  40.3 0.1 shard_map.90
  40.4 2.5 %collective-permute-start.8 = (bf16[16,3200]{1,0:T(8,128)(2,1)S(1)}, bf16[16,3200]{1,0:T(8,128)(2,1)S(1)}, u32[]{:S(2)}, u32[]{:S(2)}) collective-permute-start(bf16[16,3200]{1,0:T(8,128)(2,1)S(1)} %get-tuple-element.25), channel_id=1, source_target_pairs={{0,17},{1,16},{8,25},{9,24},{16,1},{17,0},{24,9},{25,8},{2,19},{3,... | collective-permute-start | bytes 307208 | tf_op jit(solution)/shard_map/ppermute | solution.py:313
  42.9 0.5 collective-permute-start.9
  43.4 0.5 collective-permute-start.10
  43.9 3.1 %collective-permute-done.8.refs_0_ = bf16[16,3200]{1,0:T(8,128)(2,1)S(1)} collective-permute-done((bf16[16,3200]{1,0:T(8,128)(2,1)S(1)}, bf16[16,3200]{1,0:T(8,128)(2,1)S(1)}, u32[]{:S(2)}, u32[]{:S(2)}) %collective-permute-start.8) | collective-permute-done | bytes 102432 | tf_op jit(solution)/shard_map/ppermute | solution.py:313
  47.1 1.4 %collective-permute-done.9.refs_1_ = bf16[16,3200]{1,0:T(8,128)(2,1)S(1)} collective-permute-done((bf16[16,3200]{1,0:T(8,128)(2,1)S(1)}, bf16[16,3200]{1,0:T(8,128)(2,1)S(1)}, u32[]{:S(2)}, u32[]{:S(2)}) %collective-permute-start.9) | collective-permute-done | bytes 102432 | tf_op jit(solution)/shard_map/ppermute | solution.py:313
  48.5 0.0 collective-permute-done.10.refs_2_
  48.5 0.2 shard_map.91.refs_0_
  48.7 2.5 %collective-permute-start.13 = (bf16[16,3200]{1,0:T(8,128)(2,1)S(1)}, bf16[16,3200]{1,0:T(8,128)(2,1)S(1)}, u32[]{:S(2)}, u32[]{:S(2)}) collective-permute-start(bf16[16,3200]{1,0:T(8,128)(2,1)S(1)} %shard_map.91.refs_0_), channel_id=1, source_target_pairs={{0,17},{1,16},{8,25},{9,24},{16,1},{17,0},{24,9},{25,8},{2,19},{3,... | collective-permute-start | bytes 307208 | tf_op jit(solution)/shard_map/ppermute | solution.py:324
  51.2 0.5 collective-permute-start.12
  51.7 0.6 collective-permute-start.11
  52.3 0.0 collective-permute-start.14
  52.3 3.0 %collective-permute-done.13.refs_3_ = bf16[16,3200]{1,0:T(8,128)(2,1)S(1)} collective-permute-done((bf16[16,3200]{1,0:T(8,128)(2,1)S(1)}, bf16[16,3200]{1,0:T(8,128)(2,1)S(1)}, u32[]{:S(2)}, u32[]{:S(2)}) %collective-permute-start.13) | collective-permute-done | bytes 102432 | tf_op jit(solution)/shard_map/ppermute | solution.py:324
  55.3 0.0 collective-permute-start.17
  55.3 1.2 %collective-permute-done.12.refs_2_ = bf16[16,3200]{1,0:T(8,128)(2,1)S(1)} collective-permute-done((bf16[16,3200]{1,0:T(8,128)(2,1)S(1)}, bf16[16,3200]{1,0:T(8,128)(2,1)S(1)}, u32[]{:S(2)}, u32[]{:S(2)}) %collective-permute-start.12) | collective-permute-done | bytes 102432 | tf_op jit(solution)/shard_map/ppermute | solution.py:324
  56.5 0.0 collective-permute-start.16
  56.5 0.2 collective-permute-done.11.refs_1_
  56.7 0.3 collective-permute-start.15
  57.1 0.0 collective-permute-done.14.refs_4_
  57.1 0.0 collective-permute-done.17.refs_7_
  57.1 0.8 %collective-permute-done.16.refs_6_ = bf16[16,3200]{1,0:T(8,128)(2,1)S(1)} collective-permute-done((bf16[16,3200]{1,0:T(8,128)(2,1)S(1)}, bf16[16,3200]{1,0:T(8,128)(2,1)S(1)}, u32[]{:S(2)}, u32[]{:S(2)}) %collective-permute-start.16) | collective-permute-done | bytes 102432 | tf_op jit(solution)/shard_map/ppermute | solution.py:325
  57.8 0.2 collective-permute-done.15.refs_5_
  58.1 0.9 %shard_map.92 = bf16[128,3200]{1,0:T(8,128)(2,1)} custom-call(bf16[16,3200]{1,0:T(8,128)(2,1)S(1)} %shard_map.91.refs_0_, bf16[16,3200]{1,0:T(8,128)(2,1)S(1)} %collective-permute-done.11.refs_1_, bf16[16,3200]{1,0:T(8,128)(2,1)S(1)} %collective-permute-done.12.refs_2_, bf16[16,3200]{1,0:T(8,128)(2,1)S(1)} %collective-permute-done.13.refs_3_, ...), custom_call_target="tpu_custom_call" | custom-call | bytes 1638400 | tf_op jit(solution)/shard_map/pallas_call | solution.py:326
  (9 shorter events, 0.0 us)
Async XLA Ops:
  0.6 8.3 %copy-start.4 = (s32[8]{0:T(128)S(1)}, s32[8]{0:T(128)}, u32[]{:S(2)}) copy-start(s32[8]{0:T(128)} %pieces_ref.3) | copy-start | bytes 100
  0.6 25.3 %copy-start.6 = (bf16[128,512]{1,0:T(8,128)(2,1)S(1)}, bf16[128,512]{1,0:T(8,128)(2,1)}, u32[]{:S(2)}) copy-start(bf16[128,512]{1,0:T(8,128)(2,1)} %g_ref.1) | copy-start | bytes 393220
  0.7 25.3 %copy-start.5 = (bf16[128,512]{1,0:T(8,128)(2,1)S(1)}, bf16[128,512]{1,0:T(8,128)(2,1)}, u32[]{:S(2)}) copy-start(bf16[128,512]{1,0:T(8,128)(2,1)} %q_ref.1) | copy-start | bytes 393220
  0.7 8.2 %collective-permute-start = (bf16[128,256]{1,0:T(8,128)(2,1)}, bf16[128,256]{1,0:T(8,128)(2,1)S(1)}, u32[]{:S(2)}, u32[]{:S(2)}) collective-permute-start(bf16[128,256]{1,0:T(8,128)(2,1)} %param.11), channel_id=1, source_target_pairs={{0,6},{2,4},{4,0},{6,2},{1,7},{3,5},{5,1},{7,3},{8,14},{10,12},{12... | collective-permute-start | bytes 196616 | tf_op jit(solution)/shard_map/ppermute | solution.py:246
  5.8 31.4 %copy-start = (bf16[3200,256]{1,0:T(8,128)(2,1)S(1)}, bf16[3200,256]{1,0:T(8,128)(2,1)}, u32[]{:S(2)}) copy-start(bf16[3200,256]{1,0:T(8,128)(2,1)} %proj_ref.1) | copy-start | bytes 4915204
  8.9 0.8 %copy-start.3 = (bf16[128,256]{1,0:T(8,128)(2,1)S(1)}, bf16[128,256]{1,0:T(8,128)(2,1)}, u32[]{:S(2)}) copy-start(bf16[128,256]{1,0:T(8,128)(2,1)} %get-tuple-element.15.image_ref) | copy-start | bytes 196612
  10.5 9.4 %collective-permute-start.3 = (bf16[128,256]{1,0:T(8,128)(2,1)S(1)}, bf16[128,256]{1,0:T(8,128)(2,1)S(1)}, u32[]{:S(2)}, u32[]{:S(2)}) collective-permute-start(bf16[128,256]{1,0:T(8,128)(2,1)S(1)} %shard_map.87.own_ref), channel_id=1, source_target_pairs={{4,6},{6,4},{5,7},{7,5},{12,14},{14,12},{13,15},{15,13},{20,22},{2... | collective-permute-start | bytes 196616 | tf_op jit(solution)/shard_map/ppermute | solution.py:283
  11.1 8.8 %collective-permute-start.2 = (bf16[128,256]{1,0:T(8,128)(2,1)S(1)}, bf16[128,256]{1,0:T(8,128)(2,1)S(1)}, u32[]{:S(2)}, u32[]{:S(2)}) collective-permute-start(bf16[128,256]{1,0:T(8,128)(2,1)S(1)} %shard_map.87.own_ref), channel_id=1, source_target_pairs={{0,4},{2,6},{6,2},{1,5},{3,7},{7,3},{8,12},{10,14},{14,10},{9,13},... | collective-permute-start | bytes 196616 | tf_op jit(solution)/shard_map/ppermute | solution.py:283
  18.0 8.0 %collective-permute-start.1 = (bf16[128,256]{1,0:T(8,128)(2,1)S(1)}, bf16[128,256]{1,0:T(8,128)(2,1)S(1)}, u32[]{:S(2)}, u32[]{:S(2)}) collective-permute-start(bf16[128,256]{1,0:T(8,128)(2,1)S(1)} %shard_map.87.own_ref), channel_id=1, source_target_pairs={{0,6},{6,0},{4,2},{1,7},{7,1},{5,3},{8,14},{14,8},{12,10},{9,15},{... | collective-permute-start | bytes 196616 | tf_op jit(solution)/shard_map/ppermute | solution.py:283
  28.0 20.5 %copy-start.1 = (bf16[16,3200]{1,0:T(8,128)(2,1)S(1)}, bf16[16,3200]{1,0:T(8,128)(2,1)}, u32[]{:S(2)}) copy-start(bf16[16,3200]{1,0:T(8,128)(2,1)} %get-tuple-element.24.own_ref) | copy-start | bytes 307204
  28.0 20.5 %copy-start.2 = (f32[3200]{0:T(1024)S(1)}, f32[3200]{0:T(1024)}, u32[]{:S(2)}) copy-start(f32[3200]{0:T(1024)} %param.8) | copy-start | bytes 38404
  28.0 8.5 %collective-permute-start.4 = (bf16[128,256]{1,0:T(8,128)(2,1)S(1)}, bf16[128,256]{1,0:T(8,128)(2,1)S(1)}, u32[]{:S(2)}, u32[]{:S(2)}) collective-permute-start(bf16[128,256]{1,0:T(8,128)(2,1)S(1)} %get-tuple-element.18), channel_id=1, source_target_pairs={{6,0},{0,6},{2,4},{7,1},{1,7},{3,5},{14,8},{8,14},{10,12},{15,9},{... | collective-permute-start | bytes 196616 | tf_op jit(solution)/shard_map/ppermute | solution.py:292
  30.1 7.1 %collective-permute-start.5 = (bf16[128,256]{1,0:T(8,128)(2,1)S(1)}, bf16[128,256]{1,0:T(8,128)(2,1)S(1)}, u32[]{:S(2)}, u32[]{:S(2)}) collective-permute-start(bf16[128,256]{1,0:T(8,128)(2,1)S(1)} %get-tuple-element.19), channel_id=1, source_target_pairs={{4,0},{6,2},{2,6},{5,1},{7,3},{3,7},{12,8},{14,10},{10,14},{13,9},... | collective-permute-start | bytes 196616 | tf_op jit(solution)/shard_map/ppermute | solution.py:292
  31.4 5.8 %collective-permute-start.6 = (bf16[128,256]{1,0:T(8,128)(2,1)S(1)}, bf16[128,256]{1,0:T(8,128)(2,1)S(1)}, u32[]{:S(2)}, u32[]{:S(2)}) collective-permute-start(bf16[128,256]{1,0:T(8,128)(2,1)S(1)} %get-tuple-element.20), channel_id=1, source_target_pairs={{6,4},{4,6},{7,5},{5,7},{14,12},{12,14},{15,13},{13,15},{22,20},{2... | collective-permute-start | bytes 196616 | tf_op jit(solution)/shard_map/ppermute | solution.py:292
  38.5 1.8 %collective-permute-start.7 = (bf16[64,3200]{1,0:T(8,128)(2,1)S(1)}, bf16[64,3200]{1,0:T(8,128)(2,1)S(1)}, u32[]{:S(2)}, u32[]{:S(2)}) collective-permute-start(bf16[64,3200]{1,0:T(8,128)(2,1)S(1)} %get-tuple-element.22), channel_id=1, source_target_pairs={{0,8},{1,9},{8,0},{9,1},{16,24},{17,25},{24,16},{25,17},{2,10},{3,... | collective-permute-start | bytes 1228808 | tf_op jit(solution)/shard_map/ppermute | solution.py:302
  40.4 6.7 %collective-permute-start.8 = (bf16[16,3200]{1,0:T(8,128)(2,1)S(1)}, bf16[16,3200]{1,0:T(8,128)(2,1)S(1)}, u32[]{:S(2)}, u32[]{:S(2)}) collective-permute-start(bf16[16,3200]{1,0:T(8,128)(2,1)S(1)} %get-tuple-element.25), channel_id=1, source_target_pairs={{0,17},{1,16},{8,25},{9,24},{16,1},{17,0},{24,9},{25,8},{2,19},{3,... | collective-permute-start | bytes 307208 | tf_op jit(solution)/shard_map/ppermute | solution.py:313
  42.9 5.6 %collective-permute-start.9 = (bf16[16,3200]{1,0:T(8,128)(2,1)S(1)}, bf16[16,3200]{1,0:T(8,128)(2,1)S(1)}, u32[]{:S(2)}, u32[]{:S(2)}) collective-permute-start(bf16[16,3200]{1,0:T(8,128)(2,1)S(1)} %get-tuple-element.26), channel_id=1, source_target_pairs={{0,16},{1,17},{8,24},{9,25},{16,0},{17,1},{24,8},{25,9},{2,18},{3,... | collective-permute-start | bytes 307208 | tf_op jit(solution)/shard_map/ppermute | solution.py:313
  43.4 5.1 %collective-permute-start.10 = (bf16[16,3200]{1,0:T(8,128)(2,1)S(1)}, bf16[16,3200]{1,0:T(8,128)(2,1)S(1)}, u32[]{:S(2)}, u32[]{:S(2)}) collective-permute-start(bf16[16,3200]{1,0:T(8,128)(2,1)S(1)} %get-tuple-element.27), channel_id=1, source_target_pairs={{0,1},{1,0},{8,9},{9,8},{16,17},{17,16},{24,25},{25,24},{2,3},{3,2... | collective-permute-start | bytes 307208 | tf_op jit(solution)/shard_map/ppermute | solution.py:313
  48.7 6.6 %collective-permute-start.13 = (bf16[16,3200]{1,0:T(8,128)(2,1)S(1)}, bf16[16,3200]{1,0:T(8,128)(2,1)S(1)}, u32[]{:S(2)}, u32[]{:S(2)}) collective-permute-start(bf16[16,3200]{1,0:T(8,128)(2,1)S(1)} %shard_map.91.refs_0_), channel_id=1, source_target_pairs={{0,17},{1,16},{8,25},{9,24},{16,1},{17,0},{24,9},{25,8},{2,19},{3,... | collective-permute-start | bytes 307208 | tf_op jit(solution)/shard_map/ppermute | solution.py:324
  51.2 5.4 %collective-permute-start.12 = (bf16[16,3200]{1,0:T(8,128)(2,1)S(1)}, bf16[16,3200]{1,0:T(8,128)(2,1)S(1)}, u32[]{:S(2)}, u32[]{:S(2)}) collective-permute-start(bf16[16,3200]{1,0:T(8,128)(2,1)S(1)} %shard_map.91.refs_0_), channel_id=1, source_target_pairs={{0,16},{1,17},{8,24},{9,25},{16,0},{17,1},{24,8},{25,9},{2,18},{3,... | collective-permute-start | bytes 307208 | tf_op jit(solution)/shard_map/ppermute | solution.py:324
  51.7 5.0 %collective-permute-start.11 = (bf16[16,3200]{1,0:T(8,128)(2,1)S(1)}, bf16[16,3200]{1,0:T(8,128)(2,1)S(1)}, u32[]{:S(2)}, u32[]{:S(2)}) collective-permute-start(bf16[16,3200]{1,0:T(8,128)(2,1)S(1)} %shard_map.91.refs_0_), channel_id=1, source_target_pairs={{0,1},{1,0},{8,9},{9,8},{16,17},{17,16},{24,25},{25,24},{2,3},{3,2... | collective-permute-start | bytes 307208 | tf_op jit(solution)/shard_map/ppermute | solution.py:324
  52.3 4.8 %collective-permute-start.14 = (bf16[16,3200]{1,0:T(8,128)(2,1)S(1)}, bf16[16,3200]{1,0:T(8,128)(2,1)S(1)}, u32[]{:S(2)}, u32[]{:S(2)}) collective-permute-start(bf16[16,3200]{1,0:T(8,128)(2,1)S(1)} %shard_map.91.refs_0_), channel_id=1, source_target_pairs={{0,8},{1,9},{8,0},{9,1},{16,24},{17,25},{24,16},{25,17},{2,10},{3,... | collective-permute-start | bytes 307208 | tf_op jit(solution)/shard_map/ppermute | solution.py:325
  55.3 1.8 %collective-permute-start.17 = (bf16[16,3200]{1,0:T(8,128)(2,1)S(1)}, bf16[16,3200]{1,0:T(8,128)(2,1)S(1)}, u32[]{:S(2)}, u32[]{:S(2)}) collective-permute-start(bf16[16,3200]{1,0:T(8,128)(2,1)S(1)} %collective-permute-done.13.refs_3_), channel_id=1, source_target_pairs={{0,8},{1,9},{8,0},{9,1},{16,24},{17,25},{24,16},{25,17},{2,10},{3,... | collective-permute-start | bytes 307208 | tf_op jit(solution)/shard_map/ppermute | solution.py:325
  56.5 1.3 %collective-permute-start.16 = (bf16[16,3200]{1,0:T(8,128)(2,1)S(1)}, bf16[16,3200]{1,0:T(8,128)(2,1)S(1)}, u32[]{:S(2)}, u32[]{:S(2)}) collective-permute-start(bf16[16,3200]{1,0:T(8,128)(2,1)S(1)} %collective-permute-done.12.refs_2_), channel_id=1, source_target_pairs={{0,8},{1,9},{8,0},{9,1},{16,24},{17,25},{24,16},{25,17},{2,10},{3,... | collective-permute-start | bytes 307208 | tf_op jit(solution)/shard_map/ppermute | solution.py:325
  56.7 1.3 %collective-permute-start.15 = (bf16[16,3200]{1,0:T(8,128)(2,1)S(1)}, bf16[16,3200]{1,0:T(8,128)(2,1)S(1)}, u32[]{:S(2)}, u32[]{:S(2)}) collective-permute-start(bf16[16,3200]{1,0:T(8,128)(2,1)S(1)} %collective-permute-done.11.refs_1_), channel_id=1, source_target_pairs={{0,8},{1,9},{8,0},{9,1},{16,24},{17,25},{24,16},{25,17},{2,10},{3,... | collective-permute-start | bytes 307208 | tf_op jit(solution)/shard_map/ppermute | solution.py:325

commit v3 on v2

--- a/solution.py
+++ b/solution.py
@@ -12,7 +12,6 @@
 EPS = 1e-06
 NEG = -1e30
 VMEM_LIMIT = 48 * 1024 * 1024
-WIDE_LIMIT = 60 * 1024 * 1024
 WHOLE = pl.BlockSpec(memory_space=pltpu.VMEM)
 SCALARS = pl.BlockSpec(memory_space=pltpu.SMEM)
 
@@ -36,13 +35,13 @@
     return lax.dot_general(a, b, (dims, ((), ())), preferred_element_type=jnp.float32)
 
 
-def call(body, out_shape, in_specs, out_specs, flops, moved, limit=VMEM_LIMIT, **more):
+def call(body, out_shape, in_specs, out_specs, flops, moved, **more):
     return pl.pallas_call(
         body,
         out_shape=out_shape,
         in_specs=in_specs,
         out_specs=out_specs,
-        compiler_params=pltpu.CompilerParams(vmem_limit_bytes=limit),
+        compiler_params=pltpu.CompilerParams(vmem_limit_bytes=VMEM_LIMIT),
         cost_estimate=pl.CostEstimate(flops=flops, bytes_accessed=moved, transcendentals=0),
         **more,
     )
@@ -92,30 +91,23 @@
     pick = jnp.where(source == to - before, 1.0, 0.0).astype(jnp.bfloat16)
     moved = jnp.dot(pick, image_ref[...], preferred_element_type=jnp.float32)
     row = lax.broadcasted_iota(jnp.int32, moved.shape, 0)
-    out_ref[...] = jnp.where(row < before, text_ref[...].astype(jnp.float32), moved).astype(jnp.bfloat16)
-
-
-def pick_static(table, index):
-    value = jnp.int32(table[0])
-    for n in range(1, len(table)):
-        value = jnp.where(index == n, table[n], value)
-    return value
-
-
-def attend_body(seq_n, tables, q_ref, g_ref, own_ref, *refs):
-    got_refs, out_ref, grad_refs = refs[: len(tables)], refs[len(tables)], refs[len(tables) + 1 :]
+    block = jnp.where(row < before, text_ref[...].astype(jnp.float32), moved).astype(jnp.bfloat16)
+    for d in range(seq_n):
+        out_ref[d] = block
+
+
+def attend_body(seq_n, owners, q_ref, g_ref, kv_ref, out_ref, grad_ref):
     rows = q_ref.shape[0]
     group = q_ref.shape[1] // HD
     scale = 1.0 / math.sqrt(HD)
     me = lax.axis_index("seq")
-    images = [held_image(me, seq_n)] + [pick_static(table, me) for table in tables]
-    kv = jnp.concatenate([own_ref[...]] + [ref[...] for ref in got_refs], axis=0)
+    kv = jnp.concatenate([kv_ref[b] for b in owners], axis=0)
     keys, values = kv[:, :HD], kv[:, HD:]
     together = group if kv.shape[0] <= 1024 else 1
     span = together * rows
     offset = lax.broadcasted_iota(jnp.int32, (rows, span), 0)
     offset = offset - lax.rem(lax.broadcasted_iota(jnp.int32, (rows, span), 1), rows)
-    masks = [offset <= (me - image) * rows for image in images]
+    masks = [offset <= (me - j) * rows for j in range(seq_n)]
     key_total = value_total = None
     for first in range(0, group, together):
         heads = range(first, first + together)
@@ -140,20 +132,19 @@
         for n, h in enumerate(heads):
             part = jnp.transpose(mixed[:, n * rows : (n + 1) * rows])
             out_ref[:, h * HD : (h + 1) * HD] = part.astype(jnp.bfloat16)
-    for n, ref in enumerate(grad_refs):
-        ref[:, :HD] = key_total[n * rows : (n + 1) * rows].astype(jnp.bfloat16)
-        ref[:, HD:] = value_total[n * rows : (n + 1) * rows].astype(jnp.bfloat16)
-
-
-def back_body(seq_n, piece, pieces_ref, proj_ref, *refs):
-    part_refs, (keep_ref, send_ref) = refs[:-2], refs[-2:]
-    rows = part_refs[0].shape[0]
+    for j, b in enumerate(owners):
+        grad_ref[b, :, :HD] = key_total[j * rows : (j + 1) * rows].astype(jnp.bfloat16)
+        grad_ref[b, :, HD:] = value_total[j * rows : (j + 1) * rows].astype(jnp.bfloat16)
+
+
+def back_body(seq_n, piece, pieces_ref, proj_ref, part_ref, keep_ref, send_ref):
+    rows = part_ref.shape[1]
     half = rows // 2
     before = pieces_ref[2 * held_image(lax.axis_index("seq"), seq_n)]
     parity, place = group_place()
-    total = part_refs[0][...].astype(jnp.float32)
-    for ref in part_refs[1:]:
-        total += ref[...].astype(jnp.float32)
+    total = part_ref[0].astype(jnp.float32)
+    for b in range(1, seq_n):
+        total += part_ref[b].astype(jnp.float32)
     slot = lax.broadcasted_iota(jnp.int32, (rows, rows), 0)
     to = (lax.div(slot, half) ^ parity) * half
     to += (lax.div(lax.rem(slot, half), piece) ^ place) * piece + lax.rem(slot, piece)
@@ -209,18 +200,6 @@
         copy.wait()
 
 
-def rounds_of(edges):
-    rounds = []
-    for source, target in sorted(edges, key=lambda e: (-abs(e[0] - e[1]), e)):
-        for pairs in rounds:
-            if all(source != s and target != t for s, t in pairs):
-                pairs.append((source, target))
-                break
-        else:
-            rounds.append([(source, target)])
-    return rounds
-
-
 def on_device(vis_rows, vis_gain, key_value_proj, pieces, text_kv, queries, grad_out):
     rows, width = vis_rows.shape
     columns = key_value_proj.shape[1]
@@ -253,7 +232,6 @@
         [WHOLE, WHOLE],
         2 * rows * width * columns,
         2 * width * (rows + columns),
-        limit=WIDE_LIMIT,
         scratch_shapes=[
             pltpu.VMEM((rows, width), bf16),
             pltpu.VMEM(gain.shape, f32),
@@ -263,42 +241,34 @@
             pltpu.SemaphoreType.DMA,
         ],
     )(vis_rows, gain, key_value_proj)
-    block = call(
+    copies = call(
         functools.partial(place_body, seq_n),
-        jax.ShapeDtypeStruct((rows, columns), bf16),
+        jax.ShapeDtypeStruct((seq_n, rows, columns), bf16),
         [SCALARS, WHOLE, WHOLE],
         WHOLE,
         2 * rows * rows * columns,
         6 * rows * columns,
     )(pieces, image_kv, text)
 
-    rounds = rounds_of([(owners[j], s) for j in range(seq_n) for s in range(j, seq_n) if owners[j] != s])
-    held = [owners.index(b) for b in range(seq_n)]
-    tables = []
-    for pairs in rounds:
-        table = [seq_n] * seq_n
-        for source, target in pairs:
-            table[target] = held[source]
-        tables.append(table)
-    got = [lax.ppermute(block, "seq", pairs) for pairs in rounds]
-    attended, own_grad, *grads = call(
-        functools.partial(attend_body, seq_n, tables),
-        [jax.ShapeDtypeStruct(queries.shape, bf16)] + [jax.ShapeDtypeStruct((rows, columns), bf16)] * (1 + len(got)),
-        [WHOLE] * (3 + len(got)),
-        [WHOLE] * (2 + len(got)),
+    blocks = lax.all_to_all(copies, "seq", 0, 0)
+    attended, grads = call(
+        functools.partial(attend_body, seq_n, owners),
+        [jax.ShapeDtypeStruct(queries.shape, bf16), jax.ShapeDtypeStruct(blocks.shape, bf16)],
+        [WHOLE] * 3,
+        [WHOLE, WHOLE],
         10 * seq_n * rows * rows * queries.shape[1],
         6 * rows * queries.shape[1] + 4 * seq_n * rows * columns,
-    )(queries, grad_out, block, *got)
-    parts = [lax.ppermute(g, "seq", [(t, s) for s, t in pairs]) for g, pairs in zip(grads, rounds)]
+    )(queries, grad_out, blocks)
+    parts = lax.all_to_all(grads, "seq", 0, 0)
 
     keep, send = call(
         functools.partial(back_body, seq_n, piece),
         [jax.ShapeDtypeStruct((rows // 2, width), f32), jax.ShapeDtypeStruct((rows // 2, width), bf16)],
-        [SCALARS] + [WHOLE] * (2 + len(parts)),
+        [SCALARS, WHOLE, WHOLE],
         [WHOLE, WHOLE],
         2 * rows * width * columns,
         2 * width * columns + 3 * rows * width,
-    )(pieces, key_value_proj, own_grad, *parts)
+    )(pieces, key_value_proj, parts)
     other = lax.ppermute(send, names, core_pairs)
     steps = list(range(1, count))
     own_sum, *sends = call(

time: 59.6 us -> 58.1 us (0.975)
  blocking collectives: 0 us -> 22.2 us
  starting transfers between devices: 26 us -> 12.6 us
  waiting for transfers between devices: 22.9 us -> 11.8 us
  local copies, waits for them, and re-layouts: 0.86 us -> 3.31 us
  Pallas kernels: 8.4 us -> 7.27 us
    all_to_all x0 -> x2, blocking collectives: none -> 22.2 us  [the longest x1 11.3 us: on_device(): blocks = lax.all_to_all(copies, 'seq', 0, 0)]
    ppermute x6 -> x0, starting transfers between devices: 13.4 us -> none  [the longest x3 9.42 us: on_device(): got = [lax.ppermute(block, 'seq', pairs) for pairs in rounds]]
    ppermute x6 -> x0, waiting for transfers between devices: 11.2 us -> none  [the longest x3 6.01 us: on_device(): got = [lax.ppermute(block, 'seq', pairs) for pairs in rounds]]
    unnamed x14 -> x16, local copies, waits for them, and re-layouts: 0.86 us -> 3.31 us
    pallas_call x1, Pallas kernels: 3.12 us -> 2 us  [on_device(): call(functools.partial(project_body, piece), [jax.ShapeDtypeStruct((rows,...]
  transfers between devices with their start and end apart: 18 -> 12, of which waited for: 11 -> 8; matrix products, arithmetic and copies ran while one was open for 0% -> 0% of each run, Pallas kernels for 5% -> 3%
where the time goes in v3:
time: 58.1 us; the launch traced here: 57.8 us
  blocking collectives  22.2 us (38%)
  starting transfers between devices  12.6 us (22%)
  waiting for transfers between devices  11.8 us (20%)
  Pallas kernels  7.27 us (13%)
  local copies, waits for them, and re-layouts  3.31 us (6%)
  between operations  0.72 us (1%)
    all_to_all x1, blocking collectives, on_device(): blocks = lax.all_to_all(copies, 'seq', 0, 0)  11.3 us
    all_to_all x1, blocking collectives, on_device(): parts = lax.all_to_all(grads, 'seq', 0, 0)  10.9 us
    ppermute x1, starting transfers between devices, on_device(): text = lax.ppermute(text_kv, 'seq', [(j, owners[j]) for j in range(seq_n)])  5.1 us
    ppermute x3, waiting for transfers between devices, on_device(): lax.ppermute(sends[d - 1], names, far_pairs(d))  4.59 us
    ppermute x3, waiting for transfers between devices, on_device(): mines[d] = lax.ppermute(mine, names, far_pairs(d))  4.45 us
    ppermute x3, starting transfers between devices, on_device(): lax.ppermute(sends[d - 1], names, far_pairs(d))  3.55 us
    ppermute x3, starting transfers between devices, on_device(): mines[d] = lax.ppermute(mine, names, far_pairs(d))  3.55 us
    unnamed x16, local copies, waits for them, and re-layouts  3.31 us
  transfers between devices with their start and end apart: 12, of which 8 were waited for; matrix products, arithmetic and copies ran while one was open for 0% of the time, Pallas kernels for 3%

profile of v3, /device:TPU:0, one launch (start us, length us, event | category | flops | bytes accessed | tf_op | source)
XLA Modules:
  0.0 57.8 jit_solution(1055956387859200811)
XLA Ops:
  0.6 0.0 copy-start.5
  0.6 5.1 %collective-permute-start = (bf16[128,256]{1,0:T(8,128)(2,1)}, bf16[128,256]{1,0:T(8,128)(2,1)S(1)}, u32[]{:S(2)}, u32[]{:S(2)}) collective-permute-start(bf16[128,256]{1,0:T(8,128)(2,1)} %param.11), channel_id=1, source_target_pairs={{0,6},{2,4},{4,0},{6,2},{1,7},{3,5},{5,1},{7,3},{8,14},{10,12},{12... | collective-permute-start | bytes 196616 | tf_op jit(solution)/shard_map/ppermute | solution.py:225
  5.7 0.0 copy-start
  5.7 1.4 %copy-done = bf16[3200,256]{1,0:T(8,128)(2,1)S(1)} copy-done((bf16[3200,256]{1,0:T(8,128)(2,1)S(1)}, bf16[3200,256]{1,0:T(8,128)(2,1)}, u32[]{:S(2)}) %copy-start) | copy-done | bytes 1638424
  7.2 0.0 copy-start.2
  7.2 1.1 %copy-done.2 = bf16[128,3200]{1,0:T(8,128)(2,1)S(1)} copy-done((bf16[128,3200]{1,0:T(8,128)(2,1)S(1)}, bf16[128,3200]{1,0:T(8,128)(2,1)}, u32[]{:S(2)}) %copy-start.2) | copy-done | bytes 819224
  8.3 0.0 copy-start.3
  8.3 0.7 %copy-done.3 = f32[3200]{0:T(1024)S(1)} copy-done((f32[3200]{0:T(1024)S(1)}, f32[3200]{0:T(1024)}, u32[]{:S(2)}) %copy-start.3) | copy-done | bytes 12824
  9.0 0.0 copy-start.6
  9.0 0.0 copy-start.7
  9.0 2.0 %shard_map.86 = (bf16[128,256]{1,0:T(8,128)(2,1)S(1)}, bf16[16,3200]{1,0:T(8,128)(2,1)S(1)}) custom-call(bf16[128,3200]{1,0:T(8,128)(2,1)S(1)} %copy-done.2, f32[25,128]{1,0:T(8,128)S(1)} %bitcast.1, bf16[3200,256]{1,0:T(8,128)(2,1)S(1)} %copy-done), custom_call_target="tpu_custom_call" | custom-call | flops 209715200 | bytes 2457600 | tf_op jit(solution)/shard_map/pallas_call | solution.py:228
  11.0 0.0 copy-start.1
  11.1 0.0 collective-permute-done.text_ref
  11.1 0.0 copy-done.5
  11.1 0.7 %shard_map.87 = bf16[4,128,256]{2,1,0:T(8,128)(2,1)S(1)} custom-call(s32[8]{0:T(128)S(1)} %copy-done.5, bf16[128,256]{1,0:T(8,128)(2,1)S(1)} %get-tuple-element.12.image_ref, bf16[128,256]{1,0:T(8,128)(2,1)S(1)} %collective-permute-done.text_ref), custom_call_target="tpu_custom_call" | custom-call | flops 8388608 | bytes 196608 | tf_op jit(solution)/shard_map/pallas_call | solution.py:244
  11.8 11.3 %all_to_all.10.kv_ref = bf16[4,128,256]{2,1,0:T(8,128)(2,1)S(1)} all-to-all(bf16[4,128,256]{2,1,0:T(8,128)(2,1)S(1)} %shard_map.87), channel_id=1, replica_groups=mesh['sec'=4,'seq'=4,'tp'=2] {'seq'}, dimensions={0} | all-to-all | bytes 524288 | tf_op jit(solution)/shard_map/all_to_all | solution.py:253
  23.0 0.0 copy-done.6
  23.0 0.0 copy-done.7
  23.0 2.1 %shard_map.88 = (bf16[128,512]{1,0:T(8,128)(2,1)}, bf16[4,128,256]{2,1,0:T(8,128)(2,1)S(1)}) custom-call(bf16[128,512]{1,0:T(8,128)(2,1)S(1)} %copy-done.6, bf16[128,512]{1,0:T(8,128)(2,1)S(1)} %copy-done.7, bf16[4,128,256]{2,1,0:T(8,128)(2,1)S(1)} %all_to_all.10.kv_ref), custom_call_target="tpu_custom_call" | custom-call | flops 335544320 | bytes 917504 | tf_op jit(solution)/shard_map/pallas_call | solution.py:254
  25.1 10.9 %all_to_all.11.part_ref = bf16[4,128,256]{2,1,0:T(8,128)(2,1)S(1)} all-to-all(bf16[4,128,256]{2,1,0:T(8,128)(2,1)S(1)} %get-tuple-element.14), channel_id=1, replica_groups=mesh['sec'=4,'seq'=4,'tp'=2] {'seq'}, dimensions={0} | all-to-all | bytes 524288 | tf_op jit(solution)/shard_map/all_to_all | solution.py:262
  36.0 0.0 copy-done.1
  36.0 1.3 %shard_map.89 = (f32[64,3200]{1,0:T(8,128)S(1)}, bf16[64,3200]{1,0:T(8,128)(2,1)S(1)}) custom-call(s32[8]{0:T(128)S(1)} %copy-done.5, bf16[3200,256]{1,0:T(8,128)(2,1)S(1)} %copy-done.1, bf16[4,128,256]{2,1,0:T(8,128)(2,1)S(1)} %all_to_all.11.part_ref), custom_call_target="tpu_custom_call" | custom-call | flops 209715200 | bytes 2867200 | tf_op jit(solution)/shard_map/pallas_call | solution.py:264
  37.3 0.1 collective-permute-start.1
  37.4 1.7 %collective-permute-done.1.other_ref = bf16[64,3200]{1,0:T(8,128)(2,1)S(1)} collective-permute-done((bf16[64,3200]{1,0:T(8,128)(2,1)S(1)}, bf16[64,3200]{1,0:T(8,128)(2,1)S(1)}, u32[]{:S(2)}, u32[]{:S(2)}) %collective-permute-start.1) | collective-permute-done | bytes 409632 | tf_op jit(solution)/shard_map/ppermute | solution.py:272
  39.1 0.1 shard_map.90
  39.2 2.5 %collective-permute-start.2 = (bf16[16,3200]{1,0:T(8,128)(2,1)S(1)}, bf16[16,3200]{1,0:T(8,128)(2,1)S(1)}, u32[]{:S(2)}, u32[]{:S(2)}) collective-permute-start(bf16[16,3200]{1,0:T(8,128)(2,1)S(1)} %get-tuple-element.19), channel_id=1, source_target_pairs={{0,17},{1,16},{8,25},{9,24},{16,1},{17,0},{24,9},{25,8},{2,19},{3,... | collective-permute-start | bytes 307208 | tf_op jit(solution)/shard_map/ppermute | solution.py:283
  41.7 0.5 collective-permute-start.3
  42.3 0.5 collective-permute-start.4
  42.8 3.1 %collective-permute-done.2.refs_0_ = bf16[16,3200]{1,0:T(8,128)(2,1)S(1)} collective-permute-done((bf16[16,3200]{1,0:T(8,128)(2,1)S(1)}, bf16[16,3200]{1,0:T(8,128)(2,1)S(1)}, u32[]{:S(2)}, u32[]{:S(2)}) %collective-permute-start.2) | collective-permute-done | bytes 102432 | tf_op jit(solution)/shard_map/ppermute | solution.py:283
  45.9 1.4 %collective-permute-done.3.refs_1_ = bf16[16,3200]{1,0:T(8,128)(2,1)S(1)} collective-permute-done((bf16[16,3200]{1,0:T(8,128)(2,1)S(1)}, bf16[16,3200]{1,0:T(8,128)(2,1)S(1)}, u32[]{:S(2)}, u32[]{:S(2)}) %collective-permute-start.3) | collective-permute-done | bytes 102432 | tf_op jit(solution)/shard_map/ppermute | solution.py:283
  47.4 0.0 collective-permute-done.4.refs_2_
  47.4 0.0 copy-done.4
  47.4 0.2 shard_map.91.refs_0_
  47.6 2.4 %collective-permute-start.7 = (bf16[16,3200]{1,0:T(8,128)(2,1)S(1)}, bf16[16,3200]{1,0:T(8,128)(2,1)S(1)}, u32[]{:S(2)}, u32[]{:S(2)}) collective-permute-start(bf16[16,3200]{1,0:T(8,128)(2,1)S(1)} %shard_map.91.refs_0_), channel_id=1, source_target_pairs={{0,17},{1,16},{8,25},{9,24},{16,1},{17,0},{24,9},{25,8},{2,19},{3,... | collective-permute-start | bytes 307208 | tf_op jit(solution)/shard_map/ppermute | solution.py:294
  50.0 0.5 collective-permute-start.6
  50.5 0.6 collective-permute-start.5
  51.1 0.0 collective-permute-start.8
  51.1 3.0 %collective-permute-done.7.refs_3_ = bf16[16,3200]{1,0:T(8,128)(2,1)S(1)} collective-permute-done((bf16[16,3200]{1,0:T(8,128)(2,1)S(1)}, bf16[16,3200]{1,0:T(8,128)(2,1)S(1)}, u32[]{:S(2)}, u32[]{:S(2)}) %collective-permute-start.7) | collective-permute-done | bytes 102432 | tf_op jit(solution)/shard_map/ppermute | solution.py:294
  54.1 0.0 collective-permute-start.11
  54.1 1.3 %collective-permute-done.6.refs_2_ = bf16[16,3200]{1,0:T(8,128)(2,1)S(1)} collective-permute-done((bf16[16,3200]{1,0:T(8,128)(2,1)S(1)}, bf16[16,3200]{1,0:T(8,128)(2,1)S(1)}, u32[]{:S(2)}, u32[]{:S(2)}) %collective-permute-start.6) | collective-permute-done | bytes 102432 | tf_op jit(solution)/shard_map/ppermute | solution.py:294
  55.4 0.0 collective-permute-start.10
  55.4 0.2 collective-permute-done.5.refs_1_
  55.6 0.3 collective-permute-start.9
  55.9 0.0 collective-permute-done.8.refs_4_
  55.9 0.0 collective-permute-done.11.refs_7_
  55.9 0.8 %collective-permute-done.10.refs_6_ = bf16[16,3200]{1,0:T(8,128)(2,1)S(1)} collective-permute-done((bf16[16,3200]{1,0:T(8,128)(2,1)S(1)}, bf16[16,3200]{1,0:T(8,128)(2,1)S(1)}, u32[]{:S(2)}, u32[]{:S(2)}) %collective-permute-start.10) | collective-permute-done | bytes 102432 | tf_op jit(solution)/shard_map/ppermute | solution.py:295
  56.7 0.2 collective-permute-done.9.refs_5_
  56.9 0.9 %shard_map.92 = bf16[128,3200]{1,0:T(8,128)(2,1)} custom-call(bf16[16,3200]{1,0:T(8,128)(2,1)S(1)} %shard_map.91.refs_0_, bf16[16,3200]{1,0:T(8,128)(2,1)S(1)} %collective-permute-done.5.refs_1_, bf16[16,3200]{1,0:T(8,128)(2,1)S(1)} %collective-permute-done.6.refs_2_, bf16[16,3200]{1,0:T(8,128)(2,1)S(1)} %collective-permute-done.7.refs_3_, ...), custom_call_target="tpu_custom_call" | custom-call | bytes 1638400 | tf_op jit(solution)/shard_map/pallas_call | solution.py:296
  (1 shorter events, 0.0 us)
Async XLA Ops:
  0.6 10.4 %copy-start.5 = (s32[8]{0:T(128)S(1)}, s32[8]{0:T(128)}, u32[]{:S(2)}) copy-start(s32[8]{0:T(128)} %pieces_ref.3) | copy-start | bytes 100
  0.6 10.4 %collective-permute-start = (bf16[128,256]{1,0:T(8,128)(2,1)}, bf16[128,256]{1,0:T(8,128)(2,1)S(1)}, u32[]{:S(2)}, u32[]{:S(2)}) collective-permute-start(bf16[128,256]{1,0:T(8,128)(2,1)} %param.11), channel_id=1, source_target_pairs={{0,6},{2,4},{4,0},{6,2},{1,7},{3,5},{5,1},{7,3},{8,14},{10,12},{12... | collective-permute-start | bytes 196616 | tf_op jit(solution)/shard_map/ppermute | solution.py:225
  5.7 1.4 %copy-start = (bf16[3200,256]{1,0:T(8,128)(2,1)S(1)}, bf16[3200,256]{1,0:T(8,128)(2,1)}, u32[]{:S(2)}) copy-start(bf16[3200,256]{1,0:T(8,128)(2,1)} %proj_ref.1) | copy-start | bytes 4915204
  7.2 1.1 %copy-start.2 = (bf16[128,3200]{1,0:T(8,128)(2,1)S(1)}, bf16[128,3200]{1,0:T(8,128)(2,1)}, u32[]{:S(2)}) copy-start(bf16[128,3200]{1,0:T(8,128)(2,1)} %vis_hbm.1) | copy-start | bytes 2457604
  8.3 0.7 %copy-start.3 = (f32[3200]{0:T(1024)S(1)}, f32[3200]{0:T(1024)}, u32[]{:S(2)}) copy-start(f32[3200]{0:T(1024)} %param.8) | copy-start | bytes 38404
  9.0 14.0 %copy-start.6 = (bf16[128,512]{1,0:T(8,128)(2,1)S(1)}, bf16[128,512]{1,0:T(8,128)(2,1)}, u32[]{:S(2)}) copy-start(bf16[128,512]{1,0:T(8,128)(2,1)} %q_ref.1) | copy-start | bytes 393220
  9.0 14.0 %copy-start.7 = (bf16[128,512]{1,0:T(8,128)(2,1)S(1)}, bf16[128,512]{1,0:T(8,128)(2,1)}, u32[]{:S(2)}) copy-start(bf16[128,512]{1,0:T(8,128)(2,1)} %g_ref.1) | copy-start | bytes 393220
  11.0 25.0 %copy-start.1 = (bf16[3200,256]{1,0:T(8,128)(2,1)S(1)}, bf16[3200,256]{1,0:T(8,128)(2,1)}, u32[]{:S(2)}) copy-start(bf16[3200,256]{1,0:T(8,128)(2,1)} %proj_ref.1) | copy-start | bytes 4915204
  36.0 11.4 %copy-start.4 = (f32[3200]{0:T(1024)S(1)}, f32[3200]{0:T(1024)}, u32[]{:S(2)}) copy-start(f32[3200]{0:T(1024)} %param.8) | copy-start | bytes 38404
  37.3 1.8 %collective-permute-start.1 = (bf16[64,3200]{1,0:T(8,128)(2,1)S(1)}, bf16[64,3200]{1,0:T(8,128)(2,1)S(1)}, u32[]{:S(2)}, u32[]{:S(2)}) collective-permute-start(bf16[64,3200]{1,0:T(8,128)(2,1)S(1)} %get-tuple-element.16), channel_id=1, source_target_pairs={{0,8},{1,9},{8,0},{9,1},{16,24},{17,25},{24,16},{25,17},{2,10},{3,... | collective-permute-start | bytes 1228808 | tf_op jit(solution)/shard_map/ppermute | solution.py:272
  39.2 6.7 %collective-permute-start.2 = (bf16[16,3200]{1,0:T(8,128)(2,1)S(1)}, bf16[16,3200]{1,0:T(8,128)(2,1)S(1)}, u32[]{:S(2)}, u32[]{:S(2)}) collective-permute-start(bf16[16,3200]{1,0:T(8,128)(2,1)S(1)} %get-tuple-element.19), channel_id=1, source_target_pairs={{0,17},{1,16},{8,25},{9,24},{16,1},{17,0},{24,9},{25,8},{2,19},{3,... | collective-permute-start | bytes 307208 | tf_op jit(solution)/shard_map/ppermute | solution.py:283
  41.7 5.6 %collective-permute-start.3 = (bf16[16,3200]{1,0:T(8,128)(2,1)S(1)}, bf16[16,3200]{1,0:T(8,128)(2,1)S(1)}, u32[]{:S(2)}, u32[]{:S(2)}) collective-permute-start(bf16[16,3200]{1,0:T(8,128)(2,1)S(1)} %get-tuple-element.20), channel_id=1, source_target_pairs={{0,16},{1,17},{8,24},{9,25},{16,0},{17,1},{24,8},{25,9},{2,18},{3,... | collective-permute-start | bytes 307208 | tf_op jit(solution)/shard_map/ppermute | solution.py:283
  42.3 5.1 %collective-permute-start.4 = (bf16[16,3200]{1,0:T(8,128)(2,1)S(1)}, bf16[16,3200]{1,0:T(8,128)(2,1)S(1)}, u32[]{:S(2)}, u32[]{:S(2)}) collective-permute-start(bf16[16,3200]{1,0:T(8,128)(2,1)S(1)} %get-tuple-element.21), channel_id=1, source_target_pairs={{0,1},{1,0},{8,9},{9,8},{16,17},{17,16},{24,25},{25,24},{2,3},{3,2... | collective-permute-start | bytes 307208 | tf_op jit(solution)/shard_map/ppermute | solution.py:283
  47.6 6.6 %collective-permute-start.7 = (bf16[16,3200]{1,0:T(8,128)(2,1)S(1)}, bf16[16,3200]{1,0:T(8,128)(2,1)S(1)}, u32[]{:S(2)}, u32[]{:S(2)}) collective-permute-start(bf16[16,3200]{1,0:T(8,128)(2,1)S(1)} %shard_map.91.refs_0_), channel_id=1, source_target_pairs={{0,17},{1,16},{8,25},{9,24},{16,1},{17,0},{24,9},{25,8},{2,19},{3,... | collective-permute-start | bytes 307208 | tf_op jit(solution)/shard_map/ppermute | solution.py:294
  50.0 5.4 %collective-permute-start.6 = (bf16[16,3200]{1,0:T(8,128)(2,1)S(1)}, bf16[16,3200]{1,0:T(8,128)(2,1)S(1)}, u32[]{:S(2)}, u32[]{:S(2)}) collective-permute-start(bf16[16,3200]{1,0:T(8,128)(2,1)S(1)} %shard_map.91.refs_0_), channel_id=1, source_target_pairs={{0,16},{1,17},{8,24},{9,25},{16,0},{17,1},{24,8},{25,9},{2,18},{3,... | collective-permute-start | bytes 307208 | tf_op jit(solution)/shard_map/ppermute | solution.py:294
  50.5 5.0 %collective-permute-start.5 = (bf16[16,3200]{1,0:T(8,128)(2,1)S(1)}, bf16[16,3200]{1,0:T(8,128)(2,1)S(1)}, u32[]{:S(2)}, u32[]{:S(2)}) collective-permute-start(bf16[16,3200]{1,0:T(8,128)(2,1)S(1)} %shard_map.91.refs_0_), channel_id=1, source_target_pairs={{0,1},{1,0},{8,9},{9,8},{16,17},{17,16},{24,25},{25,24},{2,3},{3,2... | collective-permute-start | bytes 307208 | tf_op jit(solution)/shard_map/ppermute | solution.py:294
  51.1 4.8 %collective-permute-start.8 = (bf16[16,3200]{1,0:T(8,128)(2,1)S(1)}, bf16[16,3200]{1,0:T(8,128)(2,1)S(1)}, u32[]{:S(2)}, u32[]{:S(2)}) collective-permute-start(bf16[16,3200]{1,0:T(8,128)(2,1)S(1)} %shard_map.91.refs_0_), channel_id=1, source_target_pairs={{0,8},{1,9},{8,0},{9,1},{16,24},{17,25},{24,16},{25,17},{2,10},{3,... | collective-permute-start | bytes 307208 | tf_op jit(solution)/shard_map/ppermute | solution.py:295
  54.1 1.8 %collective-permute-start.11 = (bf16[16,3200]{1,0:T(8,128)(2,1)S(1)}, bf16[16,3200]{1,0:T(8,128)(2,1)S(1)}, u32[]{:S(2)}, u32[]{:S(2)}) collective-permute-start(bf16[16,3200]{1,0:T(8,128)(2,1)S(1)} %collective-permute-done.7.refs_3_), channel_id=1, source_target_pairs={{0,8},{1,9},{8,0},{9,1},{16,24},{17,25},{24,16},{25,17},{2,10},{3,... | collective-permute-start | bytes 307208 | tf_op jit(solution)/shard_map/ppermute | solution.py:295
  55.4 1.3 %collective-permute-start.10 = (bf16[16,3200]{1,0:T(8,128)(2,1)S(1)}, bf16[16,3200]{1,0:T(8,128)(2,1)S(1)}, u32[]{:S(2)}, u32[]{:S(2)}) collective-permute-start(bf16[16,3200]{1,0:T(8,128)(2,1)S(1)} %collective-permute-done.6.refs_2_), channel_id=1, source_target_pairs={{0,8},{1,9},{8,0},{9,1},{16,24},{17,25},{24,16},{25,17},{2,10},{3,... | collective-permute-start | bytes 307208 | tf_op jit(solution)/shard_map/ppermute | solution.py:295
  55.6 1.3 %collective-permute-start.9 = (bf16[16,3200]{1,0:T(8,128)(2,1)S(1)}, bf16[16,3200]{1,0:T(8,128)(2,1)S(1)}, u32[]{:S(2)}, u32[]{:S(2)}) collective-permute-start(bf16[16,3200]{1,0:T(8,128)(2,1)S(1)} %collective-permute-done.5.refs_1_), channel_id=1, source_target_pairs={{0,8},{1,9},{8,0},{9,1},{16,24},{17,25},{24,16},{25,17},{2,10},{3,... | collective-permute-start | bytes 307208 | tf_op jit(solution)/shard_map/ppermute | solution.py:295

commit v4 on v3

--- a/solution.py
+++ b/solution.py
@@ -12,6 +12,7 @@
 EPS = 1e-06
 NEG = -1e30
 VMEM_LIMIT = 48 * 1024 * 1024
+WIDE_LIMIT = 60 * 1024 * 1024
 WHOLE = pl.BlockSpec(memory_space=pltpu.VMEM)
 SCALARS = pl.BlockSpec(memory_space=pltpu.SMEM)
 
@@ -35,13 +36,13 @@
     return lax.dot_general(a, b, (dims, ((), ())), preferred_element_type=jnp.float32)
 
 
-def call(body, out_shape, in_specs, out_specs, flops, moved, **more):
+def call(body, out_shape, in_specs, out_specs, flops, moved, limit=VMEM_LIMIT, **more):
     return pl.pallas_call(
         body,
         out_shape=out_shape,
         in_specs=in_specs,
         out_specs=out_specs,
-        compiler_params=pltpu.CompilerParams(vmem_limit_bytes=VMEM_LIMIT),
+        compiler_params=pltpu.CompilerParams(vmem_limit_bytes=limit),
         cost_estimate=pl.CostEstimate(flops=flops, bytes_accessed=moved, transcendentals=0),
         **more,
     )
@@ -83,15 +84,20 @@
     own_ref[...] = vis[pl.ds(start, piece), :]
 
 
-def place_body(seq_n, pieces_ref, image_ref, text_ref, out_ref):
+def shift_body(seq_n, pieces_ref, image_ref, out_ref):
     rows = image_ref.shape[0]
     before = pieces_ref[2 * held_image(lax.axis_index("seq"), seq_n)]
     to = lax.broadcasted_iota(jnp.int32, (rows, rows), 0)
     source = lax.broadcasted_iota(jnp.int32, (rows, rows), 1)
     pick = jnp.where(source == to - before, 1.0, 0.0).astype(jnp.bfloat16)
-    moved = jnp.dot(pick, image_ref[...], preferred_element_type=jnp.float32)
-    row = lax.broadcasted_iota(jnp.int32, moved.shape, 0)
-    block = jnp.where(row < before, text_ref[...].astype(jnp.float32), moved).astype(jnp.bfloat16)
+    out_ref[...] = jnp.dot(pick, image_ref[...], preferred_element_type=jnp.float32).astype(jnp.bfloat16)
+
+
+def place_body(seq_n, pieces_ref, image_ref, text_ref, out_ref):
+    before = pieces_ref[2 * held_image(lax.axis_index("seq"), seq_n)]
+    row = lax.broadcasted_iota(jnp.int32, image_ref.shape, 0)
+    text, image = text_ref[...].astype(jnp.float32), image_ref[...].astype(jnp.float32)
+    block = jnp.where(row < before, text, image).astype(jnp.bfloat16)
     for d in range(seq_n):
         out_ref[d] = block
 
@@ -118,13 +124,13 @@
             [jnp.where(mask, scores[n * rows : (n + 1) * rows], NEG) for n, mask in enumerate(masks)], axis=0
         )
         top = jnp.max(scores, axis=0, keepdims=True)
-        weights = jnp.exp((scores - top) * scale)
+        weights = jnp.exp2((scores - top) * (scale * math.log2(math.e)))
         weights = weights * (1.0 / jnp.sum(weights, axis=0, keepdims=True))
         low = weights.astype(jnp.bfloat16)
         mixed = dot(values, low, ((0,), (0,)))
         dprob = dot(values, g, ((1,), (1,)))
         drift = jnp.sum(low.astype(jnp.float32) * dprob, axis=0, keepdims=True)
-        dscore = (weights * (dprob - drift) * scale).astype(jnp.bfloat16)
+        dscore = (weights * (dprob - drift)).astype(jnp.bfloat16)
         dkeys = jnp.dot(dscore, q, preferred_element_type=jnp.float32)
         dvalues = jnp.dot(low, g, preferred_element_type=jnp.float32)
         key_total = dkeys if key_total is None else key_total + dkeys
@@ -133,7 +139,7 @@
             part = jnp.transpose(mixed[:, n * rows : (n + 1) * rows])
             out_ref[:, h * HD : (h + 1) * HD] = part.astype(jnp.bfloat16)
     for j, b in enumerate(owners):
-        grad_ref[b, :, :HD] = key_total[j * rows : (j + 1) * rows].astype(jnp.bfloat16)
+        grad_ref[b, :, :HD] = (key_total[j * rows : (j + 1) * rows] * scale).astype(jnp.bfloat16)
         grad_ref[b, :, HD:] = value_total[j * rows : (j + 1) * rows].astype(jnp.bfloat16)
 
 
@@ -191,7 +197,7 @@
     parity, place = group_place()
     copies = []
     for n, ref in enumerate(part_refs):
-        core, step = divmod(n, count)
+        core, step = n // count, count - 1 - n % count
         row = ((parity ^ core) * count + (place ^ step)) * piece
         copy = pltpu.make_async_copy(ref, out_hbm.at[pl.ds(pl.multiple_of(row, piece), piece), :], sems.at[n])
         copy.start()
@@ -232,6 +238,7 @@
         [WHOLE, WHOLE],
         2 * rows * width * columns,
         2 * width * (rows + columns),
+        limit=WIDE_LIMIT,
         scratch_shapes=[
             pltpu.VMEM((rows, width), bf16),
             pltpu.VMEM(gain.shape, f32),
@@ -241,14 +248,22 @@
             pltpu.SemaphoreType.DMA,
         ],
     )(vis_rows, gain, key_value_proj)
+    shifted = call(
+        functools.partial(shift_body, seq_n),
+        jax.ShapeDtypeStruct((rows, columns), bf16),
+        [SCALARS, WHOLE],
+        WHOLE,
+        2 * rows * rows * columns,
+        4 * rows * columns,
+    )(pieces, image_kv)
     copies = call(
         functools.partial(place_body, seq_n),
         jax.ShapeDtypeStruct((seq_n, rows, columns), bf16),
         [SCALARS, WHOLE, WHOLE],
         WHOLE,
-        2 * rows * rows * columns,
+        0,
         6 * rows * columns,
-    )(pieces, image_kv, text)
+    )(pieces, shifted, text)
 
     blocks = lax.all_to_all(copies, "seq", 0, 0)
     attended, grads = call(
@@ -279,8 +294,7 @@
         0,
         6 * rows // 2 * width,
     )(keep, other)
-    far_first = steps[::-1]
-    shares = [lax.ppermute(sends[d - 1], names, far_pairs(d)) for d in far_first]
+    shares = [lax.ppermute(sends[d - 1], names, far_pairs(d)) for d in steps]
     mine = call(
         final_body,
         jax.ShapeDtypeStruct((piece, width), bf16),
@@ -290,9 +304,9 @@
         12 * piece * width,
     )(own_sum, own_rows, gain, *shares)
     mines = {0: mine}
-    for d in far_first:
+    for d in steps:
         mines[d] = lax.ppermute(mine, names, far_pairs(d))
-    theirs = {d: lax.ppermute(mines[d], names, core_pairs) for d in [0] + far_first}
+    theirs = {d: lax.ppermute(mines[d], names, core_pairs) for d in range(count)}
     vis_grad = call(
         functools.partial(gather_body, count),
         jax.ShapeDtypeStruct((rows, width), bf16),
@@ -301,7 +315,7 @@
         0,
         4 * rows * width,
         scratch_shapes=[pltpu.SemaphoreType.DMA((n,))],
-    )(*[mines[d] for d in range(count)], *[theirs[d] for d in range(count)])
+    )(*[mines[d] for d in reversed(range(count))], *[theirs[d] for d in reversed(range(count))])
     return (attended, vis_grad)
 
 

time: 58.1 us -> 58.1 us (level)
  local copies, waits for them, and re-layouts: 3.31 us -> 0.98 us
  Pallas kernels: 7.27 us -> 8.8 us
  waiting for transfers between devices: 11.8 us -> 12.9 us
    unnamed x16 -> x14, local copies, waits for them, and re-layouts: 3.31 us -> 0.98 us
    pallas_call x1, Pallas kernels: 2 us -> 3.04 us  [on_device(): call(functools.partial(project_body, piece), [jax.ShapeDtypeStruct((rows,...]
    pallas_call x0 -> x1, Pallas kernels: none -> 0.69 us  [on_device(): call(functools.partial(shift_body, seq_n), jax.ShapeDtypeStruct((rows, co...]
  transfers between devices with their start and end apart: 12 -> 12, of which waited for: 8 -> 8; matrix products, arithmetic and copies ran while one was open for 0% -> 0% of each run, Pallas kernels for 3% -> 6%
where the time goes in v4:
time: 58.1 us; the launch traced here: 57.9 us
  blocking collectives  22.2 us (38%)
  waiting for transfers between devices  12.9 us (22%)
  starting transfers between devices  12.3 us (21%)
  Pallas kernels  8.8 us (15%)
  local copies, waits for them, and re-layouts  0.98 us (2%)
  between operations  0.74 us (1%)
    all_to_all x1, blocking collectives, on_device(): blocks = lax.all_to_all(copies, 'seq', 0, 0)  11.3 us
    all_to_all x1, blocking collectives, on_device(): parts = lax.all_to_all(grads, 'seq', 0, 0)  10.9 us
    ppermute x1, starting transfers between devices, on_device(): text = lax.ppermute(text_kv, 'seq', [(j, owners[j]) for j in range(seq_n)])  5.1 us
    ppermute x3, waiting for transfers between devices, on_device(): shares = [lax.ppermute(sends[d - 1], names, far_pairs(d)) for d in steps]  5.09 us
    ppermute x3, waiting for transfers between devices, on_device(): mines[d] = lax.ppermute(mine, names, far_pairs(d))  4.8 us
    ppermute x3, starting transfers between devices, on_device(): shares = [lax.ppermute(sends[d - 1], names, far_pairs(d)) for d in steps]  3.55 us
    ppermute x3, starting transfers between devices, on_device(): mines[d] = lax.ppermute(mine, names, far_pairs(d))  3.55 us
    pallas_call x1, Pallas kernels, on_device(): call(functools.partial(project_body, piece), [jax.ShapeDtypeStruct((rows,...  3.04 us
  transfers between devices with their start and end apart: 12, of which 8 were waited for; matrix products, arithmetic and copies ran while one was open for 0% of the time, Pallas kernels for 6%

profile of v4, /device:TPU:0, one launch (start us, length us, event | category | flops | bytes accessed | tf_op | source)
XLA Modules:
  0.0 57.9 jit_solution(6246899785866584361)
XLA Ops:
  0.6 0.0 copy-start.4
  0.6 5.1 %collective-permute-start = (bf16[128,256]{1,0:T(8,128)(2,1)}, bf16[128,256]{1,0:T(8,128)(2,1)S(1)}, u32[]{:S(2)}, u32[]{:S(2)}) collective-permute-start(bf16[128,256]{1,0:T(8,128)(2,1)} %param.11), channel_id=1, source_target_pairs={{0,6},{2,4},{4,0},{6,2},{1,7},{3,5},{5,1},{7,3},{8,14},{10,12},{12... | collective-permute-start | bytes 196616 | tf_op jit(solution)/shard_map/ppermute | solution.py:231
  5.7 0.0 copy-start.5
  5.7 0.0 copy-start.6
  5.7 3.0 %shard_map.86 = (bf16[128,256]{1,0:T(8,128)(2,1)}, bf16[16,3200]{1,0:T(8,128)(2,1)}) custom-call(bf16[128,3200]{1,0:T(8,128)(2,1)} %vis_hbm.1, f32[25,128]{1,0:T(8,128)} %bitcast.1, bf16[3200,256]{1,0:T(8,128)(2,1)} %proj_ref.1), custom_call_target="tpu_custom_call" | custom-call | flops 209715200 | bytes 2457600 | tf_op jit(solution)/shard_map/pallas_call | solution.py:234
  8.8 0.0 copy-start
  8.8 0.0 copy-done.4
  8.8 0.0 copy-start.3
  8.8 0.9 %copy-done.3 = bf16[128,256]{1,0:T(8,128)(2,1)S(1)} copy-done((bf16[128,256]{1,0:T(8,128)(2,1)S(1)}, bf16[128,256]{1,0:T(8,128)(2,1)}, u32[]{:S(2)}) %copy-start.3) | copy-done | bytes 65560
  9.8 0.7 %shard_map.87.image_ref = bf16[128,256]{1,0:T(8,128)(2,1)S(1)} custom-call(s32[8]{0:T(128)S(1)} %copy-done.4, bf16[128,256]{1,0:T(8,128)(2,1)S(1)} %copy-done.3), custom_call_target="tpu_custom_call" | custom-call | flops 8388608 | bytes 131072 | tf_op jit(solution)/shard_map/pallas_call | solution.py:251
  10.5 0.0 collective-permute-done.text_ref
  10.5 0.6 shard_map.88
  11.1 11.3 %all_to_all.10.kv_ref = bf16[4,128,256]{2,1,0:T(8,128)(2,1)S(1)} all-to-all(bf16[4,128,256]{2,1,0:T(8,128)(2,1)S(1)} %shard_map.88), channel_id=1, replica_groups=mesh['sec'=4,'seq'=4,'tp'=2] {'seq'}, dimensions={0} | all-to-all | bytes 524288 | tf_op jit(solution)/shard_map/all_to_all | solution.py:268
  22.3 0.0 copy-done.5
  22.3 0.0 copy-done.6
  22.3 2.0 %shard_map.89 = (bf16[128,512]{1,0:T(8,128)(2,1)}, bf16[4,128,256]{2,1,0:T(8,128)(2,1)S(1)}) custom-call(bf16[128,512]{1,0:T(8,128)(2,1)S(1)} %copy-done.5, bf16[128,512]{1,0:T(8,128)(2,1)S(1)} %copy-done.6, bf16[4,128,256]{2,1,0:T(8,128)(2,1)S(1)} %all_to_all.10.kv_ref), custom_call_target="tpu_custom_call" | custom-call | flops 335544320 | bytes 917504 | tf_op jit(solution)/shard_map/pallas_call | solution.py:269
  24.3 10.9 %all_to_all.11.part_ref = bf16[4,128,256]{2,1,0:T(8,128)(2,1)S(1)} all-to-all(bf16[4,128,256]{2,1,0:T(8,128)(2,1)S(1)} %get-tuple-element.14), channel_id=1, replica_groups=mesh['sec'=4,'seq'=4,'tp'=2] {'seq'}, dimensions={0} | all-to-all | bytes 524288 | tf_op jit(solution)/shard_map/all_to_all | solution.py:277
  35.2 0.0 copy-done
  35.2 0.0 copy-start.1
  35.2 0.0 copy-start.2
  35.2 1.3 %shard_map.90 = (f32[64,3200]{1,0:T(8,128)S(1)}, bf16[64,3200]{1,0:T(8,128)(2,1)S(1)}) custom-call(s32[8]{0:T(128)S(1)} %copy-done.4, bf16[3200,256]{1,0:T(8,128)(2,1)S(1)} %copy-done, bf16[4,128,256]{2,1,0:T(8,128)(2,1)S(1)} %all_to_all.11.part_ref), custom_call_target="tpu_custom_call" | custom-call | flops 209715200 | bytes 2867200 | tf_op jit(solution)/shard_map/pallas_call | solution.py:279
  36.5 0.1 collective-permute-start.1
  36.6 1.7 %collective-permute-done.1.other_ref = bf16[64,3200]{1,0:T(8,128)(2,1)S(1)} collective-permute-done((bf16[64,3200]{1,0:T(8,128)(2,1)S(1)}, bf16[64,3200]{1,0:T(8,128)(2,1)S(1)}, u32[]{:S(2)}, u32[]{:S(2)}) %collective-permute-start.1) | collective-permute-done | bytes 409632 | tf_op jit(solution)/shard_map/ppermute | solution.py:287
  38.3 0.1 shard_map.91
  38.4 1.6 %collective-permute-start.2 = (bf16[16,3200]{1,0:T(8,128)(2,1)S(1)}, bf16[16,3200]{1,0:T(8,128)(2,1)S(1)}, u32[]{:S(2)}, u32[]{:S(2)}) collective-permute-start(bf16[16,3200]{1,0:T(8,128)(2,1)S(1)} %get-tuple-element.19), channel_id=1, source_target_pairs={{0,1},{1,0},{8,9},{9,8},{16,17},{17,16},{24,25},{25,24},{2,3},{3,2... | collective-permute-start | bytes 307208 | tf_op jit(solution)/shard_map/ppermute | solution.py:297
  40.0 1.5 %collective-permute-start.3 = (bf16[16,3200]{1,0:T(8,128)(2,1)S(1)}, bf16[16,3200]{1,0:T(8,128)(2,1)S(1)}, u32[]{:S(2)}, u32[]{:S(2)}) collective-permute-start(bf16[16,3200]{1,0:T(8,128)(2,1)S(1)} %get-tuple-element.20), channel_id=1, source_target_pairs={{0,16},{1,17},{8,24},{9,25},{16,0},{17,1},{24,8},{25,9},{2,18},{3,... | collective-permute-start | bytes 307208 | tf_op jit(solution)/shard_map/ppermute | solution.py:297
  41.5 0.5 collective-permute-start.4
  42.0 1.4 %collective-permute-done.2.refs_0_ = bf16[16,3200]{1,0:T(8,128)(2,1)S(1)} collective-permute-done((bf16[16,3200]{1,0:T(8,128)(2,1)S(1)}, bf16[16,3200]{1,0:T(8,128)(2,1)S(1)}, u32[]{:S(2)}, u32[]{:S(2)}) %collective-permute-start.2) | collective-permute-done | bytes 102432 | tf_op jit(solution)/shard_map/ppermute | solution.py:297
  43.4 2.3 %collective-permute-done.3.refs_1_ = bf16[16,3200]{1,0:T(8,128)(2,1)S(1)} collective-permute-done((bf16[16,3200]{1,0:T(8,128)(2,1)S(1)}, bf16[16,3200]{1,0:T(8,128)(2,1)S(1)}, u32[]{:S(2)}, u32[]{:S(2)}) %collective-permute-start.3) | collective-permute-done | bytes 102432 | tf_op jit(solution)/shard_map/ppermute | solution.py:297
  45.7 1.3 %collective-permute-done.4.refs_2_ = bf16[16,3200]{1,0:T(8,128)(2,1)S(1)} collective-permute-done((bf16[16,3200]{1,0:T(8,128)(2,1)S(1)}, bf16[16,3200]{1,0:T(8,128)(2,1)S(1)}, u32[]{:S(2)}, u32[]{:S(2)}) %collective-permute-start.4) | collective-permute-done | bytes 102432 | tf_op jit(solution)/shard_map/ppermute | solution.py:297
  47.1 0.0 copy-done.1
  47.1 0.0 copy-done.2
  47.1 0.2 shard_map.92.refs_3_
  47.3 1.3 %collective-permute-start.7 = (bf16[16,3200]{1,0:T(8,128)(2,1)S(1)}, bf16[16,3200]{1,0:T(8,128)(2,1)S(1)}, u32[]{:S(2)}, u32[]{:S(2)}) collective-permute-start(bf16[16,3200]{1,0:T(8,128)(2,1)S(1)} %shard_map.92.refs_3_), channel_id=1, source_target_pairs={{0,1},{1,0},{8,9},{9,8},{16,17},{17,16},{24,25},{25,24},{2,3},{3,2... | collective-permute-start | bytes 307208 | tf_op jit(solution)/shard_map/ppermute | solution.py:308
  48.6 1.5 %collective-permute-start.6 = (bf16[16,3200]{1,0:T(8,128)(2,1)S(1)}, bf16[16,3200]{1,0:T(8,128)(2,1)S(1)}, u32[]{:S(2)}, u32[]{:S(2)}) collective-permute-start(bf16[16,3200]{1,0:T(8,128)(2,1)S(1)} %shard_map.92.refs_3_), channel_id=1, source_target_pairs={{0,16},{1,17},{8,24},{9,25},{16,0},{17,1},{24,8},{25,9},{2,18},{3,... | collective-permute-start | bytes 307208 | tf_op jit(solution)/shard_map/ppermute | solution.py:308
  50.1 0.7 %collective-permute-start.5 = (bf16[16,3200]{1,0:T(8,128)(2,1)S(1)}, bf16[16,3200]{1,0:T(8,128)(2,1)S(1)}, u32[]{:S(2)}, u32[]{:S(2)}) collective-permute-start(bf16[16,3200]{1,0:T(8,128)(2,1)S(1)} %shard_map.92.refs_3_), channel_id=1, source_target_pairs={{0,17},{1,16},{8,25},{9,24},{16,1},{17,0},{24,9},{25,8},{2,19},{3,... | collective-permute-start | bytes 307208 | tf_op jit(solution)/shard_map/ppermute | solution.py:308
  50.8 0.0 collective-permute-start.11
  50.8 2.1 %collective-permute-done.7.refs_2_ = bf16[16,3200]{1,0:T(8,128)(2,1)S(1)} collective-permute-done((bf16[16,3200]{1,0:T(8,128)(2,1)S(1)}, bf16[16,3200]{1,0:T(8,128)(2,1)S(1)}, u32[]{:S(2)}, u32[]{:S(2)}) %collective-permute-start.7) | collective-permute-done | bytes 102432 | tf_op jit(solution)/shard_map/ppermute | solution.py:308
  52.9 0.0 collective-permute-start.10
  52.9 0.5 collective-permute-done.6.refs_1_
  53.4 0.0 collective-permute-start.9
  53.4 2.2 %collective-permute-done.5.refs_0_ = bf16[16,3200]{1,0:T(8,128)(2,1)S(1)} collective-permute-done((bf16[16,3200]{1,0:T(8,128)(2,1)S(1)}, bf16[16,3200]{1,0:T(8,128)(2,1)S(1)}, u32[]{:S(2)}, u32[]{:S(2)}) %collective-permute-start.5) | collective-permute-done | bytes 102432 | tf_op jit(solution)/shard_map/ppermute | solution.py:308
  55.6 0.0 collective-permute-start.8
  55.6 0.0 collective-permute-done.11.refs_7_
  55.6 0.0 collective-permute-done.10.refs_6_
  55.6 0.0 collective-permute-done.9.refs_5_
  55.6 1.3 %collective-permute-done.8.refs_4_ = bf16[16,3200]{1,0:T(8,128)(2,1)S(1)} collective-permute-done((bf16[16,3200]{1,0:T(8,128)(2,1)S(1)}, bf16[16,3200]{1,0:T(8,128)(2,1)S(1)}, u32[]{:S(2)}, u32[]{:S(2)}) %collective-permute-start.8) | collective-permute-done | bytes 102432 | tf_op jit(solution)/shard_map/ppermute | solution.py:309
  56.9 0.9 %shard_map.93 = bf16[128,3200]{1,0:T(8,128)(2,1)} custom-call(bf16[16,3200]{1,0:T(8,128)(2,1)S(1)} %collective-permute-done.5.refs_0_, bf16[16,3200]{1,0:T(8,128)(2,1)S(1)} %collective-permute-done.6.refs_1_, bf16[16,3200]{1,0:T(8,128)(2,1)S(1)} %collective-permute-done.7.refs_2_, bf16[16,3200]{1,0:T(8,128)(2,1)S(1)} %shard_map.92.refs_3_, ...), custom_call_target="tpu_custom_call" | custom-call | bytes 1638400 | tf_op jit(solution)/shard_map/pallas_call | solution.py:310
Async XLA Ops:
  0.6 8.2 %copy-start.4 = (s32[8]{0:T(128)S(1)}, s32[8]{0:T(128)}, u32[]{:S(2)}) copy-start(s32[8]{0:T(128)} %pieces_ref.5) | copy-start | bytes 100
  0.6 9.8 %collective-permute-start = (bf16[128,256]{1,0:T(8,128)(2,1)}, bf16[128,256]{1,0:T(8,128)(2,1)S(1)}, u32[]{:S(2)}, u32[]{:S(2)}) collective-permute-start(bf16[128,256]{1,0:T(8,128)(2,1)} %param.11), channel_id=1, source_target_pairs={{0,6},{2,4},{4,0},{6,2},{1,7},{3,5},{5,1},{7,3},{8,14},{10,12},{12... | collective-permute-start | bytes 196616 | tf_op jit(solution)/shard_map/ppermute | solution.py:231
  5.7 16.6 %copy-start.5 = (bf16[128,512]{1,0:T(8,128)(2,1)S(1)}, bf16[128,512]{1,0:T(8,128)(2,1)}, u32[]{:S(2)}) copy-start(bf16[128,512]{1,0:T(8,128)(2,1)} %q_ref.1) | copy-start | bytes 393220
  5.7 16.6 %copy-start.6 = (bf16[128,512]{1,0:T(8,128)(2,1)S(1)}, bf16[128,512]{1,0:T(8,128)(2,1)}, u32[]{:S(2)}) copy-start(bf16[128,512]{1,0:T(8,128)(2,1)} %g_ref.1) | copy-start | bytes 393220
  8.8 26.4 %copy-start = (bf16[3200,256]{1,0:T(8,128)(2,1)S(1)}, bf16[3200,256]{1,0:T(8,128)(2,1)}, u32[]{:S(2)}) copy-start(bf16[3200,256]{1,0:T(8,128)(2,1)} %proj_ref.1) | copy-start | bytes 4915204
  8.8 1.0 %copy-start.3 = (bf16[128,256]{1,0:T(8,128)(2,1)S(1)}, bf16[128,256]{1,0:T(8,128)(2,1)}, u32[]{:S(2)}) copy-start(bf16[128,256]{1,0:T(8,128)(2,1)} %get-tuple-element.12.image_ref) | copy-start | bytes 196612
  35.2 11.9 %copy-start.1 = (bf16[16,3200]{1,0:T(8,128)(2,1)S(1)}, bf16[16,3200]{1,0:T(8,128)(2,1)}, u32[]{:S(2)}) copy-start(bf16[16,3200]{1,0:T(8,128)(2,1)} %get-tuple-element.18.own_ref) | copy-start | bytes 307204
  35.2 11.9 %copy-start.2 = (f32[3200]{0:T(1024)S(1)}, f32[3200]{0:T(1024)}, u32[]{:S(2)}) copy-start(f32[3200]{0:T(1024)} %param.8) | copy-start | bytes 38404
  36.5 1.8 %collective-permute-start.1 = (bf16[64,3200]{1,0:T(8,128)(2,1)S(1)}, bf16[64,3200]{1,0:T(8,128)(2,1)S(1)}, u32[]{:S(2)}, u32[]{:S(2)}) collective-permute-start(bf16[64,3200]{1,0:T(8,128)(2,1)S(1)} %get-tuple-element.16), channel_id=1, source_target_pairs={{0,8},{1,9},{8,0},{9,1},{16,24},{17,25},{24,16},{25,17},{2,10},{3,... | collective-permute-start | bytes 1228808 | tf_op jit(solution)/shard_map/ppermute | solution.py:287
  38.4 5.0 %collective-permute-start.2 = (bf16[16,3200]{1,0:T(8,128)(2,1)S(1)}, bf16[16,3200]{1,0:T(8,128)(2,1)S(1)}, u32[]{:S(2)}, u32[]{:S(2)}) collective-permute-start(bf16[16,3200]{1,0:T(8,128)(2,1)S(1)} %get-tuple-element.19), channel_id=1, source_target_pairs={{0,1},{1,0},{8,9},{9,8},{16,17},{17,16},{24,25},{25,24},{2,3},{3,2... | collective-permute-start | bytes 307208 | tf_op jit(solution)/shard_map/ppermute | solution.py:297
  40.0 5.7 %collective-permute-start.3 = (bf16[16,3200]{1,0:T(8,128)(2,1)S(1)}, bf16[16,3200]{1,0:T(8,128)(2,1)S(1)}, u32[]{:S(2)}, u32[]{:S(2)}) collective-permute-start(bf16[16,3200]{1,0:T(8,128)(2,1)S(1)} %get-tuple-element.20), channel_id=1, source_target_pairs={{0,16},{1,17},{8,24},{9,25},{16,0},{17,1},{24,8},{25,9},{2,18},{3,... | collective-permute-start | bytes 307208 | tf_op jit(solution)/shard_map/ppermute | solution.py:297
  41.5 5.6 %collective-permute-start.4 = (bf16[16,3200]{1,0:T(8,128)(2,1)S(1)}, bf16[16,3200]{1,0:T(8,128)(2,1)S(1)}, u32[]{:S(2)}, u32[]{:S(2)}) collective-permute-start(bf16[16,3200]{1,0:T(8,128)(2,1)S(1)} %get-tuple-element.21), channel_id=1, source_target_pairs={{0,17},{1,16},{8,25},{9,24},{16,1},{17,0},{24,9},{25,8},{2,19},{3,... | collective-permute-start | bytes 307208 | tf_op jit(solution)/shard_map/ppermute | solution.py:297
  47.3 5.6 %collective-permute-start.7 = (bf16[16,3200]{1,0:T(8,128)(2,1)S(1)}, bf16[16,3200]{1,0:T(8,128)(2,1)S(1)}, u32[]{:S(2)}, u32[]{:S(2)}) collective-permute-start(bf16[16,3200]{1,0:T(8,128)(2,1)S(1)} %shard_map.92.refs_3_), channel_id=1, source_target_pairs={{0,1},{1,0},{8,9},{9,8},{16,17},{17,16},{24,25},{25,24},{2,3},{3,2... | collective-permute-start | bytes 307208 | tf_op jit(solution)/shard_map/ppermute | solution.py:308
  48.6 4.8 %collective-permute-start.6 = (bf16[16,3200]{1,0:T(8,128)(2,1)S(1)}, bf16[16,3200]{1,0:T(8,128)(2,1)S(1)}, u32[]{:S(2)}, u32[]{:S(2)}) collective-permute-start(bf16[16,3200]{1,0:T(8,128)(2,1)S(1)} %shard_map.92.refs_3_), channel_id=1, source_target_pairs={{0,16},{1,17},{8,24},{9,25},{16,0},{17,1},{24,8},{25,9},{2,18},{3,... | collective-permute-start | bytes 307208 | tf_op jit(solution)/shard_map/ppermute | solution.py:308
  50.1 5.6 %collective-permute-start.5 = (bf16[16,3200]{1,0:T(8,128)(2,1)S(1)}, bf16[16,3200]{1,0:T(8,128)(2,1)S(1)}, u32[]{:S(2)}, u32[]{:S(2)}) collective-permute-start(bf16[16,3200]{1,0:T(8,128)(2,1)S(1)} %shard_map.92.refs_3_), channel_id=1, source_target_pairs={{0,17},{1,16},{8,25},{9,24},{16,1},{17,0},{24,9},{25,8},{2,19},{3,... | collective-permute-start | bytes 307208 | tf_op jit(solution)/shard_map/ppermute | solution.py:308
  50.8 4.8 %collective-permute-start.11 = (bf16[16,3200]{1,0:T(8,128)(2,1)S(1)}, bf16[16,3200]{1,0:T(8,128)(2,1)S(1)}, u32[]{:S(2)}, u32[]{:S(2)}) collective-permute-start(bf16[16,3200]{1,0:T(8,128)(2,1)S(1)} %shard_map.92.refs_3_), channel_id=1, source_target_pairs={{0,8},{1,9},{8,0},{9,1},{16,24},{17,25},{24,16},{25,17},{2,10},{3,... | collective-permute-start | bytes 307208 | tf_op jit(solution)/shard_map/ppermute | solution.py:309
  52.9 2.8 %collective-permute-start.10 = (bf16[16,3200]{1,0:T(8,128)(2,1)S(1)}, bf16[16,3200]{1,0:T(8,128)(2,1)S(1)}, u32[]{:S(2)}, u32[]{:S(2)}) collective-permute-start(bf16[16,3200]{1,0:T(8,128)(2,1)S(1)} %collective-permute-done.7.refs_2_), channel_id=1, source_target_pairs={{0,8},{1,9},{8,0},{9,1},{16,24},{17,25},{24,16},{25,17},{2,10},{3,... | collective-permute-start | bytes 307208 | tf_op jit(solution)/shard_map/ppermute | solution.py:309
  53.4 2.2 %collective-permute-start.9 = (bf16[16,3200]{1,0:T(8,128)(2,1)S(1)}, bf16[16,3200]{1,0:T(8,128)(2,1)S(1)}, u32[]{:S(2)}, u32[]{:S(2)}) collective-permute-start(bf16[16,3200]{1,0:T(8,128)(2,1)S(1)} %collective-permute-done.6.refs_1_), channel_id=1, source_target_pairs={{0,8},{1,9},{8,0},{9,1},{16,24},{17,25},{24,16},{25,17},{2,10},{3,... | collective-permute-start | bytes 307208 | tf_op jit(solution)/shard_map/ppermute | solution.py:309
  55.6 1.3 %collective-permute-start.8 = (bf16[16,3200]{1,0:T(8,128)(2,1)S(1)}, bf16[16,3200]{1,0:T(8,128)(2,1)S(1)}, u32[]{:S(2)}, u32[]{:S(2)}) collective-permute-start(bf16[16,3200]{1,0:T(8,128)(2,1)S(1)} %collective-permute-done.5.refs_0_), channel_id=1, source_target_pairs={{0,8},{1,9},{8,0},{9,1},{16,24},{17,25},{24,16},{25,17},{2,10},{3,... | collective-permute-start | bytes 307208 | tf_op jit(solution)/shard_map/ppermute | solution.py:309

commit v5 on v4

--- a/solution.py
+++ b/solution.py
@@ -15,11 +15,6 @@
 WIDE_LIMIT = 60 * 1024 * 1024
 WHOLE = pl.BlockSpec(memory_space=pltpu.VMEM)
 SCALARS = pl.BlockSpec(memory_space=pltpu.SMEM)
-
-
-def owner_block(image, count):
-    half = count // 2
-    return image - half if image >= half else half + (image + 1) % half
 
 
 def held_image(block, count):
@@ -84,30 +79,26 @@
     own_ref[...] = vis[pl.ds(start, piece), :]
 
 
-def shift_body(seq_n, pieces_ref, image_ref, out_ref):
-    rows = image_ref.shape[0]
-    before = pieces_ref[2 * held_image(lax.axis_index("seq"), seq_n)]
-    to = lax.broadcasted_iota(jnp.int32, (rows, rows), 0)
-    source = lax.broadcasted_iota(jnp.int32, (rows, rows), 1)
-    pick = jnp.where(source == to - before, 1.0, 0.0).astype(jnp.bfloat16)
-    out_ref[...] = jnp.dot(pick, image_ref[...], preferred_element_type=jnp.float32).astype(jnp.bfloat16)
-
-
-def place_body(seq_n, pieces_ref, image_ref, text_ref, out_ref):
-    before = pieces_ref[2 * held_image(lax.axis_index("seq"), seq_n)]
-    row = lax.broadcasted_iota(jnp.int32, image_ref.shape, 0)
-    text, image = text_ref[...].astype(jnp.float32), image_ref[...].astype(jnp.float32)
-    block = jnp.where(row < before, text, image).astype(jnp.bfloat16)
-    for d in range(seq_n):
-        out_ref[d] = block
-
-
-def attend_body(seq_n, owners, q_ref, g_ref, kv_ref, out_ref, grad_ref):
+def attend_body(seq_n, pieces_ref, q_ref, g_ref, *refs):
+    image_refs, text_refs = refs[:seq_n], refs[seq_n : 2 * seq_n]
+    out_ref, grad_refs = refs[2 * seq_n], refs[2 * seq_n + 1 : 3 * seq_n + 1]
+    image, text = refs[3 * seq_n + 1 :]
     rows = q_ref.shape[0]
     group = q_ref.shape[1] // HD
     scale = 1.0 / math.sqrt(HD)
     me = lax.axis_index("seq")
-    kv = jnp.concatenate([kv_ref[b] for b in owners], axis=0)
+    for r in range(seq_n):
+        image[held_image(me ^ r, seq_n)] = image_refs[r][...]
+        text[me ^ r] = text_refs[r][...]
+    ahead = lax.broadcasted_iota(jnp.int32, (rows, rows), 0) - lax.broadcasted_iota(jnp.int32, (rows, rows), 1)
+    row = lax.broadcasted_iota(jnp.int32, image.shape[1:], 0)
+    blocks = []
+    for j in range(seq_n):
+        before = pieces_ref[2 * j]
+        pick = jnp.where(ahead == before, 1.0, 0.0).astype(jnp.bfloat16)
+        placed = jnp.dot(pick, image[j], preferred_element_type=jnp.float32)
+        blocks.append(jnp.where(row < before, text[j].astype(jnp.float32), placed).astype(jnp.bfloat16))
+    kv = jnp.concatenate(blocks, axis=0)
     keys, values = kv[:, :HD], kv[:, HD:]
     together = group if kv.shape[0] <= 1024 else 1
     span = together * rows
@@ -138,19 +129,22 @@
         for n, h in enumerate(heads):
             part = jnp.transpose(mixed[:, n * rows : (n + 1) * rows])
             out_ref[:, h * HD : (h + 1) * HD] = part.astype(jnp.bfloat16)
-    for j, b in enumerate(owners):
-        grad_ref[b, :, :HD] = (key_total[j * rows : (j + 1) * rows] * scale).astype(jnp.bfloat16)
-        grad_ref[b, :, HD:] = value_total[j * rows : (j + 1) * rows].astype(jnp.bfloat16)
-
-
-def back_body(seq_n, piece, pieces_ref, proj_ref, part_ref, keep_ref, send_ref):
-    rows = part_ref.shape[1]
+    for j in range(seq_n):
+        image[j, :, :HD] = (key_total[j * rows : (j + 1) * rows] * scale).astype(jnp.bfloat16)
+        image[j, :, HD:] = value_total[j * rows : (j + 1) * rows].astype(jnp.bfloat16)
+    for r, ref in enumerate(grad_refs):
+        ref[...] = image[held_image(me ^ r, seq_n)]
+
+
+def back_body(seq_n, piece, pieces_ref, proj_ref, *refs):
+    part_refs, (keep_ref, send_ref) = refs[:-2], refs[-2:]
+    rows = part_refs[0].shape[0]
     half = rows // 2
     before = pieces_ref[2 * held_image(lax.axis_index("seq"), seq_n)]
     parity, place = group_place()
-    total = part_ref[0].astype(jnp.float32)
-    for b in range(1, seq_n):
-        total += part_ref[b].astype(jnp.float32)
+    total = part_refs[0][...].astype(jnp.float32)
+    for ref in part_refs[1:]:
+        total += ref[...].astype(jnp.float32)
     slot = lax.broadcasted_iota(jnp.int32, (rows, rows), 0)
     to = (lax.div(slot, half) ^ parity) * half
     to += (lax.div(lax.rem(slot, half), piece) ^ place) * piece + lax.rem(slot, piece)
@@ -215,7 +209,6 @@
     count = n // 2
     piece = rows // n
     bf16, f32 = jnp.bfloat16, jnp.float32
-    owners = [owner_block(j, seq_n) for j in range(seq_n)]
     names = ("sec", "tp")
     core_pairs = [(i, (i // tp_n ^ 1) * tp_n + i % tp_n) for i in range(n)]
 
@@ -228,7 +221,10 @@
         return pairs
 
     gain = vis_gain.reshape(width // HD, HD)
-    text = lax.ppermute(text_kv, "seq", [(j, owners[j]) for j in range(seq_n)])
+    far = sorted(range(1, seq_n), reverse=True)
+    partners = {r: [(d, d ^ r) for d in range(seq_n)] for r in far}
+    text = {r: lax.ppermute(text_kv, "seq", partners[r]) for r in far}
+    text[0] = text_kv
     chunks = len(cuts(width))
     hbm = pl.BlockSpec(memory_space=pltpu.HBM)
     image_kv, own_rows = call(
@@ -248,42 +244,29 @@
             pltpu.SemaphoreType.DMA,
         ],
     )(vis_rows, gain, key_value_proj)
-    shifted = call(
-        functools.partial(shift_body, seq_n),
-        jax.ShapeDtypeStruct((rows, columns), bf16),
-        [SCALARS, WHOLE],
-        WHOLE,
-        2 * rows * rows * columns,
-        4 * rows * columns,
-    )(pieces, image_kv)
-    copies = call(
-        functools.partial(place_body, seq_n),
-        jax.ShapeDtypeStruct((seq_n, rows, columns), bf16),
-        [SCALARS, WHOLE, WHOLE],
-        WHOLE,
-        0,
-        6 * rows * columns,
-    )(pieces, shifted, text)
-
-    blocks = lax.all_to_all(copies, "seq", 0, 0)
-    attended, grads = call(
-        functools.partial(attend_body, seq_n, owners),
-        [jax.ShapeDtypeStruct(queries.shape, bf16), jax.ShapeDtypeStruct(blocks.shape, bf16)],
-        [WHOLE] * 3,
-        [WHOLE, WHOLE],
+    image = {r: lax.ppermute(image_kv, "seq", partners[r]) for r in far}
+    image[0] = image_kv
+    order = range(seq_n)
+    attended, *grads = call(
+        functools.partial(attend_body, seq_n),
+        [jax.ShapeDtypeStruct(queries.shape, bf16)] + [jax.ShapeDtypeStruct((rows, columns), bf16)] * seq_n,
+        [SCALARS] + [WHOLE] * (2 + 2 * seq_n),
+        [WHOLE] * (1 + seq_n),
         10 * seq_n * rows * rows * queries.shape[1],
         6 * rows * queries.shape[1] + 4 * seq_n * rows * columns,
-    )(queries, grad_out, blocks)
-    parts = lax.all_to_all(grads, "seq", 0, 0)
+        scratch_shapes=[pltpu.VMEM((seq_n, rows, columns), bf16)] * 2,
+    )(pieces, queries, grad_out, *[image[r] for r in order], *[text[r] for r in order])
+    parts = {r: lax.ppermute(grads[r], "seq", partners[r]) for r in far}
+    parts[0] = grads[0]
 
     keep, send = call(
         functools.partial(back_body, seq_n, piece),
         [jax.ShapeDtypeStruct((rows // 2, width), f32), jax.ShapeDtypeStruct((rows // 2, width), bf16)],
-        [SCALARS, WHOLE, WHOLE],
+        [SCALARS] + [WHOLE] * (1 + seq_n),
         [WHOLE, WHOLE],
         2 * rows * width * columns,
         2 * width * columns + 3 * rows * width,
-    )(pieces, key_value_proj, parts)
+    )(pieces, key_value_proj, parts[0], *[parts[r] for r in far])
     other = lax.ppermute(send, names, core_pairs)
     steps = list(range(1, count))
     own_sum, *sends = call(

time: 58.1 us -> 53.2 us (0.916)
  blocking collectives: 22.2 us -> 0 us
  starting transfers between devices: 12.3 us -> 21.8 us
  waiting for transfers between devices: 12.9 us -> 21.3 us
    all_to_all x2 -> x0, blocking collectives: 22.2 us -> none  [the longest x1 11.3 us: on_device(): blocks = lax.all_to_all(copies, 'seq', 0, 0)]
    ppermute x1 -> x9, starting transfers between devices: 5.1 us -> 14.6 us  [the longest x3 5.68 us: on_device(): text = {r: lax.ppermute(text_kv, 'seq', partners[r]) for r in far}]
    ppermute x1 -> x9, waiting for transfers between devices: 0.01 us -> 8.48 us  [the longest x3 4.95 us: on_device(): image = {r: lax.ppermute(image_kv, 'seq', partners[r]) for r in far}]
    pallas_call x3 -> x1, Pallas kernels: 3.24 us -> 2.67 us  [on_device(): call(functools.partial(attend_body, seq_n), [jax.ShapeDtypeStruct(queries...]
  transfers between devices with their start and end apart: 12 -> 20, of which waited for: 8 -> 13; matrix products, arithmetic and copies ran while one was open for 0% -> 0% of each run, Pallas kernels for 6% -> 6%
where the time goes in v5:
time: 53.2 us; the launch traced here: 53 us
  starting transfers between devices  21.8 us (41%)
  waiting for transfers between devices  21.3 us (40%)
  Pallas kernels  8.31 us (16%)
  local copies, waits for them, and re-layouts  0.86 us (2%)
  between operations  0.75 us (1%)
    ppermute x3, starting transfers between devices, on_device(): text = {r: lax.ppermute(text_kv, 'seq', partners[r]) for r in far}  5.68 us
    ppermute x3, waiting for transfers between devices, on_device(): shares = [lax.ppermute(sends[d - 1], names, far_pairs(d)) for d in steps]  5.02 us
    ppermute x3, waiting for transfers between devices, on_device(): image = {r: lax.ppermute(image_kv, 'seq', partners[r]) for r in far}  4.95 us
    ppermute x3, waiting for transfers between devices, on_device(): mines[d] = lax.ppermute(mine, names, far_pairs(d))  4.8 us
    ppermute x3, starting transfers between devices, on_device(): image = {r: lax.ppermute(image_kv, 'seq', partners[r]) for r in far}  4.53 us
    ppermute x3, starting transfers between devices, on_device(): parts = {r: lax.ppermute(grads[r], 'seq', partners[r]) for r in far}  4.39 us
    ppermute x3, starting transfers between devices, on_device(): shares = [lax.ppermute(sends[d - 1], names, far_pairs(d)) for d in steps]  3.55 us
    ppermute x3, starting transfers between devices, on_device(): mines[d] = lax.ppermute(mine, names, far_pairs(d))  3.55 us
  transfers between devices with their start and end apart: 20, of which 13 were waited for; matrix products, arithmetic and copies ran while one was open for 0% of the time, Pallas kernels for 6%

profile of v5, /device:TPU:0, one launch (start us, length us, event | category | flops | bytes accessed | tf_op | source)
XLA Modules:
  0.0 53.0 jit_solution(9367516808098775430)
XLA Ops:
  0.6 0.0 copy-start.6
  0.7 4.1 %collective-permute-start.4 = (bf16[128,256]{1,0:T(8,128)(2,1)}, bf16[128,256]{1,0:T(8,128)(2,1)S(1)}, u32[]{:S(2)}, u32[]{:S(2)}) collective-permute-start(bf16[128,256]{1,0:T(8,128)(2,1)} %refs_4_.1), channel_id=1, source_target_pairs={{0,4},{2,6},{4,0},{6,2},{1,5},{3,7},{5,1},{7,3},{8,12},{10,14},{12... | collective-permute-start | bytes 196616 | tf_op jit(solution)/shard_map/ppermute | solution.py:226
  4.8 1.6 %collective-permute-start.3 = (bf16[128,256]{1,0:T(8,128)(2,1)}, bf16[128,256]{1,0:T(8,128)(2,1)S(1)}, u32[]{:S(2)}, u32[]{:S(2)}) collective-permute-start(bf16[128,256]{1,0:T(8,128)(2,1)} %refs_4_.1), channel_id=1, source_target_pairs={{0,2},{2,0},{4,6},{6,4},{1,3},{3,1},{5,7},{7,5},{8,10},{10,8},{12,... | collective-permute-start | bytes 196616 | tf_op jit(solution)/shard_map/ppermute | solution.py:226
  6.3 0.0 collective-permute-start.5
  6.4 3.1 %shard_map.86 = (bf16[128,256]{1,0:T(8,128)(2,1)}, bf16[16,3200]{1,0:T(8,128)(2,1)}) custom-call(bf16[128,3200]{1,0:T(8,128)(2,1)} %vis_hbm.1, f32[25,128]{1,0:T(8,128)} %bitcast.1, bf16[3200,256]{1,0:T(8,128)(2,1)} %proj_ref.1), custom_call_target="tpu_custom_call" | custom-call | flops 209715200 | bytes 2457600 | tf_op jit(solution)/shard_map/pallas_call | solution.py:230
  9.5 3.9 %collective-permute-start.2 = (bf16[128,256]{1,0:T(8,128)(2,1)}, bf16[128,256]{1,0:T(8,128)(2,1)S(1)}, u32[]{:S(2)}, u32[]{:S(2)}) collective-permute-start(bf16[128,256]{1,0:T(8,128)(2,1)} %get-tuple-element.15.refs_0_), channel_id=1, source_target_pairs={{0,6},{2,4},{4,2},{6,0},{1,7},{3,5},{5,3},{7,1},{8,14},{10,12},{12... | collective-permute-start | bytes 196616 | tf_op jit(solution)/shard_map/ppermute | solution.py:247
  13.4 0.0 collective-permute-start.1
  13.4 0.0 collective-permute-done.4.refs_6_
  13.4 0.6 %collective-permute-start = (bf16[128,256]{1,0:T(8,128)(2,1)}, bf16[128,256]{1,0:T(8,128)(2,1)S(1)}, u32[]{:S(2)}, u32[]{:S(2)}) collective-permute-start(bf16[128,256]{1,0:T(8,128)(2,1)} %get-tuple-element.15.refs_0_), channel_id=1, source_target_pairs={{0,2},{2,0},{4,6},{6,4},{1,3},{3,1},{5,7},{7,5},{8,10},{10,8},{12,... | collective-permute-start | bytes 196616 | tf_op jit(solution)/shard_map/ppermute | solution.py:247
  14.0 0.0 collective-permute-done.3.refs_5_
  14.0 0.0 collective-permute-done.5.refs_7_
  14.0 1.9 %collective-permute-done.2.refs_3_ = bf16[128,256]{1,0:T(8,128)(2,1)S(1)} collective-permute-done((bf16[128,256]{1,0:T(8,128)(2,1)}, bf16[128,256]{1,0:T(8,128)(2,1)S(1)}, u32[]{:S(2)}, u32[]{:S(2)}) %collective-permute-start.2) | collective-permute-done | bytes 65568 | tf_op jit(solution)/shard_map/ppermute | solution.py:247
  15.9 2.9 %collective-permute-done.1.refs_2_ = bf16[128,256]{1,0:T(8,128)(2,1)S(1)} collective-permute-done((bf16[128,256]{1,0:T(8,128)(2,1)}, bf16[128,256]{1,0:T(8,128)(2,1)S(1)}, u32[]{:S(2)}, u32[]{:S(2)}) %collective-permute-start.1) | collective-permute-done | bytes 65568 | tf_op jit(solution)/shard_map/ppermute | solution.py:247
  18.8 0.2 collective-permute-done.refs_1_
  19.0 0.8 %copy-done.7 = bf16[128,256]{1,0:T(8,128)(2,1)S(1)} copy-done((bf16[128,256]{1,0:T(8,128)(2,1)S(1)}, bf16[128,256]{1,0:T(8,128)(2,1)}, u32[]{:S(2)}) %copy-start.7) | copy-done | bytes 65560
  19.8 2.7 %shard_map.87 = (bf16[128,512]{1,0:T(8,128)(2,1)}, bf16[128,256]{1,0:T(8,128)(2,1)S(1)}, bf16[128,256]{1,0:T(8,128)(2,1)S(1)}, bf16[128,256]{1,0:T(8,128)(2,1)S(1)}, bf16[128,256]{1,0:T(8,128)(2,1)S(1)}) custom-call(s32[8]{0:T(128)S(1)} %copy-done.3, bf16[128,512]{1,0:T(8,128)(2,1)S(1)} %copy-done.4, bf16[128,512]{1,0:T(8,128)(2,1)S(1)} %copy-done.5, ...), custom_call_target="tpu_custom_call" | custom-call | flops 335544320 | bytes 917504 | tf_op jit(solution)/shard_map/pallas_call | solution.py:250
  22.5 2.1 %collective-permute-start.6 = (bf16[128,256]{1,0:T(8,128)(2,1)S(1)}, bf16[128,256]{1,0:T(8,128)(2,1)S(1)}, u32[]{:S(2)}, u32[]{:S(2)}) collective-permute-start(bf16[128,256]{1,0:T(8,128)(2,1)S(1)} %get-tuple-element.18), channel_id=1, source_target_pairs={{0,6},{2,4},{4,2},{6,0},{1,7},{3,5},{5,3},{7,1},{8,14},{10,12},{12... | collective-permute-start | bytes 196616 | tf_op jit(solution)/shard_map/ppermute | solution.py:259
  24.6 0.0 collective-permute-start.7
  24.6 2.3 %collective-permute-start.8 = (bf16[128,256]{1,0:T(8,128)(2,1)S(1)}, bf16[128,256]{1,0:T(8,128)(2,1)S(1)}, u32[]{:S(2)}, u32[]{:S(2)}) collective-permute-start(bf16[128,256]{1,0:T(8,128)(2,1)S(1)} %get-tuple-element.20), channel_id=1, source_target_pairs={{0,2},{2,0},{4,6},{6,4},{1,3},{3,1},{5,7},{7,5},{8,10},{10,8},{12,... | collective-permute-start | bytes 196616 | tf_op jit(solution)/shard_map/ppermute | solution.py:259
  26.9 1.8 %collective-permute-done.6.refs_1_ = bf16[128,256]{1,0:T(8,128)(2,1)S(1)} collective-permute-done((bf16[128,256]{1,0:T(8,128)(2,1)S(1)}, bf16[128,256]{1,0:T(8,128)(2,1)S(1)}, u32[]{:S(2)}, u32[]{:S(2)}) %collective-permute-start.6) | collective-permute-done | bytes 65568 | tf_op jit(solution)/shard_map/ppermute | solution.py:259
  28.7 1.7 %collective-permute-done.7.refs_2_ = bf16[128,256]{1,0:T(8,128)(2,1)S(1)} collective-permute-done((bf16[128,256]{1,0:T(8,128)(2,1)S(1)}, bf16[128,256]{1,0:T(8,128)(2,1)S(1)}, u32[]{:S(2)}, u32[]{:S(2)}) %collective-permute-start.7) | collective-permute-done | bytes 65568 | tf_op jit(solution)/shard_map/ppermute | solution.py:259
  30.4 0.0 collective-permute-done.8.refs_3_
  30.4 1.3 %shard_map.88 = (f32[64,3200]{1,0:T(8,128)S(1)}, bf16[64,3200]{1,0:T(8,128)(2,1)S(1)}) custom-call(s32[8]{0:T(128)S(1)} %copy-done.3, bf16[3200,256]{1,0:T(8,128)(2,1)S(1)} %copy-done, bf16[128,256]{1,0:T(8,128)(2,1)S(1)} %get-tuple-element.17.refs_0_, bf16[128,256]{1,0:T(8,128)(2,1)S(1)} %collective-permute-done.6.refs_1_, ...), custom_call_target="tpu_custom_call" | custom-call | flops 209715200 | bytes 2867200 | tf_op jit(solution)/shard_map/pallas_call | solution.py:262
  31.7 0.1 collective-permute-start.9
  31.8 1.7 %collective-permute-done.9.other_ref = bf16[64,3200]{1,0:T(8,128)(2,1)S(1)} collective-permute-done((bf16[64,3200]{1,0:T(8,128)(2,1)S(1)}, bf16[64,3200]{1,0:T(8,128)(2,1)S(1)}, u32[]{:S(2)}, u32[]{:S(2)}) %collective-permute-start.9) | collective-permute-done | bytes 409632 | tf_op jit(solution)/shard_map/ppermute | solution.py:270
  33.6 0.1 shard_map.89
  33.6 1.5 %collective-permute-start.10 = (bf16[16,3200]{1,0:T(8,128)(2,1)S(1)}, bf16[16,3200]{1,0:T(8,128)(2,1)S(1)}, u32[]{:S(2)}, u32[]{:S(2)}) collective-permute-start(bf16[16,3200]{1,0:T(8,128)(2,1)S(1)} %get-tuple-element.25), channel_id=1, source_target_pairs={{0,1},{1,0},{8,9},{9,8},{16,17},{17,16},{24,25},{25,24},{2,3},{3,2... | collective-permute-start | bytes 307208 | tf_op jit(solution)/shard_map/ppermute | solution.py:280
  35.2 1.5 %collective-permute-start.11 = (bf16[16,3200]{1,0:T(8,128)(2,1)S(1)}, bf16[16,3200]{1,0:T(8,128)(2,1)S(1)}, u32[]{:S(2)}, u32[]{:S(2)}) collective-permute-start(bf16[16,3200]{1,0:T(8,128)(2,1)S(1)} %get-tuple-element.26), channel_id=1, source_target_pairs={{0,16},{1,17},{8,24},{9,25},{16,0},{17,1},{24,8},{25,9},{2,18},{3,... | collective-permute-start | bytes 307208 | tf_op jit(solution)/shard_map/ppermute | solution.py:280
  36.7 0.5 %collective-permute-start.12 = (bf16[16,3200]{1,0:T(8,128)(2,1)S(1)}, bf16[16,3200]{1,0:T(8,128)(2,1)S(1)}, u32[]{:S(2)}, u32[]{:S(2)}) collective-permute-start(bf16[16,3200]{1,0:T(8,128)(2,1)S(1)} %get-tuple-element.27), channel_id=1, source_target_pairs={{0,17},{1,16},{8,25},{9,24},{16,1},{17,0},{24,9},{25,8},{2,19},{3,... | collective-permute-start | bytes 307208 | tf_op jit(solution)/shard_map/ppermute | solution.py:280
  37.2 1.4 %collective-permute-done.10.refs_0_ = bf16[16,3200]{1,0:T(8,128)(2,1)S(1)} collective-permute-done((bf16[16,3200]{1,0:T(8,128)(2,1)S(1)}, bf16[16,3200]{1,0:T(8,128)(2,1)S(1)}, u32[]{:S(2)}, u32[]{:S(2)}) %collective-permute-start.10) | collective-permute-done | bytes 102432 | tf_op jit(solution)/shard_map/ppermute | solution.py:280
  38.6 2.2 %collective-permute-done.11.refs_1_ = bf16[16,3200]{1,0:T(8,128)(2,1)S(1)} collective-permute-done((bf16[16,3200]{1,0:T(8,128)(2,1)S(1)}, bf16[16,3200]{1,0:T(8,128)(2,1)S(1)}, u32[]{:S(2)}, u32[]{:S(2)}) %collective-permute-start.11) | collective-permute-done | bytes 102432 | tf_op jit(solution)/shard_map/ppermute | solution.py:280
  40.9 1.3 %collective-permute-done.12.refs_2_ = bf16[16,3200]{1,0:T(8,128)(2,1)S(1)} collective-permute-done((bf16[16,3200]{1,0:T(8,128)(2,1)S(1)}, bf16[16,3200]{1,0:T(8,128)(2,1)S(1)}, u32[]{:S(2)}, u32[]{:S(2)}) %collective-permute-start.12) | collective-permute-done | bytes 102432 | tf_op jit(solution)/shard_map/ppermute | solution.py:280
  42.2 0.2 shard_map.90.refs_3_
  42.4 1.3 %collective-permute-start.15 = (bf16[16,3200]{1,0:T(8,128)(2,1)S(1)}, bf16[16,3200]{1,0:T(8,128)(2,1)S(1)}, u32[]{:S(2)}, u32[]{:S(2)}) collective-permute-start(bf16[16,3200]{1,0:T(8,128)(2,1)S(1)} %shard_map.90.refs_3_), channel_id=1, source_target_pairs={{0,1},{1,0},{8,9},{9,8},{16,17},{17,16},{24,25},{25,24},{2,3},{3,2... | collective-permute-start | bytes 307208 | tf_op jit(solution)/shard_map/ppermute | solution.py:291
  43.7 1.5 %collective-permute-start.14 = (bf16[16,3200]{1,0:T(8,128)(2,1)S(1)}, bf16[16,3200]{1,0:T(8,128)(2,1)S(1)}, u32[]{:S(2)}, u32[]{:S(2)}) collective-permute-start(bf16[16,3200]{1,0:T(8,128)(2,1)S(1)} %shard_map.90.refs_3_), channel_id=1, source_target_pairs={{0,16},{1,17},{8,24},{9,25},{16,0},{17,1},{24,8},{25,9},{2,18},{3,... | collective-permute-start | bytes 307208 | tf_op jit(solution)/shard_map/ppermute | solution.py:291
  45.2 0.7 %collective-permute-start.13 = (bf16[16,3200]{1,0:T(8,128)(2,1)S(1)}, bf16[16,3200]{1,0:T(8,128)(2,1)S(1)}, u32[]{:S(2)}, u32[]{:S(2)}) collective-permute-start(bf16[16,3200]{1,0:T(8,128)(2,1)S(1)} %shard_map.90.refs_3_), channel_id=1, source_target_pairs={{0,17},{1,16},{8,25},{9,24},{16,1},{17,0},{24,9},{25,8},{2,19},{3,... | collective-permute-start | bytes 307208 | tf_op jit(solution)/shard_map/ppermute | solution.py:291
  46.0 0.0 collective-permute-start.19
  46.0 2.1 %collective-permute-done.15.refs_2_ = bf16[16,3200]{1,0:T(8,128)(2,1)S(1)} collective-permute-done((bf16[16,3200]{1,0:T(8,128)(2,1)S(1)}, bf16[16,3200]{1,0:T(8,128)(2,1)S(1)}, u32[]{:S(2)}, u32[]{:S(2)}) %collective-permute-start.15) | collective-permute-done | bytes 102432 | tf_op jit(solution)/shard_map/ppermute | solution.py:291
  48.0 0.0 collective-permute-start.18
  48.0 0.5 collective-permute-done.14.refs_1_
  48.6 0.0 collective-permute-start.17
  48.6 2.2 %collective-permute-done.13.refs_0_ = bf16[16,3200]{1,0:T(8,128)(2,1)S(1)} collective-permute-done((bf16[16,3200]{1,0:T(8,128)(2,1)S(1)}, bf16[16,3200]{1,0:T(8,128)(2,1)S(1)}, u32[]{:S(2)}, u32[]{:S(2)}) %collective-permute-start.13) | collective-permute-done | bytes 102432 | tf_op jit(solution)/shard_map/ppermute | solution.py:291
  50.8 0.0 collective-permute-start.16
  50.8 0.0 collective-permute-done.19.refs_7_
  50.8 0.0 collective-permute-done.18.refs_6_
  50.8 0.0 collective-permute-done.17.refs_5_
  50.8 1.3 %collective-permute-done.16.refs_4_ = bf16[16,3200]{1,0:T(8,128)(2,1)S(1)} collective-permute-done((bf16[16,3200]{1,0:T(8,128)(2,1)S(1)}, bf16[16,3200]{1,0:T(8,128)(2,1)S(1)}, u32[]{:S(2)}, u32[]{:S(2)}) %collective-permute-start.16) | collective-permute-done | bytes 102432 | tf_op jit(solution)/shard_map/ppermute | solution.py:292
  52.1 0.9 %shard_map.91 = bf16[128,3200]{1,0:T(8,128)(2,1)} custom-call(bf16[16,3200]{1,0:T(8,128)(2,1)S(1)} %collective-permute-done.13.refs_0_, bf16[16,3200]{1,0:T(8,128)(2,1)S(1)} %collective-permute-done.14.refs_1_, bf16[16,3200]{1,0:T(8,128)(2,1)S(1)} %collective-permute-done.15.refs_2_, bf16[16,3200]{1,0:T(8,128)(2,1)S(1)} %shard_map.90.refs_3_, ...), custom_call_target="tpu_custom_call" | custom-call | bytes 1638400 | tf_op jit(solution)/shard_map/pallas_call | solution.py:293
  (14 shorter events, 0.0 us)
Async XLA Ops:
  0.6 18.3 %copy-start.6 = (bf16[128,256]{1,0:T(8,128)(2,1)S(1)}, bf16[128,256]{1,0:T(8,128)(2,1)}, u32[]{:S(2)}) copy-start(bf16[128,256]{1,0:T(8,128)(2,1)} %refs_4_.1) | copy-start | bytes 196612
  0.6 18.3 %copy-start.3 = (s32[8]{0:T(128)S(1)}, s32[8]{0:T(128)}, u32[]{:S(2)}) copy-start(s32[8]{0:T(128)} %pieces_ref.3) | copy-start | bytes 100
  0.7 18.3 %copy-start.5 = (bf16[128,512]{1,0:T(8,128)(2,1)S(1)}, bf16[128,512]{1,0:T(8,128)(2,1)}, u32[]{:S(2)}) copy-start(bf16[128,512]{1,0:T(8,128)(2,1)} %g_ref.1) | copy-start | bytes 393220
  0.7 18.3 %copy-start.4 = (bf16[128,512]{1,0:T(8,128)(2,1)S(1)}, bf16[128,512]{1,0:T(8,128)(2,1)}, u32[]{:S(2)}) copy-start(bf16[128,512]{1,0:T(8,128)(2,1)} %q_ref.1) | copy-start | bytes 393220
  0.7 12.7 %collective-permute-start.4 = (bf16[128,256]{1,0:T(8,128)(2,1)}, bf16[128,256]{1,0:T(8,128)(2,1)S(1)}, u32[]{:S(2)}, u32[]{:S(2)}) collective-permute-start(bf16[128,256]{1,0:T(8,128)(2,1)} %refs_4_.1), channel_id=1, source_target_pairs={{0,4},{2,6},{4,0},{6,2},{1,5},{3,7},{5,1},{7,3},{8,12},{10,14},{12... | collective-permute-start | bytes 196616 | tf_op jit(solution)/shard_map/ppermute | solution.py:226
  4.8 9.2 %collective-permute-start.3 = (bf16[128,256]{1,0:T(8,128)(2,1)}, bf16[128,256]{1,0:T(8,128)(2,1)S(1)}, u32[]{:S(2)}, u32[]{:S(2)}) collective-permute-start(bf16[128,256]{1,0:T(8,128)(2,1)} %refs_4_.1), channel_id=1, source_target_pairs={{0,2},{2,0},{4,6},{6,4},{1,3},{3,1},{5,7},{7,5},{8,10},{10,8},{12,... | collective-permute-start | bytes 196616 | tf_op jit(solution)/shard_map/ppermute | solution.py:226
  6.3 7.7 %collective-permute-start.5 = (bf16[128,256]{1,0:T(8,128)(2,1)}, bf16[128,256]{1,0:T(8,128)(2,1)S(1)}, u32[]{:S(2)}, u32[]{:S(2)}) collective-permute-start(bf16[128,256]{1,0:T(8,128)(2,1)} %refs_4_.1), channel_id=1, source_target_pairs={{0,6},{2,4},{4,2},{6,0},{1,7},{3,5},{5,3},{7,1},{8,14},{10,12},{12... | collective-permute-start | bytes 196616 | tf_op jit(solution)/shard_map/ppermute | solution.py:226
  6.4 24.1 %copy-start = (bf16[3200,256]{1,0:T(8,128)(2,1)S(1)}, bf16[3200,256]{1,0:T(8,128)(2,1)}, u32[]{:S(2)}) copy-start(bf16[3200,256]{1,0:T(8,128)(2,1)} %proj_ref.1) | copy-start | bytes 4915204
  9.5 6.4 %collective-permute-start.2 = (bf16[128,256]{1,0:T(8,128)(2,1)}, bf16[128,256]{1,0:T(8,128)(2,1)S(1)}, u32[]{:S(2)}, u32[]{:S(2)}) collective-permute-start(bf16[128,256]{1,0:T(8,128)(2,1)} %get-tuple-element.15.refs_0_), channel_id=1, source_target_pairs={{0,6},{2,4},{4,2},{6,0},{1,7},{3,5},{5,3},{7,1},{8,14},{10,12},{12... | collective-permute-start | bytes 196616 | tf_op jit(solution)/shard_map/ppermute | solution.py:247
  13.4 5.4 %collective-permute-start.1 = (bf16[128,256]{1,0:T(8,128)(2,1)}, bf16[128,256]{1,0:T(8,128)(2,1)S(1)}, u32[]{:S(2)}, u32[]{:S(2)}) collective-permute-start(bf16[128,256]{1,0:T(8,128)(2,1)} %get-tuple-element.15.refs_0_), channel_id=1, source_target_pairs={{0,4},{2,6},{4,0},{6,2},{1,5},{3,7},{5,1},{7,3},{8,12},{10,14},{12... | collective-permute-start | bytes 196616 | tf_op jit(solution)/shard_map/ppermute | solution.py:247
  13.4 5.6 %collective-permute-start = (bf16[128,256]{1,0:T(8,128)(2,1)}, bf16[128,256]{1,0:T(8,128)(2,1)S(1)}, u32[]{:S(2)}, u32[]{:S(2)}) collective-permute-start(bf16[128,256]{1,0:T(8,128)(2,1)} %get-tuple-element.15.refs_0_), channel_id=1, source_target_pairs={{0,2},{2,0},{4,6},{6,4},{1,3},{3,1},{5,7},{7,5},{8,10},{10,8},{12,... | collective-permute-start | bytes 196616 | tf_op jit(solution)/shard_map/ppermute | solution.py:247
  19.0 0.8 %copy-start.7 = (bf16[128,256]{1,0:T(8,128)(2,1)S(1)}, bf16[128,256]{1,0:T(8,128)(2,1)}, u32[]{:S(2)}) copy-start(bf16[128,256]{1,0:T(8,128)(2,1)} %get-tuple-element.15.refs_0_) | copy-start | bytes 196612
  22.5 19.7 %copy-start.1 = (bf16[16,3200]{1,0:T(8,128)(2,1)S(1)}, bf16[16,3200]{1,0:T(8,128)(2,1)}, u32[]{:S(2)}) copy-start(bf16[16,3200]{1,0:T(8,128)(2,1)} %get-tuple-element.24.own_ref) | copy-start | bytes 307204
  22.5 19.7 %copy-start.2 = (f32[3200]{0:T(1024)S(1)}, f32[3200]{0:T(1024)}, u32[]{:S(2)}) copy-start(f32[3200]{0:T(1024)} %param.8) | copy-start | bytes 38404
  22.5 6.2 %collective-permute-start.6 = (bf16[128,256]{1,0:T(8,128)(2,1)S(1)}, bf16[128,256]{1,0:T(8,128)(2,1)S(1)}, u32[]{:S(2)}, u32[]{:S(2)}) collective-permute-start(bf16[128,256]{1,0:T(8,128)(2,1)S(1)} %get-tuple-element.18), channel_id=1, source_target_pairs={{0,6},{2,4},{4,2},{6,0},{1,7},{3,5},{5,3},{7,1},{8,14},{10,12},{12... | collective-permute-start | bytes 196616 | tf_op jit(solution)/shard_map/ppermute | solution.py:259
  24.6 5.8 %collective-permute-start.7 = (bf16[128,256]{1,0:T(8,128)(2,1)S(1)}, bf16[128,256]{1,0:T(8,128)(2,1)S(1)}, u32[]{:S(2)}, u32[]{:S(2)}) collective-permute-start(bf16[128,256]{1,0:T(8,128)(2,1)S(1)} %get-tuple-element.19), channel_id=1, source_target_pairs={{0,4},{2,6},{4,0},{6,2},{1,5},{3,7},{5,1},{7,3},{8,12},{10,14},{12... | collective-permute-start | bytes 196616 | tf_op jit(solution)/shard_map/ppermute | solution.py:259
  24.6 5.8 %collective-permute-start.8 = (bf16[128,256]{1,0:T(8,128)(2,1)S(1)}, bf16[128,256]{1,0:T(8,128)(2,1)S(1)}, u32[]{:S(2)}, u32[]{:S(2)}) collective-permute-start(bf16[128,256]{1,0:T(8,128)(2,1)S(1)} %get-tuple-element.20), channel_id=1, source_target_pairs={{0,2},{2,0},{4,6},{6,4},{1,3},{3,1},{5,7},{7,5},{8,10},{10,8},{12,... | collective-permute-start | bytes 196616 | tf_op jit(solution)/shard_map/ppermute | solution.py:259
  31.7 1.8 %collective-permute-start.9 = (bf16[64,3200]{1,0:T(8,128)(2,1)S(1)}, bf16[64,3200]{1,0:T(8,128)(2,1)S(1)}, u32[]{:S(2)}, u32[]{:S(2)}) collective-permute-start(bf16[64,3200]{1,0:T(8,128)(2,1)S(1)} %get-tuple-element.22), channel_id=1, source_target_pairs={{0,8},{1,9},{8,0},{9,1},{16,24},{17,25},{24,16},{25,17},{2,10},{3,... | collective-permute-start | bytes 1228808 | tf_op jit(solution)/shard_map/ppermute | solution.py:270
  33.6 5.0 %collective-permute-start.10 = (bf16[16,3200]{1,0:T(8,128)(2,1)S(1)}, bf16[16,3200]{1,0:T(8,128)(2,1)S(1)}, u32[]{:S(2)}, u32[]{:S(2)}) collective-permute-start(bf16[16,3200]{1,0:T(8,128)(2,1)S(1)} %get-tuple-element.25), channel_id=1, source_target_pairs={{0,1},{1,0},{8,9},{9,8},{16,17},{17,16},{24,25},{25,24},{2,3},{3,2... | collective-permute-start | bytes 307208 | tf_op jit(solution)/shard_map/ppermute | solution.py:280
  35.2 5.7 %collective-permute-start.11 = (bf16[16,3200]{1,0:T(8,128)(2,1)S(1)}, bf16[16,3200]{1,0:T(8,128)(2,1)S(1)}, u32[]{:S(2)}, u32[]{:S(2)}) collective-permute-start(bf16[16,3200]{1,0:T(8,128)(2,1)S(1)} %get-tuple-element.26), channel_id=1, source_target_pairs={{0,16},{1,17},{8,24},{9,25},{16,0},{17,1},{24,8},{25,9},{2,18},{3,... | collective-permute-start | bytes 307208 | tf_op jit(solution)/shard_map/ppermute | solution.py:280
  36.7 5.6 %collective-permute-start.12 = (bf16[16,3200]{1,0:T(8,128)(2,1)S(1)}, bf16[16,3200]{1,0:T(8,128)(2,1)S(1)}, u32[]{:S(2)}, u32[]{:S(2)}) collective-permute-start(bf16[16,3200]{1,0:T(8,128)(2,1)S(1)} %get-tuple-element.27), channel_id=1, source_target_pairs={{0,17},{1,16},{8,25},{9,24},{16,1},{17,0},{24,9},{25,8},{2,19},{3,... | collective-permute-start | bytes 307208 | tf_op jit(solution)/shard_map/ppermute | solution.py:280
  42.4 5.6 %collective-permute-start.15 = (bf16[16,3200]{1,0:T(8,128)(2,1)S(1)}, bf16[16,3200]{1,0:T(8,128)(2,1)S(1)}, u32[]{:S(2)}, u32[]{:S(2)}) collective-permute-start(bf16[16,3200]{1,0:T(8,128)(2,1)S(1)} %shard_map.90.refs_3_), channel_id=1, source_target_pairs={{0,1},{1,0},{8,9},{9,8},{16,17},{17,16},{24,25},{25,24},{2,3},{3,2... | collective-permute-start | bytes 307208 | tf_op jit(solution)/shard_map/ppermute | solution.py:291
  43.7 4.8 %collective-permute-start.14 = (bf16[16,3200]{1,0:T(8,128)(2,1)S(1)}, bf16[16,3200]{1,0:T(8,128)(2,1)S(1)}, u32[]{:S(2)}, u32[]{:S(2)}) collective-permute-start(bf16[16,3200]{1,0:T(8,128)(2,1)S(1)} %shard_map.90.refs_3_), channel_id=1, source_target_pairs={{0,16},{1,17},{8,24},{9,25},{16,0},{17,1},{24,8},{25,9},{2,18},{3,... | collective-permute-start | bytes 307208 | tf_op jit(solution)/shard_map/ppermute | solution.py:291
  45.2 5.6 %collective-permute-start.13 = (bf16[16,3200]{1,0:T(8,128)(2,1)S(1)}, bf16[16,3200]{1,0:T(8,128)(2,1)S(1)}, u32[]{:S(2)}, u32[]{:S(2)}) collective-permute-start(bf16[16,3200]{1,0:T(8,128)(2,1)S(1)} %shard_map.90.refs_3_), channel_id=1, source_target_pairs={{0,17},{1,16},{8,25},{9,24},{16,1},{17,0},{24,9},{25,8},{2,19},{3,... | collective-permute-start | bytes 307208 | tf_op jit(solution)/shard_map/ppermute | solution.py:291
  46.0 4.8 %collective-permute-start.19 = (bf16[16,3200]{1,0:T(8,128)(2,1)S(1)}, bf16[16,3200]{1,0:T(8,128)(2,1)S(1)}, u32[]{:S(2)}, u32[]{:S(2)}) collective-permute-start(bf16[16,3200]{1,0:T(8,128)(2,1)S(1)} %shard_map.90.refs_3_), channel_id=1, source_target_pairs={{0,8},{1,9},{8,0},{9,1},{16,24},{17,25},{24,16},{25,17},{2,10},{3,... | collective-permute-start | bytes 307208 | tf_op jit(solution)/shard_map/ppermute | solution.py:292
  48.0 2.8 %collective-permute-start.18 = (bf16[16,3200]{1,0:T(8,128)(2,1)S(1)}, bf16[16,3200]{1,0:T(8,128)(2,1)S(1)}, u32[]{:S(2)}, u32[]{:S(2)}) collective-permute-start(bf16[16,3200]{1,0:T(8,128)(2,1)S(1)} %collective-permute-done.15.refs_2_), channel_id=1, source_target_pairs={{0,8},{1,9},{8,0},{9,1},{16,24},{17,25},{24,16},{25,17},{2,10},{3,... | collective-permute-start | bytes 307208 | tf_op jit(solution)/shard_map/ppermute | solution.py:292
  48.6 2.2 %collective-permute-start.17 = (bf16[16,3200]{1,0:T(8,128)(2,1)S(1)}, bf16[16,3200]{1,0:T(8,128)(2,1)S(1)}, u32[]{:S(2)}, u32[]{:S(2)}) collective-permute-start(bf16[16,3200]{1,0:T(8,128)(2,1)S(1)} %collective-permute-done.14.refs_1_), channel_id=1, source_target_pairs={{0,8},{1,9},{8,0},{9,1},{16,24},{17,25},{24,16},{25,17},{2,10},{3,... | collective-permute-start | bytes 307208 | tf_op jit(solution)/shard_map/ppermute | solution.py:292
  50.8 1.3 %collective-permute-start.16 = (bf16[16,3200]{1,0:T(8,128)(2,1)S(1)}, bf16[16,3200]{1,0:T(8,128)(2,1)S(1)}, u32[]{:S(2)}, u32[]{:S(2)}) collective-permute-start(bf16[16,3200]{1,0:T(8,128)(2,1)S(1)} %collective-permute-done.13.refs_0_), channel_id=1, source_target_pairs={{0,8},{1,9},{8,0},{9,1},{16,24},{17,25},{24,16},{25,17},{2,10},{3,... | collective-permute-start | bytes 307208 | tf_op jit(solution)/shard_map/ppermute | solution.py:292

commit v6 on v4

--- a/solution.py
+++ b/solution.py
@@ -12,7 +12,7 @@
 EPS = 1e-06
 NEG = -1e30
 VMEM_LIMIT = 48 * 1024 * 1024
-WIDE_LIMIT = 60 * 1024 * 1024
+WIDE_LIMIT = 854 * 64 * 1024
 WHOLE = pl.BlockSpec(memory_space=pltpu.VMEM)
 SCALARS = pl.BlockSpec(memory_space=pltpu.SMEM)
 
@@ -97,23 +97,22 @@
     before = pieces_ref[2 * held_image(lax.axis_index("seq"), seq_n)]
     row = lax.broadcasted_iota(jnp.int32, image_ref.shape, 0)
     text, image = text_ref[...].astype(jnp.float32), image_ref[...].astype(jnp.float32)
-    block = jnp.where(row < before, text, image).astype(jnp.bfloat16)
-    for d in range(seq_n):
-        out_ref[d] = block
-
-
-def attend_body(seq_n, owners, q_ref, g_ref, kv_ref, out_ref, grad_ref):
+    out_ref[...] = jnp.where(row < before, text, image).astype(jnp.bfloat16)
+
+
+def attend_body(seq_n, q_ref, g_ref, *refs):
+    block_refs, out_ref, grad_refs = refs[:seq_n], refs[seq_n], refs[seq_n + 1 :]
     rows = q_ref.shape[0]
     group = q_ref.shape[1] // HD
     scale = 1.0 / math.sqrt(HD)
     me = lax.axis_index("seq")
-    kv = jnp.concatenate([kv_ref[b] for b in owners], axis=0)
+    kv = jnp.concatenate([ref[...] for ref in block_refs], axis=0)
     keys, values = kv[:, :HD], kv[:, HD:]
     together = group if kv.shape[0] <= 1024 else 1
     span = together * rows
     offset = lax.broadcasted_iota(jnp.int32, (rows, span), 0)
     offset = offset - lax.rem(lax.broadcasted_iota(jnp.int32, (rows, span), 1), rows)
-    masks = [offset <= (me - j) * rows for j in range(seq_n)]
+    masks = [offset <= (me - held_image(me ^ r, seq_n)) * rows for r in range(seq_n)]
     key_total = value_total = None
     for first in range(0, group, together):
         heads = range(first, first + together)
@@ -138,19 +137,20 @@
         for n, h in enumerate(heads):
             part = jnp.transpose(mixed[:, n * rows : (n + 1) * rows])
             out_ref[:, h * HD : (h + 1) * HD] = part.astype(jnp.bfloat16)
-    for j, b in enumerate(owners):
-        grad_ref[b, :, :HD] = (key_total[j * rows : (j + 1) * rows] * scale).astype(jnp.bfloat16)
-        grad_ref[b, :, HD:] = value_total[j * rows : (j + 1) * rows].astype(jnp.bfloat16)
-
-
-def back_body(seq_n, piece, pieces_ref, proj_ref, part_ref, keep_ref, send_ref):
-    rows = part_ref.shape[1]
+    for r, ref in enumerate(grad_refs):
+        ref[:, :HD] = (key_total[r * rows : (r + 1) * rows] * scale).astype(jnp.bfloat16)
+        ref[:, HD:] = value_total[r * rows : (r + 1) * rows].astype(jnp.bfloat16)
+
+
+def back_body(seq_n, piece, pieces_ref, proj_ref, *refs):
+    part_refs, (keep_ref, send_ref) = refs[:-2], refs[-2:]
+    rows = part_refs[0].shape[0]
     half = rows // 2
     before = pieces_ref[2 * held_image(lax.axis_index("seq"), seq_n)]
     parity, place = group_place()
-    total = part_ref[0].astype(jnp.float32)
-    for b in range(1, seq_n):
-        total += part_ref[b].astype(jnp.float32)
+    total = part_refs[0][...].astype(jnp.float32)
+    for ref in part_refs[1:]:
+        total += ref[...].astype(jnp.float32)
     slot = lax.broadcasted_iota(jnp.int32, (rows, rows), 0)
     to = (lax.div(slot, half) ^ parity) * half
     to += (lax.div(lax.rem(slot, half), piece) ^ place) * piece + lax.rem(slot, piece)
@@ -215,7 +215,6 @@
     count = n // 2
     piece = rows // n
     bf16, f32 = jnp.bfloat16, jnp.float32
-    owners = [owner_block(j, seq_n) for j in range(seq_n)]
     names = ("sec", "tp")
     core_pairs = [(i, (i // tp_n ^ 1) * tp_n + i % tp_n) for i in range(n)]
 
@@ -228,7 +227,9 @@
         return pairs
 
     gain = vis_gain.reshape(width // HD, HD)
-    text = lax.ppermute(text_kv, "seq", [(j, owners[j]) for j in range(seq_n)])
+    far = sorted(range(1, seq_n), reverse=True)
+    partners = {r: [(d, d ^ r) for d in range(seq_n)] for r in far}
+    text = lax.ppermute(text_kv, "seq", [(j, owner_block(j, seq_n)) for j in range(seq_n)])
     chunks = len(cuts(width))
     hbm = pl.BlockSpec(memory_space=pltpu.HBM)
     image_kv, own_rows = call(
@@ -256,34 +257,34 @@
         2 * rows * rows * columns,
         4 * rows * columns,
     )(pieces, image_kv)
-    copies = call(
+    block = call(
         functools.partial(place_body, seq_n),
-        jax.ShapeDtypeStruct((seq_n, rows, columns), bf16),
+        jax.ShapeDtypeStruct((rows, columns), bf16),
         [SCALARS, WHOLE, WHOLE],
         WHOLE,
         0,
         6 * rows * columns,
     )(pieces, shifted, text)
-
-    blocks = lax.all_to_all(copies, "seq", 0, 0)
-    attended, grads = call(
-        functools.partial(attend_body, seq_n, owners),
-        [jax.ShapeDtypeStruct(queries.shape, bf16), jax.ShapeDtypeStruct(blocks.shape, bf16)],
-        [WHOLE] * 3,
-        [WHOLE, WHOLE],
+    blocks = {r: lax.ppermute(block, "seq", partners[r]) for r in far}
+    attended, *grads = call(
+        functools.partial(attend_body, seq_n),
+        [jax.ShapeDtypeStruct(queries.shape, bf16)] + [jax.ShapeDtypeStruct((rows, columns), bf16)] * seq_n,
+        [WHOLE] * (2 + seq_n),
+        [WHOLE] * (1 + seq_n),
         10 * seq_n * rows * rows * queries.shape[1],
         6 * rows * queries.shape[1] + 4 * seq_n * rows * columns,
-    )(queries, grad_out, blocks)
-    parts = lax.all_to_all(grads, "seq", 0, 0)
+    )(queries, grad_out, block, *[blocks[r] for r in range(1, seq_n)])
+    parts = {r: lax.ppermute(grads[r], "seq", partners[r]) for r in far}
+    parts[0] = grads[0]
 
     keep, send = call(
         functools.partial(back_body, seq_n, piece),
         [jax.ShapeDtypeStruct((rows // 2, width), f32), jax.ShapeDtypeStruct((rows // 2, width), bf16)],
-        [SCALARS, WHOLE, WHOLE],
+        [SCALARS] + [WHOLE] * (1 + seq_n),
         [WHOLE, WHOLE],
         2 * rows * width * columns,
         2 * width * columns + 3 * rows * width,
-    )(pieces, key_value_proj, parts)
+    )(pieces, key_value_proj, parts[0], *[parts[r] for r in far])
     other = lax.ppermute(send, names, core_pairs)
     steps = list(range(1, count))
     own_sum, *sends = call(

time: 58.1 us -> 50.7 us (0.87)
  blocking collectives: 22.2 us -> 0 us
  starting transfers between devices: 12.3 us -> 21.1 us
  waiting for transfers between devices: 12.9 us -> 19.8 us
  Pallas kernels: 8.8 us -> 8.12 us
    all_to_all x2 -> x0, blocking collectives: 22.2 us -> none  [the longest x1 11.3 us: on_device(): blocks = lax.all_to_all(copies, 'seq', 0, 0)]
    ppermute x1 -> x7, starting transfers between devices: 5.1 us -> 13.9 us  [the longest x1 5.1 us: on_device(): lax.ppermute(text_kv, 'seq', [(j, owner_block(j, seq_n)) for j in range(s...]
    ppermute x1 -> x7, waiting for transfers between devices: 0.01 us -> 6.86 us  [the longest x3 3.77 us: on_device(): blocks = {r: lax.ppermute(block, 'seq', partners[r]) for r in far}]
    pallas_call x1, Pallas kernels: 3.04 us -> 2.37 us  [on_device(): call(functools.partial(project_body, piece), [jax.ShapeDtypeStruct((rows,...]
  transfers between devices with their start and end apart: 12 -> 18, of which waited for: 8 -> 12; matrix products, arithmetic and copies ran while one was open for 0% -> 0% of each run, Pallas kernels for 6% -> 6%
where the time goes in v6:
time: 50.7 us; the launch traced here: 50.5 us
  starting transfers between devices  21.1 us (42%)
  waiting for transfers between devices  19.8 us (39%)
  Pallas kernels  8.12 us (16%)
  local copies, waits for them, and re-layouts  0.73 us (1%)
  between operations  0.73 us (1%)
    ppermute x1, starting transfers between devices, on_device(): lax.ppermute(text_kv, 'seq', [(j, owner_block(j, seq_n)) for j in range(s...  5.1 us
    ppermute x3, waiting for transfers between devices, on_device(): shares = [lax.ppermute(sends[d - 1], names, far_pairs(d)) for d in steps]  5.08 us
    ppermute x3, waiting for transfers between devices, on_device(): mines[d] = lax.ppermute(mine, names, far_pairs(d))  4.8 us
    ppermute x3, starting transfers between devices, on_device(): blocks = {r: lax.ppermute(block, 'seq', partners[r]) for r in far}  4.45 us
    ppermute x3, starting transfers between devices, on_device(): parts = {r: lax.ppermute(grads[r], 'seq', partners[r]) for r in far}  4.39 us
    ppermute x3, waiting for transfers between devices, on_device(): blocks = {r: lax.ppermute(block, 'seq', partners[r]) for r in far}  3.77 us
    ppermute x3, starting transfers between devices, on_device(): shares = [lax.ppermute(sends[d - 1], names, far_pairs(d)) for d in steps]  3.55 us
    ppermute x3, starting transfers between devices, on_device(): mines[d] = lax.ppermute(mine, names, far_pairs(d))  3.55 us
  transfers between devices with their start and end apart: 18, of which 12 were waited for; matrix products, arithmetic and copies ran while one was open for 0% of the time, Pallas kernels for 6%

profile of v6, /device:TPU:0, one launch (start us, length us, event | category | flops | bytes accessed | tf_op | source)
XLA Modules:
  0.0 50.5 jit_solution(12480649426129888466)
XLA Ops:
  0.6 0.0 copy-start.2
  0.6 5.1 %collective-permute-start = (bf16[128,256]{1,0:T(8,128)(2,1)}, bf16[128,256]{1,0:T(8,128)(2,1)S(1)}, u32[]{:S(2)}, u32[]{:S(2)}) collective-permute-start(bf16[128,256]{1,0:T(8,128)(2,1)} %param.11), channel_id=1, source_target_pairs={{0,6},{2,4},{4,0},{6,2},{1,7},{3,5},{5,1},{7,3},{8,14},{10,12},{12... | collective-permute-start | bytes 196616 | tf_op jit(solution)/shard_map/ppermute | solution.py:232
  5.7 0.7 %copy-done.1 = f32[3200]{0:T(1024)S(1)} copy-done((f32[3200]{0:T(1024)S(1)}, f32[3200]{0:T(1024)}, u32[]{:S(2)}) %copy-start.1) | copy-done | bytes 12824
  6.5 2.4 %shard_map.86 = (bf16[128,256]{1,0:T(8,128)(2,1)S(1)}, bf16[16,3200]{1,0:T(8,128)(2,1)S(1)}) custom-call(bf16[128,3200]{1,0:T(8,128)(2,1)} %vis_hbm.1, f32[25,128]{1,0:T(8,128)S(1)} %bitcast.1, bf16[3200,256]{1,0:T(8,128)(2,1)} %proj_ref.1), custom_call_target="tpu_custom_call" | custom-call | flops 209715200 | bytes 2457600 | tf_op jit(solution)/shard_map/pallas_call | solution.py:235
  8.8 0.0 copy-done.2
  8.9 0.7 %shard_map.87.image_ref = bf16[128,256]{1,0:T(8,128)(2,1)S(1)} custom-call(s32[8]{0:T(128)S(1)} %copy-done.2, bf16[128,256]{1,0:T(8,128)(2,1)S(1)} %get-tuple-element.15.image_ref), custom_call_target="tpu_custom_call" | custom-call | flops 8388608 | bytes 131072 | tf_op jit(solution)/shard_map/pallas_call | solution.py:252
  9.5 0.0 collective-permute-done.text_ref
  9.6 0.6 %shard_map.88.refs_0_ = bf16[128,256]{1,0:T(8,128)(2,1)S(1)} custom-call(s32[8]{0:T(128)S(1)} %copy-done.2, bf16[128,256]{1,0:T(8,128)(2,1)S(1)} %shard_map.87.image_ref, bf16[128,256]{1,0:T(8,128)(2,1)S(1)} %collective-permute-done.text_ref), custom_call_target="tpu_custom_call" | custom-call | bytes 196608 | tf_op jit(solution)/shard_map/pallas_call | solution.py:260
  10.1 2.5 %collective-permute-start.3 = (bf16[128,256]{1,0:T(8,128)(2,1)S(1)}, bf16[128,256]{1,0:T(8,128)(2,1)S(1)}, u32[]{:S(2)}, u32[]{:S(2)}) collective-permute-start(bf16[128,256]{1,0:T(8,128)(2,1)S(1)} %shard_map.88.refs_0_), channel_id=1, source_target_pairs={{0,6},{2,4},{4,2},{6,0},{1,7},{3,5},{5,3},{7,1},{8,14},{10,12},{12... | collective-permute-start | bytes 196616 | tf_op jit(solution)/shard_map/ppermute | solution.py:268
  12.7 0.0 collective-permute-start.2
  12.7 1.9 %collective-permute-start.1 = (bf16[128,256]{1,0:T(8,128)(2,1)S(1)}, bf16[128,256]{1,0:T(8,128)(2,1)S(1)}, u32[]{:S(2)}, u32[]{:S(2)}) collective-permute-start(bf16[128,256]{1,0:T(8,128)(2,1)S(1)} %shard_map.88.refs_0_), channel_id=1, source_target_pairs={{0,2},{2,0},{4,6},{6,4},{1,3},{3,1},{5,7},{7,5},{8,10},{10,8},{12,... | collective-permute-start | bytes 196616 | tf_op jit(solution)/shard_map/ppermute | solution.py:268
  14.6 2.3 %collective-permute-done.3.refs_3_ = bf16[128,256]{1,0:T(8,128)(2,1)S(1)} collective-permute-done((bf16[128,256]{1,0:T(8,128)(2,1)S(1)}, bf16[128,256]{1,0:T(8,128)(2,1)S(1)}, u32[]{:S(2)}, u32[]{:S(2)}) %collective-permute-start.3) | collective-permute-done | bytes 65568 | tf_op jit(solution)/shard_map/ppermute | solution.py:268
  16.8 1.5 %collective-permute-done.2.refs_2_ = bf16[128,256]{1,0:T(8,128)(2,1)S(1)} collective-permute-done((bf16[128,256]{1,0:T(8,128)(2,1)S(1)}, bf16[128,256]{1,0:T(8,128)(2,1)S(1)}, u32[]{:S(2)}, u32[]{:S(2)}) %collective-permute-start.2) | collective-permute-done | bytes 65568 | tf_op jit(solution)/shard_map/ppermute | solution.py:268
  18.4 0.0 collective-permute-done.1.refs_1_
  18.4 0.0 copy-done.4
  18.4 2.0 %shard_map.89 = (bf16[128,512]{1,0:T(8,128)(2,1)}, bf16[128,256]{1,0:T(8,128)(2,1)S(1)}, bf16[128,256]{1,0:T(8,128)(2,1)S(1)}, bf16[128,256]{1,0:T(8,128)(2,1)S(1)}, bf16[128,256]{1,0:T(8,128)(2,1)S(1)}) custom-call(bf16[128,512]{1,0:T(8,128)(2,1)S(1)} %copy-done.3, bf16[128,512]{1,0:T(8,128)(2,1)S(1)} %copy-done.4, bf16[128,256]{1,0:T(8,128)(2,1)S(1)} %shard_map.88.refs_0_, ...), custom_call_target="tpu_custom_call" | custom-call | flops 335544320 | bytes 917504 | tf_op jit(solution)/shard_map/pallas_call | solution.py:269
  20.3 2.0 %collective-permute-start.4 = (bf16[128,256]{1,0:T(8,128)(2,1)S(1)}, bf16[128,256]{1,0:T(8,128)(2,1)S(1)}, u32[]{:S(2)}, u32[]{:S(2)}) collective-permute-start(bf16[128,256]{1,0:T(8,128)(2,1)S(1)} %get-tuple-element.18), channel_id=1, source_target_pairs={{0,6},{2,4},{4,2},{6,0},{1,7},{3,5},{5,3},{7,1},{8,14},{10,12},{12... | collective-permute-start | bytes 196616 | tf_op jit(solution)/shard_map/ppermute | solution.py:277
  22.3 0.1 collective-permute-start.5
  22.4 2.3 %collective-permute-start.6 = (bf16[128,256]{1,0:T(8,128)(2,1)S(1)}, bf16[128,256]{1,0:T(8,128)(2,1)S(1)}, u32[]{:S(2)}, u32[]{:S(2)}) collective-permute-start(bf16[128,256]{1,0:T(8,128)(2,1)S(1)} %get-tuple-element.20), channel_id=1, source_target_pairs={{0,2},{2,0},{4,6},{6,4},{1,3},{3,1},{5,7},{7,5},{8,10},{10,8},{12,... | collective-permute-start | bytes 196616 | tf_op jit(solution)/shard_map/ppermute | solution.py:277
  24.7 1.7 %collective-permute-done.4.refs_1_ = bf16[128,256]{1,0:T(8,128)(2,1)S(1)} collective-permute-done((bf16[128,256]{1,0:T(8,128)(2,1)S(1)}, bf16[128,256]{1,0:T(8,128)(2,1)S(1)}, u32[]{:S(2)}, u32[]{:S(2)}) %collective-permute-start.4) | collective-permute-done | bytes 65568 | tf_op jit(solution)/shard_map/ppermute | solution.py:277
  26.4 1.4 %collective-permute-done.5.refs_2_ = bf16[128,256]{1,0:T(8,128)(2,1)S(1)} collective-permute-done((bf16[128,256]{1,0:T(8,128)(2,1)S(1)}, bf16[128,256]{1,0:T(8,128)(2,1)S(1)}, u32[]{:S(2)}, u32[]{:S(2)}) %collective-permute-start.5) | collective-permute-done | bytes 65568 | tf_op jit(solution)/shard_map/ppermute | solution.py:277
  27.8 0.0 collective-permute-done.6.refs_3_
  27.8 1.3 %shard_map.90 = (f32[64,3200]{1,0:T(8,128)S(1)}, bf16[64,3200]{1,0:T(8,128)(2,1)S(1)}) custom-call(s32[8]{0:T(128)S(1)} %copy-done.2, bf16[3200,256]{1,0:T(8,128)(2,1)S(1)} %copy-done, bf16[128,256]{1,0:T(8,128)(2,1)S(1)} %get-tuple-element.17.refs_0_, bf16[128,256]{1,0:T(8,128)(2,1)S(1)} %collective-permute-done.4.refs_1_, ...), custom_call_target="tpu_custom_call" | custom-call | flops 209715200 | bytes 2867200 | tf_op jit(solution)/shard_map/pallas_call | solution.py:280
  29.1 0.1 collective-permute-start.7
  29.2 1.7 %collective-permute-done.7.other_ref = bf16[64,3200]{1,0:T(8,128)(2,1)S(1)} collective-permute-done((bf16[64,3200]{1,0:T(8,128)(2,1)S(1)}, bf16[64,3200]{1,0:T(8,128)(2,1)S(1)}, u32[]{:S(2)}, u32[]{:S(2)}) %collective-permute-start.7) | collective-permute-done | bytes 409632 | tf_op jit(solution)/shard_map/ppermute | solution.py:288
  30.9 0.1 shard_map.91
  31.0 1.6 %collective-permute-start.8 = (bf16[16,3200]{1,0:T(8,128)(2,1)S(1)}, bf16[16,3200]{1,0:T(8,128)(2,1)S(1)}, u32[]{:S(2)}, u32[]{:S(2)}) collective-permute-start(bf16[16,3200]{1,0:T(8,128)(2,1)S(1)} %get-tuple-element.25), channel_id=1, source_target_pairs={{0,1},{1,0},{8,9},{9,8},{16,17},{17,16},{24,25},{25,24},{2,3},{3,2... | collective-permute-start | bytes 307208 | tf_op jit(solution)/shard_map/ppermute | solution.py:298
  32.6 1.5 %collective-permute-start.9 = (bf16[16,3200]{1,0:T(8,128)(2,1)S(1)}, bf16[16,3200]{1,0:T(8,128)(2,1)S(1)}, u32[]{:S(2)}, u32[]{:S(2)}) collective-permute-start(bf16[16,3200]{1,0:T(8,128)(2,1)S(1)} %get-tuple-element.26), channel_id=1, source_target_pairs={{0,16},{1,17},{8,24},{9,25},{16,0},{17,1},{24,8},{25,9},{2,18},{3,... | collective-permute-start | bytes 307208 | tf_op jit(solution)/shard_map/ppermute | solution.py:298
  34.1 0.5 collective-permute-start.10
  34.6 1.4 %collective-permute-done.8.refs_0_ = bf16[16,3200]{1,0:T(8,128)(2,1)S(1)} collective-permute-done((bf16[16,3200]{1,0:T(8,128)(2,1)S(1)}, bf16[16,3200]{1,0:T(8,128)(2,1)S(1)}, u32[]{:S(2)}, u32[]{:S(2)}) %collective-permute-start.8) | collective-permute-done | bytes 102432 | tf_op jit(solution)/shard_map/ppermute | solution.py:298
  36.0 2.3 %collective-permute-done.9.refs_1_ = bf16[16,3200]{1,0:T(8,128)(2,1)S(1)} collective-permute-done((bf16[16,3200]{1,0:T(8,128)(2,1)S(1)}, bf16[16,3200]{1,0:T(8,128)(2,1)S(1)}, u32[]{:S(2)}, u32[]{:S(2)}) %collective-permute-start.9) | collective-permute-done | bytes 102432 | tf_op jit(solution)/shard_map/ppermute | solution.py:298
  38.3 1.3 %collective-permute-done.10.refs_2_ = bf16[16,3200]{1,0:T(8,128)(2,1)S(1)} collective-permute-done((bf16[16,3200]{1,0:T(8,128)(2,1)S(1)}, bf16[16,3200]{1,0:T(8,128)(2,1)S(1)}, u32[]{:S(2)}, u32[]{:S(2)}) %collective-permute-start.10) | collective-permute-done | bytes 102432 | tf_op jit(solution)/shard_map/ppermute | solution.py:298
  39.7 0.2 shard_map.92.refs_3_
  39.9 1.3 %collective-permute-start.13 = (bf16[16,3200]{1,0:T(8,128)(2,1)S(1)}, bf16[16,3200]{1,0:T(8,128)(2,1)S(1)}, u32[]{:S(2)}, u32[]{:S(2)}) collective-permute-start(bf16[16,3200]{1,0:T(8,128)(2,1)S(1)} %shard_map.92.refs_3_), channel_id=1, source_target_pairs={{0,1},{1,0},{8,9},{9,8},{16,17},{17,16},{24,25},{25,24},{2,3},{3,2... | collective-permute-start | bytes 307208 | tf_op jit(solution)/shard_map/ppermute | solution.py:309
  41.2 1.5 %collective-permute-start.12 = (bf16[16,3200]{1,0:T(8,128)(2,1)S(1)}, bf16[16,3200]{1,0:T(8,128)(2,1)S(1)}, u32[]{:S(2)}, u32[]{:S(2)}) collective-permute-start(bf16[16,3200]{1,0:T(8,128)(2,1)S(1)} %shard_map.92.refs_3_), channel_id=1, source_target_pairs={{0,16},{1,17},{8,24},{9,25},{16,0},{17,1},{24,8},{25,9},{2,18},{3,... | collective-permute-start | bytes 307208 | tf_op jit(solution)/shard_map/ppermute | solution.py:309
  42.7 0.7 %collective-permute-start.11 = (bf16[16,3200]{1,0:T(8,128)(2,1)S(1)}, bf16[16,3200]{1,0:T(8,128)(2,1)S(1)}, u32[]{:S(2)}, u32[]{:S(2)}) collective-permute-start(bf16[16,3200]{1,0:T(8,128)(2,1)S(1)} %shard_map.92.refs_3_), channel_id=1, source_target_pairs={{0,17},{1,16},{8,25},{9,24},{16,1},{17,0},{24,9},{25,8},{2,19},{3,... | collective-permute-start | bytes 307208 | tf_op jit(solution)/shard_map/ppermute | solution.py:309
  43.4 0.0 collective-permute-start.17
  43.4 2.1 %collective-permute-done.13.refs_2_ = bf16[16,3200]{1,0:T(8,128)(2,1)S(1)} collective-permute-done((bf16[16,3200]{1,0:T(8,128)(2,1)S(1)}, bf16[16,3200]{1,0:T(8,128)(2,1)S(1)}, u32[]{:S(2)}, u32[]{:S(2)}) %collective-permute-start.13) | collective-permute-done | bytes 102432 | tf_op jit(solution)/shard_map/ppermute | solution.py:309
  45.5 0.0 collective-permute-start.16
  45.5 0.5 %collective-permute-done.12.refs_1_ = bf16[16,3200]{1,0:T(8,128)(2,1)S(1)} collective-permute-done((bf16[16,3200]{1,0:T(8,128)(2,1)S(1)}, bf16[16,3200]{1,0:T(8,128)(2,1)S(1)}, u32[]{:S(2)}, u32[]{:S(2)}) %collective-permute-start.12) | collective-permute-done | bytes 102432 | tf_op jit(solution)/shard_map/ppermute | solution.py:309
  46.0 0.0 collective-permute-start.15
  46.0 2.2 %collective-permute-done.11.refs_0_ = bf16[16,3200]{1,0:T(8,128)(2,1)S(1)} collective-permute-done((bf16[16,3200]{1,0:T(8,128)(2,1)S(1)}, bf16[16,3200]{1,0:T(8,128)(2,1)S(1)}, u32[]{:S(2)}, u32[]{:S(2)}) %collective-permute-start.11) | collective-permute-done | bytes 102432 | tf_op jit(solution)/shard_map/ppermute | solution.py:309
  48.2 0.0 collective-permute-start.14
  48.2 0.0 collective-permute-done.17.refs_7_
  48.2 0.0 collective-permute-done.16.refs_6_
  48.2 0.0 collective-permute-done.15.refs_5_
  48.2 1.3 %collective-permute-done.14.refs_4_ = bf16[16,3200]{1,0:T(8,128)(2,1)S(1)} collective-permute-done((bf16[16,3200]{1,0:T(8,128)(2,1)S(1)}, bf16[16,3200]{1,0:T(8,128)(2,1)S(1)}, u32[]{:S(2)}, u32[]{:S(2)}) %collective-permute-start.14) | collective-permute-done | bytes 102432 | tf_op jit(solution)/shard_map/ppermute | solution.py:310
  49.5 0.9 %shard_map.93 = bf16[128,3200]{1,0:T(8,128)(2,1)} custom-call(bf16[16,3200]{1,0:T(8,128)(2,1)S(1)} %collective-permute-done.11.refs_0_, bf16[16,3200]{1,0:T(8,128)(2,1)S(1)} %collective-permute-done.12.refs_1_, bf16[16,3200]{1,0:T(8,128)(2,1)S(1)} %collective-permute-done.13.refs_2_, bf16[16,3200]{1,0:T(8,128)(2,1)S(1)} %shard_map.92.refs_3_, ...), custom_call_target="tpu_custom_call" | custom-call | bytes 1638400 | tf_op jit(solution)/shard_map/pallas_call | solution.py:311
  (6 shorter events, 0.0 us)
Async XLA Ops:
  0.6 8.2 %copy-start.2 = (s32[8]{0:T(128)S(1)}, s32[8]{0:T(128)}, u32[]{:S(2)}) copy-start(s32[8]{0:T(128)} %pieces_ref.5) | copy-start | bytes 100
  0.6 8.9 %collective-permute-start = (bf16[128,256]{1,0:T(8,128)(2,1)}, bf16[128,256]{1,0:T(8,128)(2,1)S(1)}, u32[]{:S(2)}, u32[]{:S(2)}) collective-permute-start(bf16[128,256]{1,0:T(8,128)(2,1)} %param.11), channel_id=1, source_target_pairs={{0,6},{2,4},{4,0},{6,2},{1,7},{3,5},{5,1},{7,3},{8,14},{10,12},{12... | collective-permute-start | bytes 196616 | tf_op jit(solution)/shard_map/ppermute | solution.py:232
  5.7 0.7 %copy-start.1 = (f32[3200]{0:T(1024)S(1)}, f32[3200]{0:T(1024)}, u32[]{:S(2)}) copy-start(f32[3200]{0:T(1024)} %param.8) | copy-start | bytes 38404
  6.5 11.9 %copy-start.3 = (bf16[128,512]{1,0:T(8,128)(2,1)S(1)}, bf16[128,512]{1,0:T(8,128)(2,1)}, u32[]{:S(2)}) copy-start(bf16[128,512]{1,0:T(8,128)(2,1)} %q_ref.1) | copy-start | bytes 393220
  6.5 11.9 %copy-start.4 = (bf16[128,512]{1,0:T(8,128)(2,1)S(1)}, bf16[128,512]{1,0:T(8,128)(2,1)}, u32[]{:S(2)}) copy-start(bf16[128,512]{1,0:T(8,128)(2,1)} %g_ref.1) | copy-start | bytes 393220
  6.5 21.4 %copy-start = (bf16[3200,256]{1,0:T(8,128)(2,1)S(1)}, bf16[3200,256]{1,0:T(8,128)(2,1)}, u32[]{:S(2)}) copy-start(bf16[3200,256]{1,0:T(8,128)(2,1)} %proj_ref.1) | copy-start | bytes 4915204
  10.1 6.7 %collective-permute-start.3 = (bf16[128,256]{1,0:T(8,128)(2,1)S(1)}, bf16[128,256]{1,0:T(8,128)(2,1)S(1)}, u32[]{:S(2)}, u32[]{:S(2)}) collective-permute-start(bf16[128,256]{1,0:T(8,128)(2,1)S(1)} %shard_map.88.refs_0_), channel_id=1, source_target_pairs={{0,6},{2,4},{4,2},{6,0},{1,7},{3,5},{5,3},{7,1},{8,14},{10,12},{12... | collective-permute-start | bytes 196616 | tf_op jit(solution)/shard_map/ppermute | solution.py:268
  12.7 5.7 %collective-permute-start.2 = (bf16[128,256]{1,0:T(8,128)(2,1)S(1)}, bf16[128,256]{1,0:T(8,128)(2,1)S(1)}, u32[]{:S(2)}, u32[]{:S(2)}) collective-permute-start(bf16[128,256]{1,0:T(8,128)(2,1)S(1)} %shard_map.88.refs_0_), channel_id=1, source_target_pairs={{0,4},{2,6},{4,0},{6,2},{1,5},{3,7},{5,1},{7,3},{8,12},{10,14},{12... | collective-permute-start | bytes 196616 | tf_op jit(solution)/shard_map/ppermute | solution.py:268
  12.7 5.7 %collective-permute-start.1 = (bf16[128,256]{1,0:T(8,128)(2,1)S(1)}, bf16[128,256]{1,0:T(8,128)(2,1)S(1)}, u32[]{:S(2)}, u32[]{:S(2)}) collective-permute-start(bf16[128,256]{1,0:T(8,128)(2,1)S(1)} %shard_map.88.refs_0_), channel_id=1, source_target_pairs={{0,2},{2,0},{4,6},{6,4},{1,3},{3,1},{5,7},{7,5},{8,10},{10,8},{12,... | collective-permute-start | bytes 196616 | tf_op jit(solution)/shard_map/ppermute | solution.py:268
  20.3 6.1 %collective-permute-start.4 = (bf16[128,256]{1,0:T(8,128)(2,1)S(1)}, bf16[128,256]{1,0:T(8,128)(2,1)S(1)}, u32[]{:S(2)}, u32[]{:S(2)}) collective-permute-start(bf16[128,256]{1,0:T(8,128)(2,1)S(1)} %get-tuple-element.18), channel_id=1, source_target_pairs={{0,6},{2,4},{4,2},{6,0},{1,7},{3,5},{5,3},{7,1},{8,14},{10,12},{12... | collective-permute-start | bytes 196616 | tf_op jit(solution)/shard_map/ppermute | solution.py:277
  22.3 5.5 %collective-permute-start.5 = (bf16[128,256]{1,0:T(8,128)(2,1)S(1)}, bf16[128,256]{1,0:T(8,128)(2,1)S(1)}, u32[]{:S(2)}, u32[]{:S(2)}) collective-permute-start(bf16[128,256]{1,0:T(8,128)(2,1)S(1)} %get-tuple-element.19), channel_id=1, source_target_pairs={{0,4},{2,6},{4,0},{6,2},{1,5},{3,7},{5,1},{7,3},{8,12},{10,14},{12... | collective-permute-start | bytes 196616 | tf_op jit(solution)/shard_map/ppermute | solution.py:277
  22.4 5.4 %collective-permute-start.6 = (bf16[128,256]{1,0:T(8,128)(2,1)S(1)}, bf16[128,256]{1,0:T(8,128)(2,1)S(1)}, u32[]{:S(2)}, u32[]{:S(2)}) collective-permute-start(bf16[128,256]{1,0:T(8,128)(2,1)S(1)} %get-tuple-element.20), channel_id=1, source_target_pairs={{0,2},{2,0},{4,6},{6,4},{1,3},{3,1},{5,7},{7,5},{8,10},{10,8},{12,... | collective-permute-start | bytes 196616 | tf_op jit(solution)/shard_map/ppermute | solution.py:277
  29.1 1.8 %collective-permute-start.7 = (bf16[64,3200]{1,0:T(8,128)(2,1)S(1)}, bf16[64,3200]{1,0:T(8,128)(2,1)S(1)}, u32[]{:S(2)}, u32[]{:S(2)}) collective-permute-start(bf16[64,3200]{1,0:T(8,128)(2,1)S(1)} %get-tuple-element.22), channel_id=1, source_target_pairs={{0,8},{1,9},{8,0},{9,1},{16,24},{17,25},{24,16},{25,17},{2,10},{3,... | collective-permute-start | bytes 1228808 | tf_op jit(solution)/shard_map/ppermute | solution.py:288
  31.0 5.0 %collective-permute-start.8 = (bf16[16,3200]{1,0:T(8,128)(2,1)S(1)}, bf16[16,3200]{1,0:T(8,128)(2,1)S(1)}, u32[]{:S(2)}, u32[]{:S(2)}) collective-permute-start(bf16[16,3200]{1,0:T(8,128)(2,1)S(1)} %get-tuple-element.25), channel_id=1, source_target_pairs={{0,1},{1,0},{8,9},{9,8},{16,17},{17,16},{24,25},{25,24},{2,3},{3,2... | collective-permute-start | bytes 307208 | tf_op jit(solution)/shard_map/ppermute | solution.py:298
  32.6 5.7 %collective-permute-start.9 = (bf16[16,3200]{1,0:T(8,128)(2,1)S(1)}, bf16[16,3200]{1,0:T(8,128)(2,1)S(1)}, u32[]{:S(2)}, u32[]{:S(2)}) collective-permute-start(bf16[16,3200]{1,0:T(8,128)(2,1)S(1)} %get-tuple-element.26), channel_id=1, source_target_pairs={{0,16},{1,17},{8,24},{9,25},{16,0},{17,1},{24,8},{25,9},{2,18},{3,... | collective-permute-start | bytes 307208 | tf_op jit(solution)/shard_map/ppermute | solution.py:298
  34.1 5.6 %collective-permute-start.10 = (bf16[16,3200]{1,0:T(8,128)(2,1)S(1)}, bf16[16,3200]{1,0:T(8,128)(2,1)S(1)}, u32[]{:S(2)}, u32[]{:S(2)}) collective-permute-start(bf16[16,3200]{1,0:T(8,128)(2,1)S(1)} %get-tuple-element.27), channel_id=1, source_target_pairs={{0,17},{1,16},{8,25},{9,24},{16,1},{17,0},{24,9},{25,8},{2,19},{3,... | collective-permute-start | bytes 307208 | tf_op jit(solution)/shard_map/ppermute | solution.py:298
  39.9 5.6 %collective-permute-start.13 = (bf16[16,3200]{1,0:T(8,128)(2,1)S(1)}, bf16[16,3200]{1,0:T(8,128)(2,1)S(1)}, u32[]{:S(2)}, u32[]{:S(2)}) collective-permute-start(bf16[16,3200]{1,0:T(8,128)(2,1)S(1)} %shard_map.92.refs_3_), channel_id=1, source_target_pairs={{0,1},{1,0},{8,9},{9,8},{16,17},{17,16},{24,25},{25,24},{2,3},{3,2... | collective-permute-start | bytes 307208 | tf_op jit(solution)/shard_map/ppermute | solution.py:309
  41.2 4.8 %collective-permute-start.12 = (bf16[16,3200]{1,0:T(8,128)(2,1)S(1)}, bf16[16,3200]{1,0:T(8,128)(2,1)S(1)}, u32[]{:S(2)}, u32[]{:S(2)}) collective-permute-start(bf16[16,3200]{1,0:T(8,128)(2,1)S(1)} %shard_map.92.refs_3_), channel_id=1, source_target_pairs={{0,16},{1,17},{8,24},{9,25},{16,0},{17,1},{24,8},{25,9},{2,18},{3,... | collective-permute-start | bytes 307208 | tf_op jit(solution)/shard_map/ppermute | solution.py:309
  42.7 5.6 %collective-permute-start.11 = (bf16[16,3200]{1,0:T(8,128)(2,1)S(1)}, bf16[16,3200]{1,0:T(8,128)(2,1)S(1)}, u32[]{:S(2)}, u32[]{:S(2)}) collective-permute-start(bf16[16,3200]{1,0:T(8,128)(2,1)S(1)} %shard_map.92.refs_3_), channel_id=1, source_target_pairs={{0,17},{1,16},{8,25},{9,24},{16,1},{17,0},{24,9},{25,8},{2,19},{3,... | collective-permute-start | bytes 307208 | tf_op jit(solution)/shard_map/ppermute | solution.py:309
  43.4 4.8 %collective-permute-start.17 = (bf16[16,3200]{1,0:T(8,128)(2,1)S(1)}, bf16[16,3200]{1,0:T(8,128)(2,1)S(1)}, u32[]{:S(2)}, u32[]{:S(2)}) collective-permute-start(bf16[16,3200]{1,0:T(8,128)(2,1)S(1)} %shard_map.92.refs_3_), channel_id=1, source_target_pairs={{0,8},{1,9},{8,0},{9,1},{16,24},{17,25},{24,16},{25,17},{2,10},{3,... | collective-permute-start | bytes 307208 | tf_op jit(solution)/shard_map/ppermute | solution.py:310
  45.5 2.8 %collective-permute-start.16 = (bf16[16,3200]{1,0:T(8,128)(2,1)S(1)}, bf16[16,3200]{1,0:T(8,128)(2,1)S(1)}, u32[]{:S(2)}, u32[]{:S(2)}) collective-permute-start(bf16[16,3200]{1,0:T(8,128)(2,1)S(1)} %collective-permute-done.13.refs_2_), channel_id=1, source_target_pairs={{0,8},{1,9},{8,0},{9,1},{16,24},{17,25},{24,16},{25,17},{2,10},{3,... | collective-permute-start | bytes 307208 | tf_op jit(solution)/shard_map/ppermute | solution.py:310
  46.0 2.2 %collective-permute-start.15 = (bf16[16,3200]{1,0:T(8,128)(2,1)S(1)}, bf16[16,3200]{1,0:T(8,128)(2,1)S(1)}, u32[]{:S(2)}, u32[]{:S(2)}) collective-permute-start(bf16[16,3200]{1,0:T(8,128)(2,1)S(1)} %collective-permute-done.12.refs_1_), channel_id=1, source_target_pairs={{0,8},{1,9},{8,0},{9,1},{16,24},{17,25},{24,16},{25,17},{2,10},{3,... | collective-permute-start | bytes 307208 | tf_op jit(solution)/shard_map/ppermute | solution.py:310
  48.2 1.3 %collective-permute-start.14 = (bf16[16,3200]{1,0:T(8,128)(2,1)S(1)}, bf16[16,3200]{1,0:T(8,128)(2,1)S(1)}, u32[]{:S(2)}, u32[]{:S(2)}) collective-permute-start(bf16[16,3200]{1,0:T(8,128)(2,1)S(1)} %collective-permute-done.11.refs_0_), channel_id=1, source_target_pairs={{0,8},{1,9},{8,0},{9,1},{16,24},{17,25},{24,16},{25,17},{2,10},{3,... | collective-permute-start | bytes 307208 | tf_op jit(solution)/shard_map/ppermute | solution.py:310

commit v7 on v6

--- a/solution.py
+++ b/solution.py
@@ -1,5 +1,6 @@
 import functools
 import math
+import random
 
 import jax
 import jax.numpy as jnp
@@ -25,6 +26,59 @@
 def held_image(block, count):
     half = count // 2
     return jnp.where(block < half, block + half, lax.rem(block + half - 1, half))
+
+
+def colour(edges, count):
+    sent, got = [{} for _ in range(count)], [{} for _ in range(count)]
+    for s, t in edges:
+        a = min(c for c in range(count) if c not in sent[s])
+        b = min(c for c in range(count) if c not in got[t])
+        if a != b:
+            path, at, back, c = [], t, True, a
+            while c in (got if back else sent)[at]:
+                near = (got if back else sent)[at][c]
+                path.append((near, at, c) if back else (at, near, c))
+                at, back, c = near, not back, a + b - c
+            for u, v, c in path:
+                del sent[u][c], got[v][c]
+            for u, v, c in path:
+                sent[u][a + b - c], got[v][a + b - c] = v, u
+        sent[s][a], got[t][a] = t, s
+    return [{s: sent[s][c] for s in range(count) if c in sent[s]} for c in sorted({c for x in sent for c in x})]
+
+
+def completed(pairs, count):
+    sources = [s for s in range(count) if s not in pairs]
+    targets = [t for t in range(count) if t not in pairs.values()]
+    full = dict(pairs)
+    for d in sources:
+        if d in targets:
+            full[d] = d
+    full.update(zip([s for s in sources if s not in targets], [t for t in targets if t not in sources]))
+    return full
+
+
+def crossings(rounds, count):
+    flows = [0] * (2 * count)
+    for pairs in rounds:
+        for s, t in completed(pairs, count).items():
+            for k in range(min(s, t), max(s, t)):
+                flows[2 * k + (t > s)] += 1
+    return len(rounds), max(flows), sum(flows)
+
+
+def rounds_of(edges, count):
+    draw, tries = random.Random(0), [list(edges)]
+    for _ in range(300 if count <= 8 else 0):
+        tries.append(draw.sample(edges, len(edges)))
+    return min((colour(order, count) for order in tries), key=lambda rounds: crossings(rounds, count))
+
+
+def pick_static(table, index):
+    value = jnp.int32(table[0])
+    for n in range(1, len(table)):
+        value = jnp.where(index == n, table[n], value)
+    return value
 
 
 def group_place():
@@ -100,8 +154,9 @@
     out_ref[...] = jnp.where(row < before, text, image).astype(jnp.bfloat16)
 
 
-def attend_body(seq_n, q_ref, g_ref, *refs):
-    block_refs, out_ref, grad_refs = refs[:seq_n], refs[seq_n], refs[seq_n + 1 :]
+def attend_body(seq_n, tables, q_ref, g_ref, *refs):
+    held = len(tables) + 1
+    block_refs, out_ref, grad_refs = refs[:held], refs[held], refs[held + 1 :]
     rows = q_ref.shape[0]
     group = q_ref.shape[1] // HD
     scale = 1.0 / math.sqrt(HD)
@@ -112,7 +167,8 @@
     span = together * rows
     offset = lax.broadcasted_iota(jnp.int32, (rows, span), 0)
     offset = offset - lax.rem(lax.broadcasted_iota(jnp.int32, (rows, span), 1), rows)
-    masks = [offset <= (me - held_image(me ^ r, seq_n)) * rows for r in range(seq_n)]
+    images = [held_image(me, seq_n)] + [pick_static(table, me) for table in tables]
+    masks = [offset <= (me - image) * rows for image in images]
     key_total = value_total = None
     for first in range(0, group, together):
         heads = range(first, first + together)
@@ -143,7 +199,7 @@
 
 
 def back_body(seq_n, piece, pieces_ref, proj_ref, *refs):
-    part_refs, (keep_ref, send_ref) = refs[:-2], refs[-2:]
+    part_refs, (grad_ref, send_ref) = refs[:-2], refs[-2:]
     rows = part_refs[0].shape[0]
     half = rows // 2
     before = pieces_ref[2 * held_image(lax.axis_index("seq"), seq_n)]
@@ -152,14 +208,18 @@
     for ref in part_refs[1:]:
         total += ref[...].astype(jnp.float32)
     slot = lax.broadcasted_iota(jnp.int32, (rows, rows), 0)
-    to = (lax.div(slot, half) ^ parity) * half
+    to = (1 - (lax.div(slot, half) ^ parity)) * half
     to += (lax.div(lax.rem(slot, half), piece) ^ place) * piece + lax.rem(slot, piece)
     source = lax.broadcasted_iota(jnp.int32, (rows, rows), 1)
     pick = jnp.where(source == to + before, 1.0, 0.0).astype(jnp.bfloat16)
     image_grad = jnp.dot(pick, total.astype(jnp.bfloat16), preferred_element_type=jnp.float32)
-    product = dot(image_grad.astype(jnp.bfloat16), proj_ref[...], ((1,), (1,)))
-    keep_ref[...] = product[:half]
-    send_ref[...] = product[half:].astype(jnp.bfloat16)
+    image_grad = image_grad.astype(jnp.bfloat16)
+    send_ref[...] = dot(image_grad[:half], proj_ref[...], ((1,), (1,))).astype(jnp.bfloat16)
+    grad_ref[...] = image_grad[half:]
+
+
+def keep_body(grad_ref, proj_ref, keep_ref):
+    keep_ref[...] = dot(grad_ref[...], proj_ref[...], ((1,), (1,)))
 
 
 def pair_body(piece, keep_ref, other_ref, own_ref, *send_refs):
@@ -191,14 +251,13 @@
         out_ref[:, c : c + HD] = (scaled[n] * inverse - own * lead).astype(jnp.bfloat16)
 
 
-def gather_body(count, *refs):
-    part_refs, out_hbm, sems = refs[: 2 * count], refs[2 * count], refs[2 * count + 1]
+def gather_body(count, core, *refs):
+    part_refs, (out_hbm, sems) = refs[:count], refs[-2:]
     piece = part_refs[0].shape[0]
     parity, place = group_place()
     copies = []
     for n, ref in enumerate(part_refs):
-        core, step = n // count, count - 1 - n % count
-        row = ((parity ^ core) * count + (place ^ step)) * piece
+        row = ((parity ^ core) * count + (place ^ (count - 1 - n))) * piece
         copy = pltpu.make_async_copy(ref, out_hbm.at[pl.ds(pl.multiple_of(row, piece), piece), :], sems.at[n])
         copy.start()
         copies.append(copy)
@@ -227,9 +286,13 @@
         return pairs
 
     gain = vis_gain.reshape(width // HD, HD)
-    far = sorted(range(1, seq_n), reverse=True)
-    partners = {r: [(d, d ^ r) for d in range(seq_n)] for r in far}
-    text = lax.ppermute(text_kv, "seq", [(j, owner_block(j, seq_n)) for j in range(seq_n)])
+    owners = [owner_block(j, seq_n) for j in range(seq_n)]
+    held = [owners.index(b) for b in range(seq_n)]
+    edges = [(owners[j], d) for j in range(seq_n) for d in range(j, seq_n) if owners[j] != d]
+    rounds = rounds_of(edges, seq_n)
+    forth = [sorted(completed(pairs, seq_n).items()) for pairs in rounds]
+    tables = [[next((held[s] for s, t in pairs.items() if t == d), seq_n) for d in range(seq_n)] for pairs in rounds]
+    text = lax.ppermute(text_kv, "seq", list(enumerate(owners)))
     chunks = len(cuts(width))
     hbm = pl.BlockSpec(memory_space=pltpu.HBM)
     image_kv, own_rows = call(
@@ -265,26 +328,35 @@
         0,
         6 * rows * columns,
     )(pieces, shifted, text)
-    blocks = {r: lax.ppermute(block, "seq", partners[r]) for r in far}
+    blocks = [lax.ppermute(block, "seq", pairs) for pairs in forth]
     attended, *grads = call(
-        functools.partial(attend_body, seq_n),
-        [jax.ShapeDtypeStruct(queries.shape, bf16)] + [jax.ShapeDtypeStruct((rows, columns), bf16)] * seq_n,
-        [WHOLE] * (2 + seq_n),
-        [WHOLE] * (1 + seq_n),
+        functools.partial(attend_body, seq_n, tables),
+        [jax.ShapeDtypeStruct(queries.shape, bf16)]
+        + [jax.ShapeDtypeStruct((rows, columns), bf16)] * (1 + len(blocks)),
+        [WHOLE] * (3 + len(blocks)),
+        [WHOLE] * (2 + len(blocks)),
         10 * seq_n * rows * rows * queries.shape[1],
         6 * rows * queries.shape[1] + 4 * seq_n * rows * columns,
-    )(queries, grad_out, block, *[blocks[r] for r in range(1, seq_n)])
-    parts = {r: lax.ppermute(grads[r], "seq", partners[r]) for r in far}
-    parts[0] = grads[0]
-
-    keep, send = call(
+    )(queries, grad_out, block, *blocks)
+    parts = [lax.ppermute(g, "seq", [(t, s) for s, t in pairs]) for g, pairs in zip(grads[1:], forth)]
+
+    half = rows // 2
+    grad_rows, send = call(
         functools.partial(back_body, seq_n, piece),
-        [jax.ShapeDtypeStruct((rows // 2, width), f32), jax.ShapeDtypeStruct((rows // 2, width), bf16)],
-        [SCALARS] + [WHOLE] * (1 + seq_n),
+        [jax.ShapeDtypeStruct((half, columns), bf16), jax.ShapeDtypeStruct((half, width), bf16)],
+        [SCALARS] + [WHOLE] * (2 + len(parts)),
         [WHOLE, WHOLE],
-        2 * rows * width * columns,
-        2 * width * columns + 3 * rows * width,
-    )(pieces, key_value_proj, parts[0], *[parts[r] for r in far])
+        rows * width * columns,
+        2 * width * columns + rows * width,
+    )(pieces, key_value_proj, grads[0], *parts)
+    keep = call(
+        keep_body,
+        jax.ShapeDtypeStruct((half, width), f32),
+        [WHOLE, WHOLE],
+        WHOLE,
+        rows * width * columns,
+        2 * width * columns + 2 * rows * width,
+    )(grad_rows, key_value_proj)
     other = lax.ppermute(send, names, core_pairs)
     steps = list(range(1, count))
     own_sum, *sends = call(
@@ -308,15 +380,19 @@
     for d in steps:
         mines[d] = lax.ppermute(mine, names, far_pairs(d))
     theirs = {d: lax.ppermute(mines[d], names, core_pairs) for d in range(count)}
-    vis_grad = call(
-        functools.partial(gather_body, count),
-        jax.ShapeDtypeStruct((rows, width), bf16),
-        [WHOLE] * n,
-        hbm,
-        0,
-        4 * rows * width,
-        scratch_shapes=[pltpu.SemaphoreType.DMA((n,))],
-    )(*[mines[d] for d in reversed(range(count))], *[theirs[d] for d in reversed(range(count))])
+    vis_grad = None
+    for core, parts in enumerate((mines, theirs)):
+        done = [] if vis_grad is None else [vis_grad]
+        vis_grad = call(
+            functools.partial(gather_body, count, core),
+            jax.ShapeDtypeStruct((rows, width), bf16),
+            [WHOLE] * count + [hbm] * len(done),
+            hbm,
+            0,
+            2 * rows * width,
+            scratch_shapes=[pltpu.SemaphoreType.DMA((count,))],
+            input_output_aliases={count: 0} if done else {},
+        )(*[parts[d] for d in reversed(range(count))], *done)
     return (attended, vis_grad)
 
 

time: 50.7 us -> 56.5 us (1.11)
  waiting for transfers between devices: 19.8 us -> 22.1 us
  starting transfers between devices: 21.1 us -> 23.2 us
  Pallas kernels: 8.12 us -> 9.32 us
    ppermute x7, waiting for transfers between devices: 6.86 us -> 10.6 us  [the longest x3 6.37 us: on_device(): lax.ppermute(g, 'seq', [(t, s) for s, t in pairs])]
    ppermute x7, starting transfers between devices: 13.9 us -> 16.1 us  [the longest x3 6.9 us: on_device(): blocks = [lax.ppermute(block, 'seq', pairs) for pairs in forth]]
    pallas_call x3 -> x5, Pallas kernels: 4.22 us -> 5.42 us  [the longest x1 1.97 us: on_device(): call(functools.partial(attend_body, seq_n, tables), [jax.ShapeDtypeStruct...]
    ppermute x4, waiting for transfers between devices: 1.29 us -> 0.49 us  [on_device(): lax.ppermute(mines[d], names, core_pairs)]
    ppermute x1, waiting for transfers between devices: 1.73 us -> 1.11 us  [on_device(): other = lax.ppermute(send, names, core_pairs)]
  transfers between devices with their start and end apart: 18 -> 18, of which waited for: 12 -> 11; matrix products, arithmetic and copies ran while one was open for 0% -> 0% of each run, Pallas kernels for 6% -> 8%
where the time goes in v7:
time: 56.5 us; the launch traced here: 56.2 us
  starting transfers between devices  23.2 us (41%)
  waiting for transfers between devices  22.1 us (39%)
  Pallas kernels  9.32 us (16%)
  between operations  0.78 us (1%)
  local copies, waits for them, and re-layouts  0.73 us (1%)
    ppermute x3, starting transfers between devices, on_device(): blocks = [lax.ppermute(block, 'seq', pairs) for pairs in forth]  6.9 us
    ppermute x3, waiting for transfers between devices, on_device(): lax.ppermute(g, 'seq', [(t, s) for s, t in pairs])  6.37 us
    ppermute x1, starting transfers between devices, on_device(): text = lax.ppermute(text_kv, 'seq', list(enumerate(owners)))  5.1 us
    ppermute x3, waiting for transfers between devices, on_device(): shares = [lax.ppermute(sends[d - 1], names, far_pairs(d)) for d in steps]  5.09 us
    ppermute x3, waiting for transfers between devices, on_device(): mines[d] = lax.ppermute(mine, names, far_pairs(d))  4.8 us
    ppermute x3, waiting for transfers between devices, on_device(): blocks = [lax.ppermute(block, 'seq', pairs) for pairs in forth]  4.24 us
    ppermute x3, starting transfers between devices, on_device(): lax.ppermute(g, 'seq', [(t, s) for s, t in pairs])  4.05 us
    ppermute x3, starting transfers between devices, on_device(): shares = [lax.ppermute(sends[d - 1], names, far_pairs(d)) for d in steps]  3.55 us
  transfers between devices with their start and end apart: 18, of which 11 were waited for; matrix products, arithmetic and copies ran while one was open for 0% of the time, Pallas kernels for 8%

profile of v7, /device:TPU:0, one launch (start us, length us, event | category | flops | bytes accessed | tf_op | source)
XLA Modules:
  0.0 56.2 jit_solution(9765606876733626075)
XLA Ops:
  0.6 5.1 %collective-permute-start = (bf16[128,256]{1,0:T(8,128)(2,1)}, bf16[128,256]{1,0:T(8,128)(2,1)S(1)}, u32[]{:S(2)}, u32[]{:S(2)}) collective-permute-start(bf16[128,256]{1,0:T(8,128)(2,1)} %param.11), channel_id=1, source_target_pairs={{0,6},{2,4},{4,0},{6,2},{1,7},{3,5},{5,1},{7,3},{8,14},{10,12},{12... | collective-permute-start | bytes 196616 | tf_op jit(solution)/shard_map/ppermute | solution.py:295
  5.7 0.7 %copy-done.1 = f32[3200]{0:T(1024)S(1)} copy-done((f32[3200]{0:T(1024)S(1)}, f32[3200]{0:T(1024)}, u32[]{:S(2)}) %copy-start.1) | copy-done | bytes 12824
  6.5 2.4 %shard_map.86 = (bf16[128,256]{1,0:T(8,128)(2,1)S(1)}, bf16[16,3200]{1,0:T(8,128)(2,1)S(1)}) custom-call(bf16[128,3200]{1,0:T(8,128)(2,1)} %vis_hbm.1, f32[25,128]{1,0:T(8,128)S(1)} %bitcast.1, bf16[3200,256]{1,0:T(8,128)(2,1)} %proj_ref.3), custom_call_target="tpu_custom_call" | custom-call | flops 209715200 | bytes 2457600 | tf_op jit(solution)/shard_map/pallas_call | solution.py:298
  8.8 0.0 copy-done.2
  8.9 0.7 %shard_map.87.image_ref = bf16[128,256]{1,0:T(8,128)(2,1)S(1)} custom-call(s32[8]{0:T(128)S(1)} %copy-done.2, bf16[128,256]{1,0:T(8,128)(2,1)S(1)} %get-tuple-element.15.image_ref), custom_call_target="tpu_custom_call" | custom-call | flops 8388608 | bytes 131072 | tf_op jit(solution)/shard_map/pallas_call | solution.py:315
  9.5 0.0 collective-permute-done.text_ref
  9.6 0.6 %shard_map.88.refs_0_ = bf16[128,256]{1,0:T(8,128)(2,1)S(1)} custom-call(s32[8]{0:T(128)S(1)} %copy-done.2, bf16[128,256]{1,0:T(8,128)(2,1)S(1)} %shard_map.87.image_ref, bf16[128,256]{1,0:T(8,128)(2,1)S(1)} %collective-permute-done.text_ref), custom_call_target="tpu_custom_call" | custom-call | bytes 196608 | tf_op jit(solution)/shard_map/pallas_call | solution.py:323
  10.1 4.4 %collective-permute-start.3 = (bf16[128,256]{1,0:T(8,128)(2,1)S(1)}, bf16[128,256]{1,0:T(8,128)(2,1)S(1)}, u32[]{:S(2)}, u32[]{:S(2)}) collective-permute-start(bf16[128,256]{1,0:T(8,128)(2,1)S(1)} %shard_map.88.refs_0_), channel_id=1, source_target_pairs={{0,6},{2,0},{4,4},{6,2},{1,7},{3,1},{5,5},{7,3},{8,14},{10,8},{12,... | collective-permute-start | bytes 196616 | tf_op jit(solution)/shard_map/ppermute | solution.py:331
  14.5 0.7 %collective-permute-start.2 = (bf16[128,256]{1,0:T(8,128)(2,1)S(1)}, bf16[128,256]{1,0:T(8,128)(2,1)S(1)}, u32[]{:S(2)}, u32[]{:S(2)}) collective-permute-start(bf16[128,256]{1,0:T(8,128)(2,1)S(1)} %shard_map.88.refs_0_), channel_id=1, source_target_pairs={{0,0},{2,2},{4,6},{6,4},{1,1},{3,3},{5,7},{7,5},{8,8},{10,10},{12,... | collective-permute-start | bytes 196616 | tf_op jit(solution)/shard_map/ppermute | solution.py:331
  15.2 1.9 %collective-permute-start.1 = (bf16[128,256]{1,0:T(8,128)(2,1)S(1)}, bf16[128,256]{1,0:T(8,128)(2,1)S(1)}, u32[]{:S(2)}, u32[]{:S(2)}) collective-permute-start(bf16[128,256]{1,0:T(8,128)(2,1)S(1)} %shard_map.88.refs_0_), channel_id=1, source_target_pairs={{0,4},{2,6},{4,2},{6,0},{1,5},{3,7},{5,3},{7,1},{8,12},{10,14},{12... | collective-permute-start | bytes 196616 | tf_op jit(solution)/shard_map/ppermute | solution.py:331
  17.1 0.0 collective-permute-done.3.refs_3_
  17.1 0.0 collective-permute-done.2.refs_2_
  17.1 4.2 %collective-permute-done.1.refs_1_ = bf16[128,256]{1,0:T(8,128)(2,1)S(1)} collective-permute-done((bf16[128,256]{1,0:T(8,128)(2,1)S(1)}, bf16[128,256]{1,0:T(8,128)(2,1)S(1)}, u32[]{:S(2)}, u32[]{:S(2)}) %collective-permute-start.1) | collective-permute-done | bytes 65568 | tf_op jit(solution)/shard_map/ppermute | solution.py:331
  21.3 2.0 %shard_map.89 = (bf16[128,512]{1,0:T(8,128)(2,1)}, bf16[128,256]{1,0:T(8,128)(2,1)S(1)}, bf16[128,256]{1,0:T(8,128)(2,1)S(1)}, bf16[128,256]{1,0:T(8,128)(2,1)S(1)}, bf16[128,256]{1,0:T(8,128)(2,1)S(1)}) custom-call(bf16[128,512]{1,0:T(8,128)(2,1)S(1)} %copy-done.3, bf16[128,512]{1,0:T(8,128)(2,1)S(1)} %copy-done.4, bf16[128,256]{1,0:T(8,128)(2,1)S(1)} %shard_map.88.refs_0_, ...), custom_call_target="tpu_custom_call" | custom-call | flops 335544320 | bytes 917504 | tf_op jit(solution)/shard_map/pallas_call | solution.py:332
  23.3 0.7 %collective-permute-start.4 = (bf16[128,256]{1,0:T(8,128)(2,1)S(1)}, bf16[128,256]{1,0:T(8,128)(2,1)S(1)}, u32[]{:S(2)}, u32[]{:S(2)}) collective-permute-start(bf16[128,256]{1,0:T(8,128)(2,1)S(1)} %get-tuple-element.18), channel_id=1, source_target_pairs={{4,0},{6,2},{2,4},{0,6},{5,1},{7,3},{3,5},{1,7},{12,8},{14,10},{10... | collective-permute-start | bytes 196616 | tf_op jit(solution)/shard_map/ppermute | solution.py:341
  24.0 0.7 %collective-permute-start.5 = (bf16[128,256]{1,0:T(8,128)(2,1)S(1)}, bf16[128,256]{1,0:T(8,128)(2,1)S(1)}, u32[]{:S(2)}, u32[]{:S(2)}) collective-permute-start(bf16[128,256]{1,0:T(8,128)(2,1)S(1)} %get-tuple-element.19), channel_id=1, source_target_pairs={{0,0},{2,2},{6,4},{4,6},{1,1},{3,3},{7,5},{5,7},{8,8},{10,10},{14,... | collective-permute-start | bytes 196616 | tf_op jit(solution)/shard_map/ppermute | solution.py:341
  24.6 2.7 %collective-permute-start.6 = (bf16[128,256]{1,0:T(8,128)(2,1)S(1)}, bf16[128,256]{1,0:T(8,128)(2,1)S(1)}, u32[]{:S(2)}, u32[]{:S(2)}) collective-permute-start(bf16[128,256]{1,0:T(8,128)(2,1)S(1)} %get-tuple-element.20), channel_id=1, source_target_pairs={{6,0},{0,2},{4,4},{2,6},{7,1},{1,3},{5,5},{3,7},{14,8},{8,10},{12,... | collective-permute-start | bytes 196616 | tf_op jit(solution)/shard_map/ppermute | solution.py:341
  27.3 1.1 %collective-permute-done.4.refs_1_ = bf16[128,256]{1,0:T(8,128)(2,1)S(1)} collective-permute-done((bf16[128,256]{1,0:T(8,128)(2,1)S(1)}, bf16[128,256]{1,0:T(8,128)(2,1)S(1)}, u32[]{:S(2)}, u32[]{:S(2)}) %collective-permute-start.4) | collective-permute-done | bytes 65568 | tf_op jit(solution)/shard_map/ppermute | solution.py:341
  28.4 0.0 collective-permute-done.5.refs_2_
  28.5 5.3 %collective-permute-done.6.refs_3_ = bf16[128,256]{1,0:T(8,128)(2,1)S(1)} collective-permute-done((bf16[128,256]{1,0:T(8,128)(2,1)S(1)}, bf16[128,256]{1,0:T(8,128)(2,1)S(1)}, u32[]{:S(2)}, u32[]{:S(2)}) %collective-permute-start.6) | collective-permute-done | bytes 65568 | tf_op jit(solution)/shard_map/ppermute | solution.py:341
  33.7 1.3 %shard_map.90 = (bf16[64,256]{1,0:T(8,128)(2,1)S(1)}, bf16[64,3200]{1,0:T(8,128)(2,1)S(1)}) custom-call(s32[8]{0:T(128)S(1)} %copy-done.2, bf16[3200,256]{1,0:T(8,128)(2,1)S(1)} %copy-done, bf16[128,256]{1,0:T(8,128)(2,1)S(1)} %get-tuple-element.17.refs_0_, bf16[128,256]{1,0:T(8,128)(2,1)S(1)} %collective-permute-done.4.refs_1_, ...), custom_call_target="tpu_custom_call" | custom-call | flops 104857600 | bytes 2048000 | tf_op jit(solution)/shard_map/pallas_call | solution.py:344
  35.0 0.1 collective-permute-start.7
  35.1 0.6 %shard_map.91.keep_ref = f32[64,3200]{1,0:T(8,128)S(1)} custom-call(bf16[64,256]{1,0:T(8,128)(2,1)S(1)} %get-tuple-element.21.grad_ref, bf16[3200,256]{1,0:T(8,128)(2,1)S(1)} %copy-done), custom_call_target="tpu_custom_call" | custom-call | flops 104857600 | bytes 2457600 | tf_op jit(solution)/shard_map/pallas_call | solution.py:352
  35.7 1.1 %collective-permute-done.7.other_ref = bf16[64,3200]{1,0:T(8,128)(2,1)S(1)} collective-permute-done((bf16[64,3200]{1,0:T(8,128)(2,1)S(1)}, bf16[64,3200]{1,0:T(8,128)(2,1)S(1)}, u32[]{:S(2)}, u32[]{:S(2)}) %collective-permute-start.7) | collective-permute-done | bytes 409632 | tf_op jit(solution)/shard_map/ppermute | solution.py:360
  36.8 0.1 shard_map.92
  36.9 1.6 %collective-permute-start.8 = (bf16[16,3200]{1,0:T(8,128)(2,1)S(1)}, bf16[16,3200]{1,0:T(8,128)(2,1)S(1)}, u32[]{:S(2)}, u32[]{:S(2)}) collective-permute-start(bf16[16,3200]{1,0:T(8,128)(2,1)S(1)} %get-tuple-element.25), channel_id=1, source_target_pairs={{0,1},{1,0},{8,9},{9,8},{16,17},{17,16},{24,25},{25,24},{2,3},{3,2... | collective-permute-start | bytes 307208 | tf_op jit(solution)/shard_map/ppermute | solution.py:370
  38.5 1.5 %collective-permute-start.9 = (bf16[16,3200]{1,0:T(8,128)(2,1)S(1)}, bf16[16,3200]{1,0:T(8,128)(2,1)S(1)}, u32[]{:S(2)}, u32[]{:S(2)}) collective-permute-start(bf16[16,3200]{1,0:T(8,128)(2,1)S(1)} %get-tuple-element.26), channel_id=1, source_target_pairs={{0,16},{1,17},{8,24},{9,25},{16,0},{17,1},{24,8},{25,9},{2,18},{3,... | collective-permute-start | bytes 307208 | tf_op jit(solution)/shard_map/ppermute | solution.py:370
  40.0 0.5 collective-permute-start.10
  40.5 1.4 %collective-permute-done.8.refs_0_ = bf16[16,3200]{1,0:T(8,128)(2,1)S(1)} collective-permute-done((bf16[16,3200]{1,0:T(8,128)(2,1)S(1)}, bf16[16,3200]{1,0:T(8,128)(2,1)S(1)}, u32[]{:S(2)}, u32[]{:S(2)}) %collective-permute-start.8) | collective-permute-done | bytes 102432 | tf_op jit(solution)/shard_map/ppermute | solution.py:370
  41.9 2.3 %collective-permute-done.9.refs_1_ = bf16[16,3200]{1,0:T(8,128)(2,1)S(1)} collective-permute-done((bf16[16,3200]{1,0:T(8,128)(2,1)S(1)}, bf16[16,3200]{1,0:T(8,128)(2,1)S(1)}, u32[]{:S(2)}, u32[]{:S(2)}) %collective-permute-start.9) | collective-permute-done | bytes 102432 | tf_op jit(solution)/shard_map/ppermute | solution.py:370
  44.2 1.3 %collective-permute-done.10.refs_2_ = bf16[16,3200]{1,0:T(8,128)(2,1)S(1)} collective-permute-done((bf16[16,3200]{1,0:T(8,128)(2,1)S(1)}, bf16[16,3200]{1,0:T(8,128)(2,1)S(1)}, u32[]{:S(2)}, u32[]{:S(2)}) %collective-permute-start.10) | collective-permute-done | bytes 102432 | tf_op jit(solution)/shard_map/ppermute | solution.py:370
  45.5 0.2 shard_map.93.refs_3_
  45.7 1.3 %collective-permute-start.15 = (bf16[16,3200]{1,0:T(8,128)(2,1)S(1)}, bf16[16,3200]{1,0:T(8,128)(2,1)S(1)}, u32[]{:S(2)}, u32[]{:S(2)}) collective-permute-start(bf16[16,3200]{1,0:T(8,128)(2,1)S(1)} %shard_map.93.refs_3_), channel_id=1, source_target_pairs={{0,1},{1,0},{8,9},{9,8},{16,17},{17,16},{24,25},{25,24},{2,3},{3,2... | collective-permute-start | bytes 307208 | tf_op jit(solution)/shard_map/ppermute | solution.py:381
  47.1 1.5 %collective-permute-start.13 = (bf16[16,3200]{1,0:T(8,128)(2,1)S(1)}, bf16[16,3200]{1,0:T(8,128)(2,1)S(1)}, u32[]{:S(2)}, u32[]{:S(2)}) collective-permute-start(bf16[16,3200]{1,0:T(8,128)(2,1)S(1)} %shard_map.93.refs_3_), channel_id=1, source_target_pairs={{0,16},{1,17},{8,24},{9,25},{16,0},{17,1},{24,8},{25,9},{2,18},{3,... | collective-permute-start | bytes 307208 | tf_op jit(solution)/shard_map/ppermute | solution.py:381
  48.5 0.7 %collective-permute-start.11 = (bf16[16,3200]{1,0:T(8,128)(2,1)S(1)}, bf16[16,3200]{1,0:T(8,128)(2,1)S(1)}, u32[]{:S(2)}, u32[]{:S(2)}) collective-permute-start(bf16[16,3200]{1,0:T(8,128)(2,1)S(1)} %shard_map.93.refs_3_), channel_id=1, source_target_pairs={{0,17},{1,16},{8,25},{9,24},{16,1},{17,0},{24,9},{25,8},{2,19},{3,... | collective-permute-start | bytes 307208 | tf_op jit(solution)/shard_map/ppermute | solution.py:381
  49.3 0.0 collective-permute-start.17
  49.3 2.1 %collective-permute-done.15.refs_2_ = bf16[16,3200]{1,0:T(8,128)(2,1)S(1)} collective-permute-done((bf16[16,3200]{1,0:T(8,128)(2,1)S(1)}, bf16[16,3200]{1,0:T(8,128)(2,1)S(1)}, u32[]{:S(2)}, u32[]{:S(2)}) %collective-permute-start.15) | collective-permute-done | bytes 102432 | tf_op jit(solution)/shard_map/ppermute | solution.py:381
  51.4 0.0 collective-permute-start.16
  51.4 0.5 collective-permute-done.13.refs_1_
  51.9 0.0 collective-permute-start.14
  51.9 2.2 %collective-permute-done.11.refs_0_ = bf16[16,3200]{1,0:T(8,128)(2,1)S(1)} collective-permute-done((bf16[16,3200]{1,0:T(8,128)(2,1)S(1)}, bf16[16,3200]{1,0:T(8,128)(2,1)S(1)}, u32[]{:S(2)}, u32[]{:S(2)}) %collective-permute-start.11) | collective-permute-done | bytes 102432 | tf_op jit(solution)/shard_map/ppermute | solution.py:381
  54.1 0.0 collective-permute-start.12
  54.1 0.8 %shard_map.94.refs_4_ = bf16[128,3200]{1,0:T(8,128)(2,1)} custom-call(bf16[16,3200]{1,0:T(8,128)(2,1)S(1)} %collective-permute-done.11.refs_0_, bf16[16,3200]{1,0:T(8,128)(2,1)S(1)} %collective-permute-done.13.refs_1_, bf16[16,3200]{1,0:T(8,128)(2,1)S(1)} %collective-permute-done.15.refs_2_, bf16[16,3200]{1,0:T(8,128)(2,1)S(1)} %shard_map.93.refs_3_), custom_call_target="tpu_custom_call" | custom-call | bytes 819200 | tf_op jit(solution)/shard_map/pallas_call | solution.py:386
  54.9 0.0 collective-permute-done.17.refs_3_
  54.9 0.0 collective-permute-done.16.refs_2_
  54.9 0.0 collective-permute-done.14.refs_1_
  54.9 0.5 collective-permute-done.12.refs_0_
  55.4 0.8 %shard_map.95 = bf16[128,3200]{1,0:T(8,128)(2,1)} custom-call(bf16[16,3200]{1,0:T(8,128)(2,1)S(1)} %collective-permute-done.12.refs_0_, bf16[16,3200]{1,0:T(8,128)(2,1)S(1)} %collective-permute-done.14.refs_1_, bf16[16,3200]{1,0:T(8,128)(2,1)S(1)} %collective-permute-done.16.refs_2_, ...), custom_call_target="tpu_custom_call", output_to_operand_aliasing={{}: (4, {})} | custom-call | bytes 819200 | tf_op jit(solution)/shard_map/pallas_call | solution.py:386
  (8 shorter events, 0.0 us)
Async XLA Ops:
  0.6 8.2 %copy-start.2 = (s32[8]{0:T(128)S(1)}, s32[8]{0:T(128)}, u32[]{:S(2)}) copy-start(s32[8]{0:T(128)} %pieces_ref.5) | copy-start | bytes 100
  0.6 8.9 %collective-permute-start = (bf16[128,256]{1,0:T(8,128)(2,1)}, bf16[128,256]{1,0:T(8,128)(2,1)S(1)}, u32[]{:S(2)}, u32[]{:S(2)}) collective-permute-start(bf16[128,256]{1,0:T(8,128)(2,1)} %param.11), channel_id=1, source_target_pairs={{0,6},{2,4},{4,0},{6,2},{1,7},{3,5},{5,1},{7,3},{8,14},{10,12},{12... | collective-permute-start | bytes 196616 | tf_op jit(solution)/shard_map/ppermute | solution.py:295
  5.7 0.7 %copy-start.1 = (f32[3200]{0:T(1024)S(1)}, f32[3200]{0:T(1024)}, u32[]{:S(2)}) copy-start(f32[3200]{0:T(1024)} %param.8) | copy-start | bytes 38404
  6.5 14.8 %copy-start.3 = (bf16[128,512]{1,0:T(8,128)(2,1)S(1)}, bf16[128,512]{1,0:T(8,128)(2,1)}, u32[]{:S(2)}) copy-start(bf16[128,512]{1,0:T(8,128)(2,1)} %q_ref.1) | copy-start | bytes 393220
  6.5 14.8 %copy-start.4 = (bf16[128,512]{1,0:T(8,128)(2,1)S(1)}, bf16[128,512]{1,0:T(8,128)(2,1)}, u32[]{:S(2)}) copy-start(bf16[128,512]{1,0:T(8,128)(2,1)} %g_ref.1) | copy-start | bytes 393220
  6.5 27.3 %copy-start = (bf16[3200,256]{1,0:T(8,128)(2,1)S(1)}, bf16[3200,256]{1,0:T(8,128)(2,1)}, u32[]{:S(2)}) copy-start(bf16[3200,256]{1,0:T(8,128)(2,1)} %proj_ref.3) | copy-start | bytes 4915204
  10.1 6.9 %collective-permute-start.3 = (bf16[128,256]{1,0:T(8,128)(2,1)S(1)}, bf16[128,256]{1,0:T(8,128)(2,1)S(1)}, u32[]{:S(2)}, u32[]{:S(2)}) collective-permute-start(bf16[128,256]{1,0:T(8,128)(2,1)S(1)} %shard_map.88.refs_0_), channel_id=1, source_target_pairs={{0,6},{2,0},{4,4},{6,2},{1,7},{3,1},{5,5},{7,3},{8,14},{10,8},{12,... | collective-permute-start | bytes 196616 | tf_op jit(solution)/shard_map/ppermute | solution.py:331
  14.5 2.6 %collective-permute-start.2 = (bf16[128,256]{1,0:T(8,128)(2,1)S(1)}, bf16[128,256]{1,0:T(8,128)(2,1)S(1)}, u32[]{:S(2)}, u32[]{:S(2)}) collective-permute-start(bf16[128,256]{1,0:T(8,128)(2,1)S(1)} %shard_map.88.refs_0_), channel_id=1, source_target_pairs={{0,0},{2,2},{4,6},{6,4},{1,1},{3,3},{5,7},{7,5},{8,8},{10,10},{12,... | collective-permute-start | bytes 196616 | tf_op jit(solution)/shard_map/ppermute | solution.py:331
  15.2 6.1 %collective-permute-start.1 = (bf16[128,256]{1,0:T(8,128)(2,1)S(1)}, bf16[128,256]{1,0:T(8,128)(2,1)S(1)}, u32[]{:S(2)}, u32[]{:S(2)}) collective-permute-start(bf16[128,256]{1,0:T(8,128)(2,1)S(1)} %shard_map.88.refs_0_), channel_id=1, source_target_pairs={{0,4},{2,6},{4,2},{6,0},{1,5},{3,7},{5,3},{7,1},{8,12},{10,14},{12... | collective-permute-start | bytes 196616 | tf_op jit(solution)/shard_map/ppermute | solution.py:331
  23.3 5.2 %collective-permute-start.4 = (bf16[128,256]{1,0:T(8,128)(2,1)S(1)}, bf16[128,256]{1,0:T(8,128)(2,1)S(1)}, u32[]{:S(2)}, u32[]{:S(2)}) collective-permute-start(bf16[128,256]{1,0:T(8,128)(2,1)S(1)} %get-tuple-element.18), channel_id=1, source_target_pairs={{4,0},{6,2},{2,4},{0,6},{5,1},{7,3},{3,5},{1,7},{12,8},{14,10},{10... | collective-permute-start | bytes 196616 | tf_op jit(solution)/shard_map/ppermute | solution.py:341
  24.0 4.5 %collective-permute-start.5 = (bf16[128,256]{1,0:T(8,128)(2,1)S(1)}, bf16[128,256]{1,0:T(8,128)(2,1)S(1)}, u32[]{:S(2)}, u32[]{:S(2)}) collective-permute-start(bf16[128,256]{1,0:T(8,128)(2,1)S(1)} %get-tuple-element.19), channel_id=1, source_target_pairs={{0,0},{2,2},{6,4},{4,6},{1,1},{3,3},{7,5},{5,7},{8,8},{10,10},{14,... | collective-permute-start | bytes 196616 | tf_op jit(solution)/shard_map/ppermute | solution.py:341
  24.6 9.1 %collective-permute-start.6 = (bf16[128,256]{1,0:T(8,128)(2,1)S(1)}, bf16[128,256]{1,0:T(8,128)(2,1)S(1)}, u32[]{:S(2)}, u32[]{:S(2)}) collective-permute-start(bf16[128,256]{1,0:T(8,128)(2,1)S(1)} %get-tuple-element.20), channel_id=1, source_target_pairs={{6,0},{0,2},{4,4},{2,6},{7,1},{1,3},{5,5},{3,7},{14,8},{8,10},{12,... | collective-permute-start | bytes 196616 | tf_op jit(solution)/shard_map/ppermute | solution.py:341
  35.0 1.8 %collective-permute-start.7 = (bf16[64,3200]{1,0:T(8,128)(2,1)S(1)}, bf16[64,3200]{1,0:T(8,128)(2,1)S(1)}, u32[]{:S(2)}, u32[]{:S(2)}) collective-permute-start(bf16[64,3200]{1,0:T(8,128)(2,1)S(1)} %get-tuple-element.22), channel_id=1, source_target_pairs={{0,8},{1,9},{8,0},{9,1},{16,24},{17,25},{24,16},{25,17},{2,10},{3,... | collective-permute-start | bytes 1228808 | tf_op jit(solution)/shard_map/ppermute | solution.py:360
  36.9 5.0 %collective-permute-start.8 = (bf16[16,3200]{1,0:T(8,128)(2,1)S(1)}, bf16[16,3200]{1,0:T(8,128)(2,1)S(1)}, u32[]{:S(2)}, u32[]{:S(2)}) collective-permute-start(bf16[16,3200]{1,0:T(8,128)(2,1)S(1)} %get-tuple-element.25), channel_id=1, source_target_pairs={{0,1},{1,0},{8,9},{9,8},{16,17},{17,16},{24,25},{25,24},{2,3},{3,2... | collective-permute-start | bytes 307208 | tf_op jit(solution)/shard_map/ppermute | solution.py:370
  38.5 5.7 %collective-permute-start.9 = (bf16[16,3200]{1,0:T(8,128)(2,1)S(1)}, bf16[16,3200]{1,0:T(8,128)(2,1)S(1)}, u32[]{:S(2)}, u32[]{:S(2)}) collective-permute-start(bf16[16,3200]{1,0:T(8,128)(2,1)S(1)} %get-tuple-element.26), channel_id=1, source_target_pairs={{0,16},{1,17},{8,24},{9,25},{16,0},{17,1},{24,8},{25,9},{2,18},{3,... | collective-permute-start | bytes 307208 | tf_op jit(solution)/shard_map/ppermute | solution.py:370
  40.0 5.6 %collective-permute-start.10 = (bf16[16,3200]{1,0:T(8,128)(2,1)S(1)}, bf16[16,3200]{1,0:T(8,128)(2,1)S(1)}, u32[]{:S(2)}, u32[]{:S(2)}) collective-permute-start(bf16[16,3200]{1,0:T(8,128)(2,1)S(1)} %get-tuple-element.27), channel_id=1, source_target_pairs={{0,17},{1,16},{8,25},{9,24},{16,1},{17,0},{24,9},{25,8},{2,19},{3,... | collective-permute-start | bytes 307208 | tf_op jit(solution)/shard_map/ppermute | solution.py:370
  45.7 5.6 %collective-permute-start.15 = (bf16[16,3200]{1,0:T(8,128)(2,1)S(1)}, bf16[16,3200]{1,0:T(8,128)(2,1)S(1)}, u32[]{:S(2)}, u32[]{:S(2)}) collective-permute-start(bf16[16,3200]{1,0:T(8,128)(2,1)S(1)} %shard_map.93.refs_3_), channel_id=1, source_target_pairs={{0,1},{1,0},{8,9},{9,8},{16,17},{17,16},{24,25},{25,24},{2,3},{3,2... | collective-permute-start | bytes 307208 | tf_op jit(solution)/shard_map/ppermute | solution.py:381
  47.1 4.8 %collective-permute-start.13 = (bf16[16,3200]{1,0:T(8,128)(2,1)S(1)}, bf16[16,3200]{1,0:T(8,128)(2,1)S(1)}, u32[]{:S(2)}, u32[]{:S(2)}) collective-permute-start(bf16[16,3200]{1,0:T(8,128)(2,1)S(1)} %shard_map.93.refs_3_), channel_id=1, source_target_pairs={{0,16},{1,17},{8,24},{9,25},{16,0},{17,1},{24,8},{25,9},{2,18},{3,... | collective-permute-start | bytes 307208 | tf_op jit(solution)/shard_map/ppermute | solution.py:381
  48.5 5.6 %collective-permute-start.11 = (bf16[16,3200]{1,0:T(8,128)(2,1)S(1)}, bf16[16,3200]{1,0:T(8,128)(2,1)S(1)}, u32[]{:S(2)}, u32[]{:S(2)}) collective-permute-start(bf16[16,3200]{1,0:T(8,128)(2,1)S(1)} %shard_map.93.refs_3_), channel_id=1, source_target_pairs={{0,17},{1,16},{8,25},{9,24},{16,1},{17,0},{24,9},{25,8},{2,19},{3,... | collective-permute-start | bytes 307208 | tf_op jit(solution)/shard_map/ppermute | solution.py:381
  49.3 5.6 %collective-permute-start.17 = (bf16[16,3200]{1,0:T(8,128)(2,1)S(1)}, bf16[16,3200]{1,0:T(8,128)(2,1)S(1)}, u32[]{:S(2)}, u32[]{:S(2)}) collective-permute-start(bf16[16,3200]{1,0:T(8,128)(2,1)S(1)} %shard_map.93.refs_3_), channel_id=1, source_target_pairs={{0,8},{1,9},{8,0},{9,1},{16,24},{17,25},{24,16},{25,17},{2,10},{3,... | collective-permute-start | bytes 307208 | tf_op jit(solution)/shard_map/ppermute | solution.py:382
  51.4 3.5 %collective-permute-start.16 = (bf16[16,3200]{1,0:T(8,128)(2,1)S(1)}, bf16[16,3200]{1,0:T(8,128)(2,1)S(1)}, u32[]{:S(2)}, u32[]{:S(2)}) collective-permute-start(bf16[16,3200]{1,0:T(8,128)(2,1)S(1)} %collective-permute-done.15.refs_2_), channel_id=1, source_target_pairs={{0,8},{1,9},{8,0},{9,1},{16,24},{17,25},{24,16},{25,17},{2,10},{3,... | collective-permute-start | bytes 307208 | tf_op jit(solution)/shard_map/ppermute | solution.py:382
  51.9 3.0 %collective-permute-start.14 = (bf16[16,3200]{1,0:T(8,128)(2,1)S(1)}, bf16[16,3200]{1,0:T(8,128)(2,1)S(1)}, u32[]{:S(2)}, u32[]{:S(2)}) collective-permute-start(bf16[16,3200]{1,0:T(8,128)(2,1)S(1)} %collective-permute-done.13.refs_1_), channel_id=1, source_target_pairs={{0,8},{1,9},{8,0},{9,1},{16,24},{17,25},{24,16},{25,17},{2,10},{3,... | collective-permute-start | bytes 307208 | tf_op jit(solution)/shard_map/ppermute | solution.py:382
  54.1 1.3 %collective-permute-start.12 = (bf16[16,3200]{1,0:T(8,128)(2,1)S(1)}, bf16[16,3200]{1,0:T(8,128)(2,1)S(1)}, u32[]{:S(2)}, u32[]{:S(2)}) collective-permute-start(bf16[16,3200]{1,0:T(8,128)(2,1)S(1)} %collective-permute-done.11.refs_0_), channel_id=1, source_target_pairs={{0,8},{1,9},{8,0},{9,1},{16,24},{17,25},{24,16},{25,17},{2,10},{3,... | collective-permute-start | bytes 307208 | tf_op jit(solution)/shard_map/ppermute | solution.py:382

commit v8 on v6

--- a/solution.py
+++ b/solution.py
@@ -1,4 +1,5 @@
 import functools
+import itertools
 import math
 
 import jax
@@ -25,6 +26,35 @@
 def held_image(block, count):
     half = count // 2
     return jnp.where(block < half, block + half, lax.rem(block + half - 1, half))
+
+
+def flows(rounds, count):
+    load = [0] * (2 * count)
+    for pairs in rounds:
+        for s, t in enumerate(pairs):
+            for k in range(min(s, t), max(s, t)):
+                load[2 * k + (t > s)] += 1
+    return max(load), sum(load)
+
+
+def rounds_of(edges, count):
+    best = [tuple(d ^ r for d in range(count)) for r in range(count - 1, 0, -1)]
+    if count > 4:
+        return best
+    whole = [p for p in itertools.permutations(range(count)) if all(s != t for s, t in enumerate(p))]
+    for size in range(1, count):
+        found = [c for c in itertools.combinations(whole, size) if all(any(p[s] == t for p in c) for s, t in edges)]
+        if found:
+            far = lambda p: max(abs(s - t) for s, t in enumerate(p))
+            return sorted(min(found, key=lambda c: flows(c, count)), key=far)
+    return best
+
+
+def pick_static(table, index):
+    value = jnp.int32(table[0])
+    for n in range(1, len(table)):
+        value = jnp.where(index == n, table[n], value)
+    return value
 
 
 def group_place():
@@ -100,46 +130,83 @@
     out_ref[...] = jnp.where(row < before, text, image).astype(jnp.bfloat16)
 
 
-def attend_body(seq_n, q_ref, g_ref, *refs):
-    block_refs, out_ref, grad_refs = refs[:seq_n], refs[seq_n], refs[seq_n + 1 :]
+def heads_of(ref, heads):
+    return jnp.concatenate([ref[:, h * HD : (h + 1) * HD] for h in heads], axis=0)
+
+
+def head_groups(group, keys):
+    together = group if keys <= 1024 else 1
+    return [range(first, first + together) for first in range(0, group, together)]
+
+
+def grad_parts(chosen, rows, scale, low_ref, dscore_ref, q_ref, g_ref, grad_refs):
+    totals = [None] * len(chosen)
+    for heads in head_groups(q_ref.shape[1] // HD, low_ref.shape[0]):
+        q, g = heads_of(q_ref, heads), heads_of(g_ref, heads)
+        span = slice(heads[0] * rows, (heads[-1] + 1) * rows)
+        for n, r in enumerate(chosen):
+            part = slice(r * rows, (r + 1) * rows)
+            dkeys = jnp.dot(dscore_ref[part, span], q, preferred_element_type=jnp.float32)
+            dvalues = jnp.dot(low_ref[part, span], g, preferred_element_type=jnp.float32)
+            if totals[n] is not None:
+                dkeys, dvalues = totals[n][0] + dkeys, totals[n][1] + dvalues
+            totals[n] = dkeys, dvalues
+    for (dkeys, dvalues), ref in zip(totals, grad_refs):
+        ref[:, :HD] = (dkeys * scale).astype(jnp.bfloat16)
+        ref[:, HD:] = dvalues.astype(jnp.bfloat16)
+
+
+def weigh_body(seq_n, tables, early, pieces_ref, q_ref, g_ref, text_ref, own_ref, raw_ref, *refs):
+    count = len(tables)
+    block_refs, (low_ref, dscore_ref, values_ref) = refs[:count], refs[count : count + 3]
+    grad_refs = refs[count + 3 :]
     rows = q_ref.shape[0]
     group = q_ref.shape[1] // HD
     scale = 1.0 / math.sqrt(HD)
     me = lax.axis_index("seq")
-    kv = jnp.concatenate([ref[...] for ref in block_refs], axis=0)
+    before = pieces_ref[2 * me]
+    ahead = lax.broadcasted_iota(jnp.int32, (rows, rows), 0) - lax.broadcasted_iota(jnp.int32, (rows, rows), 1)
+    pick = jnp.where(ahead == before, 1.0, 0.0).astype(jnp.bfloat16)
+    placed = jnp.dot(pick, raw_ref[...], preferred_element_type=jnp.float32)
+    row = lax.broadcasted_iota(jnp.int32, placed.shape, 0)
+    mine = jnp.where(row < before, text_ref[...].astype(jnp.float32), placed).astype(jnp.bfloat16)
+    kv = jnp.concatenate([own_ref[...], mine] + [ref[...] for ref in block_refs], axis=0)
     keys, values = kv[:, :HD], kv[:, HD:]
-    together = group if kv.shape[0] <= 1024 else 1
-    span = together * rows
-    offset = lax.broadcasted_iota(jnp.int32, (rows, span), 0)
-    offset = offset - lax.rem(lax.broadcasted_iota(jnp.int32, (rows, span), 1), rows)
-    masks = [offset <= (me - held_image(me ^ r, seq_n)) * rows for r in range(seq_n)]
-    key_total = value_total = None
-    for first in range(0, group, together):
-        heads = range(first, first + together)
-        q = jnp.concatenate([q_ref[:, h * HD : (h + 1) * HD] for h in heads], axis=0)
-        g = jnp.concatenate([g_ref[:, h * HD : (h + 1) * HD] for h in heads], axis=0)
+    values_ref[...] = values
+    images = [held_image(me, seq_n), me] + [pick_static(table, me) for table in tables]
+    for heads in head_groups(group, kv.shape[0]):
+        q, g = heads_of(q_ref, heads), heads_of(g_ref, heads)
+        offset = lax.broadcasted_iota(jnp.int32, (rows, q.shape[0]), 0)
+        offset = offset - lax.rem(lax.broadcasted_iota(jnp.int32, (rows, q.shape[0]), 1), rows)
         scores = dot(keys, q, ((1,), (1,)))
         scores = jnp.concatenate(
-            [jnp.where(mask, scores[n * rows : (n + 1) * rows], NEG) for n, mask in enumerate(masks)], axis=0
+            [
+                jnp.where(offset <= (me - image) * rows, scores[n * rows : (n + 1) * rows], NEG)
+                for n, image in enumerate(images)
+            ],
+            axis=0,
         )
         top = jnp.max(scores, axis=0, keepdims=True)
         weights = jnp.exp2((scores - top) * (scale * math.log2(math.e)))
         weights = weights * (1.0 / jnp.sum(weights, axis=0, keepdims=True))
         low = weights.astype(jnp.bfloat16)
-        mixed = dot(values, low, ((0,), (0,)))
         dprob = dot(values, g, ((1,), (1,)))
         drift = jnp.sum(low.astype(jnp.float32) * dprob, axis=0, keepdims=True)
-        dscore = (weights * (dprob - drift)).astype(jnp.bfloat16)
-        dkeys = jnp.dot(dscore, q, preferred_element_type=jnp.float32)
-        dvalues = jnp.dot(low, g, preferred_element_type=jnp.float32)
-        key_total = dkeys if key_total is None else key_total + dkeys
-        value_total = dvalues if value_total is None else value_total + dvalues
+        span = slice(heads[0] * rows, (heads[-1] + 1) * rows)
+        low_ref[:, span] = low
+        dscore_ref[:, span] = (weights * (dprob - drift)).astype(jnp.bfloat16)
+    grad_parts(early, rows, scale, low_ref, dscore_ref, q_ref, g_ref, grad_refs)
+
+
+def mix_body(late, q_ref, g_ref, low_ref, dscore_ref, values_ref, out_ref, *grad_refs):
+    rows = q_ref.shape[0]
+    grad_parts(late, rows, 1.0 / math.sqrt(HD), low_ref, dscore_ref, q_ref, g_ref, grad_refs)
+    for heads in head_groups(q_ref.shape[1] // HD, low_ref.shape[0]):
+        span = slice(heads[0] * rows, (heads[-1] + 1) * rows)
+        mixed = dot(values_ref[...], low_ref[:, span], ((0,), (0,)))
         for n, h in enumerate(heads):
             part = jnp.transpose(mixed[:, n * rows : (n + 1) * rows])
             out_ref[:, h * HD : (h + 1) * HD] = part.astype(jnp.bfloat16)
-    for r, ref in enumerate(grad_refs):
-        ref[:, :HD] = (key_total[r * rows : (r + 1) * rows] * scale).astype(jnp.bfloat16)
-        ref[:, HD:] = value_total[r * rows : (r + 1) * rows].astype(jnp.bfloat16)
 
 
 def back_body(seq_n, piece, pieces_ref, proj_ref, *refs):
@@ -191,14 +258,13 @@
         out_ref[:, c : c + HD] = (scaled[n] * inverse - own * lead).astype(jnp.bfloat16)
 
 
-def gather_body(count, *refs):
-    part_refs, out_hbm, sems = refs[: 2 * count], refs[2 * count], refs[2 * count + 1]
+def gather_body(count, core, *refs):
+    part_refs, (out_hbm, sems) = refs[:count], refs[-2:]
     piece = part_refs[0].shape[0]
     parity, place = group_place()
     copies = []
     for n, ref in enumerate(part_refs):
-        core, step = n // count, count - 1 - n % count
-        row = ((parity ^ core) * count + (place ^ step)) * piece
+        row = ((parity ^ core) * count + (place ^ (count - 1 - n))) * piece
         copy = pltpu.make_async_copy(ref, out_hbm.at[pl.ds(pl.multiple_of(row, piece), piece), :], sems.at[n])
         copy.start()
         copies.append(copy)
@@ -227,9 +293,20 @@
         return pairs
 
     gain = vis_gain.reshape(width // HD, HD)
-    far = sorted(range(1, seq_n), reverse=True)
-    partners = {r: [(d, d ^ r) for d in range(seq_n)] for r in far}
-    text = lax.ppermute(text_kv, "seq", [(j, owner_block(j, seq_n)) for j in range(seq_n)])
+    owners = [owner_block(j, seq_n) for j in range(seq_n)]
+    held = [owners.index(b) for b in range(seq_n)]
+    home = [(owners[j], j) for j in range(seq_n)]
+    edges = {(owners[j], d) for j in range(seq_n) for d in range(j + 1, seq_n) if owners[j] != d}
+    tables, forth, left = [], [], set(edges)
+    for pairs in rounds_of(sorted(edges), seq_n):
+        table = [seq_n] * seq_n
+        for s, t in enumerate(pairs):
+            if (s, t) in left:
+                table[t] = held[s]
+        left -= set(enumerate(pairs))
+        tables.append(table)
+        forth.append(list(enumerate(pairs)))
+    text = lax.ppermute(text_kv, "seq", list(enumerate(owners)))
     chunks = len(cuts(width))
     hbm = pl.BlockSpec(memory_space=pltpu.HBM)
     image_kv, own_rows = call(
@@ -249,6 +326,7 @@
             pltpu.SemaphoreType.DMA,
         ],
     )(vis_rows, gain, key_value_proj)
+    raw = lax.ppermute(image_kv, "seq", home)
     shifted = call(
         functools.partial(shift_body, seq_n),
         jax.ShapeDtypeStruct((rows, columns), bf16),
@@ -265,26 +343,38 @@
         0,
         6 * rows * columns,
     )(pieces, shifted, text)
-    blocks = {r: lax.ppermute(block, "seq", partners[r]) for r in far}
-    attended, *grads = call(
-        functools.partial(attend_body, seq_n),
-        [jax.ShapeDtypeStruct(queries.shape, bf16)] + [jax.ShapeDtypeStruct((rows, columns), bf16)] * seq_n,
-        [WHOLE] * (2 + seq_n),
-        [WHOLE] * (1 + seq_n),
-        10 * seq_n * rows * rows * queries.shape[1],
-        6 * rows * queries.shape[1] + 4 * seq_n * rows * columns,
-    )(queries, grad_out, block, *[blocks[r] for r in range(1, seq_n)])
-    parts = {r: lax.ppermute(grads[r], "seq", partners[r]) for r in far}
-    parts[0] = grads[0]
+    blocks = [lax.ppermute(block, "seq", pairs) for pairs in forth]
+    total = 2 + len(blocks)
+    early, late = list(range(1, total)), [0]
+    kv_shape = jax.ShapeDtypeStruct((rows, columns), bf16)
+    wide_shape = jax.ShapeDtypeStruct((total * rows, queries.shape[1] // HD * rows), bf16)
+    low, dscore, values, *grads = call(
+        functools.partial(weigh_body, seq_n, tables, early),
+        [wide_shape, wide_shape, jax.ShapeDtypeStruct((total * rows, HD), bf16)] + [kv_shape] * len(early),
+        [SCALARS] + [WHOLE] * (3 + total),
+        [WHOLE] * (3 + len(early)),
+        8 * total * rows * rows * queries.shape[1],
+        4 * rows * queries.shape[1] + 4 * total * rows * columns,
+    )(pieces, queries, grad_out, text_kv, block, raw, *blocks)
+    attended, own_grad = call(
+        functools.partial(mix_body, late),
+        [jax.ShapeDtypeStruct(queries.shape, bf16)] + [kv_shape] * len(late),
+        [WHOLE] * 5,
+        [WHOLE] * (1 + len(late)),
+        2 * total * rows * rows * queries.shape[1],
+        6 * rows * queries.shape[1] + 4 * total * rows * columns,
+    )(queries, grad_out, low, dscore, values)
+    back = list(zip(grads, [home] + forth))
+    parts = [lax.ppermute(g, "seq", [(t, s) for s, t in pairs]) for g, pairs in back[:1] + back[:0:-1]]
 
     keep, send = call(
         functools.partial(back_body, seq_n, piece),
         [jax.ShapeDtypeStruct((rows // 2, width), f32), jax.ShapeDtypeStruct((rows // 2, width), bf16)],
-        [SCALARS] + [WHOLE] * (1 + seq_n),
+        [SCALARS] + [WHOLE] * (2 + len(parts)),
         [WHOLE, WHOLE],
         2 * rows * width * columns,
         2 * width * columns + 3 * rows * width,
-    )(pieces, key_value_proj, parts[0], *[parts[r] for r in far])
+    )(pieces, key_value_proj, own_grad, *parts)
     other = lax.ppermute(send, names, core_pairs)
     steps = list(range(1, count))
     own_sum, *sends = call(
@@ -295,7 +385,7 @@
         0,
         6 * rows // 2 * width,
     )(keep, other)
-    shares = [lax.ppermute(sends[d - 1], names, far_pairs(d)) for d in steps]
+    shares = [lax.ppermute(sends[d - 1], names, far_pairs(d)) for d in steps[::-1]]
     mine = call(
         final_body,
         jax.ShapeDtypeStruct((piece, width), bf16),
@@ -308,15 +398,19 @@
     for d in steps:
         mines[d] = lax.ppermute(mine, names, far_pairs(d))
     theirs = {d: lax.ppermute(mines[d], names, core_pairs) for d in range(count)}
-    vis_grad = call(
-        functools.partial(gather_body, count),
-        jax.ShapeDtypeStruct((rows, width), bf16),
-        [WHOLE] * n,
-        hbm,
-        0,
-        4 * rows * width,
-        scratch_shapes=[pltpu.SemaphoreType.DMA((n,))],
-    )(*[mines[d] for d in reversed(range(count))], *[theirs[d] for d in reversed(range(count))])
+    vis_grad = None
+    for core, parts in enumerate((mines, theirs)):
+        done = [] if vis_grad is None else [vis_grad]
+        vis_grad = call(
+            functools.partial(gather_body, count, core),
+            jax.ShapeDtypeStruct((rows, width), bf16),
+            [WHOLE] * count + [hbm] * len(done),
+            hbm,
+            0,
+            2 * rows * width,
+            scratch_shapes=[pltpu.SemaphoreType.DMA((count,))],
+            input_output_aliases={count: 0} if done else {},
+        )(*[parts[d] for d in reversed(range(count))], *done)
     return (attended, vis_grad)
 
 

time: 50.7 us -> 50.5 us (level)
  Pallas kernels: 8.12 us -> 9.51 us
  starting transfers between devices: 21.1 us -> 19.9 us
    pallas_call x2 -> x4, Pallas kernels: 2.92 us -> 4.41 us  [the longest x1 1.85 us: on_device(): call(functools.partial(weigh_body, seq_n, tables, early), [wide_shape, wi...]
    ppermute x10, starting transfers between devices: 17.5 us -> 16.2 us  [the longest x1 5.1 us: on_device(): text = lax.ppermute(text_kv, 'seq', list(enumerate(owners)))]
    ppermute x4, waiting for transfers between devices: 1.29 us -> 0.49 us  [on_device(): lax.ppermute(mines[d], names, core_pairs)]
  transfers between devices with their start and end apart: 18 -> 18, of which waited for: 12 -> 12; matrix products, arithmetic and copies ran while one was open for 0% -> 0% of each run, Pallas kernels for 6% -> 11%
where the time goes in v8:
time: 50.5 us; the launch traced here: 50.2 us
  starting transfers between devices  19.9 us (39%)
  waiting for transfers between devices  19.3 us (38%)
  Pallas kernels  9.51 us (19%)
  between operations  0.78 us (2%)
  local copies, waits for them, and re-layouts  0.74 us (1%)
    ppermute x1, starting transfers between devices, on_device(): text = lax.ppermute(text_kv, 'seq', list(enumerate(owners)))  5.1 us
    ppermute x3, waiting for transfers between devices, on_device(): mines[d] = lax.ppermute(mine, names, far_pairs(d))  5 us
    ppermute x3, waiting for transfers between devices, on_device(): lax.ppermute(sends[d - 1], names, far_pairs(d))  4.59 us
    ppermute x2, starting transfers between devices, on_device(): blocks = [lax.ppermute(block, 'seq', pairs) for pairs in forth]  3.86 us
    ppermute x3, starting transfers between devices, on_device(): lax.ppermute(g, 'seq', [(t, s) for s, t in pairs])  3.68 us
    ppermute x3, starting transfers between devices, on_device(): lax.ppermute(sends[d - 1], names, far_pairs(d))  3.55 us
    ppermute x3, starting transfers between devices, on_device(): mines[d] = lax.ppermute(mine, names, far_pairs(d))  3.55 us
    ppermute x3, waiting for transfers between devices, on_device(): lax.ppermute(g, 'seq', [(t, s) for s, t in pairs])  3.25 us
  transfers between devices with their start and end apart: 18, of which 12 were waited for; matrix products, arithmetic and copies ran while one was open for 0% of the time, Pallas kernels for 11%

profile of v8, /device:TPU:0, one launch (start us, length us, event | category | flops | bytes accessed | tf_op | source)
XLA Modules:
  0.0 50.2 jit_solution(2312516056628971888)
XLA Ops:
  0.7 5.1 %collective-permute-start = (bf16[128,256]{1,0:T(8,128)(2,1)}, bf16[128,256]{1,0:T(8,128)(2,1)S(1)}, u32[]{:S(2)}, u32[]{:S(2)}) collective-permute-start(bf16[128,256]{1,0:T(8,128)(2,1)} %text_ref.1), channel_id=1, source_target_pairs={{0,6},{2,4},{4,0},{6,2},{1,7},{3,5},{5,1},{7,3},{8,14},{10,12},{12... | collective-permute-start | bytes 196616 | tf_op jit(solution)/shard_map/ppermute | solution.py:309
  5.8 0.7 %copy-done.3 = f32[3200]{0:T(1024)S(1)} copy-done((f32[3200]{0:T(1024)S(1)}, f32[3200]{0:T(1024)}, u32[]{:S(2)}) %copy-start.3) | copy-done | bytes 12824
  6.5 2.3 %shard_map.86 = (bf16[128,256]{1,0:T(8,128)(2,1)S(1)}, bf16[16,3200]{1,0:T(8,128)(2,1)S(1)}) custom-call(bf16[128,3200]{1,0:T(8,128)(2,1)} %vis_hbm.1, f32[25,128]{1,0:T(8,128)S(1)} %bitcast.1, bf16[3200,256]{1,0:T(8,128)(2,1)} %proj_ref.1), custom_call_target="tpu_custom_call" | custom-call | flops 209715200 | bytes 2457600 | tf_op jit(solution)/shard_map/pallas_call | solution.py:312
  8.7 0.0 copy-start
  8.8 0.1 collective-permute-start.1
  8.8 0.7 %shard_map.87.image_ref = bf16[128,256]{1,0:T(8,128)(2,1)S(1)} custom-call(s32[8]{0:T(128)S(1)} %copy-done.4, bf16[128,256]{1,0:T(8,128)(2,1)S(1)} %get-tuple-element.18.image_ref), custom_call_target="tpu_custom_call" | custom-call | flops 8388608 | bytes 131072 | tf_op jit(solution)/shard_map/pallas_call | solution.py:330
  9.5 0.0 collective-permute-done.text_ref
  9.5 0.6 %shard_map.88.own_ref = bf16[128,256]{1,0:T(8,128)(2,1)S(1)} custom-call(s32[8]{0:T(128)S(1)} %copy-done.4, bf16[128,256]{1,0:T(8,128)(2,1)S(1)} %shard_map.87.image_ref, bf16[128,256]{1,0:T(8,128)(2,1)S(1)} %collective-permute-done.text_ref), custom_call_target="tpu_custom_call" | custom-call | bytes 196608 | tf_op jit(solution)/shard_map/pallas_call | solution.py:338
  10.1 3.9 %collective-permute-start.3 = (bf16[128,256]{1,0:T(8,128)(2,1)S(1)}, bf16[128,256]{1,0:T(8,128)(2,1)S(1)}, u32[]{:S(2)}, u32[]{:S(2)}) collective-permute-start(bf16[128,256]{1,0:T(8,128)(2,1)S(1)} %shard_map.88.own_ref), channel_id=1, source_target_pairs={{0,6},{2,4},{4,0},{6,2},{1,7},{3,5},{5,1},{7,3},{8,14},{10,12},{12... | collective-permute-start | bytes 196616 | tf_op jit(solution)/shard_map/ppermute | solution.py:346
  14.0 0.0 collective-permute-start.2
  14.0 1.6 %collective-permute-done.1.raw_ref = bf16[128,256]{1,0:T(8,128)(2,1)S(1)} collective-permute-done((bf16[128,256]{1,0:T(8,128)(2,1)S(1)}, bf16[128,256]{1,0:T(8,128)(2,1)S(1)}, u32[]{:S(2)}, u32[]{:S(2)}) %collective-permute-start.1) | collective-permute-done | bytes 65568 | tf_op jit(solution)/shard_map/ppermute | solution.py:329
  15.6 1.4 %collective-permute-done.3.refs_1_ = bf16[128,256]{1,0:T(8,128)(2,1)S(1)} collective-permute-done((bf16[128,256]{1,0:T(8,128)(2,1)S(1)}, bf16[128,256]{1,0:T(8,128)(2,1)S(1)}, u32[]{:S(2)}, u32[]{:S(2)}) %collective-permute-start.3) | collective-permute-done | bytes 65568 | tf_op jit(solution)/shard_map/ppermute | solution.py:346
  17.0 1.3 %collective-permute-done.2.refs_0_ = bf16[128,256]{1,0:T(8,128)(2,1)S(1)} collective-permute-done((bf16[128,256]{1,0:T(8,128)(2,1)S(1)}, bf16[128,256]{1,0:T(8,128)(2,1)S(1)}, u32[]{:S(2)}, u32[]{:S(2)}) %collective-permute-start.2) | collective-permute-done | bytes 65568 | tf_op jit(solution)/shard_map/ppermute | solution.py:346
  18.3 1.8 %shard_map.89 = (bf16[512,512]{1,0:T(8,128)(2,1)S(1)}, bf16[512,512]{1,0:T(8,128)(2,1)S(1)}, bf16[512,128]{1,0:T(8,128)(2,1)S(1)}, bf16[128,256]{1,0:T(8,128)(2,...) custom-call(s32[8]{0:T(128)S(1)} %copy-done.4, bf16[128,512]{1,0:T(8,128)(2,1)S(1)} %copy-done.1, ...), custom_call_target="tpu_custom_call" | custom-call | flops 268435456 | bytes 786432 | tf_op jit(solution)/shard_map/pallas_call | solution.py:351
  20.1 1.9 %collective-permute-start.4 = (bf16[128,256]{1,0:T(8,128)(2,1)S(1)}, bf16[128,256]{1,0:T(8,128)(2,1)S(1)}, u32[]{:S(2)}, u32[]{:S(2)}) collective-permute-start(bf16[128,256]{1,0:T(8,128)(2,1)S(1)} %get-tuple-element.24), channel_id=1, source_target_pairs={{0,6},{2,4},{4,0},{6,2},{1,7},{3,5},{5,1},{7,3},{8,14},{10,12},{12... | collective-permute-start | bytes 196616 | tf_op jit(solution)/shard_map/ppermute | solution.py:368
  22.0 1.1 %collective-permute-start.5 = (bf16[128,256]{1,0:T(8,128)(2,1)S(1)}, bf16[128,256]{1,0:T(8,128)(2,1)S(1)}, u32[]{:S(2)}, u32[]{:S(2)}) collective-permute-start(bf16[128,256]{1,0:T(8,128)(2,1)S(1)} %get-tuple-element.25), channel_id=1, source_target_pairs={{6,0},{4,2},{0,4},{2,6},{7,1},{5,3},{1,5},{3,7},{14,8},{12,10},{8,... | collective-permute-start | bytes 196616 | tf_op jit(solution)/shard_map/ppermute | solution.py:368
  23.1 0.7 %collective-permute-start.6 = (bf16[128,256]{1,0:T(8,128)(2,1)S(1)}, bf16[128,256]{1,0:T(8,128)(2,1)S(1)}, u32[]{:S(2)}, u32[]{:S(2)}) collective-permute-start(bf16[128,256]{1,0:T(8,128)(2,1)S(1)} %get-tuple-element.26), channel_id=1, source_target_pairs={{2,0},{0,2},{6,4},{4,6},{3,1},{1,3},{7,5},{5,7},{10,8},{8,10},{14,... | collective-permute-start | bytes 196616 | tf_op jit(solution)/shard_map/ppermute | solution.py:368
  23.8 1.0 %shard_map.90 = (bf16[128,512]{1,0:T(8,128)(2,1)}, bf16[128,256]{1,0:T(8,128)(2,1)S(1)}) custom-call(bf16[128,512]{1,0:T(8,128)(2,1)S(1)} %copy-done.1, bf16[128,512]{1,0:T(8,128)(2,1)S(1)} %copy-done.2, bf16[512,512]{1,0:T(8,128)(2,1)S(1)} %get-tuple-element.19.low_ref, bf16[512,512]{1,0:T(8,128)(2,1)S(1)} %get-tuple-element.20.dscore_ref, ...), custom_call_target="tpu_custom_call" | custom-call | flops 67108864 | bytes 917504 | tf_op jit(solution)/shard_map/pallas_call | solution.py:359
  24.8 1.6 %collective-permute-done.4.refs_1_ = bf16[128,256]{1,0:T(8,128)(2,1)S(1)} collective-permute-done((bf16[128,256]{1,0:T(8,128)(2,1)S(1)}, bf16[128,256]{1,0:T(8,128)(2,1)S(1)}, u32[]{:S(2)}, u32[]{:S(2)}) %collective-permute-start.4) | collective-permute-done | bytes 65568 | tf_op jit(solution)/shard_map/ppermute | solution.py:368
  26.4 1.6 %collective-permute-done.5.refs_2_ = bf16[128,256]{1,0:T(8,128)(2,1)S(1)} collective-permute-done((bf16[128,256]{1,0:T(8,128)(2,1)S(1)}, bf16[128,256]{1,0:T(8,128)(2,1)S(1)}, u32[]{:S(2)}, u32[]{:S(2)}) %collective-permute-start.5) | collective-permute-done | bytes 65568 | tf_op jit(solution)/shard_map/ppermute | solution.py:368
  28.1 0.0 collective-permute-done.6.refs_3_
  28.1 1.3 %shard_map.91 = (f32[64,3200]{1,0:T(8,128)S(1)}, bf16[64,3200]{1,0:T(8,128)(2,1)S(1)}) custom-call(s32[8]{0:T(128)S(1)} %copy-done.4, bf16[3200,256]{1,0:T(8,128)(2,1)S(1)} %copy-done, bf16[128,256]{1,0:T(8,128)(2,1)S(1)} %get-tuple-element.23.refs_0_, bf16[128,256]{1,0:T(8,128)(2,1)S(1)} %collective-permute-done.4.refs_1_, ...), custom_call_target="tpu_custom_call" | custom-call | flops 209715200 | bytes 2867200 | tf_op jit(solution)/shard_map/pallas_call | solution.py:370
  29.4 0.1 collective-permute-start.7
  29.4 1.7 %collective-permute-done.7.other_ref = bf16[64,3200]{1,0:T(8,128)(2,1)S(1)} collective-permute-done((bf16[64,3200]{1,0:T(8,128)(2,1)S(1)}, bf16[64,3200]{1,0:T(8,128)(2,1)S(1)}, u32[]{:S(2)}, u32[]{:S(2)}) %collective-permute-start.7) | collective-permute-done | bytes 409632 | tf_op jit(solution)/shard_map/ppermute | solution.py:378
  31.2 0.1 shard_map.92
  31.3 2.5 %collective-permute-start.8 = (bf16[16,3200]{1,0:T(8,128)(2,1)S(1)}, bf16[16,3200]{1,0:T(8,128)(2,1)S(1)}, u32[]{:S(2)}, u32[]{:S(2)}) collective-permute-start(bf16[16,3200]{1,0:T(8,128)(2,1)S(1)} %get-tuple-element.31), channel_id=1, source_target_pairs={{0,17},{1,16},{8,25},{9,24},{16,1},{17,0},{24,9},{25,8},{2,19},{3,... | collective-permute-start | bytes 307208 | tf_op jit(solution)/shard_map/ppermute | solution.py:388
  33.8 0.5 %collective-permute-start.9 = (bf16[16,3200]{1,0:T(8,128)(2,1)S(1)}, bf16[16,3200]{1,0:T(8,128)(2,1)S(1)}, u32[]{:S(2)}, u32[]{:S(2)}) collective-permute-start(bf16[16,3200]{1,0:T(8,128)(2,1)S(1)} %get-tuple-element.32), channel_id=1, source_target_pairs={{0,16},{1,17},{8,24},{9,25},{16,0},{17,1},{24,8},{25,9},{2,18},{3,... | collective-permute-start | bytes 307208 | tf_op jit(solution)/shard_map/ppermute | solution.py:388
  34.3 0.5 %collective-permute-start.10 = (bf16[16,3200]{1,0:T(8,128)(2,1)S(1)}, bf16[16,3200]{1,0:T(8,128)(2,1)S(1)}, u32[]{:S(2)}, u32[]{:S(2)}) collective-permute-start(bf16[16,3200]{1,0:T(8,128)(2,1)S(1)} %get-tuple-element.33), channel_id=1, source_target_pairs={{0,1},{1,0},{8,9},{9,8},{16,17},{17,16},{24,25},{25,24},{2,3},{3,2... | collective-permute-start | bytes 307208 | tf_op jit(solution)/shard_map/ppermute | solution.py:388
  34.8 3.1 %collective-permute-done.8.refs_0_ = bf16[16,3200]{1,0:T(8,128)(2,1)S(1)} collective-permute-done((bf16[16,3200]{1,0:T(8,128)(2,1)S(1)}, bf16[16,3200]{1,0:T(8,128)(2,1)S(1)}, u32[]{:S(2)}, u32[]{:S(2)}) %collective-permute-start.8) | collective-permute-done | bytes 102432 | tf_op jit(solution)/shard_map/ppermute | solution.py:388
  38.0 1.4 %collective-permute-done.9.refs_1_ = bf16[16,3200]{1,0:T(8,128)(2,1)S(1)} collective-permute-done((bf16[16,3200]{1,0:T(8,128)(2,1)S(1)}, bf16[16,3200]{1,0:T(8,128)(2,1)S(1)}, u32[]{:S(2)}, u32[]{:S(2)}) %collective-permute-start.9) | collective-permute-done | bytes 102432 | tf_op jit(solution)/shard_map/ppermute | solution.py:388
  39.4 0.0 collective-permute-done.10.refs_2_
  39.4 0.2 shard_map.93.refs_3_
  39.6 1.5 %collective-permute-start.15 = (bf16[16,3200]{1,0:T(8,128)(2,1)S(1)}, bf16[16,3200]{1,0:T(8,128)(2,1)S(1)}, u32[]{:S(2)}, u32[]{:S(2)}) collective-permute-start(bf16[16,3200]{1,0:T(8,128)(2,1)S(1)} %shard_map.93.refs_3_), channel_id=1, source_target_pairs={{0,1},{1,0},{8,9},{9,8},{16,17},{17,16},{24,25},{25,24},{2,3},{3,2... | collective-permute-start | bytes 307208 | tf_op jit(solution)/shard_map/ppermute | solution.py:399
  41.1 1.5 %collective-permute-start.13 = (bf16[16,3200]{1,0:T(8,128)(2,1)S(1)}, bf16[16,3200]{1,0:T(8,128)(2,1)S(1)}, u32[]{:S(2)}, u32[]{:S(2)}) collective-permute-start(bf16[16,3200]{1,0:T(8,128)(2,1)S(1)} %shard_map.93.refs_3_), channel_id=1, source_target_pairs={{0,16},{1,17},{8,24},{9,25},{16,0},{17,1},{24,8},{25,9},{2,18},{3,... | collective-permute-start | bytes 307208 | tf_op jit(solution)/shard_map/ppermute | solution.py:399
  42.6 0.5 %collective-permute-start.11 = (bf16[16,3200]{1,0:T(8,128)(2,1)S(1)}, bf16[16,3200]{1,0:T(8,128)(2,1)S(1)}, u32[]{:S(2)}, u32[]{:S(2)}) collective-permute-start(bf16[16,3200]{1,0:T(8,128)(2,1)S(1)} %shard_map.93.refs_3_), channel_id=1, source_target_pairs={{0,17},{1,16},{8,25},{9,24},{16,1},{17,0},{24,9},{25,8},{2,19},{3,... | collective-permute-start | bytes 307208 | tf_op jit(solution)/shard_map/ppermute | solution.py:399
  43.2 0.0 collective-permute-start.17
  43.2 1.2 %collective-permute-done.15.refs_2_ = bf16[16,3200]{1,0:T(8,128)(2,1)S(1)} collective-permute-done((bf16[16,3200]{1,0:T(8,128)(2,1)S(1)}, bf16[16,3200]{1,0:T(8,128)(2,1)S(1)}, u32[]{:S(2)}, u32[]{:S(2)}) %collective-permute-start.15) | collective-permute-done | bytes 102432 | tf_op jit(solution)/shard_map/ppermute | solution.py:399
  44.3 0.0 collective-permute-start.16
  44.3 2.3 %collective-permute-done.13.refs_1_ = bf16[16,3200]{1,0:T(8,128)(2,1)S(1)} collective-permute-done((bf16[16,3200]{1,0:T(8,128)(2,1)S(1)}, bf16[16,3200]{1,0:T(8,128)(2,1)S(1)}, u32[]{:S(2)}, u32[]{:S(2)}) %collective-permute-start.13) | collective-permute-done | bytes 102432 | tf_op jit(solution)/shard_map/ppermute | solution.py:399
  46.6 0.0 collective-permute-start.14
  46.6 1.6 %collective-permute-done.11.refs_0_ = bf16[16,3200]{1,0:T(8,128)(2,1)S(1)} collective-permute-done((bf16[16,3200]{1,0:T(8,128)(2,1)S(1)}, bf16[16,3200]{1,0:T(8,128)(2,1)S(1)}, u32[]{:S(2)}, u32[]{:S(2)}) %collective-permute-start.11) | collective-permute-done | bytes 102432 | tf_op jit(solution)/shard_map/ppermute | solution.py:399
  48.2 0.0 collective-permute-start.12
  48.2 0.8 %shard_map.94.refs_4_ = bf16[128,3200]{1,0:T(8,128)(2,1)} custom-call(bf16[16,3200]{1,0:T(8,128)(2,1)S(1)} %collective-permute-done.11.refs_0_, bf16[16,3200]{1,0:T(8,128)(2,1)S(1)} %collective-permute-done.13.refs_1_, bf16[16,3200]{1,0:T(8,128)(2,1)S(1)} %collective-permute-done.15.refs_2_, bf16[16,3200]{1,0:T(8,128)(2,1)S(1)} %shard_map.93.refs_3_), custom_call_target="tpu_custom_call" | custom-call | bytes 819200 | tf_op jit(solution)/shard_map/pallas_call | solution.py:404
  49.0 0.0 collective-permute-done.17.refs_3_
  49.0 0.0 collective-permute-done.16.refs_2_
  49.0 0.0 collective-permute-done.14.refs_1_
  49.0 0.5 collective-permute-done.12.refs_0_
  49.5 0.8 %shard_map.95 = bf16[128,3200]{1,0:T(8,128)(2,1)} custom-call(bf16[16,3200]{1,0:T(8,128)(2,1)S(1)} %collective-permute-done.12.refs_0_, bf16[16,3200]{1,0:T(8,128)(2,1)S(1)} %collective-permute-done.14.refs_1_, bf16[16,3200]{1,0:T(8,128)(2,1)S(1)} %collective-permute-done.16.refs_2_, ...), custom_call_target="tpu_custom_call", output_to_operand_aliasing={{}: (4, {})} | custom-call | bytes 819200 | tf_op jit(solution)/shard_map/pallas_call | solution.py:404
  (10 shorter events, 0.0 us)
Async XLA Ops:
  0.6 17.6 %copy-start.2 = (bf16[128,512]{1,0:T(8,128)(2,1)S(1)}, bf16[128,512]{1,0:T(8,128)(2,1)}, u32[]{:S(2)}) copy-start(bf16[128,512]{1,0:T(8,128)(2,1)} %g_ref.3) | copy-start | bytes 393220
  0.6 17.6 %copy-start.1 = (bf16[128,512]{1,0:T(8,128)(2,1)S(1)}, bf16[128,512]{1,0:T(8,128)(2,1)}, u32[]{:S(2)}) copy-start(bf16[128,512]{1,0:T(8,128)(2,1)} %q_ref.3) | copy-start | bytes 393220
  0.7 8.9 %collective-permute-start = (bf16[128,256]{1,0:T(8,128)(2,1)}, bf16[128,256]{1,0:T(8,128)(2,1)S(1)}, u32[]{:S(2)}, u32[]{:S(2)}) collective-permute-start(bf16[128,256]{1,0:T(8,128)(2,1)} %text_ref.1), channel_id=1, source_target_pairs={{0,6},{2,4},{4,0},{6,2},{1,7},{3,5},{5,1},{7,3},{8,14},{10,12},{12... | collective-permute-start | bytes 196616 | tf_op jit(solution)/shard_map/ppermute | solution.py:309
  5.8 0.7 %copy-start.3 = (f32[3200]{0:T(1024)S(1)}, f32[3200]{0:T(1024)}, u32[]{:S(2)}) copy-start(f32[3200]{0:T(1024)} %param.8) | copy-start | bytes 38404
  6.5 2.4 %copy-start.4 = (s32[8]{0:T(128)S(1)}, s32[8]{0:T(128)}, u32[]{:S(2)}) copy-start(s32[8]{0:T(128)} %pieces_ref.7) | copy-start | bytes 100
  6.5 11.8 %copy-start.5 = (bf16[128,256]{1,0:T(8,128)(2,1)S(1)}, bf16[128,256]{1,0:T(8,128)(2,1)}, u32[]{:S(2)}) copy-start(bf16[128,256]{1,0:T(8,128)(2,1)} %text_ref.1) | copy-start | bytes 196612
  8.7 19.3 %copy-start = (bf16[3200,256]{1,0:T(8,128)(2,1)S(1)}, bf16[3200,256]{1,0:T(8,128)(2,1)}, u32[]{:S(2)}) copy-start(bf16[3200,256]{1,0:T(8,128)(2,1)} %proj_ref.1) | copy-start | bytes 4915204
  8.8 6.8 %collective-permute-start.1 = (bf16[128,256]{1,0:T(8,128)(2,1)S(1)}, bf16[128,256]{1,0:T(8,128)(2,1)S(1)}, u32[]{:S(2)}, u32[]{:S(2)}) collective-permute-start(bf16[128,256]{1,0:T(8,128)(2,1)S(1)} %get-tuple-element.18.image_ref), channel_id=1, source_target_pairs={{6,0},{4,2},{0,4},{2,6},{7,1},{5,3},{1,5},{3,7},{14,8},{12,10},{8,... | collective-permute-start | bytes 196616 | tf_op jit(solution)/shard_map/ppermute | solution.py:329
  10.1 6.8 %collective-permute-start.3 = (bf16[128,256]{1,0:T(8,128)(2,1)S(1)}, bf16[128,256]{1,0:T(8,128)(2,1)S(1)}, u32[]{:S(2)}, u32[]{:S(2)}) collective-permute-start(bf16[128,256]{1,0:T(8,128)(2,1)S(1)} %shard_map.88.own_ref), channel_id=1, source_target_pairs={{0,6},{2,4},{4,0},{6,2},{1,7},{3,5},{5,1},{7,3},{8,14},{10,12},{12... | collective-permute-start | bytes 196616 | tf_op jit(solution)/shard_map/ppermute | solution.py:346
  14.0 4.3 %collective-permute-start.2 = (bf16[128,256]{1,0:T(8,128)(2,1)S(1)}, bf16[128,256]{1,0:T(8,128)(2,1)S(1)}, u32[]{:S(2)}, u32[]{:S(2)}) collective-permute-start(bf16[128,256]{1,0:T(8,128)(2,1)S(1)} %shard_map.88.own_ref), channel_id=1, source_target_pairs={{0,2},{2,0},{4,6},{6,4},{1,3},{3,1},{5,7},{7,5},{8,10},{10,8},{12,... | collective-permute-start | bytes 196616 | tf_op jit(solution)/shard_map/ppermute | solution.py:346
  20.1 6.3 %collective-permute-start.4 = (bf16[128,256]{1,0:T(8,128)(2,1)S(1)}, bf16[128,256]{1,0:T(8,128)(2,1)S(1)}, u32[]{:S(2)}, u32[]{:S(2)}) collective-permute-start(bf16[128,256]{1,0:T(8,128)(2,1)S(1)} %get-tuple-element.24), channel_id=1, source_target_pairs={{0,6},{2,4},{4,0},{6,2},{1,7},{3,5},{5,1},{7,3},{8,14},{10,12},{12... | collective-permute-start | bytes 196616 | tf_op jit(solution)/shard_map/ppermute | solution.py:368
  22.0 6.1 %collective-permute-start.5 = (bf16[128,256]{1,0:T(8,128)(2,1)S(1)}, bf16[128,256]{1,0:T(8,128)(2,1)S(1)}, u32[]{:S(2)}, u32[]{:S(2)}) collective-permute-start(bf16[128,256]{1,0:T(8,128)(2,1)S(1)} %get-tuple-element.25), channel_id=1, source_target_pairs={{6,0},{4,2},{0,4},{2,6},{7,1},{5,3},{1,5},{3,7},{14,8},{12,10},{8,... | collective-permute-start | bytes 196616 | tf_op jit(solution)/shard_map/ppermute | solution.py:368
  23.1 5.0 %collective-permute-start.6 = (bf16[128,256]{1,0:T(8,128)(2,1)S(1)}, bf16[128,256]{1,0:T(8,128)(2,1)S(1)}, u32[]{:S(2)}, u32[]{:S(2)}) collective-permute-start(bf16[128,256]{1,0:T(8,128)(2,1)S(1)} %get-tuple-element.26), channel_id=1, source_target_pairs={{2,0},{0,2},{6,4},{4,6},{3,1},{1,3},{7,5},{5,7},{10,8},{8,10},{14,... | collective-permute-start | bytes 196616 | tf_op jit(solution)/shard_map/ppermute | solution.py:368
  29.4 1.8 %collective-permute-start.7 = (bf16[64,3200]{1,0:T(8,128)(2,1)S(1)}, bf16[64,3200]{1,0:T(8,128)(2,1)S(1)}, u32[]{:S(2)}, u32[]{:S(2)}) collective-permute-start(bf16[64,3200]{1,0:T(8,128)(2,1)S(1)} %get-tuple-element.28), channel_id=1, source_target_pairs={{0,8},{1,9},{8,0},{9,1},{16,24},{17,25},{24,16},{25,17},{2,10},{3,... | collective-permute-start | bytes 1228808 | tf_op jit(solution)/shard_map/ppermute | solution.py:378
  31.3 6.7 %collective-permute-start.8 = (bf16[16,3200]{1,0:T(8,128)(2,1)S(1)}, bf16[16,3200]{1,0:T(8,128)(2,1)S(1)}, u32[]{:S(2)}, u32[]{:S(2)}) collective-permute-start(bf16[16,3200]{1,0:T(8,128)(2,1)S(1)} %get-tuple-element.31), channel_id=1, source_target_pairs={{0,17},{1,16},{8,25},{9,24},{16,1},{17,0},{24,9},{25,8},{2,19},{3,... | collective-permute-start | bytes 307208 | tf_op jit(solution)/shard_map/ppermute | solution.py:388
  33.8 5.6 %collective-permute-start.9 = (bf16[16,3200]{1,0:T(8,128)(2,1)S(1)}, bf16[16,3200]{1,0:T(8,128)(2,1)S(1)}, u32[]{:S(2)}, u32[]{:S(2)}) collective-permute-start(bf16[16,3200]{1,0:T(8,128)(2,1)S(1)} %get-tuple-element.32), channel_id=1, source_target_pairs={{0,16},{1,17},{8,24},{9,25},{16,0},{17,1},{24,8},{25,9},{2,18},{3,... | collective-permute-start | bytes 307208 | tf_op jit(solution)/shard_map/ppermute | solution.py:388
  34.3 5.1 %collective-permute-start.10 = (bf16[16,3200]{1,0:T(8,128)(2,1)S(1)}, bf16[16,3200]{1,0:T(8,128)(2,1)S(1)}, u32[]{:S(2)}, u32[]{:S(2)}) collective-permute-start(bf16[16,3200]{1,0:T(8,128)(2,1)S(1)} %get-tuple-element.33), channel_id=1, source_target_pairs={{0,1},{1,0},{8,9},{9,8},{16,17},{17,16},{24,25},{25,24},{2,3},{3,2... | collective-permute-start | bytes 307208 | tf_op jit(solution)/shard_map/ppermute | solution.py:388
  39.6 4.7 %collective-permute-start.15 = (bf16[16,3200]{1,0:T(8,128)(2,1)S(1)}, bf16[16,3200]{1,0:T(8,128)(2,1)S(1)}, u32[]{:S(2)}, u32[]{:S(2)}) collective-permute-start(bf16[16,3200]{1,0:T(8,128)(2,1)S(1)} %shard_map.93.refs_3_), channel_id=1, source_target_pairs={{0,1},{1,0},{8,9},{9,8},{16,17},{17,16},{24,25},{25,24},{2,3},{3,2... | collective-permute-start | bytes 307208 | tf_op jit(solution)/shard_map/ppermute | solution.py:399
  41.1 5.5 %collective-permute-start.13 = (bf16[16,3200]{1,0:T(8,128)(2,1)S(1)}, bf16[16,3200]{1,0:T(8,128)(2,1)S(1)}, u32[]{:S(2)}, u32[]{:S(2)}) collective-permute-start(bf16[16,3200]{1,0:T(8,128)(2,1)S(1)} %shard_map.93.refs_3_), channel_id=1, source_target_pairs={{0,16},{1,17},{8,24},{9,25},{16,0},{17,1},{24,8},{25,9},{2,18},{3,... | collective-permute-start | bytes 307208 | tf_op jit(solution)/shard_map/ppermute | solution.py:399
  42.6 5.6 %collective-permute-start.11 = (bf16[16,3200]{1,0:T(8,128)(2,1)S(1)}, bf16[16,3200]{1,0:T(8,128)(2,1)S(1)}, u32[]{:S(2)}, u32[]{:S(2)}) collective-permute-start(bf16[16,3200]{1,0:T(8,128)(2,1)S(1)} %shard_map.93.refs_3_), channel_id=1, source_target_pairs={{0,17},{1,16},{8,25},{9,24},{16,1},{17,0},{24,9},{25,8},{2,19},{3,... | collective-permute-start | bytes 307208 | tf_op jit(solution)/shard_map/ppermute | solution.py:399
  43.2 5.8 %collective-permute-start.17 = (bf16[16,3200]{1,0:T(8,128)(2,1)S(1)}, bf16[16,3200]{1,0:T(8,128)(2,1)S(1)}, u32[]{:S(2)}, u32[]{:S(2)}) collective-permute-start(bf16[16,3200]{1,0:T(8,128)(2,1)S(1)} %shard_map.93.refs_3_), channel_id=1, source_target_pairs={{0,8},{1,9},{8,0},{9,1},{16,24},{17,25},{24,16},{25,17},{2,10},{3,... | collective-permute-start | bytes 307208 | tf_op jit(solution)/shard_map/ppermute | solution.py:400
  44.3 4.6 %collective-permute-start.16 = (bf16[16,3200]{1,0:T(8,128)(2,1)S(1)}, bf16[16,3200]{1,0:T(8,128)(2,1)S(1)}, u32[]{:S(2)}, u32[]{:S(2)}) collective-permute-start(bf16[16,3200]{1,0:T(8,128)(2,1)S(1)} %collective-permute-done.15.refs_2_), channel_id=1, source_target_pairs={{0,8},{1,9},{8,0},{9,1},{16,24},{17,25},{24,16},{25,17},{2,10},{3,... | collective-permute-start | bytes 307208 | tf_op jit(solution)/shard_map/ppermute | solution.py:400
  46.6 2.4 %collective-permute-start.14 = (bf16[16,3200]{1,0:T(8,128)(2,1)S(1)}, bf16[16,3200]{1,0:T(8,128)(2,1)S(1)}, u32[]{:S(2)}, u32[]{:S(2)}) collective-permute-start(bf16[16,3200]{1,0:T(8,128)(2,1)S(1)} %collective-permute-done.13.refs_1_), channel_id=1, source_target_pairs={{0,8},{1,9},{8,0},{9,1},{16,24},{17,25},{24,16},{25,17},{2,10},{3,... | collective-permute-start | bytes 307208 | tf_op jit(solution)/shard_map/ppermute | solution.py:400
  48.2 1.3 %collective-permute-start.12 = (bf16[16,3200]{1,0:T(8,128)(2,1)S(1)}, bf16[16,3200]{1,0:T(8,128)(2,1)S(1)}, u32[]{:S(2)}, u32[]{:S(2)}) collective-permute-start(bf16[16,3200]{1,0:T(8,128)(2,1)S(1)} %collective-permute-done.11.refs_0_), channel_id=1, source_target_pairs={{0,8},{1,9},{8,0},{9,1},{16,24},{17,25},{24,16},{25,17},{2,10},{3,... | collective-permute-start | bytes 307208 | tf_op jit(solution)/shard_map/ppermute | solution.py:400

commit v9 on v8

--- a/solution.py
+++ b/solution.py
@@ -114,20 +114,18 @@
     own_ref[...] = vis[pl.ds(start, piece), :]
 
 
-def shift_body(seq_n, pieces_ref, image_ref, out_ref):
+def placed(before, rows, image_ref, text_ref):
+    ahead = lax.broadcasted_iota(jnp.int32, (rows, rows), 0) - lax.broadcasted_iota(jnp.int32, (rows, rows), 1)
+    pick = jnp.where(ahead == before, 1.0, 0.0).astype(jnp.bfloat16)
+    image = jnp.dot(pick, image_ref[...], preferred_element_type=jnp.float32)
+    row = lax.broadcasted_iota(jnp.int32, image.shape, 0)
+    return jnp.where(row < before, text_ref[...].astype(jnp.float32), image).astype(jnp.bfloat16)
+
+
+def place_body(seq_n, pieces_ref, image_ref, text_ref, out_ref):
     rows = image_ref.shape[0]
     before = pieces_ref[2 * held_image(lax.axis_index("seq"), seq_n)]
-    to = lax.broadcasted_iota(jnp.int32, (rows, rows), 0)
-    source = lax.broadcasted_iota(jnp.int32, (rows, rows), 1)
-    pick = jnp.where(source == to - before, 1.0, 0.0).astype(jnp.bfloat16)
-    out_ref[...] = jnp.dot(pick, image_ref[...], preferred_element_type=jnp.float32).astype(jnp.bfloat16)
-
-
-def place_body(seq_n, pieces_ref, image_ref, text_ref, out_ref):
-    before = pieces_ref[2 * held_image(lax.axis_index("seq"), seq_n)]
-    row = lax.broadcasted_iota(jnp.int32, image_ref.shape, 0)
-    text, image = text_ref[...].astype(jnp.float32), image_ref[...].astype(jnp.float32)
-    out_ref[...] = jnp.where(row < before, text, image).astype(jnp.bfloat16)
+    out_ref[...] = placed(before, rows, image_ref, text_ref)
 
 
 def heads_of(ref, heads):
@@ -145,7 +143,7 @@
         q, g = heads_of(q_ref, heads), heads_of(g_ref, heads)
         span = slice(heads[0] * rows, (heads[-1] + 1) * rows)
         for n, r in enumerate(chosen):
-            part = slice(r * rows, (r + 1) * rows)
+            part = pl.ds(pl.multiple_of(r * rows, rows), rows)
             dkeys = jnp.dot(dscore_ref[part, span], q, preferred_element_type=jnp.float32)
             dvalues = jnp.dot(low_ref[part, span], g, preferred_element_type=jnp.float32)
             if totals[n] is not None:
@@ -156,7 +154,7 @@
         ref[:, HD:] = dvalues.astype(jnp.bfloat16)
 
 
-def weigh_body(seq_n, tables, early, pieces_ref, q_ref, g_ref, text_ref, own_ref, raw_ref, *refs):
+def weigh_body(seq_n, tables, backs, pieces_ref, q_ref, g_ref, text_ref, own_ref, raw_ref, *refs):
     count = len(tables)
     block_refs, (low_ref, dscore_ref, values_ref) = refs[:count], refs[count : count + 3]
     grad_refs = refs[count + 3 :]
@@ -164,12 +162,7 @@
     group = q_ref.shape[1] // HD
     scale = 1.0 / math.sqrt(HD)
     me = lax.axis_index("seq")
-    before = pieces_ref[2 * me]
-    ahead = lax.broadcasted_iota(jnp.int32, (rows, rows), 0) - lax.broadcasted_iota(jnp.int32, (rows, rows), 1)
-    pick = jnp.where(ahead == before, 1.0, 0.0).astype(jnp.bfloat16)
-    placed = jnp.dot(pick, raw_ref[...], preferred_element_type=jnp.float32)
-    row = lax.broadcasted_iota(jnp.int32, placed.shape, 0)
-    mine = jnp.where(row < before, text_ref[...].astype(jnp.float32), placed).astype(jnp.bfloat16)
+    mine = placed(pieces_ref[2 * me], rows, raw_ref, text_ref)
     kv = jnp.concatenate([own_ref[...], mine] + [ref[...] for ref in block_refs], axis=0)
     keys, values = kv[:, :HD], kv[:, HD:]
     values_ref[...] = values
@@ -195,6 +188,7 @@
         span = slice(heads[0] * rows, (heads[-1] + 1) * rows)
         low_ref[:, span] = low
         dscore_ref[:, span] = (weights * (dprob - drift)).astype(jnp.bfloat16)
+    early = [pick_static(table, me) for table in backs]
     grad_parts(early, rows, scale, low_ref, dscore_ref, q_ref, g_ref, grad_refs)
 
 
@@ -327,14 +321,6 @@
         ],
     )(vis_rows, gain, key_value_proj)
     raw = lax.ppermute(image_kv, "seq", home)
-    shifted = call(
-        functools.partial(shift_body, seq_n),
-        jax.ShapeDtypeStruct((rows, columns), bf16),
-        [SCALARS, WHOLE],
-        WHOLE,
-        2 * rows * rows * columns,
-        4 * rows * columns,
-    )(pieces, image_kv)
     block = call(
         functools.partial(place_body, seq_n),
         jax.ShapeDtypeStruct((rows, columns), bf16),
@@ -342,30 +328,39 @@
         WHOLE,
         0,
         6 * rows * columns,
-    )(pieces, shifted, text)
+    )(pieces, image_kv, text)
     blocks = [lax.ppermute(block, "seq", pairs) for pairs in forth]
     total = 2 + len(blocks)
-    early, late = list(range(1, total)), [0]
+    pairs_back, backs = [], []
+    for r in range(seq_n - 1, 0, -1):
+        pairs_back.append([(d, d ^ r) for d in range(seq_n)])
+        table = []
+        for d in range(seq_n):
+            block_of = [held[d], d] + [t[d] for t in tables]
+            want = held[d ^ r]
+            if want > d:
+                want = max(block_of)
+            table.append(block_of.index(want, 1))
+        backs.append(table)
     kv_shape = jax.ShapeDtypeStruct((rows, columns), bf16)
     wide_shape = jax.ShapeDtypeStruct((total * rows, queries.shape[1] // HD * rows), bf16)
     low, dscore, values, *grads = call(
-        functools.partial(weigh_body, seq_n, tables, early),
-        [wide_shape, wide_shape, jax.ShapeDtypeStruct((total * rows, HD), bf16)] + [kv_shape] * len(early),
+        functools.partial(weigh_body, seq_n, tables, backs),
+        [wide_shape, wide_shape, jax.ShapeDtypeStruct((total * rows, HD), bf16)] + [kv_shape] * len(backs),
         [SCALARS] + [WHOLE] * (3 + total),
-        [WHOLE] * (3 + len(early)),
+        [WHOLE] * (3 + len(backs)),
         8 * total * rows * rows * queries.shape[1],
         4 * rows * queries.shape[1] + 4 * total * rows * columns,
     )(pieces, queries, grad_out, text_kv, block, raw, *blocks)
     attended, own_grad = call(
-        functools.partial(mix_body, late),
-        [jax.ShapeDtypeStruct(queries.shape, bf16)] + [kv_shape] * len(late),
+        functools.partial(mix_body, [0]),
+        [jax.ShapeDtypeStruct(queries.shape, bf16), kv_shape],
         [WHOLE] * 5,
-        [WHOLE] * (1 + len(late)),
+        [WHOLE, WHOLE],
         2 * total * rows * rows * queries.shape[1],
         6 * rows * queries.shape[1] + 4 * total * rows * columns,
     )(queries, grad_out, low, dscore, values)
-    back = list(zip(grads, [home] + forth))
-    parts = [lax.ppermute(g, "seq", [(t, s) for s, t in pairs]) for g, pairs in back[:1] + back[:0:-1]]
+    parts = [lax.ppermute(g, "seq", pairs) for g, pairs in zip(grads, pairs_back)]
 
     keep, send = call(
         functools.partial(back_body, seq_n, piece),

time: 50.5 us -> 50.2 us (level)
  starting transfers between devices: 19.9 us -> 20.6 us
  Pallas kernels: 9.51 us -> 8.94 us
    ppermute x3, starting transfers between devices: 3.68 us -> 4.45 us  [on_device(): lax.ppermute(g, 'seq', pairs)]
    pallas_call x3 -> x2, Pallas kernels: 3.55 us -> 2.86 us  [the longest x1 1.84 us: on_device(): call(functools.partial(weigh_body, seq_n, tables, backs), [wide_shape, wi...]
    ppermute x2, waiting for transfers between devices: 2.63 us -> 2.06 us  [on_device(): blocks = [lax.ppermute(block, 'seq', pairs) for pairs in forth]]
    ppermute x1, waiting for transfers between devices: 1.63 us -> 2.2 us  [on_device(): raw = lax.ppermute(image_kv, 'seq', home)]
  transfers between devices with their start and end apart: 18 -> 18, of which waited for: 12 -> 12; matrix products, arithmetic and copies ran while one was open for 0% -> 0% of each run, Pallas kernels for 11% -> 10%
where the time goes in v9:
time: 50.2 us; the launch traced here: 50 us
  starting transfers between devices  20.6 us (41%)
  waiting for transfers between devices  18.9 us (38%)
  Pallas kernels  8.94 us (18%)
  between operations  0.77 us (2%)
  local copies, waits for them, and re-layouts  0.74 us (1%)
    ppermute x1, starting transfers between devices, on_device(): text = lax.ppermute(text_kv, 'seq', list(enumerate(owners)))  5.1 us
    ppermute x3, waiting for transfers between devices, on_device(): mines[d] = lax.ppermute(mine, names, far_pairs(d))  5 us
    ppermute x3, waiting for transfers between devices, on_device(): lax.ppermute(sends[d - 1], names, far_pairs(d))  4.6 us
    ppermute x3, starting transfers between devices, on_device(): lax.ppermute(g, 'seq', pairs)  4.45 us
    ppermute x2, starting transfers between devices, on_device(): blocks = [lax.ppermute(block, 'seq', pairs) for pairs in forth]  3.85 us
    ppermute x3, starting transfers between devices, on_device(): lax.ppermute(sends[d - 1], names, far_pairs(d))  3.55 us
    ppermute x3, starting transfers between devices, on_device(): mines[d] = lax.ppermute(mine, names, far_pairs(d))  3.55 us
    ppermute x3, waiting for transfers between devices, on_device(): lax.ppermute(g, 'seq', pairs)  2.77 us
  transfers between devices with their start and end apart: 18, of which 12 were waited for; matrix products, arithmetic and copies ran while one was open for 0% of the time, Pallas kernels for 10%

profile of v9, /device:TPU:0, one launch (start us, length us, event | category | flops | bytes accessed | tf_op | source)
XLA Modules:
  0.0 50.0 jit_solution(15753967324552413233)
XLA Ops:
  0.7 5.1 %collective-permute-start = (bf16[128,256]{1,0:T(8,128)(2,1)}, bf16[128,256]{1,0:T(8,128)(2,1)S(1)}, u32[]{:S(2)}, u32[]{:S(2)}) collective-permute-start(bf16[128,256]{1,0:T(8,128)(2,1)} %text_ref.1), channel_id=1, source_target_pairs={{0,6},{2,4},{4,0},{6,2},{1,7},{3,5},{5,1},{7,3},{8,14},{10,12},{12... | collective-permute-start | bytes 196616 | tf_op jit(solution)/shard_map/ppermute | solution.py:303
  5.8 0.7 %copy-done.3 = f32[3200]{0:T(1024)S(1)} copy-done((f32[3200]{0:T(1024)S(1)}, f32[3200]{0:T(1024)}, u32[]{:S(2)}) %copy-start.3) | copy-done | bytes 12824
  6.5 2.3 %shard_map.86 = (bf16[128,256]{1,0:T(8,128)(2,1)S(1)}, bf16[16,3200]{1,0:T(8,128)(2,1)S(1)}) custom-call(bf16[128,3200]{1,0:T(8,128)(2,1)} %vis_hbm.1, f32[25,128]{1,0:T(8,128)S(1)} %bitcast.1, bf16[3200,256]{1,0:T(8,128)(2,1)} %proj_ref.1), custom_call_target="tpu_custom_call" | custom-call | flops 209715200 | bytes 2457600 | tf_op jit(solution)/shard_map/pallas_call | solution.py:306
  8.7 0.0 copy-start
  8.8 0.1 collective-permute-start.1
  8.8 0.0 collective-permute-done.text_ref
  8.8 0.7 %shard_map.87.own_ref = bf16[128,256]{1,0:T(8,128)(2,1)S(1)} custom-call(s32[8]{0:T(128)S(1)} %copy-done.4, bf16[128,256]{1,0:T(8,128)(2,1)S(1)} %get-tuple-element.18.image_ref, bf16[128,256]{1,0:T(8,128)(2,1)S(1)} %collective-permute-done.text_ref), custom_call_target="tpu_custom_call" | custom-call | bytes 196608 | tf_op jit(solution)/shard_map/pallas_call | solution.py:324
  9.5 3.8 %collective-permute-start.3 = (bf16[128,256]{1,0:T(8,128)(2,1)S(1)}, bf16[128,256]{1,0:T(8,128)(2,1)S(1)}, u32[]{:S(2)}, u32[]{:S(2)}) collective-permute-start(bf16[128,256]{1,0:T(8,128)(2,1)S(1)} %shard_map.87.own_ref), channel_id=1, source_target_pairs={{0,6},{2,4},{4,0},{6,2},{1,7},{3,5},{5,1},{7,3},{8,14},{10,12},{12... | collective-permute-start | bytes 196616 | tf_op jit(solution)/shard_map/ppermute | solution.py:332
  13.4 0.0 collective-permute-start.2
  13.4 2.2 %collective-permute-done.1.raw_ref = bf16[128,256]{1,0:T(8,128)(2,1)S(1)} collective-permute-done((bf16[128,256]{1,0:T(8,128)(2,1)S(1)}, bf16[128,256]{1,0:T(8,128)(2,1)S(1)}, u32[]{:S(2)}, u32[]{:S(2)}) %collective-permute-start.1) | collective-permute-done | bytes 65568 | tf_op jit(solution)/shard_map/ppermute | solution.py:323
  15.6 1.3 %collective-permute-done.3.refs_1_ = bf16[128,256]{1,0:T(8,128)(2,1)S(1)} collective-permute-done((bf16[128,256]{1,0:T(8,128)(2,1)S(1)}, bf16[128,256]{1,0:T(8,128)(2,1)S(1)}, u32[]{:S(2)}, u32[]{:S(2)}) %collective-permute-start.3) | collective-permute-done | bytes 65568 | tf_op jit(solution)/shard_map/ppermute | solution.py:332
  16.9 0.8 %collective-permute-done.2.refs_0_ = bf16[128,256]{1,0:T(8,128)(2,1)S(1)} collective-permute-done((bf16[128,256]{1,0:T(8,128)(2,1)S(1)}, bf16[128,256]{1,0:T(8,128)(2,1)S(1)}, u32[]{:S(2)}, u32[]{:S(2)}) %collective-permute-start.2) | collective-permute-done | bytes 65568 | tf_op jit(solution)/shard_map/ppermute | solution.py:332
  17.7 0.0 copy-done.2
  17.7 1.8 %shard_map.88 = (bf16[512,512]{1,0:T(8,128)(2,1)S(1)}, bf16[512,512]{1,0:T(8,128)(2,1)S(1)}, bf16[512,128]{1,0:T(8,128)(2,1)S(1)}, bf16[128,256]{1,0:T(8,128)(2,...) custom-call(s32[8]{0:T(128)S(1)} %copy-done.4, bf16[128,512]{1,0:T(8,128)(2,1)S(1)} %copy-done.1, ...), custom_call_target="tpu_custom_call" | custom-call | flops 268435456 | bytes 786432 | tf_op jit(solution)/shard_map/pallas_call | solution.py:347
  19.5 1.9 %collective-permute-start.4 = (bf16[128,256]{1,0:T(8,128)(2,1)S(1)}, bf16[128,256]{1,0:T(8,128)(2,1)S(1)}, u32[]{:S(2)}, u32[]{:S(2)}) collective-permute-start(bf16[128,256]{1,0:T(8,128)(2,1)S(1)} %get-tuple-element.24), channel_id=1, source_target_pairs={{0,6},{2,4},{4,2},{6,0},{1,7},{3,5},{5,3},{7,1},{8,14},{10,12},{12... | collective-permute-start | bytes 196616 | tf_op jit(solution)/shard_map/ppermute | solution.py:363
  21.4 0.4 collective-permute-start.5
  21.7 2.2 %collective-permute-start.6 = (bf16[128,256]{1,0:T(8,128)(2,1)S(1)}, bf16[128,256]{1,0:T(8,128)(2,1)S(1)}, u32[]{:S(2)}, u32[]{:S(2)}) collective-permute-start(bf16[128,256]{1,0:T(8,128)(2,1)S(1)} %get-tuple-element.26), channel_id=1, source_target_pairs={{0,2},{2,0},{4,6},{6,4},{1,3},{3,1},{5,7},{7,5},{8,10},{10,8},{12,... | collective-permute-start | bytes 196616 | tf_op jit(solution)/shard_map/ppermute | solution.py:363
  24.0 1.0 %shard_map.89 = (bf16[128,512]{1,0:T(8,128)(2,1)}, bf16[128,256]{1,0:T(8,128)(2,1)S(1)}) custom-call(bf16[128,512]{1,0:T(8,128)(2,1)S(1)} %copy-done.1, bf16[128,512]{1,0:T(8,128)(2,1)S(1)} %copy-done.2, bf16[512,512]{1,0:T(8,128)(2,1)S(1)} %get-tuple-element.19.low_ref, bf16[512,512]{1,0:T(8,128)(2,1)S(1)} %get-tuple-element.20.dscore_ref, ...), custom_call_target="tpu_custom_call" | custom-call | flops 67108864 | bytes 917504 | tf_op jit(solution)/shard_map/pallas_call | solution.py:355
  25.0 1.0 %collective-permute-done.4.refs_1_ = bf16[128,256]{1,0:T(8,128)(2,1)S(1)} collective-permute-done((bf16[128,256]{1,0:T(8,128)(2,1)S(1)}, bf16[128,256]{1,0:T(8,128)(2,1)S(1)}, u32[]{:S(2)}, u32[]{:S(2)}) %collective-permute-start.4) | collective-permute-done | bytes 65568 | tf_op jit(solution)/shard_map/ppermute | solution.py:363
  26.0 1.8 %collective-permute-done.5.refs_2_ = bf16[128,256]{1,0:T(8,128)(2,1)S(1)} collective-permute-done((bf16[128,256]{1,0:T(8,128)(2,1)S(1)}, bf16[128,256]{1,0:T(8,128)(2,1)S(1)}, u32[]{:S(2)}, u32[]{:S(2)}) %collective-permute-start.5) | collective-permute-done | bytes 65568 | tf_op jit(solution)/shard_map/ppermute | solution.py:363
  27.7 0.0 collective-permute-done.6.refs_3_
  27.7 1.3 %shard_map.90 = (f32[64,3200]{1,0:T(8,128)S(1)}, bf16[64,3200]{1,0:T(8,128)(2,1)S(1)}) custom-call(s32[8]{0:T(128)S(1)} %copy-done.4, bf16[3200,256]{1,0:T(8,128)(2,1)S(1)} %copy-done, bf16[128,256]{1,0:T(8,128)(2,1)S(1)} %get-tuple-element.23.refs_0_, bf16[128,256]{1,0:T(8,128)(2,1)S(1)} %collective-permute-done.4.refs_1_, ...), custom_call_target="tpu_custom_call" | custom-call | flops 209715200 | bytes 2867200 | tf_op jit(solution)/shard_map/pallas_call | solution.py:365
  29.1 0.1 collective-permute-start.7
  29.1 1.7 %collective-permute-done.7.other_ref = bf16[64,3200]{1,0:T(8,128)(2,1)S(1)} collective-permute-done((bf16[64,3200]{1,0:T(8,128)(2,1)S(1)}, bf16[64,3200]{1,0:T(8,128)(2,1)S(1)}, u32[]{:S(2)}, u32[]{:S(2)}) %collective-permute-start.7) | collective-permute-done | bytes 409632 | tf_op jit(solution)/shard_map/ppermute | solution.py:373
  30.9 0.1 shard_map.91
  31.0 2.5 %collective-permute-start.8 = (bf16[16,3200]{1,0:T(8,128)(2,1)S(1)}, bf16[16,3200]{1,0:T(8,128)(2,1)S(1)}, u32[]{:S(2)}, u32[]{:S(2)}) collective-permute-start(bf16[16,3200]{1,0:T(8,128)(2,1)S(1)} %get-tuple-element.31), channel_id=1, source_target_pairs={{0,17},{1,16},{8,25},{9,24},{16,1},{17,0},{24,9},{25,8},{2,19},{3,... | collective-permute-start | bytes 307208 | tf_op jit(solution)/shard_map/ppermute | solution.py:383
  33.5 0.5 %collective-permute-start.9 = (bf16[16,3200]{1,0:T(8,128)(2,1)S(1)}, bf16[16,3200]{1,0:T(8,128)(2,1)S(1)}, u32[]{:S(2)}, u32[]{:S(2)}) collective-permute-start(bf16[16,3200]{1,0:T(8,128)(2,1)S(1)} %get-tuple-element.32), channel_id=1, source_target_pairs={{0,16},{1,17},{8,24},{9,25},{16,0},{17,1},{24,8},{25,9},{2,18},{3,... | collective-permute-start | bytes 307208 | tf_op jit(solution)/shard_map/ppermute | solution.py:383
  34.0 0.5 collective-permute-start.10
  34.5 3.1 %collective-permute-done.8.refs_0_ = bf16[16,3200]{1,0:T(8,128)(2,1)S(1)} collective-permute-done((bf16[16,3200]{1,0:T(8,128)(2,1)S(1)}, bf16[16,3200]{1,0:T(8,128)(2,1)S(1)}, u32[]{:S(2)}, u32[]{:S(2)}) %collective-permute-start.8) | collective-permute-done | bytes 102432 | tf_op jit(solution)/shard_map/ppermute | solution.py:383
  37.6 1.5 %collective-permute-done.9.refs_1_ = bf16[16,3200]{1,0:T(8,128)(2,1)S(1)} collective-permute-done((bf16[16,3200]{1,0:T(8,128)(2,1)S(1)}, bf16[16,3200]{1,0:T(8,128)(2,1)S(1)}, u32[]{:S(2)}, u32[]{:S(2)}) %collective-permute-start.9) | collective-permute-done | bytes 102432 | tf_op jit(solution)/shard_map/ppermute | solution.py:383
  39.1 0.0 collective-permute-done.10.refs_2_
  39.1 0.2 shard_map.92.refs_3_
  39.3 1.5 %collective-permute-start.15 = (bf16[16,3200]{1,0:T(8,128)(2,1)S(1)}, bf16[16,3200]{1,0:T(8,128)(2,1)S(1)}, u32[]{:S(2)}, u32[]{:S(2)}) collective-permute-start(bf16[16,3200]{1,0:T(8,128)(2,1)S(1)} %shard_map.92.refs_3_), channel_id=1, source_target_pairs={{0,1},{1,0},{8,9},{9,8},{16,17},{17,16},{24,25},{25,24},{2,3},{3,2... | collective-permute-start | bytes 307208 | tf_op jit(solution)/shard_map/ppermute | solution.py:394
  40.8 1.5 %collective-permute-start.13 = (bf16[16,3200]{1,0:T(8,128)(2,1)S(1)}, bf16[16,3200]{1,0:T(8,128)(2,1)S(1)}, u32[]{:S(2)}, u32[]{:S(2)}) collective-permute-start(bf16[16,3200]{1,0:T(8,128)(2,1)S(1)} %shard_map.92.refs_3_), channel_id=1, source_target_pairs={{0,16},{1,17},{8,24},{9,25},{16,0},{17,1},{24,8},{25,9},{2,18},{3,... | collective-permute-start | bytes 307208 | tf_op jit(solution)/shard_map/ppermute | solution.py:394
  42.3 0.5 %collective-permute-start.11 = (bf16[16,3200]{1,0:T(8,128)(2,1)S(1)}, bf16[16,3200]{1,0:T(8,128)(2,1)S(1)}, u32[]{:S(2)}, u32[]{:S(2)}) collective-permute-start(bf16[16,3200]{1,0:T(8,128)(2,1)S(1)} %shard_map.92.refs_3_), channel_id=1, source_target_pairs={{0,17},{1,16},{8,25},{9,24},{16,1},{17,0},{24,9},{25,8},{2,19},{3,... | collective-permute-start | bytes 307208 | tf_op jit(solution)/shard_map/ppermute | solution.py:394
  42.9 0.0 collective-permute-start.17
  42.9 1.2 %collective-permute-done.15.refs_2_ = bf16[16,3200]{1,0:T(8,128)(2,1)S(1)} collective-permute-done((bf16[16,3200]{1,0:T(8,128)(2,1)S(1)}, bf16[16,3200]{1,0:T(8,128)(2,1)S(1)}, u32[]{:S(2)}, u32[]{:S(2)}) %collective-permute-start.15) | collective-permute-done | bytes 102432 | tf_op jit(solution)/shard_map/ppermute | solution.py:394
  44.0 0.0 collective-permute-start.16
  44.0 2.3 %collective-permute-done.13.refs_1_ = bf16[16,3200]{1,0:T(8,128)(2,1)S(1)} collective-permute-done((bf16[16,3200]{1,0:T(8,128)(2,1)S(1)}, bf16[16,3200]{1,0:T(8,128)(2,1)S(1)}, u32[]{:S(2)}, u32[]{:S(2)}) %collective-permute-start.13) | collective-permute-done | bytes 102432 | tf_op jit(solution)/shard_map/ppermute | solution.py:394
  46.3 0.0 collective-permute-start.14
  46.3 1.6 %collective-permute-done.11.refs_0_ = bf16[16,3200]{1,0:T(8,128)(2,1)S(1)} collective-permute-done((bf16[16,3200]{1,0:T(8,128)(2,1)S(1)}, bf16[16,3200]{1,0:T(8,128)(2,1)S(1)}, u32[]{:S(2)}, u32[]{:S(2)}) %collective-permute-start.11) | collective-permute-done | bytes 102432 | tf_op jit(solution)/shard_map/ppermute | solution.py:394
  47.9 0.0 collective-permute-start.12
  47.9 0.8 %shard_map.93.refs_4_ = bf16[128,3200]{1,0:T(8,128)(2,1)} custom-call(bf16[16,3200]{1,0:T(8,128)(2,1)S(1)} %collective-permute-done.11.refs_0_, bf16[16,3200]{1,0:T(8,128)(2,1)S(1)} %collective-permute-done.13.refs_1_, bf16[16,3200]{1,0:T(8,128)(2,1)S(1)} %collective-permute-done.15.refs_2_, bf16[16,3200]{1,0:T(8,128)(2,1)S(1)} %shard_map.92.refs_3_), custom_call_target="tpu_custom_call" | custom-call | bytes 819200 | tf_op jit(solution)/shard_map/pallas_call | solution.py:399
  48.7 0.0 collective-permute-done.17.refs_3_
  48.7 0.0 collective-permute-done.16.refs_2_
  48.7 0.0 collective-permute-done.14.refs_1_
  48.7 0.5 collective-permute-done.12.refs_0_
  49.2 0.8 %shard_map.94 = bf16[128,3200]{1,0:T(8,128)(2,1)} custom-call(bf16[16,3200]{1,0:T(8,128)(2,1)S(1)} %collective-permute-done.12.refs_0_, bf16[16,3200]{1,0:T(8,128)(2,1)S(1)} %collective-permute-done.14.refs_1_, bf16[16,3200]{1,0:T(8,128)(2,1)S(1)} %collective-permute-done.16.refs_2_, ...), custom_call_target="tpu_custom_call", output_to_operand_aliasing={{}: (4, {})} | custom-call | bytes 819200 | tf_op jit(solution)/shard_map/pallas_call | solution.py:399
  (9 shorter events, 0.0 us)
Async XLA Ops:
  0.6 17.0 %copy-start.2 = (bf16[128,512]{1,0:T(8,128)(2,1)S(1)}, bf16[128,512]{1,0:T(8,128)(2,1)}, u32[]{:S(2)}) copy-start(bf16[128,512]{1,0:T(8,128)(2,1)} %g_ref.3) | copy-start | bytes 393220
  0.6 17.0 %copy-start.1 = (bf16[128,512]{1,0:T(8,128)(2,1)S(1)}, bf16[128,512]{1,0:T(8,128)(2,1)}, u32[]{:S(2)}) copy-start(bf16[128,512]{1,0:T(8,128)(2,1)} %q_ref.3) | copy-start | bytes 393220
  0.7 8.2 %collective-permute-start = (bf16[128,256]{1,0:T(8,128)(2,1)}, bf16[128,256]{1,0:T(8,128)(2,1)S(1)}, u32[]{:S(2)}, u32[]{:S(2)}) collective-permute-start(bf16[128,256]{1,0:T(8,128)(2,1)} %text_ref.1), channel_id=1, source_target_pairs={{0,6},{2,4},{4,0},{6,2},{1,7},{3,5},{5,1},{7,3},{8,14},{10,12},{12... | collective-permute-start | bytes 196616 | tf_op jit(solution)/shard_map/ppermute | solution.py:303
  5.8 0.7 %copy-start.3 = (f32[3200]{0:T(1024)S(1)}, f32[3200]{0:T(1024)}, u32[]{:S(2)}) copy-start(f32[3200]{0:T(1024)} %param.8) | copy-start | bytes 38404
  6.5 2.4 %copy-start.4 = (s32[8]{0:T(128)S(1)}, s32[8]{0:T(128)}, u32[]{:S(2)}) copy-start(s32[8]{0:T(128)} %pieces_ref.5) | copy-start | bytes 100
  6.5 11.2 %copy-start.5 = (bf16[128,256]{1,0:T(8,128)(2,1)S(1)}, bf16[128,256]{1,0:T(8,128)(2,1)}, u32[]{:S(2)}) copy-start(bf16[128,256]{1,0:T(8,128)(2,1)} %text_ref.1) | copy-start | bytes 196612
  8.7 19.0 %copy-start = (bf16[3200,256]{1,0:T(8,128)(2,1)S(1)}, bf16[3200,256]{1,0:T(8,128)(2,1)}, u32[]{:S(2)}) copy-start(bf16[3200,256]{1,0:T(8,128)(2,1)} %proj_ref.1) | copy-start | bytes 4915204
  8.8 6.8 %collective-permute-start.1 = (bf16[128,256]{1,0:T(8,128)(2,1)S(1)}, bf16[128,256]{1,0:T(8,128)(2,1)S(1)}, u32[]{:S(2)}, u32[]{:S(2)}) collective-permute-start(bf16[128,256]{1,0:T(8,128)(2,1)S(1)} %get-tuple-element.18.image_ref), channel_id=1, source_target_pairs={{6,0},{4,2},{0,4},{2,6},{7,1},{5,3},{1,5},{3,7},{14,8},{12,10},{8,... | collective-permute-start | bytes 196616 | tf_op jit(solution)/shard_map/ppermute | solution.py:323
  9.5 7.3 %collective-permute-start.3 = (bf16[128,256]{1,0:T(8,128)(2,1)S(1)}, bf16[128,256]{1,0:T(8,128)(2,1)S(1)}, u32[]{:S(2)}, u32[]{:S(2)}) collective-permute-start(bf16[128,256]{1,0:T(8,128)(2,1)S(1)} %shard_map.87.own_ref), channel_id=1, source_target_pairs={{0,6},{2,4},{4,0},{6,2},{1,7},{3,5},{5,1},{7,3},{8,14},{10,12},{12... | collective-permute-start | bytes 196616 | tf_op jit(solution)/shard_map/ppermute | solution.py:332
  13.4 4.3 %collective-permute-start.2 = (bf16[128,256]{1,0:T(8,128)(2,1)S(1)}, bf16[128,256]{1,0:T(8,128)(2,1)S(1)}, u32[]{:S(2)}, u32[]{:S(2)}) collective-permute-start(bf16[128,256]{1,0:T(8,128)(2,1)S(1)} %shard_map.87.own_ref), channel_id=1, source_target_pairs={{0,2},{2,0},{4,6},{6,4},{1,3},{3,1},{5,7},{7,5},{8,10},{10,8},{12,... | collective-permute-start | bytes 196616 | tf_op jit(solution)/shard_map/ppermute | solution.py:332
  19.5 6.5 %collective-permute-start.4 = (bf16[128,256]{1,0:T(8,128)(2,1)S(1)}, bf16[128,256]{1,0:T(8,128)(2,1)S(1)}, u32[]{:S(2)}, u32[]{:S(2)}) collective-permute-start(bf16[128,256]{1,0:T(8,128)(2,1)S(1)} %get-tuple-element.24), channel_id=1, source_target_pairs={{0,6},{2,4},{4,2},{6,0},{1,7},{3,5},{5,3},{7,1},{8,14},{10,12},{12... | collective-permute-start | bytes 196616 | tf_op jit(solution)/shard_map/ppermute | solution.py:363
  21.4 6.4 %collective-permute-start.5 = (bf16[128,256]{1,0:T(8,128)(2,1)S(1)}, bf16[128,256]{1,0:T(8,128)(2,1)S(1)}, u32[]{:S(2)}, u32[]{:S(2)}) collective-permute-start(bf16[128,256]{1,0:T(8,128)(2,1)S(1)} %get-tuple-element.25), channel_id=1, source_target_pairs={{0,4},{2,6},{4,0},{6,2},{1,5},{3,7},{5,1},{7,3},{8,12},{10,14},{12... | collective-permute-start | bytes 196616 | tf_op jit(solution)/shard_map/ppermute | solution.py:363
  21.7 6.0 %collective-permute-start.6 = (bf16[128,256]{1,0:T(8,128)(2,1)S(1)}, bf16[128,256]{1,0:T(8,128)(2,1)S(1)}, u32[]{:S(2)}, u32[]{:S(2)}) collective-permute-start(bf16[128,256]{1,0:T(8,128)(2,1)S(1)} %get-tuple-element.26), channel_id=1, source_target_pairs={{0,2},{2,0},{4,6},{6,4},{1,3},{3,1},{5,7},{7,5},{8,10},{10,8},{12,... | collective-permute-start | bytes 196616 | tf_op jit(solution)/shard_map/ppermute | solution.py:363
  29.1 1.8 %collective-permute-start.7 = (bf16[64,3200]{1,0:T(8,128)(2,1)S(1)}, bf16[64,3200]{1,0:T(8,128)(2,1)S(1)}, u32[]{:S(2)}, u32[]{:S(2)}) collective-permute-start(bf16[64,3200]{1,0:T(8,128)(2,1)S(1)} %get-tuple-element.28), channel_id=1, source_target_pairs={{0,8},{1,9},{8,0},{9,1},{16,24},{17,25},{24,16},{25,17},{2,10},{3,... | collective-permute-start | bytes 1228808 | tf_op jit(solution)/shard_map/ppermute | solution.py:373
  31.0 6.7 %collective-permute-start.8 = (bf16[16,3200]{1,0:T(8,128)(2,1)S(1)}, bf16[16,3200]{1,0:T(8,128)(2,1)S(1)}, u32[]{:S(2)}, u32[]{:S(2)}) collective-permute-start(bf16[16,3200]{1,0:T(8,128)(2,1)S(1)} %get-tuple-element.31), channel_id=1, source_target_pairs={{0,17},{1,16},{8,25},{9,24},{16,1},{17,0},{24,9},{25,8},{2,19},{3,... | collective-permute-start | bytes 307208 | tf_op jit(solution)/shard_map/ppermute | solution.py:383
  33.5 5.6 %collective-permute-start.9 = (bf16[16,3200]{1,0:T(8,128)(2,1)S(1)}, bf16[16,3200]{1,0:T(8,128)(2,1)S(1)}, u32[]{:S(2)}, u32[]{:S(2)}) collective-permute-start(bf16[16,3200]{1,0:T(8,128)(2,1)S(1)} %get-tuple-element.32), channel_id=1, source_target_pairs={{0,16},{1,17},{8,24},{9,25},{16,0},{17,1},{24,8},{25,9},{2,18},{3,... | collective-permute-start | bytes 307208 | tf_op jit(solution)/shard_map/ppermute | solution.py:383
  34.0 5.1 %collective-permute-start.10 = (bf16[16,3200]{1,0:T(8,128)(2,1)S(1)}, bf16[16,3200]{1,0:T(8,128)(2,1)S(1)}, u32[]{:S(2)}, u32[]{:S(2)}) collective-permute-start(bf16[16,3200]{1,0:T(8,128)(2,1)S(1)} %get-tuple-element.33), channel_id=1, source_target_pairs={{0,1},{1,0},{8,9},{9,8},{16,17},{17,16},{24,25},{25,24},{2,3},{3,2... | collective-permute-start | bytes 307208 | tf_op jit(solution)/shard_map/ppermute | solution.py:383
  39.3 4.7 %collective-permute-start.15 = (bf16[16,3200]{1,0:T(8,128)(2,1)S(1)}, bf16[16,3200]{1,0:T(8,128)(2,1)S(1)}, u32[]{:S(2)}, u32[]{:S(2)}) collective-permute-start(bf16[16,3200]{1,0:T(8,128)(2,1)S(1)} %shard_map.92.refs_3_), channel_id=1, source_target_pairs={{0,1},{1,0},{8,9},{9,8},{16,17},{17,16},{24,25},{25,24},{2,3},{3,2... | collective-permute-start | bytes 307208 | tf_op jit(solution)/shard_map/ppermute | solution.py:394
  40.8 5.5 %collective-permute-start.13 = (bf16[16,3200]{1,0:T(8,128)(2,1)S(1)}, bf16[16,3200]{1,0:T(8,128)(2,1)S(1)}, u32[]{:S(2)}, u32[]{:S(2)}) collective-permute-start(bf16[16,3200]{1,0:T(8,128)(2,1)S(1)} %shard_map.92.refs_3_), channel_id=1, source_target_pairs={{0,16},{1,17},{8,24},{9,25},{16,0},{17,1},{24,8},{25,9},{2,18},{3,... | collective-permute-start | bytes 307208 | tf_op jit(solution)/shard_map/ppermute | solution.py:394
  42.3 5.6 %collective-permute-start.11 = (bf16[16,3200]{1,0:T(8,128)(2,1)S(1)}, bf16[16,3200]{1,0:T(8,128)(2,1)S(1)}, u32[]{:S(2)}, u32[]{:S(2)}) collective-permute-start(bf16[16,3200]{1,0:T(8,128)(2,1)S(1)} %shard_map.92.refs_3_), channel_id=1, source_target_pairs={{0,17},{1,16},{8,25},{9,24},{16,1},{17,0},{24,9},{25,8},{2,19},{3,... | collective-permute-start | bytes 307208 | tf_op jit(solution)/shard_map/ppermute | solution.py:394
  42.9 5.8 %collective-permute-start.17 = (bf16[16,3200]{1,0:T(8,128)(2,1)S(1)}, bf16[16,3200]{1,0:T(8,128)(2,1)S(1)}, u32[]{:S(2)}, u32[]{:S(2)}) collective-permute-start(bf16[16,3200]{1,0:T(8,128)(2,1)S(1)} %shard_map.92.refs_3_), channel_id=1, source_target_pairs={{0,8},{1,9},{8,0},{9,1},{16,24},{17,25},{24,16},{25,17},{2,10},{3,... | collective-permute-start | bytes 307208 | tf_op jit(solution)/shard_map/ppermute | solution.py:395
  44.0 4.6 %collective-permute-start.16 = (bf16[16,3200]{1,0:T(8,128)(2,1)S(1)}, bf16[16,3200]{1,0:T(8,128)(2,1)S(1)}, u32[]{:S(2)}, u32[]{:S(2)}) collective-permute-start(bf16[16,3200]{1,0:T(8,128)(2,1)S(1)} %collective-permute-done.15.refs_2_), channel_id=1, source_target_pairs={{0,8},{1,9},{8,0},{9,1},{16,24},{17,25},{24,16},{25,17},{2,10},{3,... | collective-permute-start | bytes 307208 | tf_op jit(solution)/shard_map/ppermute | solution.py:395
  46.3 2.4 %collective-permute-start.14 = (bf16[16,3200]{1,0:T(8,128)(2,1)S(1)}, bf16[16,3200]{1,0:T(8,128)(2,1)S(1)}, u32[]{:S(2)}, u32[]{:S(2)}) collective-permute-start(bf16[16,3200]{1,0:T(8,128)(2,1)S(1)} %collective-permute-done.13.refs_1_), channel_id=1, source_target_pairs={{0,8},{1,9},{8,0},{9,1},{16,24},{17,25},{24,16},{25,17},{2,10},{3,... | collective-permute-start | bytes 307208 | tf_op jit(solution)/shard_map/ppermute | solution.py:395
  47.9 1.3 %collective-permute-start.12 = (bf16[16,3200]{1,0:T(8,128)(2,1)S(1)}, bf16[16,3200]{1,0:T(8,128)(2,1)S(1)}, u32[]{:S(2)}, u32[]{:S(2)}) collective-permute-start(bf16[16,3200]{1,0:T(8,128)(2,1)S(1)} %collective-permute-done.11.refs_0_), channel_id=1, source_target_pairs={{0,8},{1,9},{8,0},{9,1},{16,24},{17,25},{24,16},{25,17},{2,10},{3,... | collective-permute-start | bytes 307208 | tf_op jit(solution)/shard_map/ppermute | solution.py:395

commit v10 on v9

--- a/solution.py
+++ b/solution.py
@@ -203,24 +203,38 @@
             out_ref[:, h * HD : (h + 1) * HD] = part.astype(jnp.bfloat16)
 
 
-def back_body(seq_n, piece, pieces_ref, proj_ref, *refs):
-    part_refs, (keep_ref, send_ref) = refs[:-2], refs[-2:]
+def back_body(seq_n, count, piece, pieces_ref, proj_ref, *refs):
+    part_refs, (rest_ref, keep_ref, send_ref) = refs[:-3], refs[-3:]
     rows = part_refs[0].shape[0]
-    half = rows // 2
     before = pieces_ref[2 * held_image(lax.axis_index("seq"), seq_n)]
     parity, place = group_place()
     total = part_refs[0][...].astype(jnp.float32)
     for ref in part_refs[1:]:
         total += ref[...].astype(jnp.float32)
     slot = lax.broadcasted_iota(jnp.int32, (rows, rows), 0)
-    to = (lax.div(slot, half) ^ parity) * half
-    to += (lax.div(lax.rem(slot, half), piece) ^ place) * piece + lax.rem(slot, piece)
+    group = lax.div(slot, piece)
+    core = jnp.where(group < 2, group, jnp.where(group > count, 1, 0))
+    step = jnp.where(group < 2, count - 1, lax.rem(group + count - 3, count - 1))
+    to = ((core ^ parity) * count + (step ^ place)) * piece + lax.rem(slot, piece)
     source = lax.broadcasted_iota(jnp.int32, (rows, rows), 1)
     pick = jnp.where(source == to + before, 1.0, 0.0).astype(jnp.bfloat16)
     image_grad = jnp.dot(pick, total.astype(jnp.bfloat16), preferred_element_type=jnp.float32)
-    product = dot(image_grad.astype(jnp.bfloat16), proj_ref[...], ((1,), (1,)))
+    image_grad = image_grad.astype(jnp.bfloat16)
+    product = dot(image_grad[: 2 * piece], proj_ref[...], ((1,), (1,)))
+    keep_ref[...] = product[:piece]
+    send_ref[...] = product[piece:].astype(jnp.bfloat16)
+    rest_ref[...] = image_grad[2 * piece :]
+
+
+def rest_body(rest_ref, proj_ref, keep_ref, send_ref):
+    half = rest_ref.shape[0] // 2
+    product = dot(rest_ref[...], proj_ref[...], ((1,), (1,)))
     keep_ref[...] = product[:half]
     send_ref[...] = product[half:].astype(jnp.bfloat16)
+
+
+def last_body(keep_ref, other_ref, send_ref):
+    send_ref[...] = (keep_ref[...] + other_ref[...].astype(jnp.float32)).astype(jnp.bfloat16)
 
 
 def pair_body(piece, keep_ref, other_ref, own_ref, *send_refs):
@@ -252,13 +266,13 @@
         out_ref[:, c : c + HD] = (scaled[n] * inverse - own * lead).astype(jnp.bfloat16)
 
 
-def gather_body(count, core, *refs):
-    part_refs, (out_hbm, sems) = refs[:count], refs[-2:]
+def gather_body(count, chosen, *refs):
+    part_refs, (out_hbm, sems) = refs[: len(chosen)], refs[-2:]
     piece = part_refs[0].shape[0]
     parity, place = group_place()
     copies = []
-    for n, ref in enumerate(part_refs):
-        row = ((parity ^ core) * count + (place ^ (count - 1 - n))) * piece
+    for n, (ref, (core, step)) in enumerate(zip(part_refs, chosen)):
+        row = ((parity ^ core) * count + (place ^ step)) * piece
         copy = pltpu.make_async_copy(ref, out_hbm.at[pl.ds(pl.multiple_of(row, piece), piece), :], sems.at[n])
         copy.start()
         copies.append(copy)
@@ -362,25 +376,41 @@
     )(queries, grad_out, low, dscore, values)
     parts = [lax.ppermute(g, "seq", pairs) for g, pairs in zip(grads, pairs_back)]
 
+    def shape(height, dtype):
+        return jax.ShapeDtypeStruct((height, width), dtype)
+
+    rest, keep_last, send_last = call(
+        functools.partial(back_body, seq_n, count, piece),
+        [jax.ShapeDtypeStruct((rows - 2 * piece, columns), bf16), shape(piece, f32), shape(piece, bf16)],
+        [SCALARS] + [WHOLE] * (2 + len(parts)),
+        [WHOLE] * 3,
+        4 * piece * width * columns,
+        2 * width * columns + 6 * piece * width,
+    )(pieces, key_value_proj, own_grad, *parts)
+    other_last = lax.ppermute(send_last, names, core_pairs)
+    height = rows // 2 - piece
     keep, send = call(
-        functools.partial(back_body, seq_n, piece),
-        [jax.ShapeDtypeStruct((rows // 2, width), f32), jax.ShapeDtypeStruct((rows // 2, width), bf16)],
-        [SCALARS] + [WHOLE] * (2 + len(parts)),
+        rest_body,
+        [shape(height, f32), shape(height, bf16)],
         [WHOLE, WHOLE],
-        2 * rows * width * columns,
-        2 * width * columns + 3 * rows * width,
-    )(pieces, key_value_proj, own_grad, *parts)
+        [WHOLE, WHOLE],
+        4 * height * width * columns,
+        2 * width * columns + 6 * height * width,
+    )(rest, key_value_proj)
     other = lax.ppermute(send, names, core_pairs)
-    steps = list(range(1, count))
+    weight = 64 * rows * width * columns
+    far = call(last_body, shape(piece, bf16), [WHOLE, WHOLE], WHOLE, weight, 8 * piece * width)(keep_last, other_last)
+    shares = [lax.ppermute(far, names, far_pairs(count - 1))]
     own_sum, *sends = call(
         functools.partial(pair_body, piece),
-        [jax.ShapeDtypeStruct((piece, width), f32)] + [jax.ShapeDtypeStruct((piece, width), bf16)] * len(steps),
+        [shape(piece, f32)] + [shape(piece, bf16)] * (count - 2),
         [WHOLE, WHOLE],
-        [WHOLE] * count,
+        [WHOLE] * (count - 1),
         0,
-        6 * rows // 2 * width,
+        8 * height * width,
     )(keep, other)
-    shares = [lax.ppermute(sends[d - 1], names, far_pairs(d)) for d in steps[::-1]]
+    steps = list(range(1, count))
+    shares += [lax.ppermute(sends[d - 1], names, far_pairs(d)) for d in steps[-2::-1]]
     mine = call(
         final_body,
         jax.ShapeDtypeStruct((piece, width), bf16),
@@ -393,19 +423,22 @@
     for d in steps:
         mines[d] = lax.ppermute(mine, names, far_pairs(d))
     theirs = {d: lax.ppermute(mines[d], names, core_pairs) for d in range(count)}
+    ready = {(core, d): part[d] for core, part in enumerate((mines, theirs)) for d in range(count)}
+    order = sorted(ready, key=lambda key: (key[0], -key[1]))
+    last = (1, count - 1)
     vis_grad = None
-    for core, parts in enumerate((mines, theirs)):
+    for chosen in ([key for key in order if key != last], [last]):
         done = [] if vis_grad is None else [vis_grad]
         vis_grad = call(
-            functools.partial(gather_body, count, core),
-            jax.ShapeDtypeStruct((rows, width), bf16),
-            [WHOLE] * count + [hbm] * len(done),
+            functools.partial(gather_body, count, chosen),
+            shape(rows, bf16),
+            [WHOLE] * len(chosen) + [hbm] * len(done),
             hbm,
             0,
-            2 * rows * width,
-            scratch_shapes=[pltpu.SemaphoreType.DMA((count,))],
-            input_output_aliases={count: 0} if done else {},
-        )(*[parts[d] for d in reversed(range(count))], *done)
+            4 * piece * width * len(chosen),
+            scratch_shapes=[pltpu.SemaphoreType.DMA((len(chosen),))],
+            input_output_aliases={len(chosen): 0} if done else {},
+        )(*[ready[key] for key in chosen], *done)
     return (attended, vis_grad)
 
 

time: 50.2 us -> 49.5 us (0.986)
  waiting for transfers between devices: 18.9 us -> 16.4 us
  starting transfers between devices: 20.6 us -> 21.8 us
  Pallas kernels: 8.94 us -> 9.52 us
    ppermute x3 -> x2, waiting for transfers between devices: 4.6 us -> 1.57 us  [on_device(): lax.ppermute(sends[d - 1], names, far_pairs(d))]
    ppermute x0 -> x2, starting transfers between devices: none -> 2.57 us  [the longest x1 2.52 us: on_device(): shares = [lax.ppermute(far, names, far_pairs(count - 1))]]
    ppermute x0 -> x2, waiting for transfers between devices: none -> 2.51 us  [the longest x1 2.4 us: on_device(): shares = [lax.ppermute(far, names, far_pairs(count - 1))]]
    ppermute x3 -> x2, starting transfers between devices: 3.55 us -> 1.66 us  [on_device(): lax.ppermute(sends[d - 1], names, far_pairs(d))]
    ppermute x1, waiting for transfers between devices: 1.73 us -> 0.01 us  [on_device(): other = lax.ppermute(send, names, core_pairs)]
    pallas_call x4 -> x6, Pallas kernels: 2.94 us -> 3.52 us  [the longest x2 1.57 us: on_device(): call(functools.partial(gather_body, count, chosen), shape(rows, bf16), [W...]
  transfers between devices with their start and end apart: 18 -> 19, of which waited for: 12 -> 13; matrix products, arithmetic and copies ran while one was open for 0% -> 0% of each run, Pallas kernels for 10% -> 11%
where the time goes in v10:
time: 49.5 us; the launch traced here: 49.2 us
  starting transfers between devices  21.8 us (44%)
  waiting for transfers between devices  16.4 us (33%)
  Pallas kernels  9.52 us (19%)
  between operations  0.76 us (2%)
  local copies, waits for them, and re-layouts  0.74 us (1%)
    ppermute x1, starting transfers between devices, on_device(): text = lax.ppermute(text_kv, 'seq', list(enumerate(owners)))  5.1 us
    ppermute x3, waiting for transfers between devices, on_device(): mines[d] = lax.ppermute(mine, names, far_pairs(d))  4.95 us
    ppermute x3, starting transfers between devices, on_device(): lax.ppermute(g, 'seq', pairs)  4.45 us
    ppermute x2, starting transfers between devices, on_device(): blocks = [lax.ppermute(block, 'seq', pairs) for pairs in forth]  3.85 us
    ppermute x3, starting transfers between devices, on_device(): mines[d] = lax.ppermute(mine, names, far_pairs(d))  3.55 us
    ppermute x3, waiting for transfers between devices, on_device(): lax.ppermute(g, 'seq', pairs)  2.77 us
    ppermute x1, starting transfers between devices, on_device(): shares = [lax.ppermute(far, names, far_pairs(count - 1))]  2.52 us
    ppermute x1, waiting for transfers between devices, on_device(): shares = [lax.ppermute(far, names, far_pairs(count - 1))]  2.4 us
  transfers between devices with their start and end apart: 19, of which 13 were waited for; matrix products, arithmetic and copies ran while one was open for 0% of the time, Pallas kernels for 11%

profile of v10, /device:TPU:0, one launch (start us, length us, event | category | flops | bytes accessed | tf_op | source)
XLA Modules:
  0.0 49.2 jit_solution(4213682869589878018)
XLA Ops:
  0.7 5.1 %collective-permute-start = (bf16[128,256]{1,0:T(8,128)(2,1)}, bf16[128,256]{1,0:T(8,128)(2,1)S(1)}, u32[]{:S(2)}, u32[]{:S(2)}) collective-permute-start(bf16[128,256]{1,0:T(8,128)(2,1)} %text_ref.1), channel_id=1, source_target_pairs={{0,6},{2,4},{4,0},{6,2},{1,7},{3,5},{5,1},{7,3},{8,14},{10,12},{12... | collective-permute-start | bytes 196616 | tf_op jit(solution)/shard_map/ppermute | solution.py:317
  5.8 0.7 %copy-done.3 = f32[3200]{0:T(1024)S(1)} copy-done((f32[3200]{0:T(1024)S(1)}, f32[3200]{0:T(1024)}, u32[]{:S(2)}) %copy-start.3) | copy-done | bytes 12824
  6.5 2.3 %shard_map.86 = (bf16[128,256]{1,0:T(8,128)(2,1)S(1)}, bf16[16,3200]{1,0:T(8,128)(2,1)S(1)}) custom-call(bf16[128,3200]{1,0:T(8,128)(2,1)} %vis_hbm.1, f32[25,128]{1,0:T(8,128)S(1)} %bitcast.1, bf16[3200,256]{1,0:T(8,128)(2,1)} %proj_ref.3), custom_call_target="tpu_custom_call" | custom-call | flops 209715200 | bytes 2457600 | tf_op jit(solution)/shard_map/pallas_call | solution.py:320
  8.7 0.0 copy-start
  8.8 0.1 collective-permute-start.1
  8.8 0.0 collective-permute-done.text_ref
  8.8 0.7 %shard_map.87.own_ref = bf16[128,256]{1,0:T(8,128)(2,1)S(1)} custom-call(s32[8]{0:T(128)S(1)} %copy-done.4, bf16[128,256]{1,0:T(8,128)(2,1)S(1)} %get-tuple-element.20.image_ref, bf16[128,256]{1,0:T(8,128)(2,1)S(1)} %collective-permute-done.text_ref), custom_call_target="tpu_custom_call" | custom-call | bytes 196608 | tf_op jit(solution)/shard_map/pallas_call | solution.py:338
  9.5 3.8 %collective-permute-start.3 = (bf16[128,256]{1,0:T(8,128)(2,1)S(1)}, bf16[128,256]{1,0:T(8,128)(2,1)S(1)}, u32[]{:S(2)}, u32[]{:S(2)}) collective-permute-start(bf16[128,256]{1,0:T(8,128)(2,1)S(1)} %shard_map.87.own_ref), channel_id=1, source_target_pairs={{0,6},{2,4},{4,0},{6,2},{1,7},{3,5},{5,1},{7,3},{8,14},{10,12},{12... | collective-permute-start | bytes 196616 | tf_op jit(solution)/shard_map/ppermute | solution.py:346
  13.4 0.0 collective-permute-start.2
  13.4 2.2 %collective-permute-done.1.raw_ref = bf16[128,256]{1,0:T(8,128)(2,1)S(1)} collective-permute-done((bf16[128,256]{1,0:T(8,128)(2,1)S(1)}, bf16[128,256]{1,0:T(8,128)(2,1)S(1)}, u32[]{:S(2)}, u32[]{:S(2)}) %collective-permute-start.1) | collective-permute-done | bytes 65568 | tf_op jit(solution)/shard_map/ppermute | solution.py:337
  15.6 1.3 %collective-permute-done.3.refs_1_ = bf16[128,256]{1,0:T(8,128)(2,1)S(1)} collective-permute-done((bf16[128,256]{1,0:T(8,128)(2,1)S(1)}, bf16[128,256]{1,0:T(8,128)(2,1)S(1)}, u32[]{:S(2)}, u32[]{:S(2)}) %collective-permute-start.3) | collective-permute-done | bytes 65568 | tf_op jit(solution)/shard_map/ppermute | solution.py:346
  16.9 0.8 %collective-permute-done.2.refs_0_ = bf16[128,256]{1,0:T(8,128)(2,1)S(1)} collective-permute-done((bf16[128,256]{1,0:T(8,128)(2,1)S(1)}, bf16[128,256]{1,0:T(8,128)(2,1)S(1)}, u32[]{:S(2)}, u32[]{:S(2)}) %collective-permute-start.2) | collective-permute-done | bytes 65568 | tf_op jit(solution)/shard_map/ppermute | solution.py:346
  17.7 1.8 %shard_map.88 = (bf16[512,512]{1,0:T(8,128)(2,1)S(1)}, bf16[512,512]{1,0:T(8,128)(2,1)S(1)}, bf16[512,128]{1,0:T(8,128)(2,1)S(1)}, bf16[128,256]{1,0:T(8,128)(2,...) custom-call(s32[8]{0:T(128)S(1)} %copy-done.4, bf16[128,512]{1,0:T(8,128)(2,1)S(1)} %copy-done.1, ...), custom_call_target="tpu_custom_call" | custom-call | flops 268435456 | bytes 786432 | tf_op jit(solution)/shard_map/pallas_call | solution.py:361
  19.5 1.9 %collective-permute-start.4 = (bf16[128,256]{1,0:T(8,128)(2,1)S(1)}, bf16[128,256]{1,0:T(8,128)(2,1)S(1)}, u32[]{:S(2)}, u32[]{:S(2)}) collective-permute-start(bf16[128,256]{1,0:T(8,128)(2,1)S(1)} %get-tuple-element.26), channel_id=1, source_target_pairs={{0,6},{2,4},{4,2},{6,0},{1,7},{3,5},{5,3},{7,1},{8,14},{10,12},{12... | collective-permute-start | bytes 196616 | tf_op jit(solution)/shard_map/ppermute | solution.py:377
  21.4 0.4 collective-permute-start.5
  21.7 2.2 %collective-permute-start.6 = (bf16[128,256]{1,0:T(8,128)(2,1)S(1)}, bf16[128,256]{1,0:T(8,128)(2,1)S(1)}, u32[]{:S(2)}, u32[]{:S(2)}) collective-permute-start(bf16[128,256]{1,0:T(8,128)(2,1)S(1)} %get-tuple-element.28), channel_id=1, source_target_pairs={{0,2},{2,0},{4,6},{6,4},{1,3},{3,1},{5,7},{7,5},{8,10},{10,8},{12,... | collective-permute-start | bytes 196616 | tf_op jit(solution)/shard_map/ppermute | solution.py:377
  24.0 1.0 %shard_map.89 = (bf16[128,512]{1,0:T(8,128)(2,1)}, bf16[128,256]{1,0:T(8,128)(2,1)S(1)}) custom-call(bf16[128,512]{1,0:T(8,128)(2,1)S(1)} %copy-done.1, bf16[128,512]{1,0:T(8,128)(2,1)S(1)} %copy-done.2, bf16[512,512]{1,0:T(8,128)(2,1)S(1)} %get-tuple-element.21.low_ref, bf16[512,512]{1,0:T(8,128)(2,1)S(1)} %get-tuple-element.22.dscore_ref, ...), custom_call_target="tpu_custom_call" | custom-call | flops 67108864 | bytes 917504 | tf_op jit(solution)/shard_map/pallas_call | solution.py:369
  25.0 1.0 %collective-permute-done.4.refs_1_ = bf16[128,256]{1,0:T(8,128)(2,1)S(1)} collective-permute-done((bf16[128,256]{1,0:T(8,128)(2,1)S(1)}, bf16[128,256]{1,0:T(8,128)(2,1)S(1)}, u32[]{:S(2)}, u32[]{:S(2)}) %collective-permute-start.4) | collective-permute-done | bytes 65568 | tf_op jit(solution)/shard_map/ppermute | solution.py:377
  26.0 1.8 %collective-permute-done.5.refs_2_ = bf16[128,256]{1,0:T(8,128)(2,1)S(1)} collective-permute-done((bf16[128,256]{1,0:T(8,128)(2,1)S(1)}, bf16[128,256]{1,0:T(8,128)(2,1)S(1)}, u32[]{:S(2)}, u32[]{:S(2)}) %collective-permute-start.5) | collective-permute-done | bytes 65568 | tf_op jit(solution)/shard_map/ppermute | solution.py:377
  27.7 0.0 collective-permute-done.6.refs_3_
  27.8 1.2 %shard_map.90 = (bf16[96,256]{1,0:T(8,128)(2,1)S(1)}, f32[16,3200]{1,0:T(8,128)S(1)}, bf16[16,3200]{1,0:T(8,128)(2,1)S(1)}) custom-call(s32[8]{0:T(128)S(1)} %copy-done.4, bf16[3200,256]{1,0:T(8,128)(2,1)S(1)} %copy-done, bf16[128,256]{1,0:T(8,128)(2,1)S(1)} %get-tuple-element.25.refs_0_, bf16[128,256]{1,0:T(8,128)(2,1)S(1)} %collective-permute-done.4.refs_1_, ...), custom_call_target="tpu_custom_call" | custom-call | flops 52428800 | bytes 1945600 | tf_op jit(solution)/shard_map/pallas_call | solution.py:382
  29.0 0.1 collective-permute-start.8
  29.0 0.6 %shard_map.91 = (f32[48,3200]{1,0:T(8,128)S(1)}, bf16[48,3200]{1,0:T(8,128)(2,1)S(1)}) custom-call(bf16[96,256]{1,0:T(8,128)(2,1)S(1)} %get-tuple-element.29.rest_ref, bf16[3200,256]{1,0:T(8,128)(2,1)S(1)} %copy-done), custom_call_target="tpu_custom_call" | custom-call | flops 157286400 | bytes 2560000 | tf_op jit(solution)/shard_map/pallas_call | solution.py:392
  29.7 0.6 %collective-permute-start.7 = (bf16[48,3200]{1,0:T(8,128)(2,1)S(1)}, bf16[48,3200]{1,0:T(8,128)(2,1)S(1)}, u32[]{:S(2)}, u32[]{:S(2)}) collective-permute-start(bf16[48,3200]{1,0:T(8,128)(2,1)S(1)} %get-tuple-element.31), channel_id=1, source_target_pairs={{0,8},{1,9},{8,0},{9,1},{16,24},{17,25},{24,16},{25,17},{2,10},{3,... | collective-permute-start | bytes 921608 | tf_op jit(solution)/shard_map/ppermute | solution.py:400
  30.2 0.1 collective-permute-done.8.other_ref
  30.4 2.5 %collective-permute-start.9 = (bf16[16,3200]{1,0:T(8,128)(2,1)S(1)}, bf16[16,3200]{1,0:T(8,128)(2,1)S(1)}, u32[]{:S(2)}, u32[]{:S(2)}) collective-permute-start(bf16[16,3200]{1,0:T(8,128)(2,1)S(1)} %shard_map.93), channel_id=1, source_target_pairs={{0,17},{1,16},{8,25},{9,24},{16,1},{17,0},{24,9},{25,8},{2,19},{3,... | collective-permute-start | bytes 307208 | tf_op jit(solution)/shard_map/ppermute | solution.py:403
  32.9 0.0 collective-permute-done.7.other_ref
  32.9 0.1 shard_map.92
  33.0 0.6 %collective-permute-start.10 = (bf16[16,3200]{1,0:T(8,128)(2,1)S(1)}, bf16[16,3200]{1,0:T(8,128)(2,1)S(1)}, u32[]{:S(2)}, u32[]{:S(2)}) collective-permute-start(bf16[16,3200]{1,0:T(8,128)(2,1)S(1)} %get-tuple-element.36), channel_id=1, source_target_pairs={{0,16},{1,17},{8,24},{9,25},{16,0},{17,1},{24,8},{25,9},{2,18},{3,... | collective-permute-start | bytes 307208 | tf_op jit(solution)/shard_map/ppermute | solution.py:413
  33.6 1.1 %collective-permute-start.11 = (bf16[16,3200]{1,0:T(8,128)(2,1)S(1)}, bf16[16,3200]{1,0:T(8,128)(2,1)S(1)}, u32[]{:S(2)}, u32[]{:S(2)}) collective-permute-start(bf16[16,3200]{1,0:T(8,128)(2,1)S(1)} %get-tuple-element.37), channel_id=1, source_target_pairs={{0,1},{1,0},{8,9},{9,8},{16,17},{17,16},{24,25},{25,24},{2,3},{3,2... | collective-permute-start | bytes 307208 | tf_op jit(solution)/shard_map/ppermute | solution.py:413
  34.6 2.4 %collective-permute-done.9.refs_0_ = bf16[16,3200]{1,0:T(8,128)(2,1)S(1)} collective-permute-done((bf16[16,3200]{1,0:T(8,128)(2,1)S(1)}, bf16[16,3200]{1,0:T(8,128)(2,1)S(1)}, u32[]{:S(2)}, u32[]{:S(2)}) %collective-permute-start.9) | collective-permute-done | bytes 102432 | tf_op jit(solution)/shard_map/ppermute | solution.py:403
  37.0 1.5 %collective-permute-done.10.refs_1_ = bf16[16,3200]{1,0:T(8,128)(2,1)S(1)} collective-permute-done((bf16[16,3200]{1,0:T(8,128)(2,1)S(1)}, bf16[16,3200]{1,0:T(8,128)(2,1)S(1)}, u32[]{:S(2)}, u32[]{:S(2)}) %collective-permute-start.10) | collective-permute-done | bytes 102432 | tf_op jit(solution)/shard_map/ppermute | solution.py:413
  38.5 0.1 collective-permute-done.11.refs_2_
  38.6 0.2 shard_map.94.refs_3_
  38.8 1.6 %collective-permute-start.15 = (bf16[16,3200]{1,0:T(8,128)(2,1)S(1)}, bf16[16,3200]{1,0:T(8,128)(2,1)S(1)}, u32[]{:S(2)}, u32[]{:S(2)}) collective-permute-start(bf16[16,3200]{1,0:T(8,128)(2,1)S(1)} %shard_map.94.refs_3_), channel_id=1, source_target_pairs={{0,1},{1,0},{8,9},{9,8},{16,17},{17,16},{24,25},{25,24},{2,3},{3,2... | collective-permute-start | bytes 307208 | tf_op jit(solution)/shard_map/ppermute | solution.py:424
  40.4 1.3 %collective-permute-start.14 = (bf16[16,3200]{1,0:T(8,128)(2,1)S(1)}, bf16[16,3200]{1,0:T(8,128)(2,1)S(1)}, u32[]{:S(2)}, u32[]{:S(2)}) collective-permute-start(bf16[16,3200]{1,0:T(8,128)(2,1)S(1)} %shard_map.94.refs_3_), channel_id=1, source_target_pairs={{0,16},{1,17},{8,24},{9,25},{16,0},{17,1},{24,8},{25,9},{2,18},{3,... | collective-permute-start | bytes 307208 | tf_op jit(solution)/shard_map/ppermute | solution.py:424
  41.7 0.6 %collective-permute-start.12 = (bf16[16,3200]{1,0:T(8,128)(2,1)S(1)}, bf16[16,3200]{1,0:T(8,128)(2,1)S(1)}, u32[]{:S(2)}, u32[]{:S(2)}) collective-permute-start(bf16[16,3200]{1,0:T(8,128)(2,1)S(1)} %shard_map.94.refs_3_), channel_id=1, source_target_pairs={{0,17},{1,16},{8,25},{9,24},{16,1},{17,0},{24,9},{25,8},{2,19},{3,... | collective-permute-start | bytes 307208 | tf_op jit(solution)/shard_map/ppermute | solution.py:424
  42.3 0.0 collective-permute-start.18
  42.3 1.2 %collective-permute-done.15.refs_2_ = bf16[16,3200]{1,0:T(8,128)(2,1)S(1)} collective-permute-done((bf16[16,3200]{1,0:T(8,128)(2,1)S(1)}, bf16[16,3200]{1,0:T(8,128)(2,1)S(1)}, u32[]{:S(2)}, u32[]{:S(2)}) %collective-permute-start.15) | collective-permute-done | bytes 102432 | tf_op jit(solution)/shard_map/ppermute | solution.py:424
  43.5 0.0 collective-permute-start.17
  43.5 2.2 %collective-permute-done.14.refs_1_ = bf16[16,3200]{1,0:T(8,128)(2,1)S(1)} collective-permute-done((bf16[16,3200]{1,0:T(8,128)(2,1)S(1)}, bf16[16,3200]{1,0:T(8,128)(2,1)S(1)}, u32[]{:S(2)}, u32[]{:S(2)}) %collective-permute-start.14) | collective-permute-done | bytes 102432 | tf_op jit(solution)/shard_map/ppermute | solution.py:424
  45.7 0.0 collective-permute-start.16
  45.7 1.6 %collective-permute-done.12.refs_0_ = bf16[16,3200]{1,0:T(8,128)(2,1)S(1)} collective-permute-done((bf16[16,3200]{1,0:T(8,128)(2,1)S(1)}, bf16[16,3200]{1,0:T(8,128)(2,1)S(1)}, u32[]{:S(2)}, u32[]{:S(2)}) %collective-permute-start.12) | collective-permute-done | bytes 102432 | tf_op jit(solution)/shard_map/ppermute | solution.py:424
  47.3 0.0 collective-permute-done.17.refs_5_
  47.3 0.0 collective-permute-done.16.refs_4_
  47.3 0.9 %shard_map.95.refs_1_ = bf16[128,3200]{1,0:T(8,128)(2,1)} custom-call(bf16[16,3200]{1,0:T(8,128)(2,1)S(1)} %collective-permute-done.12.refs_0_, bf16[16,3200]{1,0:T(8,128)(2,1)S(1)} %collective-permute-done.14.refs_1_, bf16[16,3200]{1,0:T(8,128)(2,1)S(1)} %collective-permute-done.15.refs_2_, bf16[16,3200]{1,0:T(8,128)(2,1)S(1)} %shard_map.94.refs_3_, ...), custom_call_target="tpu_custom_call" | custom-call | bytes 1433600 | tf_op jit(solution)/shard_map/pallas_call | solution.py:432
  48.2 0.4 collective-permute-done.13.refs_0_
  48.6 0.6 %shard_map.96 = bf16[128,3200]{1,0:T(8,128)(2,1)} custom-call(bf16[16,3200]{1,0:T(8,128)(2,1)S(1)} %collective-permute-done.13.refs_0_, bf16[128,3200]{1,0:T(8,128)(2,1)} %shard_map.95.refs_1_), custom_call_target="tpu_custom_call", output_to_operand_aliasing={{}: (1, {})} | custom-call | bytes 204800 | tf_op jit(solution)/shard_map/pallas_call | solution.py:432
  (13 shorter events, 0.1 us)
Async XLA Ops:
  0.6 17.0 %copy-start.2 = (bf16[128,512]{1,0:T(8,128)(2,1)S(1)}, bf16[128,512]{1,0:T(8,128)(2,1)}, u32[]{:S(2)}) copy-start(bf16[128,512]{1,0:T(8,128)(2,1)} %g_ref.3) | copy-start | bytes 393220
  0.6 17.0 %copy-start.1 = (bf16[128,512]{1,0:T(8,128)(2,1)S(1)}, bf16[128,512]{1,0:T(8,128)(2,1)}, u32[]{:S(2)}) copy-start(bf16[128,512]{1,0:T(8,128)(2,1)} %q_ref.3) | copy-start | bytes 393220
  0.7 8.2 %collective-permute-start = (bf16[128,256]{1,0:T(8,128)(2,1)}, bf16[128,256]{1,0:T(8,128)(2,1)S(1)}, u32[]{:S(2)}, u32[]{:S(2)}) collective-permute-start(bf16[128,256]{1,0:T(8,128)(2,1)} %text_ref.1), channel_id=1, source_target_pairs={{0,6},{2,4},{4,0},{6,2},{1,7},{3,5},{5,1},{7,3},{8,14},{10,12},{12... | collective-permute-start | bytes 196616 | tf_op jit(solution)/shard_map/ppermute | solution.py:317
  5.8 0.7 %copy-start.3 = (f32[3200]{0:T(1024)S(1)}, f32[3200]{0:T(1024)}, u32[]{:S(2)}) copy-start(f32[3200]{0:T(1024)} %param.8) | copy-start | bytes 38404
  6.5 2.4 %copy-start.4 = (s32[8]{0:T(128)S(1)}, s32[8]{0:T(128)}, u32[]{:S(2)}) copy-start(s32[8]{0:T(128)} %pieces_ref.5) | copy-start | bytes 100
  6.5 11.2 %copy-start.5 = (bf16[128,256]{1,0:T(8,128)(2,1)S(1)}, bf16[128,256]{1,0:T(8,128)(2,1)}, u32[]{:S(2)}) copy-start(bf16[128,256]{1,0:T(8,128)(2,1)} %text_ref.1) | copy-start | bytes 196612
  8.7 19.0 %copy-start = (bf16[3200,256]{1,0:T(8,128)(2,1)S(1)}, bf16[3200,256]{1,0:T(8,128)(2,1)}, u32[]{:S(2)}) copy-start(bf16[3200,256]{1,0:T(8,128)(2,1)} %proj_ref.3) | copy-start | bytes 4915204
  8.8 6.8 %collective-permute-start.1 = (bf16[128,256]{1,0:T(8,128)(2,1)S(1)}, bf16[128,256]{1,0:T(8,128)(2,1)S(1)}, u32[]{:S(2)}, u32[]{:S(2)}) collective-permute-start(bf16[128,256]{1,0:T(8,128)(2,1)S(1)} %get-tuple-element.20.image_ref), channel_id=1, source_target_pairs={{6,0},{4,2},{0,4},{2,6},{7,1},{5,3},{1,5},{3,7},{14,8},{12,10},{8,... | collective-permute-start | bytes 196616 | tf_op jit(solution)/shard_map/ppermute | solution.py:337
  9.5 7.3 %collective-permute-start.3 = (bf16[128,256]{1,0:T(8,128)(2,1)S(1)}, bf16[128,256]{1,0:T(8,128)(2,1)S(1)}, u32[]{:S(2)}, u32[]{:S(2)}) collective-permute-start(bf16[128,256]{1,0:T(8,128)(2,1)S(1)} %shard_map.87.own_ref), channel_id=1, source_target_pairs={{0,6},{2,4},{4,0},{6,2},{1,7},{3,5},{5,1},{7,3},{8,14},{10,12},{12... | collective-permute-start | bytes 196616 | tf_op jit(solution)/shard_map/ppermute | solution.py:346
  13.4 4.3 %collective-permute-start.2 = (bf16[128,256]{1,0:T(8,128)(2,1)S(1)}, bf16[128,256]{1,0:T(8,128)(2,1)S(1)}, u32[]{:S(2)}, u32[]{:S(2)}) collective-permute-start(bf16[128,256]{1,0:T(8,128)(2,1)S(1)} %shard_map.87.own_ref), channel_id=1, source_target_pairs={{0,2},{2,0},{4,6},{6,4},{1,3},{3,1},{5,7},{7,5},{8,10},{10,8},{12,... | collective-permute-start | bytes 196616 | tf_op jit(solution)/shard_map/ppermute | solution.py:346
  19.5 6.5 %collective-permute-start.4 = (bf16[128,256]{1,0:T(8,128)(2,1)S(1)}, bf16[128,256]{1,0:T(8,128)(2,1)S(1)}, u32[]{:S(2)}, u32[]{:S(2)}) collective-permute-start(bf16[128,256]{1,0:T(8,128)(2,1)S(1)} %get-tuple-element.26), channel_id=1, source_target_pairs={{0,6},{2,4},{4,2},{6,0},{1,7},{3,5},{5,3},{7,1},{8,14},{10,12},{12... | collective-permute-start | bytes 196616 | tf_op jit(solution)/shard_map/ppermute | solution.py:377
  21.4 6.4 %collective-permute-start.5 = (bf16[128,256]{1,0:T(8,128)(2,1)S(1)}, bf16[128,256]{1,0:T(8,128)(2,1)S(1)}, u32[]{:S(2)}, u32[]{:S(2)}) collective-permute-start(bf16[128,256]{1,0:T(8,128)(2,1)S(1)} %get-tuple-element.27), channel_id=1, source_target_pairs={{0,4},{2,6},{4,0},{6,2},{1,5},{3,7},{5,1},{7,3},{8,12},{10,14},{12... | collective-permute-start | bytes 196616 | tf_op jit(solution)/shard_map/ppermute | solution.py:377
  21.7 6.0 %collective-permute-start.6 = (bf16[128,256]{1,0:T(8,128)(2,1)S(1)}, bf16[128,256]{1,0:T(8,128)(2,1)S(1)}, u32[]{:S(2)}, u32[]{:S(2)}) collective-permute-start(bf16[128,256]{1,0:T(8,128)(2,1)S(1)} %get-tuple-element.28), channel_id=1, source_target_pairs={{0,2},{2,0},{4,6},{6,4},{1,3},{3,1},{5,7},{7,5},{8,10},{10,8},{12,... | collective-permute-start | bytes 196616 | tf_op jit(solution)/shard_map/ppermute | solution.py:377
  29.0 1.4 %collective-permute-start.8 = (bf16[16,3200]{1,0:T(8,128)(2,1)S(1)}, bf16[16,3200]{1,0:T(8,128)(2,1)S(1)}, u32[]{:S(2)}, u32[]{:S(2)}) collective-permute-start(bf16[16,3200]{1,0:T(8,128)(2,1)S(1)} %get-tuple-element.35), channel_id=1, source_target_pairs={{0,8},{1,9},{8,0},{9,1},{16,24},{17,25},{24,16},{25,17},{2,10},{3,... | collective-permute-start | bytes 307208 | tf_op jit(solution)/shard_map/ppermute | solution.py:390
  29.7 3.2 %collective-permute-start.7 = (bf16[48,3200]{1,0:T(8,128)(2,1)S(1)}, bf16[48,3200]{1,0:T(8,128)(2,1)S(1)}, u32[]{:S(2)}, u32[]{:S(2)}) collective-permute-start(bf16[48,3200]{1,0:T(8,128)(2,1)S(1)} %get-tuple-element.31), channel_id=1, source_target_pairs={{0,8},{1,9},{8,0},{9,1},{16,24},{17,25},{24,16},{25,17},{2,10},{3,... | collective-permute-start | bytes 921608 | tf_op jit(solution)/shard_map/ppermute | solution.py:400
  30.4 6.7 %collective-permute-start.9 = (bf16[16,3200]{1,0:T(8,128)(2,1)S(1)}, bf16[16,3200]{1,0:T(8,128)(2,1)S(1)}, u32[]{:S(2)}, u32[]{:S(2)}) collective-permute-start(bf16[16,3200]{1,0:T(8,128)(2,1)S(1)} %shard_map.93), channel_id=1, source_target_pairs={{0,17},{1,16},{8,25},{9,24},{16,1},{17,0},{24,9},{25,8},{2,19},{3,... | collective-permute-start | bytes 307208 | tf_op jit(solution)/shard_map/ppermute | solution.py:403
  33.0 5.6 %collective-permute-start.10 = (bf16[16,3200]{1,0:T(8,128)(2,1)S(1)}, bf16[16,3200]{1,0:T(8,128)(2,1)S(1)}, u32[]{:S(2)}, u32[]{:S(2)}) collective-permute-start(bf16[16,3200]{1,0:T(8,128)(2,1)S(1)} %get-tuple-element.36), channel_id=1, source_target_pairs={{0,16},{1,17},{8,24},{9,25},{16,0},{17,1},{24,8},{25,9},{2,18},{3,... | collective-permute-start | bytes 307208 | tf_op jit(solution)/shard_map/ppermute | solution.py:413
  33.6 5.0 %collective-permute-start.11 = (bf16[16,3200]{1,0:T(8,128)(2,1)S(1)}, bf16[16,3200]{1,0:T(8,128)(2,1)S(1)}, u32[]{:S(2)}, u32[]{:S(2)}) collective-permute-start(bf16[16,3200]{1,0:T(8,128)(2,1)S(1)} %get-tuple-element.37), channel_id=1, source_target_pairs={{0,1},{1,0},{8,9},{9,8},{16,17},{17,16},{24,25},{25,24},{2,3},{3,2... | collective-permute-start | bytes 307208 | tf_op jit(solution)/shard_map/ppermute | solution.py:413
  38.8 4.7 %collective-permute-start.15 = (bf16[16,3200]{1,0:T(8,128)(2,1)S(1)}, bf16[16,3200]{1,0:T(8,128)(2,1)S(1)}, u32[]{:S(2)}, u32[]{:S(2)}) collective-permute-start(bf16[16,3200]{1,0:T(8,128)(2,1)S(1)} %shard_map.94.refs_3_), channel_id=1, source_target_pairs={{0,1},{1,0},{8,9},{9,8},{16,17},{17,16},{24,25},{25,24},{2,3},{3,2... | collective-permute-start | bytes 307208 | tf_op jit(solution)/shard_map/ppermute | solution.py:424
  40.4 5.3 %collective-permute-start.14 = (bf16[16,3200]{1,0:T(8,128)(2,1)S(1)}, bf16[16,3200]{1,0:T(8,128)(2,1)S(1)}, u32[]{:S(2)}, u32[]{:S(2)}) collective-permute-start(bf16[16,3200]{1,0:T(8,128)(2,1)S(1)} %shard_map.94.refs_3_), channel_id=1, source_target_pairs={{0,16},{1,17},{8,24},{9,25},{16,0},{17,1},{24,8},{25,9},{2,18},{3,... | collective-permute-start | bytes 307208 | tf_op jit(solution)/shard_map/ppermute | solution.py:424
  41.7 5.6 %collective-permute-start.12 = (bf16[16,3200]{1,0:T(8,128)(2,1)S(1)}, bf16[16,3200]{1,0:T(8,128)(2,1)S(1)}, u32[]{:S(2)}, u32[]{:S(2)}) collective-permute-start(bf16[16,3200]{1,0:T(8,128)(2,1)S(1)} %shard_map.94.refs_3_), channel_id=1, source_target_pairs={{0,17},{1,16},{8,25},{9,24},{16,1},{17,0},{24,9},{25,8},{2,19},{3,... | collective-permute-start | bytes 307208 | tf_op jit(solution)/shard_map/ppermute | solution.py:424
  42.3 5.0 %collective-permute-start.18 = (bf16[16,3200]{1,0:T(8,128)(2,1)S(1)}, bf16[16,3200]{1,0:T(8,128)(2,1)S(1)}, u32[]{:S(2)}, u32[]{:S(2)}) collective-permute-start(bf16[16,3200]{1,0:T(8,128)(2,1)S(1)} %shard_map.94.refs_3_), channel_id=1, source_target_pairs={{0,8},{1,9},{8,0},{9,1},{16,24},{17,25},{24,16},{25,17},{2,10},{3,... | collective-permute-start | bytes 307208 | tf_op jit(solution)/shard_map/ppermute | solution.py:425
  43.5 3.8 %collective-permute-start.17 = (bf16[16,3200]{1,0:T(8,128)(2,1)S(1)}, bf16[16,3200]{1,0:T(8,128)(2,1)S(1)}, u32[]{:S(2)}, u32[]{:S(2)}) collective-permute-start(bf16[16,3200]{1,0:T(8,128)(2,1)S(1)} %collective-permute-done.15.refs_2_), channel_id=1, source_target_pairs={{0,8},{1,9},{8,0},{9,1},{16,24},{17,25},{24,16},{25,17},{2,10},{3,... | collective-permute-start | bytes 307208 | tf_op jit(solution)/shard_map/ppermute | solution.py:425
  45.7 1.6 %collective-permute-start.16 = (bf16[16,3200]{1,0:T(8,128)(2,1)S(1)}, bf16[16,3200]{1,0:T(8,128)(2,1)S(1)}, u32[]{:S(2)}, u32[]{:S(2)}) collective-permute-start(bf16[16,3200]{1,0:T(8,128)(2,1)S(1)} %collective-permute-done.14.refs_1_), channel_id=1, source_target_pairs={{0,8},{1,9},{8,0},{9,1},{16,24},{17,25},{24,16},{25,17},{2,10},{3,... | collective-permute-start | bytes 307208 | tf_op jit(solution)/shard_map/ppermute | solution.py:425
  47.3 1.3 %collective-permute-start.13 = (bf16[16,3200]{1,0:T(8,128)(2,1)S(1)}, bf16[16,3200]{1,0:T(8,128)(2,1)S(1)}, u32[]{:S(2)}, u32[]{:S(2)}) collective-permute-start(bf16[16,3200]{1,0:T(8,128)(2,1)S(1)} %collective-permute-done.12.refs_0_), channel_id=1, source_target_pairs={{0,8},{1,9},{8,0},{9,1},{16,24},{17,25},{24,16},{25,17},{2,10},{3,... | collective-permute-start | bytes 307208 | tf_op jit(solution)/shard_map/ppermute | solution.py:425

commit v11 on v10

--- a/solution.py
+++ b/solution.py
@@ -15,7 +15,6 @@
 VMEM_LIMIT = 48 * 1024 * 1024
 WIDE_LIMIT = 854 * 64 * 1024
 WHOLE = pl.BlockSpec(memory_space=pltpu.VMEM)
-SCALARS = pl.BlockSpec(memory_space=pltpu.SMEM)
 
 
 def owner_block(image, count):
@@ -46,7 +45,8 @@
         found = [c for c in itertools.combinations(whole, size) if all(any(p[s] == t for p in c) for s, t in edges)]
         if found:
             far = lambda p: max(abs(s - t) for s, t in enumerate(p))
-            return sorted(min(found, key=lambda c: flows(c, count)), key=far)
+            found = [sorted(c, key=far) for c in found]
+            return min(found, key=lambda c: (flows(c, count)[0], flows(c[-1:], count), flows(c, count)))
     return best
 
 
@@ -114,6 +114,12 @@
     own_ref[...] = vis[pl.ds(start, piece), :]
 
 
+def text_rows(pieces_ref, image):
+    values = pieces_ref[...].astype(jnp.float32)
+    lane = lax.broadcasted_iota(jnp.int32, values.shape, 1)
+    return jnp.sum(jnp.where(lane == 2 * image, values, 0.0), axis=1, keepdims=True).astype(jnp.int32)
+
+
 def placed(before, rows, image_ref, text_ref):
     ahead = lax.broadcasted_iota(jnp.int32, (rows, rows), 0) - lax.broadcasted_iota(jnp.int32, (rows, rows), 1)
     pick = jnp.where(ahead == before, 1.0, 0.0).astype(jnp.bfloat16)
@@ -124,7 +130,7 @@
 
 def place_body(seq_n, pieces_ref, image_ref, text_ref, out_ref):
     rows = image_ref.shape[0]
-    before = pieces_ref[2 * held_image(lax.axis_index("seq"), seq_n)]
+    before = text_rows(pieces_ref, held_image(lax.axis_index("seq"), seq_n))
     out_ref[...] = placed(before, rows, image_ref, text_ref)
 
 
@@ -157,37 +163,51 @@
 def weigh_body(seq_n, tables, backs, pieces_ref, q_ref, g_ref, text_ref, own_ref, raw_ref, *refs):
     count = len(tables)
     block_refs, (low_ref, dscore_ref, values_ref) = refs[:count], refs[count : count + 3]
-    grad_refs = refs[count + 3 :]
+    grad_refs, (scores, dprob) = refs[count + 3 : -2], refs[-2:]
     rows = q_ref.shape[0]
     group = q_ref.shape[1] // HD
     scale = 1.0 / math.sqrt(HD)
     me = lax.axis_index("seq")
-    mine = placed(pieces_ref[2 * me], rows, raw_ref, text_ref)
+    mine = placed(text_rows(pieces_ref, me), rows, raw_ref, text_ref)
     kv = jnp.concatenate([own_ref[...], mine] + [ref[...] for ref in block_refs], axis=0)
     keys, values = kv[:, :HD], kv[:, HD:]
     values_ref[...] = values
     images = [held_image(me, seq_n), me] + [pick_static(table, me) for table in tables]
+    shifts = [jnp.where(image < me, 0.0, NEG) for image in images]
+    seen = lax.broadcasted_iota(jnp.int32, (rows, rows), 0) <= lax.broadcasted_iota(jnp.int32, (rows, rows), 1)
+    parts = [slice(n * rows, (n + 1) * rows) for n in range(len(images))]
+
+    def score(n, cols):
+        block = scores[parts[n], cols]
+        return jnp.where(seen, block, NEG) if n == 1 else block + shifts[n]
+
     for heads in head_groups(group, kv.shape[0]):
-        q, g = heads_of(q_ref, heads), heads_of(g_ref, heads)
-        offset = lax.broadcasted_iota(jnp.int32, (rows, q.shape[0]), 0)
-        offset = offset - lax.rem(lax.broadcasted_iota(jnp.int32, (rows, q.shape[0]), 1), rows)
-        scores = dot(keys, q, ((1,), (1,)))
-        scores = jnp.concatenate(
-            [
-                jnp.where(offset <= (me - image) * rows, scores[n * rows : (n + 1) * rows], NEG)
-                for n, image in enumerate(images)
-            ],
-            axis=0,
-        )
-        top = jnp.max(scores, axis=0, keepdims=True)
-        weights = jnp.exp2((scores - top) * (scale * math.log2(math.e)))
-        weights = weights * (1.0 / jnp.sum(weights, axis=0, keepdims=True))
-        low = weights.astype(jnp.bfloat16)
-        dprob = dot(values, g, ((1,), (1,)))
-        drift = jnp.sum(low.astype(jnp.float32) * dprob, axis=0, keepdims=True)
-        span = slice(heads[0] * rows, (heads[-1] + 1) * rows)
-        low_ref[:, span] = low
-        dscore_ref[:, span] = (weights * (dprob - drift)).astype(jnp.bfloat16)
+        scores[...] = dot(keys, heads_of(q_ref, heads), ((1,), (1,)))
+        dprob[...] = dot(values, heads_of(g_ref, heads), ((1,), (1,)))
+        for h in heads:
+            cols = slice((h - heads[0]) * rows, (h - heads[0] + 1) * rows)
+            wide = slice(h * rows, (h + 1) * rows)
+            top = score(0, cols)
+            for n in range(1, len(parts)):
+                top = jnp.maximum(top, score(n, cols))
+            top = jnp.max(top, axis=0, keepdims=True)
+            total = None
+            for n, part in enumerate(parts):
+                weights = jnp.exp2((score(n, cols) - top) * (scale * math.log2(math.e)))
+                scores[part, cols] = weights
+                total = weights if total is None else total + weights
+            inverse = 1.0 / jnp.sum(total, axis=0, keepdims=True)
+            drift = None
+            for part in parts:
+                weights = scores[part, cols] * inverse
+                scores[part, cols] = weights
+                low = weights.astype(jnp.bfloat16)
+                low_ref[part, wide] = low
+                term = low.astype(jnp.float32) * dprob[part, cols]
+                drift = term if drift is None else drift + term
+            drift = jnp.sum(drift, axis=0, keepdims=True)
+            for part in parts:
+                dscore_ref[part, wide] = (scores[part, cols] * (dprob[part, cols] - drift)).astype(jnp.bfloat16)
     early = [pick_static(table, me) for table in backs]
     grad_parts(early, rows, scale, low_ref, dscore_ref, q_ref, g_ref, grad_refs)
 
@@ -206,7 +226,7 @@
 def back_body(seq_n, count, piece, pieces_ref, proj_ref, *refs):
     part_refs, (rest_ref, keep_ref, send_ref) = refs[:-3], refs[-3:]
     rows = part_refs[0].shape[0]
-    before = pieces_ref[2 * held_image(lax.axis_index("seq"), seq_n)]
+    before = text_rows(pieces_ref, held_image(lax.axis_index("seq"), seq_n))
     parity, place = group_place()
     total = part_refs[0][...].astype(jnp.float32)
     for ref in part_refs[1:]:
@@ -301,6 +321,7 @@
         return pairs
 
     gain = vis_gain.reshape(width // HD, HD)
+    pieces = pieces.reshape(1, -1)
     owners = [owner_block(j, seq_n) for j in range(seq_n)]
     held = [owners.index(b) for b in range(seq_n)]
     home = [(owners[j], j) for j in range(seq_n)]
@@ -338,7 +359,7 @@
     block = call(
         functools.partial(place_body, seq_n),
         jax.ShapeDtypeStruct((rows, columns), bf16),
-        [SCALARS, WHOLE, WHOLE],
+        [WHOLE] * 3,
         WHOLE,
         0,
         6 * rows * columns,
@@ -346,7 +367,7 @@
     blocks = [lax.ppermute(block, "seq", pairs) for pairs in forth]
     total = 2 + len(blocks)
     pairs_back, backs = [], []
-    for r in range(seq_n - 1, 0, -1):
+    for r in sorted(range(1, seq_n), key=lambda r: (r < seq_n // 2, r)):
         pairs_back.append([(d, d ^ r) for d in range(seq_n)])
         table = []
         for d in range(seq_n):
@@ -361,10 +382,11 @@
     low, dscore, values, *grads = call(
         functools.partial(weigh_body, seq_n, tables, backs),
         [wide_shape, wide_shape, jax.ShapeDtypeStruct((total * rows, HD), bf16)] + [kv_shape] * len(backs),
-        [SCALARS] + [WHOLE] * (3 + total),
+        [WHOLE] * (4 + total),
         [WHOLE] * (3 + len(backs)),
         8 * total * rows * rows * queries.shape[1],
         4 * rows * queries.shape[1] + 4 * total * rows * columns,
+        scratch_shapes=[pltpu.VMEM((total * rows, len(head_groups(queries.shape[1] // HD, total * rows)[0]) * rows), f32)] * 2,
     )(pieces, queries, grad_out, text_kv, block, raw, *blocks)
     attended, own_grad = call(
         functools.partial(mix_body, [0]),
@@ -382,7 +404,7 @@
     rest, keep_last, send_last = call(
         functools.partial(back_body, seq_n, count, piece),
         [jax.ShapeDtypeStruct((rows - 2 * piece, columns), bf16), shape(piece, f32), shape(piece, bf16)],
-        [SCALARS] + [WHOLE] * (2 + len(parts)),
+        [WHOLE] * (3 + len(parts)),
         [WHOLE] * 3,
         4 * piece * width * columns,
         2 * width * columns + 6 * piece * width,
@@ -424,10 +446,9 @@
         mines[d] = lax.ppermute(mine, names, far_pairs(d))
     theirs = {d: lax.ppermute(mines[d], names, core_pairs) for d in range(count)}
     ready = {(core, d): part[d] for core, part in enumerate((mines, theirs)) for d in range(count)}
-    order = sorted(ready, key=lambda key: (key[0], -key[1]))
-    last = (1, count - 1)
+    early = [key for key in sorted(ready) if key[0] == 0 or key[1] in (0, count - 1)]
     vis_grad = None
-    for chosen in ([key for key in order if key != last], [last]):
+    for chosen in (early, [key for key in sorted(ready) if key not in early]):
         done = [] if vis_grad is None else [vis_grad]
         vis_grad = call(
             functools.partial(gather_body, count, chosen),

time: 49.5 us -> 47.1 us (0.952)
  Pallas kernels: 9.52 us -> 8.08 us
  starting transfers between devices: 21.8 us -> 21.2 us
    ppermute x3, starting transfers between devices: 4.45 us -> 3.55 us  [on_device(): lax.ppermute(g, 'seq', pairs)]
    ppermute x3, waiting for transfers between devices: 4.95 us -> 4.4 us  [on_device(): mines[d] = lax.ppermute(mine, names, far_pairs(d))]
    ppermute x1, waiting for transfers between devices: 2.2 us -> 2.74 us  [on_device(): raw = lax.ppermute(image_kv, 'seq', home)]
    ppermute x2, waiting for transfers between devices: 2.06 us -> 1.52 us  [on_device(): blocks = [lax.ppermute(block, 'seq', pairs) for pairs in forth]]
  transfers between devices with their start and end apart: 19 -> 19, of which waited for: 13 -> 12; matrix products, arithmetic and copies ran while one was open for 0% -> 0% of each run, Pallas kernels for 11% -> 11%
where the time goes in v11:
time: 47.1 us; the launch traced here: 46.9 us
  starting transfers between devices  21.2 us (45%)
  waiting for transfers between devices  16.1 us (34%)
  Pallas kernels  8.08 us (17%)
  between operations  0.76 us (2%)
  local copies, waits for them, and re-layouts  0.74 us (2%)
    ppermute x1, starting transfers between devices, on_device(): text = lax.ppermute(text_kv, 'seq', list(enumerate(owners)))  5.1 us
    ppermute x3, waiting for transfers between devices, on_device(): mines[d] = lax.ppermute(mine, names, far_pairs(d))  4.4 us
    ppermute x2, starting transfers between devices, on_device(): blocks = [lax.ppermute(block, 'seq', pairs) for pairs in forth]  3.85 us
    ppermute x3, starting transfers between devices, on_device(): lax.ppermute(g, 'seq', pairs)  3.55 us
    ppermute x3, starting transfers between devices, on_device(): mines[d] = lax.ppermute(mine, names, far_pairs(d))  3.55 us
    ppermute x3, waiting for transfers between devices, on_device(): lax.ppermute(g, 'seq', pairs)  3.18 us
    ppermute x1, waiting for transfers between devices, on_device(): raw = lax.ppermute(image_kv, 'seq', home)  2.74 us
    ppermute x1, starting transfers between devices, on_device(): shares = [lax.ppermute(far, names, far_pairs(count - 1))]  2.51 us
  transfers between devices with their start and end apart: 19, of which 12 were waited for; matrix products, arithmetic and copies ran while one was open for 0% of the time, Pallas kernels for 11%

profile of v11, /device:TPU:0, one launch (start us, length us, event | category | flops | bytes accessed | tf_op | source)
XLA Modules:
  0.0 46.9 jit_solution(8290017904508261842)
XLA Ops:
  0.7 5.1 %collective-permute-start = (bf16[128,256]{1,0:T(8,128)(2,1)}, bf16[128,256]{1,0:T(8,128)(2,1)S(1)}, u32[]{:S(2)}, u32[]{:S(2)}) collective-permute-start(bf16[128,256]{1,0:T(8,128)(2,1)} %text_ref.1), channel_id=1, source_target_pairs={{0,6},{2,4},{4,0},{6,2},{1,7},{3,5},{5,1},{7,3},{8,14},{10,12},{12... | collective-permute-start | bytes 196616 | tf_op jit(solution)/shard_map/ppermute | solution.py:338
  5.8 0.7 %copy-done.3 = f32[3200]{0:T(1024)S(1)} copy-done((f32[3200]{0:T(1024)S(1)}, f32[3200]{0:T(1024)}, u32[]{:S(2)}) %copy-start.3) | copy-done | bytes 12824
  6.5 2.3 %shard_map.86 = (bf16[128,256]{1,0:T(8,128)(2,1)S(1)}, bf16[16,3200]{1,0:T(8,128)(2,1)S(1)}) custom-call(bf16[128,3200]{1,0:T(8,128)(2,1)} %vis_hbm.1, f32[25,128]{1,0:T(8,128)S(1)} %bitcast.2, bf16[3200,256]{1,0:T(8,128)(2,1)} %proj_ref.3), custom_call_target="tpu_custom_call" | custom-call | flops 209715200 | bytes 2457600 | tf_op jit(solution)/shard_map/pallas_call | solution.py:341
  8.7 0.0 copy-start
  8.8 0.1 collective-permute-start.1
  8.8 0.0 collective-permute-done.text_ref
  8.8 0.2 shard_map.87.own_ref
  9.1 3.8 %collective-permute-start.3 = (bf16[128,256]{1,0:T(8,128)(2,1)S(1)}, bf16[128,256]{1,0:T(8,128)(2,1)S(1)}, u32[]{:S(2)}, u32[]{:S(2)}) collective-permute-start(bf16[128,256]{1,0:T(8,128)(2,1)S(1)} %shard_map.87.own_ref), channel_id=1, source_target_pairs={{0,6},{2,0},{4,2},{6,4},{1,7},{3,1},{5,3},{7,5},{8,14},{10,8},{12,... | collective-permute-start | bytes 196616 | tf_op jit(solution)/shard_map/ppermute | solution.py:367
  12.9 0.0 collective-permute-start.2
  12.9 2.7 %collective-permute-done.1.raw_ref = bf16[128,256]{1,0:T(8,128)(2,1)S(1)} collective-permute-done((bf16[128,256]{1,0:T(8,128)(2,1)S(1)}, bf16[128,256]{1,0:T(8,128)(2,1)S(1)}, u32[]{:S(2)}, u32[]{:S(2)}) %collective-permute-start.1) | collective-permute-done | bytes 65568 | tf_op jit(solution)/shard_map/ppermute | solution.py:358
  15.7 0.0 collective-permute-done.3.refs_1_
  15.7 1.5 %collective-permute-done.2.refs_0_ = bf16[128,256]{1,0:T(8,128)(2,1)S(1)} collective-permute-done((bf16[128,256]{1,0:T(8,128)(2,1)S(1)}, bf16[128,256]{1,0:T(8,128)(2,1)S(1)}, u32[]{:S(2)}, u32[]{:S(2)}) %collective-permute-start.2) | collective-permute-done | bytes 65568 | tf_op jit(solution)/shard_map/ppermute | solution.py:367
  17.2 1.4 %shard_map.88 = (bf16[512,512]{1,0:T(8,128)(2,1)S(1)}, bf16[512,512]{1,0:T(8,128)(2,1)S(1)}, bf16[512,128]{1,0:T(8,128)(2,1)S(1)}, bf16[128,256]{1,0:T(8,128)(2,...) custom-call(s32[1,8]{1,0:T(1,128)S(1)} %bitcast.5, bf16[128,512]{1,0:T(8,128)(2,1)S(1)} %copy-done.1, ...), custom_call_target="tpu_custom_call" | custom-call | flops 268435456 | bytes 786432 | tf_op jit(solution)/shard_map/pallas_call | solution.py:382
  18.6 1.7 %collective-permute-start.4 = (bf16[128,256]{1,0:T(8,128)(2,1)S(1)}, bf16[128,256]{1,0:T(8,128)(2,1)S(1)}, u32[]{:S(2)}, u32[]{:S(2)}) collective-permute-start(bf16[128,256]{1,0:T(8,128)(2,1)S(1)} %get-tuple-element.26), channel_id=1, source_target_pairs={{0,4},{2,6},{4,0},{6,2},{1,5},{3,7},{5,1},{7,3},{8,12},{10,14},{12... | collective-permute-start | bytes 196616 | tf_op jit(solution)/shard_map/ppermute | solution.py:399
  20.3 1.1 %collective-permute-start.5 = (bf16[128,256]{1,0:T(8,128)(2,1)S(1)}, bf16[128,256]{1,0:T(8,128)(2,1)S(1)}, u32[]{:S(2)}, u32[]{:S(2)}) collective-permute-start(bf16[128,256]{1,0:T(8,128)(2,1)S(1)} %get-tuple-element.27), channel_id=1, source_target_pairs={{0,6},{2,4},{4,2},{6,0},{1,7},{3,5},{5,3},{7,1},{8,14},{10,12},{12... | collective-permute-start | bytes 196616 | tf_op jit(solution)/shard_map/ppermute | solution.py:399
  21.4 0.8 %collective-permute-start.6 = (bf16[128,256]{1,0:T(8,128)(2,1)S(1)}, bf16[128,256]{1,0:T(8,128)(2,1)S(1)}, u32[]{:S(2)}, u32[]{:S(2)}) collective-permute-start(bf16[128,256]{1,0:T(8,128)(2,1)S(1)} %get-tuple-element.28), channel_id=1, source_target_pairs={{0,2},{2,0},{4,6},{6,4},{1,3},{3,1},{5,7},{7,5},{8,10},{10,8},{12,... | collective-permute-start | bytes 196616 | tf_op jit(solution)/shard_map/ppermute | solution.py:399
  22.1 1.0 %shard_map.89 = (bf16[128,512]{1,0:T(8,128)(2,1)}, bf16[128,256]{1,0:T(8,128)(2,1)S(1)}) custom-call(bf16[128,512]{1,0:T(8,128)(2,1)S(1)} %copy-done.1, bf16[128,512]{1,0:T(8,128)(2,1)S(1)} %copy-done.2, bf16[512,512]{1,0:T(8,128)(2,1)S(1)} %get-tuple-element.21.low_ref, bf16[512,512]{1,0:T(8,128)(2,1)S(1)} %get-tuple-element.22.dscore_ref, ...), custom_call_target="tpu_custom_call" | custom-call | flops 67108864 | bytes 917504 | tf_op jit(solution)/shard_map/pallas_call | solution.py:391
  23.1 1.4 %collective-permute-done.4.refs_1_ = bf16[128,256]{1,0:T(8,128)(2,1)S(1)} collective-permute-done((bf16[128,256]{1,0:T(8,128)(2,1)S(1)}, bf16[128,256]{1,0:T(8,128)(2,1)S(1)}, u32[]{:S(2)}, u32[]{:S(2)}) %collective-permute-start.4) | collective-permute-done | bytes 65568 | tf_op jit(solution)/shard_map/ppermute | solution.py:399
  24.6 1.7 %collective-permute-done.5.refs_2_ = bf16[128,256]{1,0:T(8,128)(2,1)S(1)} collective-permute-done((bf16[128,256]{1,0:T(8,128)(2,1)S(1)}, bf16[128,256]{1,0:T(8,128)(2,1)S(1)}, u32[]{:S(2)}, u32[]{:S(2)}) %collective-permute-start.5) | collective-permute-done | bytes 65568 | tf_op jit(solution)/shard_map/ppermute | solution.py:399
  26.3 0.0 collective-permute-done.6.refs_3_
  26.3 0.7 %shard_map.90 = (bf16[96,256]{1,0:T(8,128)(2,1)S(1)}, f32[16,3200]{1,0:T(8,128)S(1)}, bf16[16,3200]{1,0:T(8,128)(2,1)S(1)}) custom-call(s32[1,8]{1,0:T(1,128)S(1)} %bitcast.6, bf16[3200,256]{1,0:T(8,128)(2,1)S(1)} %copy-done, bf16[128,256]{1,0:T(8,128)(2,1)S(1)} %get-tuple-element.25.refs_0_, bf16[128,256]{1,0:T(8,128)(2,1)S(1)} %collective-permute-done.4.refs_1_, ...), custom_call_target="tpu_custom_call" | custom-call | flops 52428800 | bytes 1945600 | tf_op jit(solution)/shard_map/pallas_call | solution.py:404
  27.1 0.1 collective-permute-start.8
  27.1 0.6 %shard_map.91 = (f32[48,3200]{1,0:T(8,128)S(1)}, bf16[48,3200]{1,0:T(8,128)(2,1)S(1)}) custom-call(bf16[96,256]{1,0:T(8,128)(2,1)S(1)} %get-tuple-element.29.rest_ref, bf16[3200,256]{1,0:T(8,128)(2,1)S(1)} %copy-done), custom_call_target="tpu_custom_call" | custom-call | flops 157286400 | bytes 2560000 | tf_op jit(solution)/shard_map/pallas_call | solution.py:414
  27.8 0.6 %collective-permute-start.7 = (bf16[48,3200]{1,0:T(8,128)(2,1)S(1)}, bf16[48,3200]{1,0:T(8,128)(2,1)S(1)}, u32[]{:S(2)}, u32[]{:S(2)}) collective-permute-start(bf16[48,3200]{1,0:T(8,128)(2,1)S(1)} %get-tuple-element.31), channel_id=1, source_target_pairs={{0,8},{1,9},{8,0},{9,1},{16,24},{17,25},{24,16},{25,17},{2,10},{3,... | collective-permute-start | bytes 921608 | tf_op jit(solution)/shard_map/ppermute | solution.py:422
  28.3 0.1 collective-permute-done.8.other_ref
  28.5 2.5 %collective-permute-start.9 = (bf16[16,3200]{1,0:T(8,128)(2,1)S(1)}, bf16[16,3200]{1,0:T(8,128)(2,1)S(1)}, u32[]{:S(2)}, u32[]{:S(2)}) collective-permute-start(bf16[16,3200]{1,0:T(8,128)(2,1)S(1)} %shard_map.93), channel_id=1, source_target_pairs={{0,17},{1,16},{8,25},{9,24},{16,1},{17,0},{24,9},{25,8},{2,19},{3,... | collective-permute-start | bytes 307208 | tf_op jit(solution)/shard_map/ppermute | solution.py:425
  31.0 0.0 collective-permute-done.7.other_ref
  31.0 0.1 shard_map.92
  31.0 0.6 %collective-permute-start.10 = (bf16[16,3200]{1,0:T(8,128)(2,1)S(1)}, bf16[16,3200]{1,0:T(8,128)(2,1)S(1)}, u32[]{:S(2)}, u32[]{:S(2)}) collective-permute-start(bf16[16,3200]{1,0:T(8,128)(2,1)S(1)} %get-tuple-element.36), channel_id=1, source_target_pairs={{0,16},{1,17},{8,24},{9,25},{16,0},{17,1},{24,8},{25,9},{2,18},{3,... | collective-permute-start | bytes 307208 | tf_op jit(solution)/shard_map/ppermute | solution.py:435
  31.7 1.0 %collective-permute-start.11 = (bf16[16,3200]{1,0:T(8,128)(2,1)S(1)}, bf16[16,3200]{1,0:T(8,128)(2,1)S(1)}, u32[]{:S(2)}, u32[]{:S(2)}) collective-permute-start(bf16[16,3200]{1,0:T(8,128)(2,1)S(1)} %get-tuple-element.37), channel_id=1, source_target_pairs={{0,1},{1,0},{8,9},{9,8},{16,17},{17,16},{24,25},{25,24},{2,3},{3,2... | collective-permute-start | bytes 307208 | tf_op jit(solution)/shard_map/ppermute | solution.py:435
  32.7 2.5 %collective-permute-done.9.refs_0_ = bf16[16,3200]{1,0:T(8,128)(2,1)S(1)} collective-permute-done((bf16[16,3200]{1,0:T(8,128)(2,1)S(1)}, bf16[16,3200]{1,0:T(8,128)(2,1)S(1)}, u32[]{:S(2)}, u32[]{:S(2)}) %collective-permute-start.9) | collective-permute-done | bytes 102432 | tf_op jit(solution)/shard_map/ppermute | solution.py:425
  35.2 1.5 %collective-permute-done.10.refs_1_ = bf16[16,3200]{1,0:T(8,128)(2,1)S(1)} collective-permute-done((bf16[16,3200]{1,0:T(8,128)(2,1)S(1)}, bf16[16,3200]{1,0:T(8,128)(2,1)S(1)}, u32[]{:S(2)}, u32[]{:S(2)}) %collective-permute-start.10) | collective-permute-done | bytes 102432 | tf_op jit(solution)/shard_map/ppermute | solution.py:435
  36.6 0.1 collective-permute-done.11.refs_2_
  36.7 0.2 shard_map.94.refs_0_
  36.9 2.4 %collective-permute-start.16 = (bf16[16,3200]{1,0:T(8,128)(2,1)S(1)}, bf16[16,3200]{1,0:T(8,128)(2,1)S(1)}, u32[]{:S(2)}, u32[]{:S(2)}) collective-permute-start(bf16[16,3200]{1,0:T(8,128)(2,1)S(1)} %shard_map.94.refs_0_), channel_id=1, source_target_pairs={{0,17},{1,16},{8,25},{9,24},{16,1},{17,0},{24,9},{25,8},{2,19},{3,... | collective-permute-start | bytes 307208 | tf_op jit(solution)/shard_map/ppermute | solution.py:446
  39.3 0.7 %collective-permute-start.14 = (bf16[16,3200]{1,0:T(8,128)(2,1)S(1)}, bf16[16,3200]{1,0:T(8,128)(2,1)S(1)}, u32[]{:S(2)}, u32[]{:S(2)}) collective-permute-start(bf16[16,3200]{1,0:T(8,128)(2,1)S(1)} %shard_map.94.refs_0_), channel_id=1, source_target_pairs={{0,16},{1,17},{8,24},{9,25},{16,0},{17,1},{24,8},{25,9},{2,18},{3,... | collective-permute-start | bytes 307208 | tf_op jit(solution)/shard_map/ppermute | solution.py:446
  39.9 0.5 %collective-permute-start.12 = (bf16[16,3200]{1,0:T(8,128)(2,1)S(1)}, bf16[16,3200]{1,0:T(8,128)(2,1)S(1)}, u32[]{:S(2)}, u32[]{:S(2)}) collective-permute-start(bf16[16,3200]{1,0:T(8,128)(2,1)S(1)} %shard_map.94.refs_0_), channel_id=1, source_target_pairs={{0,1},{1,0},{8,9},{9,8},{16,17},{17,16},{24,25},{25,24},{2,3},{3,2... | collective-permute-start | bytes 307208 | tf_op jit(solution)/shard_map/ppermute | solution.py:446
  40.5 2.8 %collective-permute-done.16.refs_3_ = bf16[16,3200]{1,0:T(8,128)(2,1)S(1)} collective-permute-done((bf16[16,3200]{1,0:T(8,128)(2,1)S(1)}, bf16[16,3200]{1,0:T(8,128)(2,1)S(1)}, u32[]{:S(2)}, u32[]{:S(2)}) %collective-permute-start.16) | collective-permute-done | bytes 102432 | tf_op jit(solution)/shard_map/ppermute | solution.py:446
  43.3 0.0 collective-permute-start.18
  43.3 1.4 %collective-permute-done.14.refs_2_ = bf16[16,3200]{1,0:T(8,128)(2,1)S(1)} collective-permute-done((bf16[16,3200]{1,0:T(8,128)(2,1)S(1)}, bf16[16,3200]{1,0:T(8,128)(2,1)S(1)}, u32[]{:S(2)}, u32[]{:S(2)}) %collective-permute-start.14) | collective-permute-done | bytes 102432 | tf_op jit(solution)/shard_map/ppermute | solution.py:446
  44.7 0.0 collective-permute-start.15
  44.7 0.2 collective-permute-done.12.refs_1_
  44.9 0.3 collective-permute-start.13
  45.2 0.0 collective-permute-done.17.refs_4_
  45.2 0.9 %shard_map.95.refs_2_ = bf16[128,3200]{1,0:T(8,128)(2,1)} custom-call(bf16[16,3200]{1,0:T(8,128)(2,1)S(1)} %shard_map.94.refs_0_, bf16[16,3200]{1,0:T(8,128)(2,1)S(1)} %collective-permute-done.12.refs_1_, bf16[16,3200]{1,0:T(8,128)(2,1)S(1)} %collective-permute-done.14.refs_2_, bf16[16,3200]{1,0:T(8,128)(2,1)S(1)} %collective-permute-done.16.refs_3_, ...), custom_call_target="tpu_custom_call" | custom-call | bytes 1228800 | tf_op jit(solution)/shard_map/pallas_call | solution.py:453
  46.0 0.0 collective-permute-done.15.refs_1_
  46.1 0.1 collective-permute-done.13.refs_0_
  46.2 0.7 %shard_map.96 = bf16[128,3200]{1,0:T(8,128)(2,1)} custom-call(bf16[16,3200]{1,0:T(8,128)(2,1)S(1)} %collective-permute-done.13.refs_0_, bf16[16,3200]{1,0:T(8,128)(2,1)S(1)} %collective-permute-done.15.refs_1_, bf16[128,3200]{1,0:T(8,128)(2,1)} %shard_map.95.refs_2_), custom_call_target="tpu_custom_call", output_to_operand_aliasing={{}: (2, {})} | custom-call | bytes 409600 | tf_op jit(solution)/shard_map/pallas_call | solution.py:453
  (13 shorter events, 0.1 us)
Async XLA Ops:
  0.6 16.6 %copy-start.2 = (bf16[128,512]{1,0:T(8,128)(2,1)S(1)}, bf16[128,512]{1,0:T(8,128)(2,1)}, u32[]{:S(2)}) copy-start(bf16[128,512]{1,0:T(8,128)(2,1)} %g_ref.3) | copy-start | bytes 393220
  0.6 16.6 %copy-start.1 = (bf16[128,512]{1,0:T(8,128)(2,1)S(1)}, bf16[128,512]{1,0:T(8,128)(2,1)}, u32[]{:S(2)}) copy-start(bf16[128,512]{1,0:T(8,128)(2,1)} %q_ref.3) | copy-start | bytes 393220
  0.7 8.2 %collective-permute-start = (bf16[128,256]{1,0:T(8,128)(2,1)}, bf16[128,256]{1,0:T(8,128)(2,1)S(1)}, u32[]{:S(2)}, u32[]{:S(2)}) collective-permute-start(bf16[128,256]{1,0:T(8,128)(2,1)} %text_ref.1), channel_id=1, source_target_pairs={{0,6},{2,4},{4,0},{6,2},{1,7},{3,5},{5,1},{7,3},{8,14},{10,12},{12... | collective-permute-start | bytes 196616 | tf_op jit(solution)/shard_map/ppermute | solution.py:338
  5.8 0.7 %copy-start.3 = (f32[3200]{0:T(1024)S(1)}, f32[3200]{0:T(1024)}, u32[]{:S(2)}) copy-start(f32[3200]{0:T(1024)} %param.8) | copy-start | bytes 38404
  6.5 2.4 %copy-start.4 = (s32[8]{0:T(128)S(1)}, s32[8]{0:T(128)}, u32[]{:S(2)}) copy-start(s32[8]{0:T(128)} %param.10) | copy-start | bytes 100
  6.5 10.7 %copy-start.5 = (bf16[128,256]{1,0:T(8,128)(2,1)S(1)}, bf16[128,256]{1,0:T(8,128)(2,1)}, u32[]{:S(2)}) copy-start(bf16[128,256]{1,0:T(8,128)(2,1)} %text_ref.1) | copy-start | bytes 196612
  8.7 17.6 %copy-start = (bf16[3200,256]{1,0:T(8,128)(2,1)S(1)}, bf16[3200,256]{1,0:T(8,128)(2,1)}, u32[]{:S(2)}) copy-start(bf16[3200,256]{1,0:T(8,128)(2,1)} %proj_ref.3) | copy-start | bytes 4915204
  8.8 6.9 %collective-permute-start.1 = (bf16[128,256]{1,0:T(8,128)(2,1)S(1)}, bf16[128,256]{1,0:T(8,128)(2,1)S(1)}, u32[]{:S(2)}, u32[]{:S(2)}) collective-permute-start(bf16[128,256]{1,0:T(8,128)(2,1)S(1)} %get-tuple-element.20.image_ref), channel_id=1, source_target_pairs={{6,0},{4,2},{0,4},{2,6},{7,1},{5,3},{1,5},{3,7},{14,8},{12,10},{8,... | collective-permute-start | bytes 196616 | tf_op jit(solution)/shard_map/ppermute | solution.py:358
  9.1 6.6 %collective-permute-start.3 = (bf16[128,256]{1,0:T(8,128)(2,1)S(1)}, bf16[128,256]{1,0:T(8,128)(2,1)S(1)}, u32[]{:S(2)}, u32[]{:S(2)}) collective-permute-start(bf16[128,256]{1,0:T(8,128)(2,1)S(1)} %shard_map.87.own_ref), channel_id=1, source_target_pairs={{0,6},{2,0},{4,2},{6,4},{1,7},{3,1},{5,3},{7,5},{8,14},{10,8},{12,... | collective-permute-start | bytes 196616 | tf_op jit(solution)/shard_map/ppermute | solution.py:367
  12.9 4.3 %collective-permute-start.2 = (bf16[128,256]{1,0:T(8,128)(2,1)S(1)}, bf16[128,256]{1,0:T(8,128)(2,1)S(1)}, u32[]{:S(2)}, u32[]{:S(2)}) collective-permute-start(bf16[128,256]{1,0:T(8,128)(2,1)S(1)} %shard_map.87.own_ref), channel_id=1, source_target_pairs={{0,4},{2,0},{4,6},{6,2},{1,5},{3,1},{5,7},{7,3},{8,12},{10,8},{12,... | collective-permute-start | bytes 196616 | tf_op jit(solution)/shard_map/ppermute | solution.py:367
  18.6 6.0 %collective-permute-start.4 = (bf16[128,256]{1,0:T(8,128)(2,1)S(1)}, bf16[128,256]{1,0:T(8,128)(2,1)S(1)}, u32[]{:S(2)}, u32[]{:S(2)}) collective-permute-start(bf16[128,256]{1,0:T(8,128)(2,1)S(1)} %get-tuple-element.26), channel_id=1, source_target_pairs={{0,4},{2,6},{4,0},{6,2},{1,5},{3,7},{5,1},{7,3},{8,12},{10,14},{12... | collective-permute-start | bytes 196616 | tf_op jit(solution)/shard_map/ppermute | solution.py:399
  20.3 6.1 %collective-permute-start.5 = (bf16[128,256]{1,0:T(8,128)(2,1)S(1)}, bf16[128,256]{1,0:T(8,128)(2,1)S(1)}, u32[]{:S(2)}, u32[]{:S(2)}) collective-permute-start(bf16[128,256]{1,0:T(8,128)(2,1)S(1)} %get-tuple-element.27), channel_id=1, source_target_pairs={{0,6},{2,4},{4,2},{6,0},{1,7},{3,5},{5,3},{7,1},{8,14},{10,12},{12... | collective-permute-start | bytes 196616 | tf_op jit(solution)/shard_map/ppermute | solution.py:399
  21.4 5.0 %collective-permute-start.6 = (bf16[128,256]{1,0:T(8,128)(2,1)S(1)}, bf16[128,256]{1,0:T(8,128)(2,1)S(1)}, u32[]{:S(2)}, u32[]{:S(2)}) collective-permute-start(bf16[128,256]{1,0:T(8,128)(2,1)S(1)} %get-tuple-element.28), channel_id=1, source_target_pairs={{0,2},{2,0},{4,6},{6,4},{1,3},{3,1},{5,7},{7,5},{8,10},{10,8},{12,... | collective-permute-start | bytes 196616 | tf_op jit(solution)/shard_map/ppermute | solution.py:399
  27.1 1.4 %collective-permute-start.8 = (bf16[16,3200]{1,0:T(8,128)(2,1)S(1)}, bf16[16,3200]{1,0:T(8,128)(2,1)S(1)}, u32[]{:S(2)}, u32[]{:S(2)}) collective-permute-start(bf16[16,3200]{1,0:T(8,128)(2,1)S(1)} %get-tuple-element.35), channel_id=1, source_target_pairs={{0,8},{1,9},{8,0},{9,1},{16,24},{17,25},{24,16},{25,17},{2,10},{3,... | collective-permute-start | bytes 307208 | tf_op jit(solution)/shard_map/ppermute | solution.py:412
  27.8 3.2 %collective-permute-start.7 = (bf16[48,3200]{1,0:T(8,128)(2,1)S(1)}, bf16[48,3200]{1,0:T(8,128)(2,1)S(1)}, u32[]{:S(2)}, u32[]{:S(2)}) collective-permute-start(bf16[48,3200]{1,0:T(8,128)(2,1)S(1)} %get-tuple-element.31), channel_id=1, source_target_pairs={{0,8},{1,9},{8,0},{9,1},{16,24},{17,25},{24,16},{25,17},{2,10},{3,... | collective-permute-start | bytes 921608 | tf_op jit(solution)/shard_map/ppermute | solution.py:422
  28.5 6.7 %collective-permute-start.9 = (bf16[16,3200]{1,0:T(8,128)(2,1)S(1)}, bf16[16,3200]{1,0:T(8,128)(2,1)S(1)}, u32[]{:S(2)}, u32[]{:S(2)}) collective-permute-start(bf16[16,3200]{1,0:T(8,128)(2,1)S(1)} %shard_map.93), channel_id=1, source_target_pairs={{0,17},{1,16},{8,25},{9,24},{16,1},{17,0},{24,9},{25,8},{2,19},{3,... | collective-permute-start | bytes 307208 | tf_op jit(solution)/shard_map/ppermute | solution.py:425
  31.0 5.6 %collective-permute-start.10 = (bf16[16,3200]{1,0:T(8,128)(2,1)S(1)}, bf16[16,3200]{1,0:T(8,128)(2,1)S(1)}, u32[]{:S(2)}, u32[]{:S(2)}) collective-permute-start(bf16[16,3200]{1,0:T(8,128)(2,1)S(1)} %get-tuple-element.36), channel_id=1, source_target_pairs={{0,16},{1,17},{8,24},{9,25},{16,0},{17,1},{24,8},{25,9},{2,18},{3,... | collective-permute-start | bytes 307208 | tf_op jit(solution)/shard_map/ppermute | solution.py:435
  31.7 5.1 %collective-permute-start.11 = (bf16[16,3200]{1,0:T(8,128)(2,1)S(1)}, bf16[16,3200]{1,0:T(8,128)(2,1)S(1)}, u32[]{:S(2)}, u32[]{:S(2)}) collective-permute-start(bf16[16,3200]{1,0:T(8,128)(2,1)S(1)} %get-tuple-element.37), channel_id=1, source_target_pairs={{0,1},{1,0},{8,9},{9,8},{16,17},{17,16},{24,25},{25,24},{2,3},{3,2... | collective-permute-start | bytes 307208 | tf_op jit(solution)/shard_map/ppermute | solution.py:435
  36.9 6.4 %collective-permute-start.16 = (bf16[16,3200]{1,0:T(8,128)(2,1)S(1)}, bf16[16,3200]{1,0:T(8,128)(2,1)S(1)}, u32[]{:S(2)}, u32[]{:S(2)}) collective-permute-start(bf16[16,3200]{1,0:T(8,128)(2,1)S(1)} %shard_map.94.refs_0_), channel_id=1, source_target_pairs={{0,17},{1,16},{8,25},{9,24},{16,1},{17,0},{24,9},{25,8},{2,19},{3,... | collective-permute-start | bytes 307208 | tf_op jit(solution)/shard_map/ppermute | solution.py:446
  39.3 5.4 %collective-permute-start.14 = (bf16[16,3200]{1,0:T(8,128)(2,1)S(1)}, bf16[16,3200]{1,0:T(8,128)(2,1)S(1)}, u32[]{:S(2)}, u32[]{:S(2)}) collective-permute-start(bf16[16,3200]{1,0:T(8,128)(2,1)S(1)} %shard_map.94.refs_0_), channel_id=1, source_target_pairs={{0,16},{1,17},{8,24},{9,25},{16,0},{17,1},{24,8},{25,9},{2,18},{3,... | collective-permute-start | bytes 307208 | tf_op jit(solution)/shard_map/ppermute | solution.py:446
  39.9 4.9 %collective-permute-start.12 = (bf16[16,3200]{1,0:T(8,128)(2,1)S(1)}, bf16[16,3200]{1,0:T(8,128)(2,1)S(1)}, u32[]{:S(2)}, u32[]{:S(2)}) collective-permute-start(bf16[16,3200]{1,0:T(8,128)(2,1)S(1)} %shard_map.94.refs_0_), channel_id=1, source_target_pairs={{0,1},{1,0},{8,9},{9,8},{16,17},{17,16},{24,25},{25,24},{2,3},{3,2... | collective-permute-start | bytes 307208 | tf_op jit(solution)/shard_map/ppermute | solution.py:446
  40.5 4.7 %collective-permute-start.17 = (bf16[16,3200]{1,0:T(8,128)(2,1)S(1)}, bf16[16,3200]{1,0:T(8,128)(2,1)S(1)}, u32[]{:S(2)}, u32[]{:S(2)}) collective-permute-start(bf16[16,3200]{1,0:T(8,128)(2,1)S(1)} %shard_map.94.refs_0_), channel_id=1, source_target_pairs={{0,8},{1,9},{8,0},{9,1},{16,24},{17,25},{24,16},{25,17},{2,10},{3,... | collective-permute-start | bytes 307208 | tf_op jit(solution)/shard_map/ppermute | solution.py:447
  43.3 1.9 %collective-permute-start.18 = (bf16[16,3200]{1,0:T(8,128)(2,1)S(1)}, bf16[16,3200]{1,0:T(8,128)(2,1)S(1)}, u32[]{:S(2)}, u32[]{:S(2)}) collective-permute-start(bf16[16,3200]{1,0:T(8,128)(2,1)S(1)} %collective-permute-done.16.refs_3_), channel_id=1, source_target_pairs={{0,8},{1,9},{8,0},{9,1},{16,24},{17,25},{24,16},{25,17},{2,10},{3,... | collective-permute-start | bytes 307208 | tf_op jit(solution)/shard_map/ppermute | solution.py:447
  44.7 1.4 %collective-permute-start.15 = (bf16[16,3200]{1,0:T(8,128)(2,1)S(1)}, bf16[16,3200]{1,0:T(8,128)(2,1)S(1)}, u32[]{:S(2)}, u32[]{:S(2)}) collective-permute-start(bf16[16,3200]{1,0:T(8,128)(2,1)S(1)} %collective-permute-done.14.refs_2_), channel_id=1, source_target_pairs={{0,8},{1,9},{8,0},{9,1},{16,24},{17,25},{24,16},{25,17},{2,10},{3,... | collective-permute-start | bytes 307208 | tf_op jit(solution)/shard_map/ppermute | solution.py:447
  44.9 1.3 %collective-permute-start.13 = (bf16[16,3200]{1,0:T(8,128)(2,1)S(1)}, bf16[16,3200]{1,0:T(8,128)(2,1)S(1)}, u32[]{:S(2)}, u32[]{:S(2)}) collective-permute-start(bf16[16,3200]{1,0:T(8,128)(2,1)S(1)} %collective-permute-done.12.refs_1_), channel_id=1, source_target_pairs={{0,8},{1,9},{8,0},{9,1},{16,24},{17,25},{24,16},{25,17},{2,10},{3,... | collective-permute-start | bytes 307208 | tf_op jit(solution)/shard_map/ppermute | solution.py:447

commit v12 on v11

--- a/solution.py
+++ b/solution.py
@@ -223,7 +223,7 @@
             out_ref[:, h * HD : (h + 1) * HD] = part.astype(jnp.bfloat16)
 
 
-def back_body(seq_n, count, piece, pieces_ref, proj_ref, *refs):
+def back_body(seq_n, count, piece, first, pieces_ref, proj_ref, *refs):
     part_refs, (rest_ref, keep_ref, send_ref) = refs[:-3], refs[-3:]
     rows = part_refs[0].shape[0]
     before = text_rows(pieces_ref, held_image(lax.axis_index("seq"), seq_n))
@@ -234,7 +234,8 @@
     slot = lax.broadcasted_iota(jnp.int32, (rows, rows), 0)
     group = lax.div(slot, piece)
     core = jnp.where(group < 2, group, jnp.where(group > count, 1, 0))
-    step = jnp.where(group < 2, count - 1, lax.rem(group + count - 3, count - 1))
+    step = lax.rem(group + count - 3, count - 1)
+    step = jnp.where(group < 2, first, jnp.where(step >= first, step + 1, step))
     to = ((core ^ parity) * count + (step ^ place)) * piece + lax.rem(slot, piece)
     source = lax.broadcasted_iota(jnp.int32, (rows, rows), 1)
     pick = jnp.where(source == to + before, 1.0, 0.0).astype(jnp.bfloat16)
@@ -401,8 +402,9 @@
     def shape(height, dtype):
         return jax.ShapeDtypeStruct((height, width), dtype)
 
+    first, *others = [1] + list(range(count - 1, 1, -1))
     rest, keep_last, send_last = call(
-        functools.partial(back_body, seq_n, count, piece),
+        functools.partial(back_body, seq_n, count, piece, first),
         [jax.ShapeDtypeStruct((rows - 2 * piece, columns), bf16), shape(piece, f32), shape(piece, bf16)],
         [WHOLE] * (3 + len(parts)),
         [WHOLE] * 3,
@@ -422,7 +424,7 @@
     other = lax.ppermute(send, names, core_pairs)
     weight = 64 * rows * width * columns
     far = call(last_body, shape(piece, bf16), [WHOLE, WHOLE], WHOLE, weight, 8 * piece * width)(keep_last, other_last)
-    shares = [lax.ppermute(far, names, far_pairs(count - 1))]
+    shares = [lax.ppermute(far, names, far_pairs(first))]
     own_sum, *sends = call(
         functools.partial(pair_body, piece),
         [shape(piece, f32)] + [shape(piece, bf16)] * (count - 2),
@@ -431,8 +433,7 @@
         0,
         8 * height * width,
     )(keep, other)
-    steps = list(range(1, count))
-    shares += [lax.ppermute(sends[d - 1], names, far_pairs(d)) for d in steps[-2::-1]]
+    shares += [lax.ppermute(sends[d - 2], names, far_pairs(d)) for d in others]
     mine = call(
         final_body,
         jax.ShapeDtypeStruct((piece, width), bf16),
@@ -442,13 +443,15 @@
         12 * piece * width,
     )(own_sum, own_rows, gain, *shares)
     mines = {0: mine}
-    for d in steps:
+    for d in [first] + others:
         mines[d] = lax.ppermute(mine, names, far_pairs(d))
     theirs = {d: lax.ppermute(mines[d], names, core_pairs) for d in range(count)}
     ready = {(core, d): part[d] for core, part in enumerate((mines, theirs)) for d in range(count)}
-    early = [key for key in sorted(ready) if key[0] == 0 or key[1] in (0, count - 1)]
+    rank = [0] + others[::-1] + [first]
+    order = sorted(ready, key=lambda key: (key[0], rank.index(key[1])))
+    early = [key for key in order if key[0] == 0 or key[1] in (0, first)]
     vis_grad = None
-    for chosen in (early, [key for key in sorted(ready) if key not in early]):
+    for chosen in (early, [key for key in order if key not in early]):
         done = [] if vis_grad is None else [vis_grad]
         vis_grad = call(
             functools.partial(gather_body, count, chosen),

time: 47.1 us -> 48.3 us (1.025)
  waiting for transfers between devices: 16.1 us -> 17.5 us
    ppermute x3, waiting for transfers between devices: 4 us -> 5.31 us  [the longest x2 4.54 us: on_device(): shares += [lax.ppermute(sends[d - 2], names, far_pairs(d)) for d in others]]
where the time goes in v12:
time: 48.3 us; the launch traced here: 48.1 us
  starting transfers between devices  20.9 us (43%)
  waiting for transfers between devices  17.5 us (36%)
  Pallas kernels  8.1 us (17%)
  between operations  0.76 us (2%)
  local copies, waits for them, and re-layouts  0.74 us (2%)
    ppermute x1, starting transfers between devices, on_device(): text = lax.ppermute(text_kv, 'seq', list(enumerate(owners)))  5.1 us
    ppermute x2, waiting for transfers between devices, on_device(): shares += [lax.ppermute(sends[d - 2], names, far_pairs(d)) for d in others]  4.54 us
    ppermute x3, waiting for transfers between devices, on_device(): mines[d] = lax.ppermute(mine, names, far_pairs(d))  4.26 us
    ppermute x2, starting transfers between devices, on_device(): blocks = [lax.ppermute(block, 'seq', pairs) for pairs in forth]  3.85 us
    ppermute x3, starting transfers between devices, on_device(): lax.ppermute(g, 'seq', pairs)  3.55 us
    ppermute x3, starting transfers between devices, on_device(): mines[d] = lax.ppermute(mine, names, far_pairs(d))  3.55 us
    ppermute x3, waiting for transfers between devices, on_device(): lax.ppermute(g, 'seq', pairs)  3.18 us
    ppermute x1, waiting for transfers between devices, on_device(): raw = lax.ppermute(image_kv, 'seq', home)  2.74 us
  transfers between devices with their start and end apart: 19, of which 12 were waited for; matrix products, arithmetic and copies ran while one was open for 0% of the time, Pallas kernels for 11%

profile of v12, /device:TPU:0, one launch (start us, length us, event | category | flops | bytes accessed | tf_op | source)
XLA Modules:
  0.0 48.1 jit_solution(11957415260187384810)
XLA Ops:
  0.7 5.1 %collective-permute-start = (bf16[128,256]{1,0:T(8,128)(2,1)}, bf16[128,256]{1,0:T(8,128)(2,1)S(1)}, u32[]{:S(2)}, u32[]{:S(2)}) collective-permute-start(bf16[128,256]{1,0:T(8,128)(2,1)} %text_ref.1), channel_id=1, source_target_pairs={{0,6},{2,4},{4,0},{6,2},{1,7},{3,5},{5,1},{7,3},{8,14},{10,12},{12... | collective-permute-start | bytes 196616 | tf_op jit(solution)/shard_map/ppermute | solution.py:339
  5.8 0.7 %copy-done.3 = f32[3200]{0:T(1024)S(1)} copy-done((f32[3200]{0:T(1024)S(1)}, f32[3200]{0:T(1024)}, u32[]{:S(2)}) %copy-start.3) | copy-done | bytes 12824
  6.5 2.3 %shard_map.86 = (bf16[128,256]{1,0:T(8,128)(2,1)S(1)}, bf16[16,3200]{1,0:T(8,128)(2,1)S(1)}) custom-call(bf16[128,3200]{1,0:T(8,128)(2,1)} %vis_hbm.1, f32[25,128]{1,0:T(8,128)S(1)} %bitcast.2, bf16[3200,256]{1,0:T(8,128)(2,1)} %proj_ref.3), custom_call_target="tpu_custom_call" | custom-call | flops 209715200 | bytes 2457600 | tf_op jit(solution)/shard_map/pallas_call | solution.py:342
  8.7 0.0 copy-start
  8.8 0.1 collective-permute-start.1
  8.8 0.0 collective-permute-done.text_ref
  8.8 0.2 shard_map.87.own_ref
  9.1 3.8 %collective-permute-start.3 = (bf16[128,256]{1,0:T(8,128)(2,1)S(1)}, bf16[128,256]{1,0:T(8,128)(2,1)S(1)}, u32[]{:S(2)}, u32[]{:S(2)}) collective-permute-start(bf16[128,256]{1,0:T(8,128)(2,1)S(1)} %shard_map.87.own_ref), channel_id=1, source_target_pairs={{0,6},{2,0},{4,2},{6,4},{1,7},{3,1},{5,3},{7,5},{8,14},{10,8},{12,... | collective-permute-start | bytes 196616 | tf_op jit(solution)/shard_map/ppermute | solution.py:368
  12.9 0.0 collective-permute-start.2
  12.9 2.7 %collective-permute-done.1.raw_ref = bf16[128,256]{1,0:T(8,128)(2,1)S(1)} collective-permute-done((bf16[128,256]{1,0:T(8,128)(2,1)S(1)}, bf16[128,256]{1,0:T(8,128)(2,1)S(1)}, u32[]{:S(2)}, u32[]{:S(2)}) %collective-permute-start.1) | collective-permute-done | bytes 65568 | tf_op jit(solution)/shard_map/ppermute | solution.py:359
  15.7 0.0 collective-permute-done.3.refs_1_
  15.7 1.5 %collective-permute-done.2.refs_0_ = bf16[128,256]{1,0:T(8,128)(2,1)S(1)} collective-permute-done((bf16[128,256]{1,0:T(8,128)(2,1)S(1)}, bf16[128,256]{1,0:T(8,128)(2,1)S(1)}, u32[]{:S(2)}, u32[]{:S(2)}) %collective-permute-start.2) | collective-permute-done | bytes 65568 | tf_op jit(solution)/shard_map/ppermute | solution.py:368
  17.2 1.4 %shard_map.88 = (bf16[512,512]{1,0:T(8,128)(2,1)S(1)}, bf16[512,512]{1,0:T(8,128)(2,1)S(1)}, bf16[512,128]{1,0:T(8,128)(2,1)S(1)}, bf16[128,256]{1,0:T(8,128)(2,...) custom-call(s32[1,8]{1,0:T(1,128)S(1)} %bitcast.5, bf16[128,512]{1,0:T(8,128)(2,1)S(1)} %copy-done.1, ...), custom_call_target="tpu_custom_call" | custom-call | flops 268435456 | bytes 786432 | tf_op jit(solution)/shard_map/pallas_call | solution.py:383
  18.6 1.7 %collective-permute-start.4 = (bf16[128,256]{1,0:T(8,128)(2,1)S(1)}, bf16[128,256]{1,0:T(8,128)(2,1)S(1)}, u32[]{:S(2)}, u32[]{:S(2)}) collective-permute-start(bf16[128,256]{1,0:T(8,128)(2,1)S(1)} %get-tuple-element.26), channel_id=1, source_target_pairs={{0,4},{2,6},{4,0},{6,2},{1,5},{3,7},{5,1},{7,3},{8,12},{10,14},{12... | collective-permute-start | bytes 196616 | tf_op jit(solution)/shard_map/ppermute | solution.py:400
  20.3 1.1 %collective-permute-start.5 = (bf16[128,256]{1,0:T(8,128)(2,1)S(1)}, bf16[128,256]{1,0:T(8,128)(2,1)S(1)}, u32[]{:S(2)}, u32[]{:S(2)}) collective-permute-start(bf16[128,256]{1,0:T(8,128)(2,1)S(1)} %get-tuple-element.27), channel_id=1, source_target_pairs={{0,6},{2,4},{4,2},{6,0},{1,7},{3,5},{5,3},{7,1},{8,14},{10,12},{12... | collective-permute-start | bytes 196616 | tf_op jit(solution)/shard_map/ppermute | solution.py:400
  21.4 0.8 %collective-permute-start.6 = (bf16[128,256]{1,0:T(8,128)(2,1)S(1)}, bf16[128,256]{1,0:T(8,128)(2,1)S(1)}, u32[]{:S(2)}, u32[]{:S(2)}) collective-permute-start(bf16[128,256]{1,0:T(8,128)(2,1)S(1)} %get-tuple-element.28), channel_id=1, source_target_pairs={{0,2},{2,0},{4,6},{6,4},{1,3},{3,1},{5,7},{7,5},{8,10},{10,8},{12,... | collective-permute-start | bytes 196616 | tf_op jit(solution)/shard_map/ppermute | solution.py:400
  22.1 1.0 %shard_map.89 = (bf16[128,512]{1,0:T(8,128)(2,1)}, bf16[128,256]{1,0:T(8,128)(2,1)S(1)}) custom-call(bf16[128,512]{1,0:T(8,128)(2,1)S(1)} %copy-done.1, bf16[128,512]{1,0:T(8,128)(2,1)S(1)} %copy-done.2, bf16[512,512]{1,0:T(8,128)(2,1)S(1)} %get-tuple-element.21.low_ref, bf16[512,512]{1,0:T(8,128)(2,1)S(1)} %get-tuple-element.22.dscore_ref, ...), custom_call_target="tpu_custom_call" | custom-call | flops 67108864 | bytes 917504 | tf_op jit(solution)/shard_map/pallas_call | solution.py:392
  23.1 1.4 %collective-permute-done.4.refs_1_ = bf16[128,256]{1,0:T(8,128)(2,1)S(1)} collective-permute-done((bf16[128,256]{1,0:T(8,128)(2,1)S(1)}, bf16[128,256]{1,0:T(8,128)(2,1)S(1)}, u32[]{:S(2)}, u32[]{:S(2)}) %collective-permute-start.4) | collective-permute-done | bytes 65568 | tf_op jit(solution)/shard_map/ppermute | solution.py:400
  24.6 1.7 %collective-permute-done.5.refs_2_ = bf16[128,256]{1,0:T(8,128)(2,1)S(1)} collective-permute-done((bf16[128,256]{1,0:T(8,128)(2,1)S(1)}, bf16[128,256]{1,0:T(8,128)(2,1)S(1)}, u32[]{:S(2)}, u32[]{:S(2)}) %collective-permute-start.5) | collective-permute-done | bytes 65568 | tf_op jit(solution)/shard_map/ppermute | solution.py:400
  26.3 0.0 collective-permute-done.6.refs_3_
  26.3 0.7 %shard_map.90 = (bf16[96,256]{1,0:T(8,128)(2,1)S(1)}, f32[16,3200]{1,0:T(8,128)S(1)}, bf16[16,3200]{1,0:T(8,128)(2,1)S(1)}) custom-call(s32[1,8]{1,0:T(1,128)S(1)} %bitcast.6, bf16[3200,256]{1,0:T(8,128)(2,1)S(1)} %copy-done, bf16[128,256]{1,0:T(8,128)(2,1)S(1)} %get-tuple-element.25.refs_0_, bf16[128,256]{1,0:T(8,128)(2,1)S(1)} %collective-permute-done.4.refs_1_, ...), custom_call_target="tpu_custom_call" | custom-call | flops 52428800 | bytes 1945600 | tf_op jit(solution)/shard_map/pallas_call | solution.py:406
  27.1 0.1 collective-permute-start.8
  27.1 0.6 %shard_map.91 = (f32[48,3200]{1,0:T(8,128)S(1)}, bf16[48,3200]{1,0:T(8,128)(2,1)S(1)}) custom-call(bf16[96,256]{1,0:T(8,128)(2,1)S(1)} %get-tuple-element.29.rest_ref, bf16[3200,256]{1,0:T(8,128)(2,1)S(1)} %copy-done), custom_call_target="tpu_custom_call" | custom-call | flops 157286400 | bytes 2560000 | tf_op jit(solution)/shard_map/pallas_call | solution.py:416
  27.8 0.6 %collective-permute-start.7 = (bf16[48,3200]{1,0:T(8,128)(2,1)S(1)}, bf16[48,3200]{1,0:T(8,128)(2,1)S(1)}, u32[]{:S(2)}, u32[]{:S(2)}) collective-permute-start(bf16[48,3200]{1,0:T(8,128)(2,1)S(1)} %get-tuple-element.31), channel_id=1, source_target_pairs={{0,8},{1,9},{8,0},{9,1},{16,24},{17,25},{24,16},{25,17},{2,10},{3,... | collective-permute-start | bytes 921608 | tf_op jit(solution)/shard_map/ppermute | solution.py:424
  28.3 0.1 collective-permute-done.8.other_ref
  28.5 1.6 %collective-permute-start.9 = (bf16[16,3200]{1,0:T(8,128)(2,1)S(1)}, bf16[16,3200]{1,0:T(8,128)(2,1)S(1)}, u32[]{:S(2)}, u32[]{:S(2)}) collective-permute-start(bf16[16,3200]{1,0:T(8,128)(2,1)S(1)} %shard_map.93), channel_id=1, source_target_pairs={{0,1},{1,0},{8,9},{9,8},{16,17},{17,16},{24,25},{25,24},{2,3},{3,2... | collective-permute-start | bytes 307208 | tf_op jit(solution)/shard_map/ppermute | solution.py:427
  30.0 0.0 collective-permute-done.7.other_ref
  30.1 0.1 shard_map.92
  30.1 2.0 %collective-permute-start.10 = (bf16[16,3200]{1,0:T(8,128)(2,1)S(1)}, bf16[16,3200]{1,0:T(8,128)(2,1)S(1)}, u32[]{:S(2)}, u32[]{:S(2)}) collective-permute-start(bf16[16,3200]{1,0:T(8,128)(2,1)S(1)} %get-tuple-element.36), channel_id=1, source_target_pairs={{0,17},{1,16},{8,25},{9,24},{16,1},{17,0},{24,9},{25,8},{2,19},{3,... | collective-permute-start | bytes 307208 | tf_op jit(solution)/shard_map/ppermute | solution.py:436
  32.1 0.5 %collective-permute-start.11 = (bf16[16,3200]{1,0:T(8,128)(2,1)S(1)}, bf16[16,3200]{1,0:T(8,128)(2,1)S(1)}, u32[]{:S(2)}, u32[]{:S(2)}) collective-permute-start(bf16[16,3200]{1,0:T(8,128)(2,1)S(1)} %get-tuple-element.37), channel_id=1, source_target_pairs={{0,16},{1,17},{8,24},{9,25},{16,0},{17,1},{24,8},{25,9},{2,18},{3,... | collective-permute-start | bytes 307208 | tf_op jit(solution)/shard_map/ppermute | solution.py:436
  32.7 0.8 %collective-permute-done.9.refs_0_ = bf16[16,3200]{1,0:T(8,128)(2,1)S(1)} collective-permute-done((bf16[16,3200]{1,0:T(8,128)(2,1)S(1)}, bf16[16,3200]{1,0:T(8,128)(2,1)S(1)}, u32[]{:S(2)}, u32[]{:S(2)}) %collective-permute-start.9) | collective-permute-done | bytes 102432 | tf_op jit(solution)/shard_map/ppermute | solution.py:427
  33.5 3.3 %collective-permute-done.10.refs_1_ = bf16[16,3200]{1,0:T(8,128)(2,1)S(1)} collective-permute-done((bf16[16,3200]{1,0:T(8,128)(2,1)S(1)}, bf16[16,3200]{1,0:T(8,128)(2,1)S(1)}, u32[]{:S(2)}, u32[]{:S(2)}) %collective-permute-start.10) | collective-permute-done | bytes 102432 | tf_op jit(solution)/shard_map/ppermute | solution.py:436
  36.7 1.3 %collective-permute-done.11.refs_2_ = bf16[16,3200]{1,0:T(8,128)(2,1)S(1)} collective-permute-done((bf16[16,3200]{1,0:T(8,128)(2,1)S(1)}, bf16[16,3200]{1,0:T(8,128)(2,1)S(1)}, u32[]{:S(2)}, u32[]{:S(2)}) %collective-permute-start.11) | collective-permute-done | bytes 102432 | tf_op jit(solution)/shard_map/ppermute | solution.py:436
  38.0 0.2 shard_map.94.refs_0_
  38.2 0.6 %collective-permute-start.16 = (bf16[16,3200]{1,0:T(8,128)(2,1)S(1)}, bf16[16,3200]{1,0:T(8,128)(2,1)S(1)}, u32[]{:S(2)}, u32[]{:S(2)}) collective-permute-start(bf16[16,3200]{1,0:T(8,128)(2,1)S(1)} %shard_map.94.refs_0_), channel_id=1, source_target_pairs={{0,1},{1,0},{8,9},{9,8},{16,17},{17,16},{24,25},{25,24},{2,3},{3,2... | collective-permute-start | bytes 307208 | tf_op jit(solution)/shard_map/ppermute | solution.py:447
  38.8 2.4 %collective-permute-start.14 = (bf16[16,3200]{1,0:T(8,128)(2,1)S(1)}, bf16[16,3200]{1,0:T(8,128)(2,1)S(1)}, u32[]{:S(2)}, u32[]{:S(2)}) collective-permute-start(bf16[16,3200]{1,0:T(8,128)(2,1)S(1)} %shard_map.94.refs_0_), channel_id=1, source_target_pairs={{0,17},{1,16},{8,25},{9,24},{16,1},{17,0},{24,9},{25,8},{2,19},{3,... | collective-permute-start | bytes 307208 | tf_op jit(solution)/shard_map/ppermute | solution.py:447
  41.2 0.5 %collective-permute-start.12 = (bf16[16,3200]{1,0:T(8,128)(2,1)S(1)}, bf16[16,3200]{1,0:T(8,128)(2,1)S(1)}, u32[]{:S(2)}, u32[]{:S(2)}) collective-permute-start(bf16[16,3200]{1,0:T(8,128)(2,1)S(1)} %shard_map.94.refs_0_), channel_id=1, source_target_pairs={{0,16},{1,17},{8,24},{9,25},{16,0},{17,1},{24,8},{25,9},{2,18},{3,... | collective-permute-start | bytes 307208 | tf_op jit(solution)/shard_map/ppermute | solution.py:447
  41.7 0.0 collective-permute-start.17
  41.7 2.6 %collective-permute-done.16.refs_3_ = bf16[16,3200]{1,0:T(8,128)(2,1)S(1)} collective-permute-done((bf16[16,3200]{1,0:T(8,128)(2,1)S(1)}, bf16[16,3200]{1,0:T(8,128)(2,1)S(1)}, u32[]{:S(2)}, u32[]{:S(2)}) %collective-permute-start.16) | collective-permute-done | bytes 102432 | tf_op jit(solution)/shard_map/ppermute | solution.py:447
  44.3 0.4 collective-permute-done.14.refs_2_
  44.8 0.1 collective-permute-start.15
  44.9 1.2 %collective-permute-done.12.refs_1_ = bf16[16,3200]{1,0:T(8,128)(2,1)S(1)} collective-permute-done((bf16[16,3200]{1,0:T(8,128)(2,1)S(1)}, bf16[16,3200]{1,0:T(8,128)(2,1)S(1)}, u32[]{:S(2)}, u32[]{:S(2)}) %collective-permute-start.12) | collective-permute-done | bytes 102432 | tf_op jit(solution)/shard_map/ppermute | solution.py:447
  46.1 0.0 collective-permute-start.13
  46.1 0.0 collective-permute-done.17.refs_4_
  46.1 0.0 collective-permute-done.18.refs_5_
  46.1 0.9 %shard_map.95.refs_2_ = bf16[128,3200]{1,0:T(8,128)(2,1)} custom-call(bf16[16,3200]{1,0:T(8,128)(2,1)S(1)} %shard_map.94.refs_0_, bf16[16,3200]{1,0:T(8,128)(2,1)S(1)} %collective-permute-done.12.refs_1_, bf16[16,3200]{1,0:T(8,128)(2,1)S(1)} %collective-permute-done.14.refs_2_, bf16[16,3200]{1,0:T(8,128)(2,1)S(1)} %collective-permute-done.16.refs_3_, ...), custom_call_target="tpu_custom_call" | custom-call | bytes 1228800 | tf_op jit(solution)/shard_map/pallas_call | solution.py:456
  47.0 0.4 collective-permute-done.13.refs_0_
  47.4 0.7 %shard_map.96 = bf16[128,3200]{1,0:T(8,128)(2,1)} custom-call(bf16[16,3200]{1,0:T(8,128)(2,1)S(1)} %collective-permute-done.13.refs_0_, bf16[16,3200]{1,0:T(8,128)(2,1)S(1)} %collective-permute-done.15.refs_1_, bf16[128,3200]{1,0:T(8,128)(2,1)} %shard_map.95.refs_2_), custom_call_target="tpu_custom_call", output_to_operand_aliasing={{}: (2, {})} | custom-call | bytes 409600 | tf_op jit(solution)/shard_map/pallas_call | solution.py:456
  (13 shorter events, 0.1 us)
Async XLA Ops:
  0.6 16.6 %copy-start.2 = (bf16[128,512]{1,0:T(8,128)(2,1)S(1)}, bf16[128,512]{1,0:T(8,128)(2,1)}, u32[]{:S(2)}) copy-start(bf16[128,512]{1,0:T(8,128)(2,1)} %g_ref.3) | copy-start | bytes 393220
  0.6 16.6 %copy-start.1 = (bf16[128,512]{1,0:T(8,128)(2,1)S(1)}, bf16[128,512]{1,0:T(8,128)(2,1)}, u32[]{:S(2)}) copy-start(bf16[128,512]{1,0:T(8,128)(2,1)} %q_ref.3) | copy-start | bytes 393220
  0.7 8.2 %collective-permute-start = (bf16[128,256]{1,0:T(8,128)(2,1)}, bf16[128,256]{1,0:T(8,128)(2,1)S(1)}, u32[]{:S(2)}, u32[]{:S(2)}) collective-permute-start(bf16[128,256]{1,0:T(8,128)(2,1)} %text_ref.1), channel_id=1, source_target_pairs={{0,6},{2,4},{4,0},{6,2},{1,7},{3,5},{5,1},{7,3},{8,14},{10,12},{12... | collective-permute-start | bytes 196616 | tf_op jit(solution)/shard_map/ppermute | solution.py:339
  5.8 0.7 %copy-start.3 = (f32[3200]{0:T(1024)S(1)}, f32[3200]{0:T(1024)}, u32[]{:S(2)}) copy-start(f32[3200]{0:T(1024)} %param.8) | copy-start | bytes 38404
  6.5 2.4 %copy-start.4 = (s32[8]{0:T(128)S(1)}, s32[8]{0:T(128)}, u32[]{:S(2)}) copy-start(s32[8]{0:T(128)} %param.10) | copy-start | bytes 100
  6.5 10.7 %copy-start.5 = (bf16[128,256]{1,0:T(8,128)(2,1)S(1)}, bf16[128,256]{1,0:T(8,128)(2,1)}, u32[]{:S(2)}) copy-start(bf16[128,256]{1,0:T(8,128)(2,1)} %text_ref.1) | copy-start | bytes 196612
  8.7 17.6 %copy-start = (bf16[3200,256]{1,0:T(8,128)(2,1)S(1)}, bf16[3200,256]{1,0:T(8,128)(2,1)}, u32[]{:S(2)}) copy-start(bf16[3200,256]{1,0:T(8,128)(2,1)} %proj_ref.3) | copy-start | bytes 4915204
  8.8 6.9 %collective-permute-start.1 = (bf16[128,256]{1,0:T(8,128)(2,1)S(1)}, bf16[128,256]{1,0:T(8,128)(2,1)S(1)}, u32[]{:S(2)}, u32[]{:S(2)}) collective-permute-start(bf16[128,256]{1,0:T(8,128)(2,1)S(1)} %get-tuple-element.20.image_ref), channel_id=1, source_target_pairs={{6,0},{4,2},{0,4},{2,6},{7,1},{5,3},{1,5},{3,7},{14,8},{12,10},{8,... | collective-permute-start | bytes 196616 | tf_op jit(solution)/shard_map/ppermute | solution.py:359
  9.1 6.6 %collective-permute-start.3 = (bf16[128,256]{1,0:T(8,128)(2,1)S(1)}, bf16[128,256]{1,0:T(8,128)(2,1)S(1)}, u32[]{:S(2)}, u32[]{:S(2)}) collective-permute-start(bf16[128,256]{1,0:T(8,128)(2,1)S(1)} %shard_map.87.own_ref), channel_id=1, source_target_pairs={{0,6},{2,0},{4,2},{6,4},{1,7},{3,1},{5,3},{7,5},{8,14},{10,8},{12,... | collective-permute-start | bytes 196616 | tf_op jit(solution)/shard_map/ppermute | solution.py:368
  12.9 4.3 %collective-permute-start.2 = (bf16[128,256]{1,0:T(8,128)(2,1)S(1)}, bf16[128,256]{1,0:T(8,128)(2,1)S(1)}, u32[]{:S(2)}, u32[]{:S(2)}) collective-permute-start(bf16[128,256]{1,0:T(8,128)(2,1)S(1)} %shard_map.87.own_ref), channel_id=1, source_target_pairs={{0,4},{2,0},{4,6},{6,2},{1,5},{3,1},{5,7},{7,3},{8,12},{10,8},{12,... | collective-permute-start | bytes 196616 | tf_op jit(solution)/shard_map/ppermute | solution.py:368
  18.6 6.0 %collective-permute-start.4 = (bf16[128,256]{1,0:T(8,128)(2,1)S(1)}, bf16[128,256]{1,0:T(8,128)(2,1)S(1)}, u32[]{:S(2)}, u32[]{:S(2)}) collective-permute-start(bf16[128,256]{1,0:T(8,128)(2,1)S(1)} %get-tuple-element.26), channel_id=1, source_target_pairs={{0,4},{2,6},{4,0},{6,2},{1,5},{3,7},{5,1},{7,3},{8,12},{10,14},{12... | collective-permute-start | bytes 196616 | tf_op jit(solution)/shard_map/ppermute | solution.py:400
  20.3 6.1 %collective-permute-start.5 = (bf16[128,256]{1,0:T(8,128)(2,1)S(1)}, bf16[128,256]{1,0:T(8,128)(2,1)S(1)}, u32[]{:S(2)}, u32[]{:S(2)}) collective-permute-start(bf16[128,256]{1,0:T(8,128)(2,1)S(1)} %get-tuple-element.27), channel_id=1, source_target_pairs={{0,6},{2,4},{4,2},{6,0},{1,7},{3,5},{5,3},{7,1},{8,14},{10,12},{12... | collective-permute-start | bytes 196616 | tf_op jit(solution)/shard_map/ppermute | solution.py:400
  21.4 5.0 %collective-permute-start.6 = (bf16[128,256]{1,0:T(8,128)(2,1)S(1)}, bf16[128,256]{1,0:T(8,128)(2,1)S(1)}, u32[]{:S(2)}, u32[]{:S(2)}) collective-permute-start(bf16[128,256]{1,0:T(8,128)(2,1)S(1)} %get-tuple-element.28), channel_id=1, source_target_pairs={{0,2},{2,0},{4,6},{6,4},{1,3},{3,1},{5,7},{7,5},{8,10},{10,8},{12,... | collective-permute-start | bytes 196616 | tf_op jit(solution)/shard_map/ppermute | solution.py:400
  27.1 1.4 %collective-permute-start.8 = (bf16[16,3200]{1,0:T(8,128)(2,1)S(1)}, bf16[16,3200]{1,0:T(8,128)(2,1)S(1)}, u32[]{:S(2)}, u32[]{:S(2)}) collective-permute-start(bf16[16,3200]{1,0:T(8,128)(2,1)S(1)} %get-tuple-element.35), channel_id=1, source_target_pairs={{0,8},{1,9},{8,0},{9,1},{16,24},{17,25},{24,16},{25,17},{2,10},{3,... | collective-permute-start | bytes 307208 | tf_op jit(solution)/shard_map/ppermute | solution.py:414
  27.8 2.3 %collective-permute-start.7 = (bf16[48,3200]{1,0:T(8,128)(2,1)S(1)}, bf16[48,3200]{1,0:T(8,128)(2,1)S(1)}, u32[]{:S(2)}, u32[]{:S(2)}) collective-permute-start(bf16[48,3200]{1,0:T(8,128)(2,1)S(1)} %get-tuple-element.31), channel_id=1, source_target_pairs={{0,8},{1,9},{8,0},{9,1},{16,24},{17,25},{24,16},{25,17},{2,10},{3,... | collective-permute-start | bytes 921608 | tf_op jit(solution)/shard_map/ppermute | solution.py:424
  28.5 5.0 %collective-permute-start.9 = (bf16[16,3200]{1,0:T(8,128)(2,1)S(1)}, bf16[16,3200]{1,0:T(8,128)(2,1)S(1)}, u32[]{:S(2)}, u32[]{:S(2)}) collective-permute-start(bf16[16,3200]{1,0:T(8,128)(2,1)S(1)} %shard_map.93), channel_id=1, source_target_pairs={{0,1},{1,0},{8,9},{9,8},{16,17},{17,16},{24,25},{25,24},{2,3},{3,2... | collective-permute-start | bytes 307208 | tf_op jit(solution)/shard_map/ppermute | solution.py:427
  30.1 6.6 %collective-permute-start.10 = (bf16[16,3200]{1,0:T(8,128)(2,1)S(1)}, bf16[16,3200]{1,0:T(8,128)(2,1)S(1)}, u32[]{:S(2)}, u32[]{:S(2)}) collective-permute-start(bf16[16,3200]{1,0:T(8,128)(2,1)S(1)} %get-tuple-element.36), channel_id=1, source_target_pairs={{0,17},{1,16},{8,25},{9,24},{16,1},{17,0},{24,9},{25,8},{2,19},{3,... | collective-permute-start | bytes 307208 | tf_op jit(solution)/shard_map/ppermute | solution.py:436
  32.1 5.9 %collective-permute-start.11 = (bf16[16,3200]{1,0:T(8,128)(2,1)S(1)}, bf16[16,3200]{1,0:T(8,128)(2,1)S(1)}, u32[]{:S(2)}, u32[]{:S(2)}) collective-permute-start(bf16[16,3200]{1,0:T(8,128)(2,1)S(1)} %get-tuple-element.37), channel_id=1, source_target_pairs={{0,16},{1,17},{8,24},{9,25},{16,0},{17,1},{24,8},{25,9},{2,18},{3,... | collective-permute-start | bytes 307208 | tf_op jit(solution)/shard_map/ppermute | solution.py:436
  38.2 6.2 %collective-permute-start.16 = (bf16[16,3200]{1,0:T(8,128)(2,1)S(1)}, bf16[16,3200]{1,0:T(8,128)(2,1)S(1)}, u32[]{:S(2)}, u32[]{:S(2)}) collective-permute-start(bf16[16,3200]{1,0:T(8,128)(2,1)S(1)} %shard_map.94.refs_0_), channel_id=1, source_target_pairs={{0,1},{1,0},{8,9},{9,8},{16,17},{17,16},{24,25},{25,24},{2,3},{3,2... | collective-permute-start | bytes 307208 | tf_op jit(solution)/shard_map/ppermute | solution.py:447
  38.8 6.0 %collective-permute-start.14 = (bf16[16,3200]{1,0:T(8,128)(2,1)S(1)}, bf16[16,3200]{1,0:T(8,128)(2,1)S(1)}, u32[]{:S(2)}, u32[]{:S(2)}) collective-permute-start(bf16[16,3200]{1,0:T(8,128)(2,1)S(1)} %shard_map.94.refs_0_), channel_id=1, source_target_pairs={{0,17},{1,16},{8,25},{9,24},{16,1},{17,0},{24,9},{25,8},{2,19},{3,... | collective-permute-start | bytes 307208 | tf_op jit(solution)/shard_map/ppermute | solution.py:447
  41.2 4.9 %collective-permute-start.12 = (bf16[16,3200]{1,0:T(8,128)(2,1)S(1)}, bf16[16,3200]{1,0:T(8,128)(2,1)S(1)}, u32[]{:S(2)}, u32[]{:S(2)}) collective-permute-start(bf16[16,3200]{1,0:T(8,128)(2,1)S(1)} %shard_map.94.refs_0_), channel_id=1, source_target_pairs={{0,16},{1,17},{8,24},{9,25},{16,0},{17,1},{24,8},{25,9},{2,18},{3,... | collective-permute-start | bytes 307208 | tf_op jit(solution)/shard_map/ppermute | solution.py:447
  41.7 4.3 %collective-permute-start.17 = (bf16[16,3200]{1,0:T(8,128)(2,1)S(1)}, bf16[16,3200]{1,0:T(8,128)(2,1)S(1)}, u32[]{:S(2)}, u32[]{:S(2)}) collective-permute-start(bf16[16,3200]{1,0:T(8,128)(2,1)S(1)} %shard_map.94.refs_0_), channel_id=1, source_target_pairs={{0,8},{1,9},{8,0},{9,1},{16,24},{17,25},{24,16},{25,17},{2,10},{3,... | collective-permute-start | bytes 307208 | tf_op jit(solution)/shard_map/ppermute | solution.py:448
  44.3 1.7 %collective-permute-start.18 = (bf16[16,3200]{1,0:T(8,128)(2,1)S(1)}, bf16[16,3200]{1,0:T(8,128)(2,1)S(1)}, u32[]{:S(2)}, u32[]{:S(2)}) collective-permute-start(bf16[16,3200]{1,0:T(8,128)(2,1)S(1)} %collective-permute-done.16.refs_3_), channel_id=1, source_target_pairs={{0,8},{1,9},{8,0},{9,1},{16,24},{17,25},{24,16},{25,17},{2,10},{3,... | collective-permute-start | bytes 307208 | tf_op jit(solution)/shard_map/ppermute | solution.py:448
  44.8 2.2 %collective-permute-start.15 = (bf16[16,3200]{1,0:T(8,128)(2,1)S(1)}, bf16[16,3200]{1,0:T(8,128)(2,1)S(1)}, u32[]{:S(2)}, u32[]{:S(2)}) collective-permute-start(bf16[16,3200]{1,0:T(8,128)(2,1)S(1)} %collective-permute-done.14.refs_2_), channel_id=1, source_target_pairs={{0,8},{1,9},{8,0},{9,1},{16,24},{17,25},{24,16},{25,17},{2,10},{3,... | collective-permute-start | bytes 307208 | tf_op jit(solution)/shard_map/ppermute | solution.py:448
  46.1 1.3 %collective-permute-start.13 = (bf16[16,3200]{1,0:T(8,128)(2,1)S(1)}, bf16[16,3200]{1,0:T(8,128)(2,1)S(1)}, u32[]{:S(2)}, u32[]{:S(2)}) collective-permute-start(bf16[16,3200]{1,0:T(8,128)(2,1)S(1)} %collective-permute-done.12.refs_1_), channel_id=1, source_target_pairs={{0,8},{1,9},{8,0},{9,1},{16,24},{17,25},{24,16},{25,17},{2,10},{3,... | collective-permute-start | bytes 307208 | tf_op jit(solution)/shard_map/ppermute | solution.py:448

commit v13 on v11

--- a/solution.py
+++ b/solution.py
@@ -84,29 +84,31 @@
     return list(zip(edges[:-1], edges[1:]))
 
 
-def project_body(piece, vis_hbm, gain_hbm, proj_hbm, kv_ref, own_ref, vis, gain_ref, proj, vis_sems, proj_sems, gain_sem):
+def project_body(piece, vis_hbm, gain_hbm, proj_hbm, kv_ref, own_ref, vis, scaled, gain_ref, proj, vis_sems, proj_sems, gain_sem):
     rows, width = vis.shape
     gain_copy = pltpu.make_async_copy(gain_hbm, gain_ref, gain_sem)
     gain_copy.start()
-    copies = []
-    for n, (low, high) in enumerate(cuts(width)):
-        vis_copy = pltpu.make_async_copy(vis_hbm.at[:, low:high], vis.at[:, low:high], vis_sems.at[n])
-        proj_copy = pltpu.make_async_copy(proj_hbm.at[low:high, :], proj.at[low:high, :], proj_sems.at[n])
-        vis_copy.start()
-        proj_copy.start()
-        copies.append((vis_copy, proj_copy))
+    chunks = cuts(width)
+    vis_copies, proj_copies = [], []
+    for n, (low, high) in enumerate(chunks):
+        vis_copies.append(pltpu.make_async_copy(vis_hbm.at[:, low:high], vis.at[:, low:high], vis_sems.at[n]))
+        proj_copies.append(pltpu.make_async_copy(proj_hbm.at[low:high, :], proj.at[low:high, :], proj_sems.at[n]))
+    for copy in vis_copies + proj_copies[:2]:
+        copy.start()
     gain_copy.wait()
     squares = jnp.zeros((rows, HD), jnp.float32)
-    total = jnp.zeros(kv_ref.shape, jnp.float32)
-    for (low, high), (vis_copy, proj_copy) in zip(cuts(width), copies):
-        vis_copy.wait()
-        scaled = []
+    for n, (low, high) in enumerate(chunks):
+        vis_copies[n].wait()
+        for copy in proj_copies[n + 2 : n + 3]:
+            copy.start()
         for c in range(low, high, HD):
             wide = vis[:, c : c + HD].astype(jnp.float32)
             squares += wide * wide
-            scaled.append((wide * gain_ref[c // HD : c // HD + 1, :]).astype(jnp.bfloat16))
-        proj_copy.wait()
-        total += jnp.dot(jnp.concatenate(scaled, axis=1), proj[low:high, :], preferred_element_type=jnp.float32)
+            scaled[:, c : c + HD] = (wide * gain_ref[c // HD : c // HD + 1, :]).astype(jnp.bfloat16)
+    total = jnp.zeros(kv_ref.shape, jnp.float32)
+    for copy, (low, high) in zip(proj_copies, chunks):
+        copy.wait()
+        total += jnp.dot(scaled[:, low:high], proj[low:high, :], preferred_element_type=jnp.float32)
     inverse = lax.rsqrt(jnp.sum(squares, axis=1, keepdims=True) / width + EPS)
     kv_ref[...] = (total * inverse).astype(jnp.bfloat16)
     parity, place = group_place()
@@ -347,6 +349,7 @@
         2 * width * (rows + columns),
         limit=WIDE_LIMIT,
         scratch_shapes=[
+            pltpu.VMEM((rows, width), bf16),
             pltpu.VMEM((rows, width), bf16),
             pltpu.VMEM(gain.shape, f32),
             pltpu.VMEM((width, columns), bf16),

time: 47.1 us -> 47.4 us (level)
  no operation moved by 1% of the time
where the time goes in v13:
time: 47.4 us; the launch traced here: 47.2 us
  starting transfers between devices  21.3 us (45%)
  waiting for transfers between devices  16 us (34%)
  Pallas kernels  8.4 us (18%)
  between operations  0.76 us (2%)
  local copies, waits for them, and re-layouts  0.74 us (2%)
    ppermute x1, starting transfers between devices, on_device(): text = lax.ppermute(text_kv, 'seq', list(enumerate(owners)))  5.1 us
    ppermute x3, waiting for transfers between devices, on_device(): mines[d] = lax.ppermute(mine, names, far_pairs(d))  4.42 us
    ppermute x2, starting transfers between devices, on_device(): blocks = [lax.ppermute(block, 'seq', pairs) for pairs in forth]  3.85 us
    ppermute x3, starting transfers between devices, on_device(): mines[d] = lax.ppermute(mine, names, far_pairs(d))  3.55 us
    ppermute x3, starting transfers between devices, on_device(): lax.ppermute(g, 'seq', pairs)  3.55 us
    ppermute x3, waiting for transfers between devices, on_device(): lax.ppermute(g, 'seq', pairs)  3.16 us
    ppermute x1, waiting for transfers between devices, on_device(): raw = lax.ppermute(image_kv, 'seq', home)  2.74 us
    pallas_call x1, Pallas kernels, on_device(): call(functools.partial(project_body, piece), [jax.ShapeDtypeStruct((rows,...  2.57 us
  transfers between devices with their start and end apart: 19, of which 12 were waited for; matrix products, arithmetic and copies ran while one was open for 0% of the time, Pallas kernels for 11%

profile of v13, /device:TPU:0, one launch (start us, length us, event | category | flops | bytes accessed | tf_op | source)
XLA Modules:
  0.0 47.2 jit_solution(94223628052954389)
XLA Ops:
  0.7 5.1 %collective-permute-start = (bf16[128,256]{1,0:T(8,128)(2,1)}, bf16[128,256]{1,0:T(8,128)(2,1)S(1)}, u32[]{:S(2)}, u32[]{:S(2)}) collective-permute-start(bf16[128,256]{1,0:T(8,128)(2,1)} %text_ref.1), channel_id=1, source_target_pairs={{0,6},{2,4},{4,0},{6,2},{1,7},{3,5},{5,1},{7,3},{8,14},{10,12},{12... | collective-permute-start | bytes 196616 | tf_op jit(solution)/shard_map/ppermute | solution.py:340
  5.8 0.7 %copy-done.3 = f32[3200]{0:T(1024)S(1)} copy-done((f32[3200]{0:T(1024)S(1)}, f32[3200]{0:T(1024)}, u32[]{:S(2)}) %copy-start.3) | copy-done | bytes 12824
  6.5 2.6 %shard_map.86 = (bf16[128,256]{1,0:T(8,128)(2,1)S(1)}, bf16[16,3200]{1,0:T(8,128)(2,1)S(1)}) custom-call(bf16[128,3200]{1,0:T(8,128)(2,1)} %vis_hbm.1, f32[25,128]{1,0:T(8,128)S(1)} %bitcast.2, bf16[3200,256]{1,0:T(8,128)(2,1)} %proj_ref.3), custom_call_target="tpu_custom_call" | custom-call | flops 209715200 | bytes 2457600 | tf_op jit(solution)/shard_map/pallas_call | solution.py:343
  9.1 0.0 copy-start
  9.1 0.1 collective-permute-start.1
  9.1 0.0 collective-permute-done.text_ref
  9.2 0.2 shard_map.87.own_ref
  9.4 3.8 %collective-permute-start.3 = (bf16[128,256]{1,0:T(8,128)(2,1)S(1)}, bf16[128,256]{1,0:T(8,128)(2,1)S(1)}, u32[]{:S(2)}, u32[]{:S(2)}) collective-permute-start(bf16[128,256]{1,0:T(8,128)(2,1)S(1)} %shard_map.87.own_ref), channel_id=1, source_target_pairs={{0,6},{2,0},{4,2},{6,4},{1,7},{3,1},{5,3},{7,5},{8,14},{10,8},{12,... | collective-permute-start | bytes 196616 | tf_op jit(solution)/shard_map/ppermute | solution.py:370
  13.2 0.0 collective-permute-start.2
  13.2 2.7 %collective-permute-done.1.raw_ref = bf16[128,256]{1,0:T(8,128)(2,1)S(1)} collective-permute-done((bf16[128,256]{1,0:T(8,128)(2,1)S(1)}, bf16[128,256]{1,0:T(8,128)(2,1)S(1)}, u32[]{:S(2)}, u32[]{:S(2)}) %collective-permute-start.1) | collective-permute-done | bytes 65568 | tf_op jit(solution)/shard_map/ppermute | solution.py:361
  16.0 0.0 collective-permute-done.3.refs_1_
  16.0 1.5 %collective-permute-done.2.refs_0_ = bf16[128,256]{1,0:T(8,128)(2,1)S(1)} collective-permute-done((bf16[128,256]{1,0:T(8,128)(2,1)S(1)}, bf16[128,256]{1,0:T(8,128)(2,1)S(1)}, u32[]{:S(2)}, u32[]{:S(2)}) %collective-permute-start.2) | collective-permute-done | bytes 65568 | tf_op jit(solution)/shard_map/ppermute | solution.py:370
  17.5 1.4 %shard_map.88 = (bf16[512,512]{1,0:T(8,128)(2,1)S(1)}, bf16[512,512]{1,0:T(8,128)(2,1)S(1)}, bf16[512,128]{1,0:T(8,128)(2,1)S(1)}, bf16[128,256]{1,0:T(8,128)(2,...) custom-call(s32[1,8]{1,0:T(1,128)S(1)} %bitcast.5, bf16[128,512]{1,0:T(8,128)(2,1)S(1)} %copy-done.1, ...), custom_call_target="tpu_custom_call" | custom-call | flops 268435456 | bytes 786432 | tf_op jit(solution)/shard_map/pallas_call | solution.py:385
  18.9 1.7 %collective-permute-start.4 = (bf16[128,256]{1,0:T(8,128)(2,1)S(1)}, bf16[128,256]{1,0:T(8,128)(2,1)S(1)}, u32[]{:S(2)}, u32[]{:S(2)}) collective-permute-start(bf16[128,256]{1,0:T(8,128)(2,1)S(1)} %get-tuple-element.26), channel_id=1, source_target_pairs={{0,4},{2,6},{4,0},{6,2},{1,5},{3,7},{5,1},{7,3},{8,12},{10,14},{12... | collective-permute-start | bytes 196616 | tf_op jit(solution)/shard_map/ppermute | solution.py:402
  20.6 1.1 %collective-permute-start.5 = (bf16[128,256]{1,0:T(8,128)(2,1)S(1)}, bf16[128,256]{1,0:T(8,128)(2,1)S(1)}, u32[]{:S(2)}, u32[]{:S(2)}) collective-permute-start(bf16[128,256]{1,0:T(8,128)(2,1)S(1)} %get-tuple-element.27), channel_id=1, source_target_pairs={{0,6},{2,4},{4,2},{6,0},{1,7},{3,5},{5,3},{7,1},{8,14},{10,12},{12... | collective-permute-start | bytes 196616 | tf_op jit(solution)/shard_map/ppermute | solution.py:402
  21.7 0.8 %collective-permute-start.6 = (bf16[128,256]{1,0:T(8,128)(2,1)S(1)}, bf16[128,256]{1,0:T(8,128)(2,1)S(1)}, u32[]{:S(2)}, u32[]{:S(2)}) collective-permute-start(bf16[128,256]{1,0:T(8,128)(2,1)S(1)} %get-tuple-element.28), channel_id=1, source_target_pairs={{0,2},{2,0},{4,6},{6,4},{1,3},{3,1},{5,7},{7,5},{8,10},{10,8},{12,... | collective-permute-start | bytes 196616 | tf_op jit(solution)/shard_map/ppermute | solution.py:402
  22.5 1.0 %shard_map.89 = (bf16[128,512]{1,0:T(8,128)(2,1)}, bf16[128,256]{1,0:T(8,128)(2,1)S(1)}) custom-call(bf16[128,512]{1,0:T(8,128)(2,1)S(1)} %copy-done.1, bf16[128,512]{1,0:T(8,128)(2,1)S(1)} %copy-done.2, bf16[512,512]{1,0:T(8,128)(2,1)S(1)} %get-tuple-element.21.low_ref, bf16[512,512]{1,0:T(8,128)(2,1)S(1)} %get-tuple-element.22.dscore_ref, ...), custom_call_target="tpu_custom_call" | custom-call | flops 67108864 | bytes 917504 | tf_op jit(solution)/shard_map/pallas_call | solution.py:394
  23.5 1.4 %collective-permute-done.4.refs_1_ = bf16[128,256]{1,0:T(8,128)(2,1)S(1)} collective-permute-done((bf16[128,256]{1,0:T(8,128)(2,1)S(1)}, bf16[128,256]{1,0:T(8,128)(2,1)S(1)}, u32[]{:S(2)}, u32[]{:S(2)}) %collective-permute-start.4) | collective-permute-done | bytes 65568 | tf_op jit(solution)/shard_map/ppermute | solution.py:402
  24.9 1.7 %collective-permute-done.5.refs_2_ = bf16[128,256]{1,0:T(8,128)(2,1)S(1)} collective-permute-done((bf16[128,256]{1,0:T(8,128)(2,1)S(1)}, bf16[128,256]{1,0:T(8,128)(2,1)S(1)}, u32[]{:S(2)}, u32[]{:S(2)}) %collective-permute-start.5) | collective-permute-done | bytes 65568 | tf_op jit(solution)/shard_map/ppermute | solution.py:402
  26.6 0.0 collective-permute-done.6.refs_3_
  26.6 0.7 %shard_map.90 = (bf16[96,256]{1,0:T(8,128)(2,1)S(1)}, f32[16,3200]{1,0:T(8,128)S(1)}, bf16[16,3200]{1,0:T(8,128)(2,1)S(1)}) custom-call(s32[1,8]{1,0:T(1,128)S(1)} %bitcast.6, bf16[3200,256]{1,0:T(8,128)(2,1)S(1)} %copy-done, bf16[128,256]{1,0:T(8,128)(2,1)S(1)} %get-tuple-element.25.refs_0_, bf16[128,256]{1,0:T(8,128)(2,1)S(1)} %collective-permute-done.4.refs_1_, ...), custom_call_target="tpu_custom_call" | custom-call | flops 52428800 | bytes 1945600 | tf_op jit(solution)/shard_map/pallas_call | solution.py:407
  27.4 0.1 collective-permute-start.8
  27.4 0.6 %shard_map.91 = (f32[48,3200]{1,0:T(8,128)S(1)}, bf16[48,3200]{1,0:T(8,128)(2,1)S(1)}) custom-call(bf16[96,256]{1,0:T(8,128)(2,1)S(1)} %get-tuple-element.29.rest_ref, bf16[3200,256]{1,0:T(8,128)(2,1)S(1)} %copy-done), custom_call_target="tpu_custom_call" | custom-call | flops 157286400 | bytes 2560000 | tf_op jit(solution)/shard_map/pallas_call | solution.py:417
  28.1 0.6 %collective-permute-start.7 = (bf16[48,3200]{1,0:T(8,128)(2,1)S(1)}, bf16[48,3200]{1,0:T(8,128)(2,1)S(1)}, u32[]{:S(2)}, u32[]{:S(2)}) collective-permute-start(bf16[48,3200]{1,0:T(8,128)(2,1)S(1)} %get-tuple-element.31), channel_id=1, source_target_pairs={{0,8},{1,9},{8,0},{9,1},{16,24},{17,25},{24,16},{25,17},{2,10},{3,... | collective-permute-start | bytes 921608 | tf_op jit(solution)/shard_map/ppermute | solution.py:425
  28.6 0.1 collective-permute-done.8.other_ref
  28.8 2.5 %collective-permute-start.9 = (bf16[16,3200]{1,0:T(8,128)(2,1)S(1)}, bf16[16,3200]{1,0:T(8,128)(2,1)S(1)}, u32[]{:S(2)}, u32[]{:S(2)}) collective-permute-start(bf16[16,3200]{1,0:T(8,128)(2,1)S(1)} %shard_map.93), channel_id=1, source_target_pairs={{0,17},{1,16},{8,25},{9,24},{16,1},{17,0},{24,9},{25,8},{2,19},{3,... | collective-permute-start | bytes 307208 | tf_op jit(solution)/shard_map/ppermute | solution.py:428
  31.3 0.0 collective-permute-done.7.other_ref
  31.3 0.1 shard_map.92
  31.4 0.6 %collective-permute-start.10 = (bf16[16,3200]{1,0:T(8,128)(2,1)S(1)}, bf16[16,3200]{1,0:T(8,128)(2,1)S(1)}, u32[]{:S(2)}, u32[]{:S(2)}) collective-permute-start(bf16[16,3200]{1,0:T(8,128)(2,1)S(1)} %get-tuple-element.36), channel_id=1, source_target_pairs={{0,16},{1,17},{8,24},{9,25},{16,0},{17,1},{24,8},{25,9},{2,18},{3,... | collective-permute-start | bytes 307208 | tf_op jit(solution)/shard_map/ppermute | solution.py:438
  31.9 1.1 %collective-permute-start.11 = (bf16[16,3200]{1,0:T(8,128)(2,1)S(1)}, bf16[16,3200]{1,0:T(8,128)(2,1)S(1)}, u32[]{:S(2)}, u32[]{:S(2)}) collective-permute-start(bf16[16,3200]{1,0:T(8,128)(2,1)S(1)} %get-tuple-element.37), channel_id=1, source_target_pairs={{0,1},{1,0},{8,9},{9,8},{16,17},{17,16},{24,25},{25,24},{2,3},{3,2... | collective-permute-start | bytes 307208 | tf_op jit(solution)/shard_map/ppermute | solution.py:438
  33.0 2.4 %collective-permute-done.9.refs_0_ = bf16[16,3200]{1,0:T(8,128)(2,1)S(1)} collective-permute-done((bf16[16,3200]{1,0:T(8,128)(2,1)S(1)}, bf16[16,3200]{1,0:T(8,128)(2,1)S(1)}, u32[]{:S(2)}, u32[]{:S(2)}) %collective-permute-start.9) | collective-permute-done | bytes 102432 | tf_op jit(solution)/shard_map/ppermute | solution.py:428
  35.4 1.5 %collective-permute-done.10.refs_1_ = bf16[16,3200]{1,0:T(8,128)(2,1)S(1)} collective-permute-done((bf16[16,3200]{1,0:T(8,128)(2,1)S(1)}, bf16[16,3200]{1,0:T(8,128)(2,1)S(1)}, u32[]{:S(2)}, u32[]{:S(2)}) %collective-permute-start.10) | collective-permute-done | bytes 102432 | tf_op jit(solution)/shard_map/ppermute | solution.py:438
  36.9 0.1 collective-permute-done.11.refs_2_
  37.0 0.2 shard_map.94.refs_0_
  37.2 2.4 %collective-permute-start.16 = (bf16[16,3200]{1,0:T(8,128)(2,1)S(1)}, bf16[16,3200]{1,0:T(8,128)(2,1)S(1)}, u32[]{:S(2)}, u32[]{:S(2)}) collective-permute-start(bf16[16,3200]{1,0:T(8,128)(2,1)S(1)} %shard_map.94.refs_0_), channel_id=1, source_target_pairs={{0,17},{1,16},{8,25},{9,24},{16,1},{17,0},{24,9},{25,8},{2,19},{3,... | collective-permute-start | bytes 307208 | tf_op jit(solution)/shard_map/ppermute | solution.py:449
  39.6 0.7 %collective-permute-start.14 = (bf16[16,3200]{1,0:T(8,128)(2,1)S(1)}, bf16[16,3200]{1,0:T(8,128)(2,1)S(1)}, u32[]{:S(2)}, u32[]{:S(2)}) collective-permute-start(bf16[16,3200]{1,0:T(8,128)(2,1)S(1)} %shard_map.94.refs_0_), channel_id=1, source_target_pairs={{0,16},{1,17},{8,24},{9,25},{16,0},{17,1},{24,8},{25,9},{2,18},{3,... | collective-permute-start | bytes 307208 | tf_op jit(solution)/shard_map/ppermute | solution.py:449
  40.2 0.5 %collective-permute-start.12 = (bf16[16,3200]{1,0:T(8,128)(2,1)S(1)}, bf16[16,3200]{1,0:T(8,128)(2,1)S(1)}, u32[]{:S(2)}, u32[]{:S(2)}) collective-permute-start(bf16[16,3200]{1,0:T(8,128)(2,1)S(1)} %shard_map.94.refs_0_), channel_id=1, source_target_pairs={{0,1},{1,0},{8,9},{9,8},{16,17},{17,16},{24,25},{25,24},{2,3},{3,2... | collective-permute-start | bytes 307208 | tf_op jit(solution)/shard_map/ppermute | solution.py:449
  40.7 0.0 collective-permute-start.17
  40.7 2.9 %collective-permute-done.16.refs_3_ = bf16[16,3200]{1,0:T(8,128)(2,1)S(1)} collective-permute-done((bf16[16,3200]{1,0:T(8,128)(2,1)S(1)}, bf16[16,3200]{1,0:T(8,128)(2,1)S(1)}, u32[]{:S(2)}, u32[]{:S(2)}) %collective-permute-start.16) | collective-permute-done | bytes 102432 | tf_op jit(solution)/shard_map/ppermute | solution.py:449
  43.6 1.4 %collective-permute-done.14.refs_2_ = bf16[16,3200]{1,0:T(8,128)(2,1)S(1)} collective-permute-done((bf16[16,3200]{1,0:T(8,128)(2,1)S(1)}, bf16[16,3200]{1,0:T(8,128)(2,1)S(1)}, u32[]{:S(2)}, u32[]{:S(2)}) %collective-permute-start.14) | collective-permute-done | bytes 102432 | tf_op jit(solution)/shard_map/ppermute | solution.py:449
  45.0 0.2 collective-permute-done.12.refs_1_
  45.2 0.3 collective-permute-start.13
  45.5 0.0 collective-permute-done.17.refs_4_
  45.5 0.0 collective-permute-done.18.refs_5_
  45.5 0.9 %shard_map.95.refs_2_ = bf16[128,3200]{1,0:T(8,128)(2,1)} custom-call(bf16[16,3200]{1,0:T(8,128)(2,1)S(1)} %shard_map.94.refs_0_, bf16[16,3200]{1,0:T(8,128)(2,1)S(1)} %collective-permute-done.12.refs_1_, bf16[16,3200]{1,0:T(8,128)(2,1)S(1)} %collective-permute-done.14.refs_2_, bf16[16,3200]{1,0:T(8,128)(2,1)S(1)} %collective-permute-done.16.refs_3_, ...), custom_call_target="tpu_custom_call" | custom-call | bytes 1228800 | tf_op jit(solution)/shard_map/pallas_call | solution.py:456
  46.4 0.0 collective-permute-done.15.refs_1_
  46.4 0.1 collective-permute-done.13.refs_0_
  46.5 0.7 %shard_map.96 = bf16[128,3200]{1,0:T(8,128)(2,1)} custom-call(bf16[16,3200]{1,0:T(8,128)(2,1)S(1)} %collective-permute-done.13.refs_0_, bf16[16,3200]{1,0:T(8,128)(2,1)S(1)} %collective-permute-done.15.refs_1_, bf16[128,3200]{1,0:T(8,128)(2,1)} %shard_map.95.refs_2_), custom_call_target="tpu_custom_call", output_to_operand_aliasing={{}: (2, {})} | custom-call | bytes 409600 | tf_op jit(solution)/shard_map/pallas_call | solution.py:456
  (13 shorter events, 0.1 us)
Async XLA Ops:
  0.6 16.9 %copy-start.2 = (bf16[128,512]{1,0:T(8,128)(2,1)S(1)}, bf16[128,512]{1,0:T(8,128)(2,1)}, u32[]{:S(2)}) copy-start(bf16[128,512]{1,0:T(8,128)(2,1)} %g_ref.3) | copy-start | bytes 393220
  0.6 16.9 %copy-start.1 = (bf16[128,512]{1,0:T(8,128)(2,1)S(1)}, bf16[128,512]{1,0:T(8,128)(2,1)}, u32[]{:S(2)}) copy-start(bf16[128,512]{1,0:T(8,128)(2,1)} %q_ref.3) | copy-start | bytes 393220
  0.7 8.5 %collective-permute-start = (bf16[128,256]{1,0:T(8,128)(2,1)}, bf16[128,256]{1,0:T(8,128)(2,1)S(1)}, u32[]{:S(2)}, u32[]{:S(2)}) collective-permute-start(bf16[128,256]{1,0:T(8,128)(2,1)} %text_ref.1), channel_id=1, source_target_pairs={{0,6},{2,4},{4,0},{6,2},{1,7},{3,5},{5,1},{7,3},{8,14},{10,12},{12... | collective-permute-start | bytes 196616 | tf_op jit(solution)/shard_map/ppermute | solution.py:340
  5.8 0.7 %copy-start.3 = (f32[3200]{0:T(1024)S(1)}, f32[3200]{0:T(1024)}, u32[]{:S(2)}) copy-start(f32[3200]{0:T(1024)} %param.8) | copy-start | bytes 38404
  6.5 2.7 %copy-start.4 = (s32[8]{0:T(128)S(1)}, s32[8]{0:T(128)}, u32[]{:S(2)}) copy-start(s32[8]{0:T(128)} %param.10) | copy-start | bytes 100
  6.5 11.0 %copy-start.5 = (bf16[128,256]{1,0:T(8,128)(2,1)S(1)}, bf16[128,256]{1,0:T(8,128)(2,1)}, u32[]{:S(2)}) copy-start(bf16[128,256]{1,0:T(8,128)(2,1)} %text_ref.1) | copy-start | bytes 196612
  9.1 17.6 %copy-start = (bf16[3200,256]{1,0:T(8,128)(2,1)S(1)}, bf16[3200,256]{1,0:T(8,128)(2,1)}, u32[]{:S(2)}) copy-start(bf16[3200,256]{1,0:T(8,128)(2,1)} %proj_ref.3) | copy-start | bytes 4915204
  9.1 6.9 %collective-permute-start.1 = (bf16[128,256]{1,0:T(8,128)(2,1)S(1)}, bf16[128,256]{1,0:T(8,128)(2,1)S(1)}, u32[]{:S(2)}, u32[]{:S(2)}) collective-permute-start(bf16[128,256]{1,0:T(8,128)(2,1)S(1)} %get-tuple-element.20.image_ref), channel_id=1, source_target_pairs={{6,0},{4,2},{0,4},{2,6},{7,1},{5,3},{1,5},{3,7},{14,8},{12,10},{8,... | collective-permute-start | bytes 196616 | tf_op jit(solution)/shard_map/ppermute | solution.py:361
  9.4 6.6 %collective-permute-start.3 = (bf16[128,256]{1,0:T(8,128)(2,1)S(1)}, bf16[128,256]{1,0:T(8,128)(2,1)S(1)}, u32[]{:S(2)}, u32[]{:S(2)}) collective-permute-start(bf16[128,256]{1,0:T(8,128)(2,1)S(1)} %shard_map.87.own_ref), channel_id=1, source_target_pairs={{0,6},{2,0},{4,2},{6,4},{1,7},{3,1},{5,3},{7,5},{8,14},{10,8},{12,... | collective-permute-start | bytes 196616 | tf_op jit(solution)/shard_map/ppermute | solution.py:370
  13.2 4.3 %collective-permute-start.2 = (bf16[128,256]{1,0:T(8,128)(2,1)S(1)}, bf16[128,256]{1,0:T(8,128)(2,1)S(1)}, u32[]{:S(2)}, u32[]{:S(2)}) collective-permute-start(bf16[128,256]{1,0:T(8,128)(2,1)S(1)} %shard_map.87.own_ref), channel_id=1, source_target_pairs={{0,4},{2,0},{4,6},{6,2},{1,5},{3,1},{5,7},{7,3},{8,12},{10,8},{12,... | collective-permute-start | bytes 196616 | tf_op jit(solution)/shard_map/ppermute | solution.py:370
  18.9 6.0 %collective-permute-start.4 = (bf16[128,256]{1,0:T(8,128)(2,1)S(1)}, bf16[128,256]{1,0:T(8,128)(2,1)S(1)}, u32[]{:S(2)}, u32[]{:S(2)}) collective-permute-start(bf16[128,256]{1,0:T(8,128)(2,1)S(1)} %get-tuple-element.26), channel_id=1, source_target_pairs={{0,4},{2,6},{4,0},{6,2},{1,5},{3,7},{5,1},{7,3},{8,12},{10,14},{12... | collective-permute-start | bytes 196616 | tf_op jit(solution)/shard_map/ppermute | solution.py:402
  20.6 6.1 %collective-permute-start.5 = (bf16[128,256]{1,0:T(8,128)(2,1)S(1)}, bf16[128,256]{1,0:T(8,128)(2,1)S(1)}, u32[]{:S(2)}, u32[]{:S(2)}) collective-permute-start(bf16[128,256]{1,0:T(8,128)(2,1)S(1)} %get-tuple-element.27), channel_id=1, source_target_pairs={{0,6},{2,4},{4,2},{6,0},{1,7},{3,5},{5,3},{7,1},{8,14},{10,12},{12... | collective-permute-start | bytes 196616 | tf_op jit(solution)/shard_map/ppermute | solution.py:402
  21.7 5.0 %collective-permute-start.6 = (bf16[128,256]{1,0:T(8,128)(2,1)S(1)}, bf16[128,256]{1,0:T(8,128)(2,1)S(1)}, u32[]{:S(2)}, u32[]{:S(2)}) collective-permute-start(bf16[128,256]{1,0:T(8,128)(2,1)S(1)} %get-tuple-element.28), channel_id=1, source_target_pairs={{0,2},{2,0},{4,6},{6,4},{1,3},{3,1},{5,7},{7,5},{8,10},{10,8},{12,... | collective-permute-start | bytes 196616 | tf_op jit(solution)/shard_map/ppermute | solution.py:402
  27.4 1.4 %collective-permute-start.8 = (bf16[16,3200]{1,0:T(8,128)(2,1)S(1)}, bf16[16,3200]{1,0:T(8,128)(2,1)S(1)}, u32[]{:S(2)}, u32[]{:S(2)}) collective-permute-start(bf16[16,3200]{1,0:T(8,128)(2,1)S(1)} %get-tuple-element.35), channel_id=1, source_target_pairs={{0,8},{1,9},{8,0},{9,1},{16,24},{17,25},{24,16},{25,17},{2,10},{3,... | collective-permute-start | bytes 307208 | tf_op jit(solution)/shard_map/ppermute | solution.py:415
  28.1 3.2 %collective-permute-start.7 = (bf16[48,3200]{1,0:T(8,128)(2,1)S(1)}, bf16[48,3200]{1,0:T(8,128)(2,1)S(1)}, u32[]{:S(2)}, u32[]{:S(2)}) collective-permute-start(bf16[48,3200]{1,0:T(8,128)(2,1)S(1)} %get-tuple-element.31), channel_id=1, source_target_pairs={{0,8},{1,9},{8,0},{9,1},{16,24},{17,25},{24,16},{25,17},{2,10},{3,... | collective-permute-start | bytes 921608 | tf_op jit(solution)/shard_map/ppermute | solution.py:425
  28.8 6.7 %collective-permute-start.9 = (bf16[16,3200]{1,0:T(8,128)(2,1)S(1)}, bf16[16,3200]{1,0:T(8,128)(2,1)S(1)}, u32[]{:S(2)}, u32[]{:S(2)}) collective-permute-start(bf16[16,3200]{1,0:T(8,128)(2,1)S(1)} %shard_map.93), channel_id=1, source_target_pairs={{0,17},{1,16},{8,25},{9,24},{16,1},{17,0},{24,9},{25,8},{2,19},{3,... | collective-permute-start | bytes 307208 | tf_op jit(solution)/shard_map/ppermute | solution.py:428
  31.4 5.6 %collective-permute-start.10 = (bf16[16,3200]{1,0:T(8,128)(2,1)S(1)}, bf16[16,3200]{1,0:T(8,128)(2,1)S(1)}, u32[]{:S(2)}, u32[]{:S(2)}) collective-permute-start(bf16[16,3200]{1,0:T(8,128)(2,1)S(1)} %get-tuple-element.36), channel_id=1, source_target_pairs={{0,16},{1,17},{8,24},{9,25},{16,0},{17,1},{24,8},{25,9},{2,18},{3,... | collective-permute-start | bytes 307208 | tf_op jit(solution)/shard_map/ppermute | solution.py:438
  31.9 5.0 %collective-permute-start.11 = (bf16[16,3200]{1,0:T(8,128)(2,1)S(1)}, bf16[16,3200]{1,0:T(8,128)(2,1)S(1)}, u32[]{:S(2)}, u32[]{:S(2)}) collective-permute-start(bf16[16,3200]{1,0:T(8,128)(2,1)S(1)} %get-tuple-element.37), channel_id=1, source_target_pairs={{0,1},{1,0},{8,9},{9,8},{16,17},{17,16},{24,25},{25,24},{2,3},{3,2... | collective-permute-start | bytes 307208 | tf_op jit(solution)/shard_map/ppermute | solution.py:438
  37.2 6.5 %collective-permute-start.16 = (bf16[16,3200]{1,0:T(8,128)(2,1)S(1)}, bf16[16,3200]{1,0:T(8,128)(2,1)S(1)}, u32[]{:S(2)}, u32[]{:S(2)}) collective-permute-start(bf16[16,3200]{1,0:T(8,128)(2,1)S(1)} %shard_map.94.refs_0_), channel_id=1, source_target_pairs={{0,17},{1,16},{8,25},{9,24},{16,1},{17,0},{24,9},{25,8},{2,19},{3,... | collective-permute-start | bytes 307208 | tf_op jit(solution)/shard_map/ppermute | solution.py:449
  39.6 5.4 %collective-permute-start.14 = (bf16[16,3200]{1,0:T(8,128)(2,1)S(1)}, bf16[16,3200]{1,0:T(8,128)(2,1)S(1)}, u32[]{:S(2)}, u32[]{:S(2)}) collective-permute-start(bf16[16,3200]{1,0:T(8,128)(2,1)S(1)} %shard_map.94.refs_0_), channel_id=1, source_target_pairs={{0,16},{1,17},{8,24},{9,25},{16,0},{17,1},{24,8},{25,9},{2,18},{3,... | collective-permute-start | bytes 307208 | tf_op jit(solution)/shard_map/ppermute | solution.py:449
  40.2 4.9 %collective-permute-start.12 = (bf16[16,3200]{1,0:T(8,128)(2,1)S(1)}, bf16[16,3200]{1,0:T(8,128)(2,1)S(1)}, u32[]{:S(2)}, u32[]{:S(2)}) collective-permute-start(bf16[16,3200]{1,0:T(8,128)(2,1)S(1)} %shard_map.94.refs_0_), channel_id=1, source_target_pairs={{0,1},{1,0},{8,9},{9,8},{16,17},{17,16},{24,25},{25,24},{2,3},{3,2... | collective-permute-start | bytes 307208 | tf_op jit(solution)/shard_map/ppermute | solution.py:449
  40.7 4.8 %collective-permute-start.17 = (bf16[16,3200]{1,0:T(8,128)(2,1)S(1)}, bf16[16,3200]{1,0:T(8,128)(2,1)S(1)}, u32[]{:S(2)}, u32[]{:S(2)}) collective-permute-start(bf16[16,3200]{1,0:T(8,128)(2,1)S(1)} %shard_map.94.refs_0_), channel_id=1, source_target_pairs={{0,8},{1,9},{8,0},{9,1},{16,24},{17,25},{24,16},{25,17},{2,10},{3,... | collective-permute-start | bytes 307208 | tf_op jit(solution)/shard_map/ppermute | solution.py:450
  43.6 1.9 %collective-permute-start.18 = (bf16[16,3200]{1,0:T(8,128)(2,1)S(1)}, bf16[16,3200]{1,0:T(8,128)(2,1)S(1)}, u32[]{:S(2)}, u32[]{:S(2)}) collective-permute-start(bf16[16,3200]{1,0:T(8,128)(2,1)S(1)} %collective-permute-done.16.refs_3_), channel_id=1, source_target_pairs={{0,8},{1,9},{8,0},{9,1},{16,24},{17,25},{24,16},{25,17},{2,10},{3,... | collective-permute-start | bytes 307208 | tf_op jit(solution)/shard_map/ppermute | solution.py:450
  45.0 1.4 %collective-permute-start.15 = (bf16[16,3200]{1,0:T(8,128)(2,1)S(1)}, bf16[16,3200]{1,0:T(8,128)(2,1)S(1)}, u32[]{:S(2)}, u32[]{:S(2)}) collective-permute-start(bf16[16,3200]{1,0:T(8,128)(2,1)S(1)} %collective-permute-done.14.refs_2_), channel_id=1, source_target_pairs={{0,8},{1,9},{8,0},{9,1},{16,24},{17,25},{24,16},{25,17},{2,10},{3,... | collective-permute-start | bytes 307208 | tf_op jit(solution)/shard_map/ppermute | solution.py:450
  45.2 1.3 %collective-permute-start.13 = (bf16[16,3200]{1,0:T(8,128)(2,1)S(1)}, bf16[16,3200]{1,0:T(8,128)(2,1)S(1)}, u32[]{:S(2)}, u32[]{:S(2)}) collective-permute-start(bf16[16,3200]{1,0:T(8,128)(2,1)S(1)} %collective-permute-done.12.refs_1_), channel_id=1, source_target_pairs={{0,8},{1,9},{8,0},{9,1},{16,24},{17,25},{24,16},{25,17},{2,10},{3,... | collective-permute-start | bytes 307208 | tf_op jit(solution)/shard_map/ppermute | solution.py:450

commit v14 on v13

--- a/solution.py
+++ b/solution.py
@@ -93,14 +93,12 @@
     for n, (low, high) in enumerate(chunks):
         vis_copies.append(pltpu.make_async_copy(vis_hbm.at[:, low:high], vis.at[:, low:high], vis_sems.at[n]))
         proj_copies.append(pltpu.make_async_copy(proj_hbm.at[low:high, :], proj.at[low:high, :], proj_sems.at[n]))
-    for copy in vis_copies + proj_copies[:2]:
+    for copy in vis_copies + proj_copies:
         copy.start()
     gain_copy.wait()
     squares = jnp.zeros((rows, HD), jnp.float32)
     for n, (low, high) in enumerate(chunks):
         vis_copies[n].wait()
-        for copy in proj_copies[n + 2 : n + 3]:
-            copy.start()
         for c in range(low, high, HD):
             wide = vis[:, c : c + HD].astype(jnp.float32)
             squares += wide * wide

time: 47.4 us -> 47.3 us (level)
  no operation moved by 1% of the time
where the time goes in v14:
time: 47.3 us; the launch traced here: 47.1 us
  starting transfers between devices  21.2 us (45%)
  waiting for transfers between devices  16 us (34%)
  Pallas kernels  8.32 us (18%)
  between operations  0.76 us (2%)
  local copies, waits for them, and re-layouts  0.74 us (2%)
    ppermute x1, starting transfers between devices, on_device(): text = lax.ppermute(text_kv, 'seq', list(enumerate(owners)))  5.1 us
    ppermute x3, waiting for transfers between devices, on_device(): mines[d] = lax.ppermute(mine, names, far_pairs(d))  4.41 us
    ppermute x2, starting transfers between devices, on_device(): blocks = [lax.ppermute(block, 'seq', pairs) for pairs in forth]  3.85 us
    ppermute x3, starting transfers between devices, on_device(): lax.ppermute(g, 'seq', pairs)  3.55 us
    ppermute x3, starting transfers between devices, on_device(): mines[d] = lax.ppermute(mine, names, far_pairs(d))  3.55 us
    ppermute x3, waiting for transfers between devices, on_device(): lax.ppermute(g, 'seq', pairs)  3.18 us
    ppermute x1, waiting for transfers between devices, on_device(): raw = lax.ppermute(image_kv, 'seq', home)  2.75 us
    ppermute x1, starting transfers between devices, on_device(): shares = [lax.ppermute(far, names, far_pairs(count - 1))]  2.51 us
  transfers between devices with their start and end apart: 19, of which 12 were waited for; matrix products, arithmetic and copies ran while one was open for 0% of the time, Pallas kernels for 11%

profile of v14, /device:TPU:0, one launch (start us, length us, event | category | flops | bytes accessed | tf_op | source)
XLA Modules:
  0.0 47.1 jit_solution(7554485304868346752)
XLA Ops:
  0.7 5.1 %collective-permute-start = (bf16[128,256]{1,0:T(8,128)(2,1)}, bf16[128,256]{1,0:T(8,128)(2,1)S(1)}, u32[]{:S(2)}, u32[]{:S(2)}) collective-permute-start(bf16[128,256]{1,0:T(8,128)(2,1)} %text_ref.1), channel_id=1, source_target_pairs={{0,6},{2,4},{4,0},{6,2},{1,7},{3,5},{5,1},{7,3},{8,14},{10,12},{12... | collective-permute-start | bytes 196616 | tf_op jit(solution)/shard_map/ppermute | solution.py:338
  5.8 0.7 %copy-done.3 = f32[3200]{0:T(1024)S(1)} copy-done((f32[3200]{0:T(1024)S(1)}, f32[3200]{0:T(1024)}, u32[]{:S(2)}) %copy-start.3) | copy-done | bytes 12824
  6.5 2.5 %shard_map.86 = (bf16[128,256]{1,0:T(8,128)(2,1)S(1)}, bf16[16,3200]{1,0:T(8,128)(2,1)S(1)}) custom-call(bf16[128,3200]{1,0:T(8,128)(2,1)} %vis_hbm.1, f32[25,128]{1,0:T(8,128)S(1)} %bitcast.2, bf16[3200,256]{1,0:T(8,128)(2,1)} %proj_ref.3), custom_call_target="tpu_custom_call" | custom-call | flops 209715200 | bytes 2457600 | tf_op jit(solution)/shard_map/pallas_call | solution.py:341
  9.0 0.0 copy-start
  9.0 0.1 collective-permute-start.1
  9.1 0.0 collective-permute-done.text_ref
  9.1 0.2 shard_map.87.own_ref
  9.3 3.8 %collective-permute-start.3 = (bf16[128,256]{1,0:T(8,128)(2,1)S(1)}, bf16[128,256]{1,0:T(8,128)(2,1)S(1)}, u32[]{:S(2)}, u32[]{:S(2)}) collective-permute-start(bf16[128,256]{1,0:T(8,128)(2,1)S(1)} %shard_map.87.own_ref), channel_id=1, source_target_pairs={{0,6},{2,0},{4,2},{6,4},{1,7},{3,1},{5,3},{7,5},{8,14},{10,8},{12,... | collective-permute-start | bytes 196616 | tf_op jit(solution)/shard_map/ppermute | solution.py:368
  13.2 0.0 collective-permute-start.2
  13.2 2.8 %collective-permute-done.1.raw_ref = bf16[128,256]{1,0:T(8,128)(2,1)S(1)} collective-permute-done((bf16[128,256]{1,0:T(8,128)(2,1)S(1)}, bf16[128,256]{1,0:T(8,128)(2,1)S(1)}, u32[]{:S(2)}, u32[]{:S(2)}) %collective-permute-start.1) | collective-permute-done | bytes 65568 | tf_op jit(solution)/shard_map/ppermute | solution.py:359
  15.9 0.0 collective-permute-done.3.refs_1_
  15.9 1.5 %collective-permute-done.2.refs_0_ = bf16[128,256]{1,0:T(8,128)(2,1)S(1)} collective-permute-done((bf16[128,256]{1,0:T(8,128)(2,1)S(1)}, bf16[128,256]{1,0:T(8,128)(2,1)S(1)}, u32[]{:S(2)}, u32[]{:S(2)}) %collective-permute-start.2) | collective-permute-done | bytes 65568 | tf_op jit(solution)/shard_map/ppermute | solution.py:368
  17.4 1.4 %shard_map.88 = (bf16[512,512]{1,0:T(8,128)(2,1)S(1)}, bf16[512,512]{1,0:T(8,128)(2,1)S(1)}, bf16[512,128]{1,0:T(8,128)(2,1)S(1)}, bf16[128,256]{1,0:T(8,128)(2,...) custom-call(s32[1,8]{1,0:T(1,128)S(1)} %bitcast.5, bf16[128,512]{1,0:T(8,128)(2,1)S(1)} %copy-done.1, ...), custom_call_target="tpu_custom_call" | custom-call | flops 268435456 | bytes 786432 | tf_op jit(solution)/shard_map/pallas_call | solution.py:383
  18.8 1.7 %collective-permute-start.4 = (bf16[128,256]{1,0:T(8,128)(2,1)S(1)}, bf16[128,256]{1,0:T(8,128)(2,1)S(1)}, u32[]{:S(2)}, u32[]{:S(2)}) collective-permute-start(bf16[128,256]{1,0:T(8,128)(2,1)S(1)} %get-tuple-element.26), channel_id=1, source_target_pairs={{0,4},{2,6},{4,0},{6,2},{1,5},{3,7},{5,1},{7,3},{8,12},{10,14},{12... | collective-permute-start | bytes 196616 | tf_op jit(solution)/shard_map/ppermute | solution.py:400
  20.5 1.1 %collective-permute-start.5 = (bf16[128,256]{1,0:T(8,128)(2,1)S(1)}, bf16[128,256]{1,0:T(8,128)(2,1)S(1)}, u32[]{:S(2)}, u32[]{:S(2)}) collective-permute-start(bf16[128,256]{1,0:T(8,128)(2,1)S(1)} %get-tuple-element.27), channel_id=1, source_target_pairs={{0,6},{2,4},{4,2},{6,0},{1,7},{3,5},{5,3},{7,1},{8,14},{10,12},{12... | collective-permute-start | bytes 196616 | tf_op jit(solution)/shard_map/ppermute | solution.py:400
  21.6 0.8 %collective-permute-start.6 = (bf16[128,256]{1,0:T(8,128)(2,1)S(1)}, bf16[128,256]{1,0:T(8,128)(2,1)S(1)}, u32[]{:S(2)}, u32[]{:S(2)}) collective-permute-start(bf16[128,256]{1,0:T(8,128)(2,1)S(1)} %get-tuple-element.28), channel_id=1, source_target_pairs={{0,2},{2,0},{4,6},{6,4},{1,3},{3,1},{5,7},{7,5},{8,10},{10,8},{12,... | collective-permute-start | bytes 196616 | tf_op jit(solution)/shard_map/ppermute | solution.py:400
  22.4 1.0 %shard_map.89 = (bf16[128,512]{1,0:T(8,128)(2,1)}, bf16[128,256]{1,0:T(8,128)(2,1)S(1)}) custom-call(bf16[128,512]{1,0:T(8,128)(2,1)S(1)} %copy-done.1, bf16[128,512]{1,0:T(8,128)(2,1)S(1)} %copy-done.2, bf16[512,512]{1,0:T(8,128)(2,1)S(1)} %get-tuple-element.21.low_ref, bf16[512,512]{1,0:T(8,128)(2,1)S(1)} %get-tuple-element.22.dscore_ref, ...), custom_call_target="tpu_custom_call" | custom-call | flops 67108864 | bytes 917504 | tf_op jit(solution)/shard_map/pallas_call | solution.py:392
  23.4 1.4 %collective-permute-done.4.refs_1_ = bf16[128,256]{1,0:T(8,128)(2,1)S(1)} collective-permute-done((bf16[128,256]{1,0:T(8,128)(2,1)S(1)}, bf16[128,256]{1,0:T(8,128)(2,1)S(1)}, u32[]{:S(2)}, u32[]{:S(2)}) %collective-permute-start.4) | collective-permute-done | bytes 65568 | tf_op jit(solution)/shard_map/ppermute | solution.py:400
  24.8 1.7 %collective-permute-done.5.refs_2_ = bf16[128,256]{1,0:T(8,128)(2,1)S(1)} collective-permute-done((bf16[128,256]{1,0:T(8,128)(2,1)S(1)}, bf16[128,256]{1,0:T(8,128)(2,1)S(1)}, u32[]{:S(2)}, u32[]{:S(2)}) %collective-permute-start.5) | collective-permute-done | bytes 65568 | tf_op jit(solution)/shard_map/ppermute | solution.py:400
  26.6 0.0 collective-permute-done.6.refs_3_
  26.6 0.7 %shard_map.90 = (bf16[96,256]{1,0:T(8,128)(2,1)S(1)}, f32[16,3200]{1,0:T(8,128)S(1)}, bf16[16,3200]{1,0:T(8,128)(2,1)S(1)}) custom-call(s32[1,8]{1,0:T(1,128)S(1)} %bitcast.6, bf16[3200,256]{1,0:T(8,128)(2,1)S(1)} %copy-done, bf16[128,256]{1,0:T(8,128)(2,1)S(1)} %get-tuple-element.25.refs_0_, bf16[128,256]{1,0:T(8,128)(2,1)S(1)} %collective-permute-done.4.refs_1_, ...), custom_call_target="tpu_custom_call" | custom-call | flops 52428800 | bytes 1945600 | tf_op jit(solution)/shard_map/pallas_call | solution.py:405
  27.3 0.1 collective-permute-start.8
  27.4 0.6 %shard_map.91 = (f32[48,3200]{1,0:T(8,128)S(1)}, bf16[48,3200]{1,0:T(8,128)(2,1)S(1)}) custom-call(bf16[96,256]{1,0:T(8,128)(2,1)S(1)} %get-tuple-element.29.rest_ref, bf16[3200,256]{1,0:T(8,128)(2,1)S(1)} %copy-done), custom_call_target="tpu_custom_call" | custom-call | flops 157286400 | bytes 2560000 | tf_op jit(solution)/shard_map/pallas_call | solution.py:415
  28.0 0.6 %collective-permute-start.7 = (bf16[48,3200]{1,0:T(8,128)(2,1)S(1)}, bf16[48,3200]{1,0:T(8,128)(2,1)S(1)}, u32[]{:S(2)}, u32[]{:S(2)}) collective-permute-start(bf16[48,3200]{1,0:T(8,128)(2,1)S(1)} %get-tuple-element.31), channel_id=1, source_target_pairs={{0,8},{1,9},{8,0},{9,1},{16,24},{17,25},{24,16},{25,17},{2,10},{3,... | collective-permute-start | bytes 921608 | tf_op jit(solution)/shard_map/ppermute | solution.py:423
  28.6 0.1 collective-permute-done.8.other_ref
  28.7 2.5 %collective-permute-start.9 = (bf16[16,3200]{1,0:T(8,128)(2,1)S(1)}, bf16[16,3200]{1,0:T(8,128)(2,1)S(1)}, u32[]{:S(2)}, u32[]{:S(2)}) collective-permute-start(bf16[16,3200]{1,0:T(8,128)(2,1)S(1)} %shard_map.93), channel_id=1, source_target_pairs={{0,17},{1,16},{8,25},{9,24},{16,1},{17,0},{24,9},{25,8},{2,19},{3,... | collective-permute-start | bytes 307208 | tf_op jit(solution)/shard_map/ppermute | solution.py:426
  31.2 0.0 collective-permute-done.7.other_ref
  31.2 0.1 shard_map.92
  31.3 0.6 %collective-permute-start.10 = (bf16[16,3200]{1,0:T(8,128)(2,1)S(1)}, bf16[16,3200]{1,0:T(8,128)(2,1)S(1)}, u32[]{:S(2)}, u32[]{:S(2)}) collective-permute-start(bf16[16,3200]{1,0:T(8,128)(2,1)S(1)} %get-tuple-element.36), channel_id=1, source_target_pairs={{0,16},{1,17},{8,24},{9,25},{16,0},{17,1},{24,8},{25,9},{2,18},{3,... | collective-permute-start | bytes 307208 | tf_op jit(solution)/shard_map/ppermute | solution.py:436
  31.9 1.1 %collective-permute-start.11 = (bf16[16,3200]{1,0:T(8,128)(2,1)S(1)}, bf16[16,3200]{1,0:T(8,128)(2,1)S(1)}, u32[]{:S(2)}, u32[]{:S(2)}) collective-permute-start(bf16[16,3200]{1,0:T(8,128)(2,1)S(1)} %get-tuple-element.37), channel_id=1, source_target_pairs={{0,1},{1,0},{8,9},{9,8},{16,17},{17,16},{24,25},{25,24},{2,3},{3,2... | collective-permute-start | bytes 307208 | tf_op jit(solution)/shard_map/ppermute | solution.py:436
  32.9 2.4 %collective-permute-done.9.refs_0_ = bf16[16,3200]{1,0:T(8,128)(2,1)S(1)} collective-permute-done((bf16[16,3200]{1,0:T(8,128)(2,1)S(1)}, bf16[16,3200]{1,0:T(8,128)(2,1)S(1)}, u32[]{:S(2)}, u32[]{:S(2)}) %collective-permute-start.9) | collective-permute-done | bytes 102432 | tf_op jit(solution)/shard_map/ppermute | solution.py:426
  35.4 1.5 %collective-permute-done.10.refs_1_ = bf16[16,3200]{1,0:T(8,128)(2,1)S(1)} collective-permute-done((bf16[16,3200]{1,0:T(8,128)(2,1)S(1)}, bf16[16,3200]{1,0:T(8,128)(2,1)S(1)}, u32[]{:S(2)}, u32[]{:S(2)}) %collective-permute-start.10) | collective-permute-done | bytes 102432 | tf_op jit(solution)/shard_map/ppermute | solution.py:436
  36.8 0.1 collective-permute-done.11.refs_2_
  36.9 0.2 shard_map.94.refs_0_
  37.1 2.4 %collective-permute-start.16 = (bf16[16,3200]{1,0:T(8,128)(2,1)S(1)}, bf16[16,3200]{1,0:T(8,128)(2,1)S(1)}, u32[]{:S(2)}, u32[]{:S(2)}) collective-permute-start(bf16[16,3200]{1,0:T(8,128)(2,1)S(1)} %shard_map.94.refs_0_), channel_id=1, source_target_pairs={{0,17},{1,16},{8,25},{9,24},{16,1},{17,0},{24,9},{25,8},{2,19},{3,... | collective-permute-start | bytes 307208 | tf_op jit(solution)/shard_map/ppermute | solution.py:447
  39.5 0.7 %collective-permute-start.14 = (bf16[16,3200]{1,0:T(8,128)(2,1)S(1)}, bf16[16,3200]{1,0:T(8,128)(2,1)S(1)}, u32[]{:S(2)}, u32[]{:S(2)}) collective-permute-start(bf16[16,3200]{1,0:T(8,128)(2,1)S(1)} %shard_map.94.refs_0_), channel_id=1, source_target_pairs={{0,16},{1,17},{8,24},{9,25},{16,0},{17,1},{24,8},{25,9},{2,18},{3,... | collective-permute-start | bytes 307208 | tf_op jit(solution)/shard_map/ppermute | solution.py:447
  40.2 0.5 %collective-permute-start.12 = (bf16[16,3200]{1,0:T(8,128)(2,1)S(1)}, bf16[16,3200]{1,0:T(8,128)(2,1)S(1)}, u32[]{:S(2)}, u32[]{:S(2)}) collective-permute-start(bf16[16,3200]{1,0:T(8,128)(2,1)S(1)} %shard_map.94.refs_0_), channel_id=1, source_target_pairs={{0,1},{1,0},{8,9},{9,8},{16,17},{17,16},{24,25},{25,24},{2,3},{3,2... | collective-permute-start | bytes 307208 | tf_op jit(solution)/shard_map/ppermute | solution.py:447
  40.7 0.0 collective-permute-start.17
  40.7 2.9 %collective-permute-done.16.refs_3_ = bf16[16,3200]{1,0:T(8,128)(2,1)S(1)} collective-permute-done((bf16[16,3200]{1,0:T(8,128)(2,1)S(1)}, bf16[16,3200]{1,0:T(8,128)(2,1)S(1)}, u32[]{:S(2)}, u32[]{:S(2)}) %collective-permute-start.16) | collective-permute-done | bytes 102432 | tf_op jit(solution)/shard_map/ppermute | solution.py:447
  43.5 0.0 collective-permute-start.18
  43.5 1.4 %collective-permute-done.14.refs_2_ = bf16[16,3200]{1,0:T(8,128)(2,1)S(1)} collective-permute-done((bf16[16,3200]{1,0:T(8,128)(2,1)S(1)}, bf16[16,3200]{1,0:T(8,128)(2,1)S(1)}, u32[]{:S(2)}, u32[]{:S(2)}) %collective-permute-start.14) | collective-permute-done | bytes 102432 | tf_op jit(solution)/shard_map/ppermute | solution.py:447
  44.9 0.0 collective-permute-start.15
  44.9 0.2 collective-permute-done.12.refs_1_
  45.1 0.3 collective-permute-start.13
  45.4 0.9 %shard_map.95.refs_2_ = bf16[128,3200]{1,0:T(8,128)(2,1)} custom-call(bf16[16,3200]{1,0:T(8,128)(2,1)S(1)} %shard_map.94.refs_0_, bf16[16,3200]{1,0:T(8,128)(2,1)S(1)} %collective-permute-done.12.refs_1_, bf16[16,3200]{1,0:T(8,128)(2,1)S(1)} %collective-permute-done.14.refs_2_, bf16[16,3200]{1,0:T(8,128)(2,1)S(1)} %collective-permute-done.16.refs_3_, ...), custom_call_target="tpu_custom_call" | custom-call | bytes 1228800 | tf_op jit(solution)/shard_map/pallas_call | solution.py:454
  46.3 0.0 collective-permute-done.15.refs_1_
  46.3 0.1 collective-permute-done.13.refs_0_
  46.4 0.7 %shard_map.96 = bf16[128,3200]{1,0:T(8,128)(2,1)} custom-call(bf16[16,3200]{1,0:T(8,128)(2,1)S(1)} %collective-permute-done.13.refs_0_, bf16[16,3200]{1,0:T(8,128)(2,1)S(1)} %collective-permute-done.15.refs_1_, bf16[128,3200]{1,0:T(8,128)(2,1)} %shard_map.95.refs_2_), custom_call_target="tpu_custom_call", output_to_operand_aliasing={{}: (2, {})} | custom-call | bytes 409600 | tf_op jit(solution)/shard_map/pallas_call | solution.py:454
  (13 shorter events, 0.1 us)
Async XLA Ops:
  0.6 16.8 %copy-start.2 = (bf16[128,512]{1,0:T(8,128)(2,1)S(1)}, bf16[128,512]{1,0:T(8,128)(2,1)}, u32[]{:S(2)}) copy-start(bf16[128,512]{1,0:T(8,128)(2,1)} %g_ref.3) | copy-start | bytes 393220
  0.6 16.8 %copy-start.1 = (bf16[128,512]{1,0:T(8,128)(2,1)S(1)}, bf16[128,512]{1,0:T(8,128)(2,1)}, u32[]{:S(2)}) copy-start(bf16[128,512]{1,0:T(8,128)(2,1)} %q_ref.3) | copy-start | bytes 393220
  0.7 8.4 %collective-permute-start = (bf16[128,256]{1,0:T(8,128)(2,1)}, bf16[128,256]{1,0:T(8,128)(2,1)S(1)}, u32[]{:S(2)}, u32[]{:S(2)}) collective-permute-start(bf16[128,256]{1,0:T(8,128)(2,1)} %text_ref.1), channel_id=1, source_target_pairs={{0,6},{2,4},{4,0},{6,2},{1,7},{3,5},{5,1},{7,3},{8,14},{10,12},{12... | collective-permute-start | bytes 196616 | tf_op jit(solution)/shard_map/ppermute | solution.py:338
  5.8 0.7 %copy-start.3 = (f32[3200]{0:T(1024)S(1)}, f32[3200]{0:T(1024)}, u32[]{:S(2)}) copy-start(f32[3200]{0:T(1024)} %param.8) | copy-start | bytes 38404
  6.5 2.6 %copy-start.4 = (s32[8]{0:T(128)S(1)}, s32[8]{0:T(128)}, u32[]{:S(2)}) copy-start(s32[8]{0:T(128)} %param.10) | copy-start | bytes 100
  6.5 11.0 %copy-start.5 = (bf16[128,256]{1,0:T(8,128)(2,1)S(1)}, bf16[128,256]{1,0:T(8,128)(2,1)}, u32[]{:S(2)}) copy-start(bf16[128,256]{1,0:T(8,128)(2,1)} %text_ref.1) | copy-start | bytes 196612
  9.0 17.6 %copy-start = (bf16[3200,256]{1,0:T(8,128)(2,1)S(1)}, bf16[3200,256]{1,0:T(8,128)(2,1)}, u32[]{:S(2)}) copy-start(bf16[3200,256]{1,0:T(8,128)(2,1)} %proj_ref.3) | copy-start | bytes 4915204
  9.0 6.9 %collective-permute-start.1 = (bf16[128,256]{1,0:T(8,128)(2,1)S(1)}, bf16[128,256]{1,0:T(8,128)(2,1)S(1)}, u32[]{:S(2)}, u32[]{:S(2)}) collective-permute-start(bf16[128,256]{1,0:T(8,128)(2,1)S(1)} %get-tuple-element.20.image_ref), channel_id=1, source_target_pairs={{6,0},{4,2},{0,4},{2,6},{7,1},{5,3},{1,5},{3,7},{14,8},{12,10},{8,... | collective-permute-start | bytes 196616 | tf_op jit(solution)/shard_map/ppermute | solution.py:359
  9.3 6.6 %collective-permute-start.3 = (bf16[128,256]{1,0:T(8,128)(2,1)S(1)}, bf16[128,256]{1,0:T(8,128)(2,1)S(1)}, u32[]{:S(2)}, u32[]{:S(2)}) collective-permute-start(bf16[128,256]{1,0:T(8,128)(2,1)S(1)} %shard_map.87.own_ref), channel_id=1, source_target_pairs={{0,6},{2,0},{4,2},{6,4},{1,7},{3,1},{5,3},{7,5},{8,14},{10,8},{12,... | collective-permute-start | bytes 196616 | tf_op jit(solution)/shard_map/ppermute | solution.py:368
  13.2 4.3 %collective-permute-start.2 = (bf16[128,256]{1,0:T(8,128)(2,1)S(1)}, bf16[128,256]{1,0:T(8,128)(2,1)S(1)}, u32[]{:S(2)}, u32[]{:S(2)}) collective-permute-start(bf16[128,256]{1,0:T(8,128)(2,1)S(1)} %shard_map.87.own_ref), channel_id=1, source_target_pairs={{0,4},{2,0},{4,6},{6,2},{1,5},{3,1},{5,7},{7,3},{8,12},{10,8},{12,... | collective-permute-start | bytes 196616 | tf_op jit(solution)/shard_map/ppermute | solution.py:368
  18.8 6.0 %collective-permute-start.4 = (bf16[128,256]{1,0:T(8,128)(2,1)S(1)}, bf16[128,256]{1,0:T(8,128)(2,1)S(1)}, u32[]{:S(2)}, u32[]{:S(2)}) collective-permute-start(bf16[128,256]{1,0:T(8,128)(2,1)S(1)} %get-tuple-element.26), channel_id=1, source_target_pairs={{0,4},{2,6},{4,0},{6,2},{1,5},{3,7},{5,1},{7,3},{8,12},{10,14},{12... | collective-permute-start | bytes 196616 | tf_op jit(solution)/shard_map/ppermute | solution.py:400
  20.5 6.1 %collective-permute-start.5 = (bf16[128,256]{1,0:T(8,128)(2,1)S(1)}, bf16[128,256]{1,0:T(8,128)(2,1)S(1)}, u32[]{:S(2)}, u32[]{:S(2)}) collective-permute-start(bf16[128,256]{1,0:T(8,128)(2,1)S(1)} %get-tuple-element.27), channel_id=1, source_target_pairs={{0,6},{2,4},{4,2},{6,0},{1,7},{3,5},{5,3},{7,1},{8,14},{10,12},{12... | collective-permute-start | bytes 196616 | tf_op jit(solution)/shard_map/ppermute | solution.py:400
  21.6 5.0 %collective-permute-start.6 = (bf16[128,256]{1,0:T(8,128)(2,1)S(1)}, bf16[128,256]{1,0:T(8,128)(2,1)S(1)}, u32[]{:S(2)}, u32[]{:S(2)}) collective-permute-start(bf16[128,256]{1,0:T(8,128)(2,1)S(1)} %get-tuple-element.28), channel_id=1, source_target_pairs={{0,2},{2,0},{4,6},{6,4},{1,3},{3,1},{5,7},{7,5},{8,10},{10,8},{12,... | collective-permute-start | bytes 196616 | tf_op jit(solution)/shard_map/ppermute | solution.py:400
  27.3 1.4 %collective-permute-start.8 = (bf16[16,3200]{1,0:T(8,128)(2,1)S(1)}, bf16[16,3200]{1,0:T(8,128)(2,1)S(1)}, u32[]{:S(2)}, u32[]{:S(2)}) collective-permute-start(bf16[16,3200]{1,0:T(8,128)(2,1)S(1)} %get-tuple-element.35), channel_id=1, source_target_pairs={{0,8},{1,9},{8,0},{9,1},{16,24},{17,25},{24,16},{25,17},{2,10},{3,... | collective-permute-start | bytes 307208 | tf_op jit(solution)/shard_map/ppermute | solution.py:413
  28.0 3.2 %collective-permute-start.7 = (bf16[48,3200]{1,0:T(8,128)(2,1)S(1)}, bf16[48,3200]{1,0:T(8,128)(2,1)S(1)}, u32[]{:S(2)}, u32[]{:S(2)}) collective-permute-start(bf16[48,3200]{1,0:T(8,128)(2,1)S(1)} %get-tuple-element.31), channel_id=1, source_target_pairs={{0,8},{1,9},{8,0},{9,1},{16,24},{17,25},{24,16},{25,17},{2,10},{3,... | collective-permute-start | bytes 921608 | tf_op jit(solution)/shard_map/ppermute | solution.py:423
  28.7 6.7 %collective-permute-start.9 = (bf16[16,3200]{1,0:T(8,128)(2,1)S(1)}, bf16[16,3200]{1,0:T(8,128)(2,1)S(1)}, u32[]{:S(2)}, u32[]{:S(2)}) collective-permute-start(bf16[16,3200]{1,0:T(8,128)(2,1)S(1)} %shard_map.93), channel_id=1, source_target_pairs={{0,17},{1,16},{8,25},{9,24},{16,1},{17,0},{24,9},{25,8},{2,19},{3,... | collective-permute-start | bytes 307208 | tf_op jit(solution)/shard_map/ppermute | solution.py:426
  31.3 5.6 %collective-permute-start.10 = (bf16[16,3200]{1,0:T(8,128)(2,1)S(1)}, bf16[16,3200]{1,0:T(8,128)(2,1)S(1)}, u32[]{:S(2)}, u32[]{:S(2)}) collective-permute-start(bf16[16,3200]{1,0:T(8,128)(2,1)S(1)} %get-tuple-element.36), channel_id=1, source_target_pairs={{0,16},{1,17},{8,24},{9,25},{16,0},{17,1},{24,8},{25,9},{2,18},{3,... | collective-permute-start | bytes 307208 | tf_op jit(solution)/shard_map/ppermute | solution.py:436
  31.9 5.0 %collective-permute-start.11 = (bf16[16,3200]{1,0:T(8,128)(2,1)S(1)}, bf16[16,3200]{1,0:T(8,128)(2,1)S(1)}, u32[]{:S(2)}, u32[]{:S(2)}) collective-permute-start(bf16[16,3200]{1,0:T(8,128)(2,1)S(1)} %get-tuple-element.37), channel_id=1, source_target_pairs={{0,1},{1,0},{8,9},{9,8},{16,17},{17,16},{24,25},{25,24},{2,3},{3,2... | collective-permute-start | bytes 307208 | tf_op jit(solution)/shard_map/ppermute | solution.py:436
  37.1 6.4 %collective-permute-start.16 = (bf16[16,3200]{1,0:T(8,128)(2,1)S(1)}, bf16[16,3200]{1,0:T(8,128)(2,1)S(1)}, u32[]{:S(2)}, u32[]{:S(2)}) collective-permute-start(bf16[16,3200]{1,0:T(8,128)(2,1)S(1)} %shard_map.94.refs_0_), channel_id=1, source_target_pairs={{0,17},{1,16},{8,25},{9,24},{16,1},{17,0},{24,9},{25,8},{2,19},{3,... | collective-permute-start | bytes 307208 | tf_op jit(solution)/shard_map/ppermute | solution.py:447
  39.5 5.4 %collective-permute-start.14 = (bf16[16,3200]{1,0:T(8,128)(2,1)S(1)}, bf16[16,3200]{1,0:T(8,128)(2,1)S(1)}, u32[]{:S(2)}, u32[]{:S(2)}) collective-permute-start(bf16[16,3200]{1,0:T(8,128)(2,1)S(1)} %shard_map.94.refs_0_), channel_id=1, source_target_pairs={{0,16},{1,17},{8,24},{9,25},{16,0},{17,1},{24,8},{25,9},{2,18},{3,... | collective-permute-start | bytes 307208 | tf_op jit(solution)/shard_map/ppermute | solution.py:447
  40.2 4.9 %collective-permute-start.12 = (bf16[16,3200]{1,0:T(8,128)(2,1)S(1)}, bf16[16,3200]{1,0:T(8,128)(2,1)S(1)}, u32[]{:S(2)}, u32[]{:S(2)}) collective-permute-start(bf16[16,3200]{1,0:T(8,128)(2,1)S(1)} %shard_map.94.refs_0_), channel_id=1, source_target_pairs={{0,1},{1,0},{8,9},{9,8},{16,17},{17,16},{24,25},{25,24},{2,3},{3,2... | collective-permute-start | bytes 307208 | tf_op jit(solution)/shard_map/ppermute | solution.py:447
  40.7 4.7 %collective-permute-start.17 = (bf16[16,3200]{1,0:T(8,128)(2,1)S(1)}, bf16[16,3200]{1,0:T(8,128)(2,1)S(1)}, u32[]{:S(2)}, u32[]{:S(2)}) collective-permute-start(bf16[16,3200]{1,0:T(8,128)(2,1)S(1)} %shard_map.94.refs_0_), channel_id=1, source_target_pairs={{0,8},{1,9},{8,0},{9,1},{16,24},{17,25},{24,16},{25,17},{2,10},{3,... | collective-permute-start | bytes 307208 | tf_op jit(solution)/shard_map/ppermute | solution.py:448
  43.5 1.9 %collective-permute-start.18 = (bf16[16,3200]{1,0:T(8,128)(2,1)S(1)}, bf16[16,3200]{1,0:T(8,128)(2,1)S(1)}, u32[]{:S(2)}, u32[]{:S(2)}) collective-permute-start(bf16[16,3200]{1,0:T(8,128)(2,1)S(1)} %collective-permute-done.16.refs_3_), channel_id=1, source_target_pairs={{0,8},{1,9},{8,0},{9,1},{16,24},{17,25},{24,16},{25,17},{2,10},{3,... | collective-permute-start | bytes 307208 | tf_op jit(solution)/shard_map/ppermute | solution.py:448
  44.9 1.4 %collective-permute-start.15 = (bf16[16,3200]{1,0:T(8,128)(2,1)S(1)}, bf16[16,3200]{1,0:T(8,128)(2,1)S(1)}, u32[]{:S(2)}, u32[]{:S(2)}) collective-permute-start(bf16[16,3200]{1,0:T(8,128)(2,1)S(1)} %collective-permute-done.14.refs_2_), channel_id=1, source_target_pairs={{0,8},{1,9},{8,0},{9,1},{16,24},{17,25},{24,16},{25,17},{2,10},{3,... | collective-permute-start | bytes 307208 | tf_op jit(solution)/shard_map/ppermute | solution.py:448
  45.1 1.3 %collective-permute-start.13 = (bf16[16,3200]{1,0:T(8,128)(2,1)S(1)}, bf16[16,3200]{1,0:T(8,128)(2,1)S(1)}, u32[]{:S(2)}, u32[]{:S(2)}) collective-permute-start(bf16[16,3200]{1,0:T(8,128)(2,1)S(1)} %collective-permute-done.12.refs_1_), channel_id=1, source_target_pairs={{0,8},{1,9},{8,0},{9,1},{16,24},{17,25},{24,16},{25,17},{2,10},{3,... | collective-permute-start | bytes 307208 | tf_op jit(solution)/shard_map/ppermute | solution.py:448
